TPU v7x, 32 devices: a whole 2x2x4 slice. The times are simulated.
32 devices in a mesh: batch: 8 (over z, core), proto: 4 (over y, x).
Axes of the slice: x: 2, y: 2, z: 4, core: 2. Of those that a mesh axis runs over, the one named last changes fastest.
Arguments:
- slow_embed: bfloat16 [8192, 256], P('batch'), may hold values from -1 to 1
- fast_embed: bfloat16 [8192, 256], P('batch'), may hold values from -1 to 1
- prototypes: float32 [8192, 256], P('proto'), may hold values from -1 to 1
Outputs:
- proto_grad: float32 [8192, 256], P('proto')
- slow_grad: float32 [8192, 256], P('batch')
- fast_grad: float32 [8192, 256], P('batch')
All inputs are finite; a program needn't handle non-finite values.
Results may differ from a plain program's by a relative error of at most 0.0005.
The roundings to bfloat16 on the way count: a program that leaves them out, or rounds other values in their place, can miss the bound.
Values sent between devices are 32-bit elements; how exact they have to be, the bound alone decides.
No kernel may reach another device: no remote copies, remote signals or barrier semaphores. Data moves between devices by JAX's collectives and lax.ppermute only.
A program may use at most 128 MiB of HBM per device.

v0:
```python
import jax
import jax.numpy as jnp
from jax import lax
from jax.sharding import PartitionSpec as P

ITERS = 3


CODE_EPS = 0.05
TEMPER = 0.1
NORM_EPS = 1e-06


def normalize(raw_rows):
    lengths = jnp.sqrt(jnp.sum(raw_rows * raw_rows, axis=-1, keepdims=True) + 1e-12)
    return (raw_rows / lengths, lengths)


def project_back(grad_unit, unit_vec, lengths):
    along = jnp.sum(unit_vec * grad_unit, axis=-1, keepdims=True)
    return (grad_unit - unit_vec * along) / lengths


def row_total(row_terms):
    return lax.psum(row_terms, "proto")


def normalizers(proto_square, embed_square, proto_entries, embed_entries):
    totals = lax.psum((proto_square, embed_square), ("batch", "proto"))
    proto_factor = lax.rsqrt(totals[0] / proto_entries + NORM_EPS)
    embed_factor = lax.rsqrt(totals[1] / embed_entries + NORM_EPS)
    return (proto_factor, embed_factor)


def body(slow_embed, fast_embed, prototypes):
    clip_dev = slow_embed.shape[0]
    proto_dev = prototypes.shape[0]
    feat_width = prototypes.shape[1]
    batch_count = lax.axis_size("batch")
    proto_count = lax.axis_size("proto")
    clips_all = clip_dev * batch_count
    protos_all = proto_dev * proto_count
    proto_entries = float(protos_all * feat_width)
    embed_entries = float(2 * clips_all * feat_width)
    raw_views = jnp.stack([slow_embed, fast_embed]).astype(jnp.float32)
    unit_vec, lengths = normalize(raw_views)
    unit_b = unit_vec.astype(jnp.bfloat16)
    proto_unit, proto_len = normalize(prototypes)
    proto_b = proto_unit.astype(jnp.bfloat16)
    scores = jnp.einsum("vbd,kd->vbk", unit_b, proto_b, preferred_element_type=jnp.float32)
    code_table = jnp.exp(scores / CODE_EPS)
    soft_exp = jnp.exp(scores / TEMPER)
    denom_terms = jnp.sum(soft_exp, axis=2)
    denominator = lax.psum(denom_terms, "proto")
    clip_scale = jnp.ones((2, clip_dev), jnp.float32)
    for iteration in range(ITERS):
        col_total = lax.psum(jnp.sum(code_table * clip_scale[:, :, None], axis=1), "batch")
        proto_scale = 1.0 / (protos_all * col_total)
        row_terms = jnp.sum(code_table * proto_scale[:, None, :], axis=2)
        if iteration == 0:
            clip_total = row_total(row_terms)
        else:
            clip_total = row_total(row_terms)
        clip_scale = 1.0 / (clips_all * clip_total)
    codes = code_table * proto_scale[:, None, :] / clip_total[:, :, None]
    probs = soft_exp / denominator[:, :, None]
    score_grad = (jnp.stack([probs[0] - codes[1], probs[1] - codes[0]]) / TEMPER).astype(
        jnp.bfloat16
    )
    proto_rows = proto_dev // batch_count
    piece = score_grad
    grad_proto_share = lax.psum_scatter(
        jnp.einsum("vbk,vbd->kd", piece, unit_b, preferred_element_type=jnp.float32),
        "batch",
        scatter_dimension=0,
        tiled=True,
    )
    proto_first = lax.axis_index("batch") * proto_rows
    unit_share = lax.dynamic_slice_in_dim(proto_unit, proto_first, proto_rows, 0)
    len_share = lax.dynamic_slice_in_dim(proto_len, proto_first, proto_rows, 0)
    grad_proto = project_back(grad_proto_share, unit_share, len_share)
    clip_rows = clip_dev // proto_count
    piece = score_grad
    result = jnp.einsum("vbk,kd->bvd", piece, proto_b, preferred_element_type=jnp.float32)
    grad_flat = lax.psum_scatter(
        result.reshape(lax.axis_size("proto") * clip_rows, 2 * feat_width),
        "proto",
        scatter_dimension=0,
        tiled=True,
    )
    grad_unit = grad_flat.reshape(clip_rows, 2, feat_width)
    clip_first = lax.axis_index("proto") * clip_rows
    view_share = jnp.transpose(
        lax.dynamic_slice_in_dim(unit_vec, clip_first, clip_rows, 1), (1, 0, 2)
    )
    view_len = jnp.transpose(lax.dynamic_slice_in_dim(lengths, clip_first, clip_rows, 1), (1, 0, 2))
    grad_embed = project_back(grad_unit, view_share, view_len)
    proto_factor, embed_factor = normalizers(
        jnp.sum(grad_proto * grad_proto),
        jnp.sum(grad_embed * grad_embed),
        proto_entries,
        embed_entries,
    )
    proto_grad = lax.all_gather(grad_proto * proto_factor, "batch", axis=0, tiled=True)
    scaled_flat = (grad_embed * embed_factor).reshape(clip_rows, 2 * feat_width)
    gathered = lax.all_gather(scaled_flat, "proto", axis=0, tiled=True).reshape(
        clip_dev, 2, feat_width
    )
    slow_grad = gathered[:, 0, :]
    fast_grad = gathered[:, 1, :]
    return (proto_grad, slow_grad, fast_grad)


def solution(mesh):
    placed = (P("batch", None), P("batch", None), P("proto", None))
    return jax.shard_map(
        body,
        mesh=mesh,
        in_specs=placed,
        out_specs=(P("proto", None), P("batch", None), P("batch", None)),
        check_vma=False,
    )
```

profile of v0, /device:TPU:0, one launch (start us, length us, event | category | flops | bytes accessed | tf_op | source)
XLA Modules:
  0.0 414.2 jit_solution(4479811090819333001)
XLA Ops:
  7.2 1.9 multiply_reduce_fusion.5
  9.2 1.9 broadcast_divide_fusion
  11.1 1.2 copy.9
  12.4 1.2 copy.8
  13.9 7.4 %fusion.4 = (f32[2,2048]{1,0:T(2,128)S(1)}, f32[2,1024,2048]{2,1,0:T(8,128)}) fusion(f32[2048,256]{1,0:T(8,128)S(1)} %broadcast_divide_fusion, f32[2,1024]{1,0:T(2,128)S(1)} %add_sqrt_fusion.1, bf16[1,1024,256]{1,2,0:T(8,128)(2,1)S(1)} %bitcast.38, bf16[1,1024,256]{1,2,0:T(8,128)(2,1)S(1)} %bitcast.42), kind=kOutput, calls=%fused_computation.15 | convolution fusion | flops 2158489600 | bytes 19947520 | tf_op jit(solution)/shard_map/vbd,kd->vbk/dot_general | solution.py:50
  21.3 30.2 %psum.64 = f32[2,2048]{1,0:T(2,128)S(1)} all-reduce(f32[2,2048]{1,0:T(2,128)S(1)} %get-tuple-element.20), channel_id=1, replica_groups=mesh['batch'=8,'proto'=4] {'batch'}, use_global_device_ids=true, to_apply=%region_5.0 | all-reduce | flops 4096 | bytes 32768 | tf_op jit(solution)/shard_map/psum | solution.py:57
  51.6 9.0 %fusion.3 = (f32[2,1024]{1,0:T(2,128)S(1)}, f32[2,1024]{1,0:T(2,128)S(1)}) fusion(f32[2,1024,2048]{2,1,0:T(8,128)} %get-tuple-element.21, f32[2,2048]{1,0:T(2,128)S(1)} %multiply_divide_fusion.3), kind=kLoop, calls=%fused_computation.12 | loop fusion | flops 20967424 | bytes 16809984 | tf_op jit(solution)/shard_map/reduce_sum | solution.py:53
  60.6 10.1 %psum.65 = f32[2,1024]{1,0:T(2,128)S(1)} all-reduce(f32[2,1024]{1,0:T(2,128)S(1)} %get-tuple-element.7), channel_id=1, replica_groups=mesh['batch'=8,'proto'=4] {'proto'}, use_global_device_ids=true, to_apply=%region_7.0 | all-reduce | flops 2048 | bytes 16384 | tf_op jit(solution)/shard_map/psum | solution.py:25
  70.7 7.4 %multiply_reduce_fusion.2 = f32[2,2048]{1,0:T(2,128)S(1)} fusion(f32[2,1024]{1,0:T(2,128)S(1)} %multiply_divide_fusion.5, f32[2,1024,2048]{2,1,0:T(8,128)} %get-tuple-element.21), kind=kLoop, calls=%fused_computation.5 | loop fusion | flops 12578816 | bytes 16801792 | tf_op jit(solution)/shard_map/reduce_sum | solution.py:57
  78.0 25.9 %psum.66 = f32[2,2048]{1,0:T(2,128)S(1)} all-reduce(f32[2,2048]{1,0:T(2,128)S(1)} %multiply_reduce_fusion.2), channel_id=1, replica_groups=mesh['batch'=8,'proto'=4] {'batch'}, use_global_device_ids=true, to_apply=%region_9.0 | all-reduce | flops 4096 | bytes 32768 | tf_op jit(solution)/shard_map/psum | solution.py:57
  103.9 8.6 %multiply_reduce_fusion.1 = f32[2,1024]{1,0:T(2,128)S(1)} fusion(f32[2,2048]{1,0:T(2,128)S(1)} %multiply_divide_fusion.2, f32[2,1024,2048]{2,1,0:T(8,128)} %get-tuple-element.21), kind=kLoop, calls=%fused_computation.4 | loop fusion | flops 12580864 | bytes 16801792 | tf_op jit(solution)/shard_map/reduce_sum | solution.py:59
  112.5 8.1 %psum.67 = f32[2,1024]{1,0:T(2,128)S(1)} all-reduce(f32[2,1024]{1,0:T(2,128)S(1)} %multiply_reduce_fusion.1), channel_id=1, replica_groups=mesh['batch'=8,'proto'=4] {'proto'}, use_global_device_ids=true, to_apply=%region_11.0 | all-reduce | flops 2048 | bytes 16384 | tf_op jit(solution)/shard_map/psum | solution.py:25
  120.6 7.4 %multiply_reduce_fusion = f32[2,2048]{1,0:T(2,128)S(1)} fusion(f32[2,1024]{1,0:T(2,128)S(1)} %multiply_divide_fusion.4, f32[2,1024,2048]{2,1,0:T(8,128)} %get-tuple-element.21), kind=kLoop, calls=%fused_computation.3 | loop fusion | flops 12578816 | bytes 16801792 | tf_op jit(solution)/shard_map/reduce_sum | solution.py:57
  128.0 26.1 %psum.68 = f32[2,2048]{1,0:T(2,128)S(1)} all-reduce(f32[2,2048]{1,0:T(2,128)S(1)} %multiply_reduce_fusion), channel_id=1, replica_groups=mesh['batch'=8,'proto'=4] {'batch'}, use_global_device_ids=true, to_apply=%region_13.0 | all-reduce | flops 4096 | bytes 32768 | tf_op jit(solution)/shard_map/psum | solution.py:57
  154.1 8.6 %multiply_reduce_fusion.4 = f32[2,1024]{1,0:T(2,128)S(1)} fusion(f32[2,2048]{1,0:T(2,128)S(1)} %multiply_divide_fusion.1, f32[2,1024,2048]{2,1,0:T(8,128)} %get-tuple-element.21), kind=kLoop, calls=%fused_computation.10 | loop fusion | flops 12580864 | bytes 16801792 | tf_op jit(solution)/shard_map/reduce_sum | solution.py:59
  162.7 15.2 %all-reduce.1 = (f32[2,1024]{1,0:T(2,128)S(1)}, f32[2,1024]{1,0:T(2,128)S(1)}) all-reduce(f32[2,1024]{1,0:T(2,128)S(1)} %multiply_reduce_fusion.4, f32[2,1024]{1,0:T(2,128)S(1)} %get-tuple-element.6), channel_id=1, replica_groups=mesh['batch'=8,'proto'=4] {'proto'}, use_global_device_ids=true, to_apply=%region_15.0 | all-reduce | flops 4096 | bytes 32768 | tf_op jit(solution)/shard_map/psum | solution.py:25
  177.8 18.3 %fusion.2 = (f32[2,1024,2048]{2,1,0:T(8,128)}, f32[2,1024,2048]{2,1,0:T(8,128)}) fusion(f32[2,1024,2048]{2,1,0:T(8,128)} %get-tuple-element.21, f32[2,1024]{1,0:T(2,128)S(1)} %get-tuple-element.11, f32[2,1024]{1,0:T(2,128)S(1)} %get-tuple-element.10, f32[2,2048]{1,0:T(2,128)S(1)} %multiply_divide_fusion.1), kind=kLoop, calls=%fused_computation.11 | loop fusion | flops 20971520 | bytes 50364416 | tf_op jit(solution)/shard_map/div | solution.py:66
  196.1 19.1 %slice_subtract_fusion.1 = (f32[1,1024,2048]{2,1,0:T(8,128)}, f32[1,1024,2048]{2,1,0:T(8,128)}) fusion(f32[2,1024,2048]{2,1,0:T(8,128)} %get-tuple-element.17, f32[2,1024,2048]{2,1,0:T(8,128)} %get-tuple-element.16), kind=kLoop, calls=%fused_computation.14 | loop fusion | flops 4194304 | bytes 50331648 | tf_op jit(solution)/shard_map/sub | solution.py:67
  215.2 8.5 %fusion.9 = f32[256,2,1024]{2,0,1:T(8,128)} fusion(f32[2048,256]{1,0:T(8,128)S(1)} %broadcast_divide_fusion, f32[1,1024,2048]{2,1,0:T(8,128)} %get-tuple-element.15, f32[1,1024,2048]{2,1,0:T(8,128)} %get-tuple-element.14), kind=kOutput, calls=%fused_computation.27 | convolution fusion | flops 2160590848 | bytes 20971520 | tf_op jit(solution)/shard_map/vbk,kd->bvd/dot_general | solution.py:84
  223.8 8.9 %convolution_bitcast_fusion = f32[2048,256]{1,0:T(8,128)} fusion(f32[1,1024,2048]{2,1,0:T(8,128)} %get-tuple-element.15, f32[1,1024,2048]{2,1,0:T(8,128)} %get-tuple-element.14, f32[2,1024]{1,0:T(2,128)S(1)} %add_sqrt_fusion.1, bf16[1,1024,256]{1,2,0:T(8,128)(2,1)S(1)} %bitcast.39, bf16[1,1024,256]{1,2,0:T(8,128)(2,1)S(1)} %bitcast.43), kind=kOutput, calls=%fused_computation.16 | convolution fusion | flops 2162163712 | bytes 19931136 | tf_op jit(solution)/shard_map/vbk,vbd->kd/dot_general | solution.py:73
  232.9 1.6 convert_divide_fusion
  234.5 21.8 %reduce-scatter.5.cloned.1.call-done = f32[256,512]{0,1:T(8,128)} async-done(((f32[1024,512]{0,1:T(8,128)}), f32[256,512]{0,1:T(8,128)}) %reduce-scatter.5.cloned.1.call-update) | async-done | bytes 524304 | tf_op jit(solution)/shard_map/reduce_scatter | solution.py:85
  256.3 2.4 multiply_reduce_fusion.6
  258.6 36.4 %reduce-scatter.3.cloned.1.call-done = f32[256,256]{1,0:T(8,128)} async-done(((f32[2048,256]{1,0:T(8,128)}), f32[256,256]{1,0:T(8,128)}) %reduce-scatter.3.cloned.1.call-update) | async-done | bytes 262160 | tf_op jit(solution)/shard_map/reduce_scatter | solution.py:72
  296.1 1.7 multiply_reduce_fusion.7
  297.9 38.0 %all-reduce = (f32[]{:T(128)}, f32[]{:T(128)}) all-reduce(f32[]{:T(128)} %get-tuple-element.12, f32[]{:T(128)} %get-tuple-element.22), channel_id=1, replica_groups=mesh['batch'=8,'proto'=4] {'batch','proto'}, use_global_device_ids=true, to_apply=%region_19.0 | all-reduce | flops 2 | bytes 16 | tf_op jit(solution)/shard_map/psum | solution.py:29
  338.9 34.5 %all-gather.5.cloned.1.call-done = f32[1024,512]{0,1:T(8,128)} async-done(((f32[256,512]{0,1:T(8,128)}), f32[1024,512]{0,1:T(8,128)}) %all-gather.5.cloned.1.call-update) | async-done | bytes 2097168 | tf_op jit(solution)/shard_map/all_gather | solution.py:106
  373.4 1.7 slice_bitcast_fusion
  375.0 1.3 copy.14
  376.4 1.3 copy.15
  377.7 27.0 %all-gather.3.cloned.1.call-done = f32[2048,256]{1,0:T(8,128)} async-done(((f32[256,256]{1,0:T(8,128)}), f32[2048,256]{1,0:T(8,128)}) %all-gather.3.cloned.1.call-update) | async-done | bytes 2097168 | tf_op jit(solution)/shard_map/all_gather | solution.py:104
  404.6 3.0 copy.22
  (21 shorter events, 3.3 us)
Async XLA Ops:
  7.2 249.1 %reduce-scatter.5.cloned.1.call-start = ((), (), s32[]{:S(2)}) async-start(), calls=%async_computation.4 | async-start | bytes 2621440 | tf_op jit(solution)/shard_map/reduce_scatter | solution.py:85
  223.8 71.3 %reduce-scatter.3.cloned.1.call-start = ((), (), s32[]{:S(2)}) async-start(), calls=%async_computation.2 | async-start | bytes 2359296 | tf_op jit(solution)/shard_map/reduce_scatter | solution.py:72
  232.7 140.6 %all-gather.5.cloned.1.call-start = ((), (), s32[]{:S(2)}) async-start(), calls=%async_computation.5 | async-start | bytes 2621440 | tf_op jit(solution)/shard_map/all_gather | solution.py:106
  337.4 67.2 %all-gather.3.cloned.1.call-start = ((), (), s32[]{:S(2)}) async-start(), calls=%async_computation.3 | async-start | bytes 2359296 | tf_op jit(solution)/shard_map/all_gather | solution.py:104
Sparse Core Ops, SparseCore 0:
  223.9 32.3 reduce-scatter.4
  259.2 35.7 reduce-scatter.2
  337.5 35.7 all-gather.4
  375.5 29.0 all-gather.2
where the time goes:
time: 415 us; the launch traced here: 414 us
  blocking collectives  154 us (37%)
  waiting for transfers between devices  120 us (29%)
  other arithmetic  90.8 us (22%)
  matrix products  24.8 us (6%)
  between operations  15.3 us (4%)
  local copies, waits for them, and re-layouts  9.91 us (2%)
    psum x3, blocking collectives, body(): lax.psum(jnp.sum(code_table * clip_scale[:, :, None], axis=1), 'batch')  82.2 us
    psum x1, blocking collectives, normalizers(): totals = lax.psum((proto_square, embed_square), ('batch', 'proto'))  38 us
    reduce_scatter x1, waiting for transfers between devices, body(): lax.psum_scatter(jnp.einsum('vbk,vbd->kd', piece, unit_b, preferred_eleme...  36.4 us
    all_gather x1, waiting for transfers between devices, body(): lax.all_gather(scaled_flat, 'proto', axis=0, tiled=True)  34.5 us
    psum x3, blocking collectives, row_total(): return lax.psum(row_terms, 'proto')  33.3 us
    all_gather x1, waiting for transfers between devices, body(): lax.all_gather(grad_proto * proto_factor, 'batch', axis=0, tiled=True)  27 us
    reduce_scatter x1, waiting for transfers between devices, body(): lax.psum_scatter(result.reshape(lax.axis_size('proto') * clip_rows, 2 * f...  21.8 us
    sub x1, other arithmetic, body(): probs[0] - codes[1]  19.1 us
  transfers between devices with their start and end apart: 4, of which 4 were waited for; matrix products, arithmetic and copies ran while one was open for 4% of the time, Pallas kernels for 0%

commit v1 on v0

v1 whole, which is shorter than its diff:
```python
import functools

import jax
import jax.numpy as jnp
from jax import lax
from jax.experimental import pallas as pl
from jax.experimental.pallas import tpu as pltpu
from jax.sharding import PartitionSpec as P

ITERS = 3


CODE_EPS = 0.05
TEMPER = 0.1
NORM_EPS = 1e-06
LANES = 128
MIB = 1024 * 1024


def vmem_spec():
    return pl.BlockSpec(memory_space=pltpu.VMEM)


def params(limit):
    return pltpu.CompilerParams(vmem_limit_bytes=limit * MIB)


def to_columns(line):
    return jnp.broadcast_to(line, (LANES, LANES)).T


def to_line(partial):
    return jnp.sum(partial.T, axis=0, keepdims=True)


def lane_sum(block):
    total = block[:, :LANES]
    for j in range(1, block.shape[1] // LANES):
        total = total + block[:, j * LANES : (j + 1) * LANES]
    return total


def row_fold(block):
    return jnp.sum(block.reshape(block.shape[0] // 8, 8, block.shape[1]), axis=0)


def score_kernel(slow, fast, protos, t_ref, col_ref, den_ref, ub_ref, ubt_ref, cb_ref, den_s):
    clips, feats = slow.shape
    count = protos.shape[0]
    for v, src in enumerate((slow, fast)):
        for first in range(0, clips, 256):
            rows = pl.ds(first, 256)
            x = src[rows, :].astype(jnp.float32)
            length = jnp.sqrt(jnp.sum(x * x, axis=-1, keepdims=True) + 1e-12)
            u = x / length
            ub_ref[v, rows, :] = u.astype(jnp.bfloat16)
            ubt_ref[v, :, rows] = u.T.astype(jnp.bfloat16)

    def proto_rows(i, _):
        rows = pl.ds(pl.multiple_of(i * 256, 256), 256)
        w = protos[rows, :]
        length = jnp.sqrt(jnp.sum(w * w, axis=-1, keepdims=True) + 1e-12)
        cb_ref[rows, :] = (w / length).astype(jnp.bfloat16)
        return 0

    lax.fori_loop(0, count // 256, proto_rows, 0)
    den_s[...] = jnp.zeros_like(den_s)

    def chunk(j, _):
        first = pl.multiple_of(j * 256, 256)
        weights = cb_ref[pl.ds(first, 256), :]
        for v in range(2):
            cols = jnp.zeros((8, 256), jnp.float32)
            for r in range(0, clips, LANES):
                rows = pl.ds(r, LANES)
                s = lax.dot_general(
                    ub_ref[v, rows, :],
                    weights,
                    (((1,), (1,)), ((), ())),
                    preferred_element_type=jnp.float32,
                )
                t = jnp.exp(s * (1.0 / TEMPER))
                t_ref[v, rows, pl.ds(first, 256)] = t
                cols = cols + row_fold(t * t)
                den_s[v, rows, :] += lane_sum(t)
            line = jnp.sum(cols, axis=0, keepdims=True)
            for h in range(2):
                col_ref[pl.ds(v * (count // LANES) + j * 2 + h, 1), :] = line[
                    :, h * LANES : (h + 1) * LANES
                ]
        return 0

    lax.fori_loop(0, count // 256, chunk, 0)
    groups = clips // LANES
    for v in range(2):
        for i in range(groups):
            den_ref[pl.ds(v * groups + i, 1), :] = to_line(den_s[v, i * LANES : (i + 1) * LANES, :])


def scores(slow, fast, protos):
    clips, feats = slow.shape
    count = protos.shape[0]
    return pl.pallas_call(
        score_kernel,
        out_shape=(
            pltpu.VMEM((2, clips, count), jnp.float32),
            jax.ShapeDtypeStruct((2 * count // LANES, LANES), jnp.float32),
            jax.ShapeDtypeStruct((2 * clips // LANES, LANES), jnp.float32),
            jax.ShapeDtypeStruct((2, clips, feats), jnp.bfloat16),
            jax.ShapeDtypeStruct((2, feats, clips), jnp.bfloat16),
            jax.ShapeDtypeStruct((count, feats), jnp.bfloat16),
        ),
        in_specs=[vmem_spec()] * 3,
        out_specs=(vmem_spec(),) * 6,
        scratch_shapes=[pltpu.VMEM((2, clips, LANES), jnp.float32)],
        compiler_params=params(40),
        name="scores",
    )(slow, fast, protos)


def row_kernel(protos_all, extra, parts, *refs):
    t_ref, den_ref = refs[0], refs[1]
    col_parts = refs[2 : 2 + parts]
    row_ref, r_ref = refs[2 + parts :]
    clips, count = t_ref.shape[1:]
    groups, lines = clips // LANES, count // LANES
    total = col_parts[0][...]
    for part in col_parts[1:]:
        total = total + part[...]
    r_ref[...] = 1.0 / (float(protos_all) * total)
    if extra:
        row_ref[2 * groups :, :] = den_ref[...]
    for v in range(2):

        def step(i, _, v=v):
            rows = pl.ds(pl.multiple_of(i * LANES, LANES), LANES)
            acc = jnp.zeros((LANES, LANES), jnp.float32)
            for j in range(lines):
                t = t_ref[v, rows, j * LANES : (j + 1) * LANES]
                acc = acc + t * t * r_ref[v * lines + j : v * lines + j + 1, :]
            row_ref[pl.ds(v * groups + i, 1), :] = to_line(acc)
            return 0

        lax.fori_loop(0, groups, step, 0)


def row_pass(t, den, col_parts, protos_all, extra):
    clips, count = t.shape[1:]
    lines = 2 * clips // LANES
    return pl.pallas_call(
        functools.partial(row_kernel, protos_all, extra, len(col_parts)),
        out_shape=(
            jax.ShapeDtypeStruct((lines * (2 if extra else 1), LANES), jnp.float32),
            jax.ShapeDtypeStruct((2 * count // LANES, LANES), jnp.float32),
        ),
        in_specs=[vmem_spec()] * (2 + len(col_parts)),
        out_specs=(vmem_spec(),) * 2,
        compiler_params=params(16),
        name="row_pass",
    )(pltpu.with_memory_space_constraint(t, pltpu.VMEM), den, *col_parts)


def col_kernel(clips_all, parts, *refs):
    t_ref = refs[0]
    row_parts = refs[1 : 1 + parts]
    col_ref, acc_s, s_s = refs[1 + parts :]
    clips, count = t_ref.shape[1:]
    groups, lines = clips // LANES, count // LANES
    total = row_parts[0][: 2 * groups, :]
    for part in row_parts[1:]:
        total = total + part[: 2 * groups, :]
    s_s[...] = 1.0 / (float(clips_all) * total)
    acc_s[...] = jnp.zeros_like(acc_s)
    for v in range(2):

        def step(i, _, v=v):
            rows = pl.ds(pl.multiple_of(i * LANES, LANES), LANES)
            scale = to_columns(s_s[pl.ds(v * groups + i, 1), :])
            for j in range(lines):
                span = slice(j * LANES, (j + 1) * LANES)
                t = t_ref[v, rows, span]
                acc_s[v, :, span] += row_fold(t * t * scale)
            return 0

        lax.fori_loop(0, groups, step, 0)
        for j in range(lines):
            col_ref[v * lines + j : v * lines + j + 1, :] = jnp.sum(
                acc_s[v, :, j * LANES : (j + 1) * LANES], axis=0, keepdims=True
            )


def col_pass(t, row_parts, clips_all):
    clips, count = t.shape[1:]
    return pl.pallas_call(
        functools.partial(col_kernel, clips_all, len(row_parts)),
        out_shape=jax.ShapeDtypeStruct((2 * count // LANES, LANES), jnp.float32),
        in_specs=[vmem_spec()] * (1 + len(row_parts)),
        out_specs=vmem_spec(),
        scratch_shapes=[
            pltpu.VMEM((2, 8, count), jnp.float32),
            pltpu.VMEM((2 * clips // LANES, LANES), jnp.float32),
        ],
        compiler_params=params(16),
        name="col_pass",
    )(pltpu.with_memory_space_constraint(t, pltpu.VMEM), *row_parts)


def grad_kernel(parts, *refs):
    t_ref, r_ref, ubt_ref, cb_ref = refs[:4]
    row_parts = refs[4 : 4 + parts]
    den_parts = refs[4 + parts : 4 + 2 * parts]
    dc_ref, du_ref, g_s, code_s, prob_s = refs[4 + 2 * parts :]
    clips, count = t_ref.shape[1:]
    groups, lines = clips // LANES, count // LANES
    total = row_parts[0][...]
    for part in row_parts[1:]:
        total = total + part[...]
    code = (1.0 / TEMPER) / total
    total = den_parts[0][2 * groups :, :]
    for part in den_parts[1:]:
        total = total + part[2 * groups :, :]
    prob = (1.0 / TEMPER) / total
    for v in range(2):
        for i in range(groups):
            line = v * groups + i
            rows = slice(i * LANES, (i + 1) * LANES)
            code_s[v, rows, :] = to_columns(code[line : line + 1, :])
            prob_s[v, rows, :] = to_columns(prob[line : line + 1, :])

    def chunk(j, _):
        first = pl.multiple_of(j * 256, 256)
        for h in range(2):
            span = pl.ds(first + h * LANES, LANES)
            scale = [r_ref[pl.ds(v * lines + j * 2 + h, 1), :] for v in range(2)]
            for i in range(groups):
                rows = slice(i * LANES, (i + 1) * LANES)
                t = [t_ref[v, rows, span] for v in range(2)]
                q = [t[v] * t[v] * scale[v] * code_s[v, rows, :] for v in range(2)]
                for v in range(2):
                    g = t[v] * prob_s[v, rows, :] - q[1 - v]
                    g_s[v, rows, span] = g.astype(jnp.bfloat16)
        cols = pl.ds(first, 256)
        dct = jnp.dot(ubt_ref[0], g_s[0, :, cols], preferred_element_type=jnp.float32)
        dct = dct + jnp.dot(ubt_ref[1], g_s[1, :, cols], preferred_element_type=jnp.float32)
        dc_ref[cols, :] = dct.T
        return 0

    lax.fori_loop(0, count // 256, chunk, 0)
    for v in range(2):

        def rows_step(i, _, v=v):
            rows = pl.ds(pl.multiple_of(i * 256, 256), 256)
            du_ref[rows, v * cb_ref.shape[1] : (v + 1) * cb_ref.shape[1]] = jnp.dot(
                g_s[v, rows, :], cb_ref[...], preferred_element_type=jnp.float32
            )
            return 0

        lax.fori_loop(0, clips // 256, rows_step, 0)


def gradients(t, r, ubt, cb, row_parts, den_parts):
    clips, count = t.shape[1:]
    feats = cb.shape[1]
    return pl.pallas_call(
        functools.partial(grad_kernel, len(row_parts)),
        out_shape=(
            jax.ShapeDtypeStruct((count, feats), jnp.float32),
            jax.ShapeDtypeStruct((clips, 2 * feats), jnp.float32),
        ),
        in_specs=[vmem_spec()] * (4 + 2 * len(row_parts)),
        out_specs=(vmem_spec(),) * 2,
        scratch_shapes=[
            pltpu.VMEM((2, clips, count), jnp.bfloat16),
            pltpu.VMEM((2, clips, LANES), jnp.float32),
            pltpu.VMEM((2, clips, LANES), jnp.float32),
        ],
        compiler_params=params(40),
        name="gradients",
    )(
        pltpu.with_memory_space_constraint(t, pltpu.VMEM), r, ubt, cb, *row_parts, *den_parts
    )


def all_parts(own, axis):
    count = lax.axis_size(axis)
    parts = [own]
    for shift in range(1, count):
        parts.append(lax.ppermute(own, axis, [(i, (i + shift) % count) for i in range(count)]))
    return parts


def normalize(raw_rows):
    lengths = jnp.sqrt(jnp.sum(raw_rows * raw_rows, axis=-1, keepdims=True) + 1e-12)
    return (raw_rows / lengths, lengths)


def project_back(grad_unit, unit_vec, lengths):
    along = jnp.sum(unit_vec * grad_unit, axis=-1, keepdims=True)
    return (grad_unit - unit_vec * along) / lengths


def body(slow_embed, fast_embed, prototypes):
    clip_dev, feat_width = slow_embed.shape
    proto_dev = prototypes.shape[0]
    batch_count = lax.axis_size("batch")
    proto_count = lax.axis_size("proto")
    clips_all = clip_dev * batch_count
    protos_all = proto_dev * proto_count
    proto_entries = float(protos_all * feat_width)
    embed_entries = float(2 * clips_all * feat_width)

    t, col, den, unit_b, unit_bt, proto_b = scores(slow_embed, fast_embed, prototypes)
    for iteration in range(ITERS):
        rows, r = row_pass(t, den, all_parts(col, "batch"), protos_all, iteration == 0)
        row_parts = all_parts(rows, "proto")
        if iteration == 0:
            den_parts = row_parts
        if iteration + 1 < ITERS:
            col = col_pass(t, row_parts, clips_all)
    dc, du = gradients(t, r, unit_bt, proto_b, row_parts, den_parts)

    proto_rows = proto_dev // batch_count
    clip_rows = clip_dev // proto_count
    dc_share = lax.psum_scatter(dc, "batch", scatter_dimension=0, tiled=True)
    du_share = lax.psum_scatter(du, "proto", scatter_dimension=0, tiled=True)
    proto_first = lax.axis_index("batch") * proto_rows
    unit_share, len_share = normalize(
        lax.dynamic_slice_in_dim(prototypes, proto_first, proto_rows, 0)
    )
    grad_proto = project_back(dc_share, unit_share, len_share)
    clip_first = lax.axis_index("proto") * clip_rows
    views = [
        lax.dynamic_slice_in_dim(x, clip_first, clip_rows, 0).astype(jnp.float32)
        for x in (slow_embed, fast_embed)
    ]
    grad_embed = []
    for v in range(2):
        unit, length = normalize(views[v])
        grad_embed.append(
            project_back(du_share[:, v * feat_width : (v + 1) * feat_width], unit, length)
        )
    grad_embed = jnp.concatenate(grad_embed, axis=1)
    proto_all = lax.all_gather(grad_proto, "batch", axis=0, tiled=True)
    embed_all = lax.all_gather(grad_embed, "proto", axis=0, tiled=True)
    proto_square = jnp.sum(grad_proto * grad_proto)
    embed_square = jnp.sum(grad_embed * grad_embed)
    totals = lax.psum((proto_square, embed_square), ("batch", "proto"))
    proto_factor = lax.rsqrt(totals[0] / proto_entries + NORM_EPS)
    embed_factor = lax.rsqrt(totals[1] / embed_entries + NORM_EPS)
    return (
        proto_all * proto_factor,
        embed_all[:, :feat_width] * embed_factor,
        embed_all[:, feat_width:] * embed_factor,
    )


def solution(mesh):
    placed = (P("batch", None), P("batch", None), P("proto", None))
    return jax.shard_map(
        body,
        mesh=mesh,
        in_specs=placed,
        out_specs=(P("proto", None), P("batch", None), P("batch", None)),
        check_vma=False,
    )
```

time: 415 us -> 258 us (0.62)
  blocking collectives: 154 us -> 38.2 us
  other arithmetic: 90.8 us -> 15 us
  Pallas kernels: 0 us -> 44.2 us
  starting transfers between devices: 0.16 us -> 38.2 us
  matrix products: 24.8 us -> 0 us
  waiting for transfers between devices: 120 us -> 103 us
  local copies, waits for them, and re-layouts: 9.91 us -> 2.99 us
    psum x7 -> x1, blocking collectives: 154 us -> 38.2 us  [body(): totals = lax.psum((proto_square, embed_square), ('batch', 'proto'))]
    pallas_call x0 -> x7, Pallas kernels: none -> 44.2 us  [the longest x1 17.3 us: gradients(): pl.pallas_call(functools.partial(grad_kernel, len(row_parts)), out_shape=...]
    reduce_sum x6 -> x1, other arithmetic: 42.6 us -> 2.47 us  [body(): proto_square = jnp.sum(grad_proto * grad_proto)]
    all_gather x2, waiting for transfers between devices: 61.4 us -> 21.9 us  [the longest x1 21.9 us: body(): proto_all = lax.all_gather(grad_proto, 'batch', axis=0, tiled=True)]
    ppermute x0 -> x30, starting transfers between devices: none -> 38.1 us  [all_parts(): lax.ppermute(own, axis, [(i, (i + shift) % count) for i in range(count)])]
    dot_general x3 -> x0, matrix products: 24.8 us -> none  [the longest x1 8.89 us: body(): jnp.einsum('vbk,vbd->kd', piece, unit_b, preferred_element_type=jnp.float32)]
    div x8 -> x1, other arithmetic: 21.9 us -> 1.24 us  [project_back(): return (grad_unit - unit_vec * along) / lengths]
    sub x1 -> x0, other arithmetic: 19.1 us -> none  [body(): probs[0] - codes[1]]
  transfers between devices with their start and end apart: 4 -> 34, of which waited for: 4 -> 18; matrix products, arithmetic and copies ran while one was open for 4% -> 5% of each run, Pallas kernels for 0% -> 0%
where the time goes in v1:
time: 258 us; the launch traced here: 257 us
  waiting for transfers between devices  103 us (40%)
  Pallas kernels  44.2 us (17%)
  starting transfers between devices  38.2 us (15%)
  blocking collectives  38.2 us (15%)
  between operations  15.3 us (6%)
  other arithmetic  15 us (6%)
  local copies, waits for them, and re-layouts  2.99 us (1%)
    psum x1, blocking collectives, body(): totals = lax.psum((proto_square, embed_square), ('batch', 'proto'))  38.2 us
    ppermute x30, starting transfers between devices, all_parts(): lax.ppermute(own, axis, [(i, (i + shift) % count) for i in range(count)])  38.1 us
    reduce_scatter x1, waiting for transfers between devices, body(): du_share = lax.psum_scatter(du, 'proto', scatter_dimension=0, tiled=True)  34.4 us
    reduce_scatter x1, waiting for transfers between devices, body(): dc_share = lax.psum_scatter(dc, 'batch', scatter_dimension=0, tiled=True)  33.5 us
    all_gather x1, waiting for transfers between devices, body(): proto_all = lax.all_gather(grad_proto, 'batch', axis=0, tiled=True)  21.9 us
    pallas_call x1, Pallas kernels, gradients(): pl.pallas_call(functools.partial(grad_kernel, len(row_parts)), out_shape=...  17.3 us
    ppermute x30, waiting for transfers between devices, all_parts(): lax.ppermute(own, axis, [(i, (i + shift) % count) for i in range(count)])  12.7 us
    pallas_call x1, Pallas kernels, scores(): pl.pallas_call(score_kernel, out_shape=(pltpu.VMEM((2, clips, count), jnp...  12.5 us
  transfers between devices with their start and end apart: 34, of which 18 were waited for; matrix products, arithmetic and copies ran while one was open for 5% of the time, Pallas kernels for 0%

profile of v1, /device:TPU:0, one launch (start us, length us, event | category | flops | bytes accessed | tf_op | source)
XLA Modules:
  0.0 257.3 jit_solution(7438504772087391897)
XLA Ops:
  7.2 12.5 %scores.1 = (f32[2,1024,2048]{2,1,0:T(8,128)S(1)}, f32[32,128]{1,0:T(8,128)}, f32[16,128]{1,0:T(8,128)}, bf16[2,1024,256]{2,1,0:T(8,128)(2,1)}, bf16[2,256,1024]...) custom-call(bf16[1024,256]{1,0:T(8,128)(2,1)} %slow.1, bf16[1024,256]{1,0:T(8,128)(2,1)} %fast.1, f32[2048,256]{1,0:T(8,128)} %protos.1), custom_call_target="tpu_custom_call" | custom-call | tf_op jit(solution)/shard_map/scores/pallas_call | solution.py:103
  20.1 2.6 %collective-permute-start.1 = (f32[32,128]{1,0:T(8,128)}, f32[32,128]{1,0:T(8,128)S(1)}, u32[]{:S(2)}, u32[]{:S(2)}) collective-permute-start(f32[32,128]{1,0:T(8,128)} %get-tuple-element.16.refs_2_), channel_id=1, source_target_pairs={{0,8},{4,12},{8,16},{12,20},{16,24},{20,28},{24,0},{28,4},{1,9},{5... | collective-permute-start | bytes 49160 | tf_op jit(solution)/shard_map/ppermute | solution.py:288
  22.7 2.6 collective-permute-start.2
  27.7 1.4 collective-permute-start.5
  29.0 1.4 collective-permute-start.6
  33.5 3.4 %row_pass.3 = (f32[32,128]{1,0:T(8,128)S(1)}, f32[32,128]{1,0:T(8,128)}) custom-call(f32[2,1024,2048]{2,1,0:T(8,128)S(1)} %get-tuple-element.14.refs_0_, f32[16,128]{1,0:T(8,128)S(1)} %copy-done, f32[32,128]{1,0:T(8,128)S(1)} %copy-done.6, f32[32,128]{1,0:T(8,128)S(1)} %collective-permute-done.refs_3_, f32[32,128]{1,0:T(8,128)S(1)} %collective-permute-done.1.refs_4_, ...), custom_call_target="tpu_custom_call" | custom-call | tf_op jit(solution)/shard_map/row_pass/pallas_call | solution.py:150
  36.9 1.5 collective-permute-start.7
  38.4 1.5 collective-permute-start.8
  40.0 1.4 collective-permute-start.9
  42.2 1.5 collective-permute-done.9.refs_4_.refs_11_
  43.7 2.3 col_pass.2.refs_2_
  46.9 2.5 collective-permute-start.12
  54.0 1.5 collective-permute-done.15.refs_8_
  55.5 3.4 %row_pass.4 = (f32[16,128]{1,0:T(8,128)S(1)}, f32[32,128]{1,0:T(8,128)}) custom-call(f32[2,1024,2048]{2,1,0:T(8,128)S(1)} %get-tuple-element.14.refs_0_, f32[16,128]{1,0:T(8,128)S(1)} %copy-done.1, f32[32,128]{1,0:T(8,128)S(1)} %col_pass.2.refs_2_, f32[32,128]{1,0:T(8,128)S(1)} %collective-permute-done.10.refs_3_, ...), custom_call_target="tpu_custom_call" | custom-call | tf_op jit(solution)/shard_map/row_pass/pallas_call | solution.py:150
  58.9 1.4 collective-permute-start.17
  60.3 1.5 collective-permute-start.18
  64.0 1.5 collective-permute-done.19.refs_4_
  65.5 2.3 col_pass.3.refs_2_
  69.1 2.4 collective-permute-start.22
  75.0 1.4 collective-permute-start.26
  77.8 3.0 %row_pass.5 = (f32[16,128]{1,0:T(8,128)S(1)}, f32[32,128]{1,0:T(8,128)S(1)}) custom-call(f32[2,1024,2048]{2,1,0:T(8,128)S(1)} %get-tuple-element.14.refs_0_, f32[16,128]{1,0:T(8,128)S(1)} %copy-done.1, f32[32,128]{1,0:T(8,128)S(1)} %col_pass.3.refs_2_, f32[32,128]{1,0:T(8,128)S(1)} %collective-permute-done.20.refs_3_, ...), custom_call_target="tpu_custom_call" | custom-call | tf_op jit(solution)/shard_map/row_pass/pallas_call | solution.py:150
  81.4 1.5 collective-permute-start.27
  83.4 1.4 collective-permute-start.29
  87.7 17.3 %gradients.1 = (f32[2048,256]{1,0:T(8,128)}, f32[1024,512]{1,0:T(8,128)}) custom-call(f32[2,1024,2048]{2,1,0:T(8,128)S(1)} %get-tuple-element.14.refs_0_, f32[32,128]{1,0:T(8,128)} %copy-done.7, bf16[2,256,1024]{2,1,0:T(8,128)(2,1)} %get-tuple-element.20.refs_2_, bf16[2048,256]{1,0:T(8,128)(2,1)} %get-tuple-element.21.refs_3_, f32[16,128]{1,0:T(8,128)} %copy-done.8, ...), custom_call_target="tpu_custom_call" | custom-call | tf_op jit(solution)/shard_map/gradients/pallas_call | solution.py:264
  106.4 34.4 %reduce-scatter.5.cloned.1.call-done = f32[256,512]{1,0:T(8,128)} async-done(((f32[1024,512]{1,0:T(8,128)}), f32[256,512]{1,0:T(8,128)}) %reduce-scatter.5.cloned.1.call-update) | async-done | bytes 524304 | tf_op jit(solution)/shard_map/reduce_scatter | solution.py:325
  143.3 1.5 pad_maximum_fusion
  146.0 33.5 %reduce-scatter.3.cloned.1.call-done = f32[256,256]{1,0:T(8,128)} async-done(((f32[2048,256]{1,0:T(8,128)}), f32[256,256]{1,0:T(8,128)}) %reduce-scatter.3.cloned.1.call-update) | async-done | bytes 262160 | tf_op jit(solution)/shard_map/reduce_scatter | solution.py:324
  180.7 2.5 multiply_reduce_fusion.3
  183.2 38.2 %all-reduce = (f32[]{:T(128)}, f32[]{:T(128)}) all-reduce(f32[]{:T(128)} %get-tuple-element.29, f32[]{:T(128)} %get-tuple-element.34), channel_id=1, replica_groups=mesh['batch'=8,'proto'=4] {'batch','proto'}, use_global_device_ids=true, to_apply=%region_4.0 | all-reduce | flops 2 | bytes 16 | tf_op jit(solution)/shard_map/psum | solution.py:347
  222.8 3.0 %slice_multiply_fusion = (f32[1024,256]{1,0:T(8,128)}, f32[1024,256]{1,0:T(8,128)}) fusion(f32[1024,512]{1,0:T(8,128)} %all-gather.5.cloned.1.call-done, f32[]{:T(128)S(6)} %rsqrt.7), kind=kLoop, calls=%fused_computation | loop fusion | flops 524288 | bytes 4194308 | tf_op jit(solution)/shard_map/mul | solution.py:353
  225.8 21.9 %all-gather.3.cloned.1.call-done = f32[2048,256]{1,0:T(8,128)} async-done(((f32[256,256]{1,0:T(8,128)}), f32[2048,256]{1,0:T(8,128)}) %all-gather.3.cloned.1.call-update) | async-done | bytes 2097168 | tf_op jit(solution)/shard_map/all_gather | solution.py:343
  247.7 3.0 %broadcast_multiply_fusion = f32[2048,256]{1,0:T(8,128)} fusion(f32[2048,256]{1,0:T(8,128)} %all-gather.3.cloned.1.call-done, f32[]{:T(128)S(6)} %rsqrt.6), kind=kLoop, calls=%fused_computation.2 | loop fusion | flops 524288 | bytes 4194308 | tf_op jit(solution)/shard_map/mul | solution.py:351
  (88 shorter events, 30.7 us)
Async XLA Ops:
  7.2 133.6 %reduce-scatter.5.cloned.1.call-start = ((), (), s32[]{:S(2)}) async-start(), calls=%async_computation.4 | async-start | bytes 2621440 | tf_op jit(solution)/shard_map/reduce_scatter | solution.py:325
  19.7 8.0 %collective-permute-start = (f32[32,128]{1,0:T(8,128)}, f32[32,128]{1,0:T(8,128)S(1)}, u32[]{:S(2)}, u32[]{:S(2)}) collective-permute-start(f32[32,128]{1,0:T(8,128)} %get-tuple-element.16.refs_2_), channel_id=1, source_target_pairs={{0,4},{4,8},{8,12},{12,16},{16,20},{20,24},{24,28},{28,0},{1,5},{5... | collective-permute-start | bytes 49160 | tf_op jit(solution)/shard_map/ppermute | solution.py:288
  20.1 8.9 %collective-permute-start.1 = (f32[32,128]{1,0:T(8,128)}, f32[32,128]{1,0:T(8,128)S(1)}, u32[]{:S(2)}, u32[]{:S(2)}) collective-permute-start(f32[32,128]{1,0:T(8,128)} %get-tuple-element.16.refs_2_), channel_id=1, source_target_pairs={{0,8},{4,12},{8,16},{12,20},{16,24},{20,28},{24,0},{28,4},{1,9},{5... | collective-permute-start | bytes 49160 | tf_op jit(solution)/shard_map/ppermute | solution.py:288
  22.7 7.7 %collective-permute-start.2 = (f32[32,128]{1,0:T(8,128)}, f32[32,128]{1,0:T(8,128)S(1)}, u32[]{:S(2)}, u32[]{:S(2)}) collective-permute-start(f32[32,128]{1,0:T(8,128)} %get-tuple-element.16.refs_2_), channel_id=1, source_target_pairs={{0,12},{4,16},{8,20},{12,24},{16,28},{20,0},{24,4},{28,8},{1,13},{... | collective-permute-start | bytes 49160 | tf_op jit(solution)/shard_map/ppermute | solution.py:288
  25.3 5.2 %collective-permute-start.3 = (f32[32,128]{1,0:T(8,128)}, f32[32,128]{1,0:T(8,128)S(1)}, u32[]{:S(2)}, u32[]{:S(2)}) collective-permute-start(f32[32,128]{1,0:T(8,128)} %get-tuple-element.16.refs_2_), channel_id=1, source_target_pairs={{0,16},{4,20},{8,24},{12,28},{16,0},{20,4},{24,8},{28,12},{1,17},{... | collective-permute-start | bytes 49160 | tf_op jit(solution)/shard_map/ppermute | solution.py:288
  26.5 4.0 %collective-permute-start.4 = (f32[32,128]{1,0:T(8,128)}, f32[32,128]{1,0:T(8,128)S(1)}, u32[]{:S(2)}, u32[]{:S(2)}) collective-permute-start(f32[32,128]{1,0:T(8,128)} %get-tuple-element.16.refs_2_), channel_id=1, source_target_pairs={{0,20},{4,24},{8,28},{12,0},{16,4},{20,8},{24,12},{28,16},{1,21},{... | collective-permute-start | bytes 49160 | tf_op jit(solution)/shard_map/ppermute | solution.py:288
  27.7 4.0 %collective-permute-start.5 = (f32[32,128]{1,0:T(8,128)}, f32[32,128]{1,0:T(8,128)S(1)}, u32[]{:S(2)}, u32[]{:S(2)}) collective-permute-start(f32[32,128]{1,0:T(8,128)} %get-tuple-element.16.refs_2_), channel_id=1, source_target_pairs={{0,24},{4,28},{8,0},{12,4},{16,8},{20,12},{24,16},{28,20},{1,25},{... | collective-permute-start | bytes 49160 | tf_op jit(solution)/shard_map/ppermute | solution.py:288
  29.0 3.1 %collective-permute-start.6 = (f32[32,128]{1,0:T(8,128)}, f32[32,128]{1,0:T(8,128)S(1)}, u32[]{:S(2)}, u32[]{:S(2)}) collective-permute-start(f32[32,128]{1,0:T(8,128)} %get-tuple-element.16.refs_2_), channel_id=1, source_target_pairs={{0,28},{4,0},{8,4},{12,8},{16,12},{20,16},{24,20},{28,24},{1,29},{... | collective-permute-start | bytes 49160 | tf_op jit(solution)/shard_map/ppermute | solution.py:288
  36.9 4.6 %collective-permute-start.7 = (f32[32,128]{1,0:T(8,128)S(1)}, f32[32,128]{1,0:T(8,128)S(1)}, u32[]{:S(2)}, u32[]{:S(2)}) collective-permute-start(f32[32,128]{1,0:T(8,128)S(1)} %get-tuple-element.17.refs_1_.refs_8_), channel_id=1, source_target_pairs={{0,1},{1,2},{2,3},{3,0},{4,5},{5,6},{6,7},{7,4},{8,9},{9,10},{10,1... | collective-permute-start | bytes 49160 | tf_op jit(solution)/shard_map/ppermute | solution.py:288
  38.4 3.7 %collective-permute-start.8 = (f32[32,128]{1,0:T(8,128)S(1)}, f32[32,128]{1,0:T(8,128)S(1)}, u32[]{:S(2)}, u32[]{:S(2)}) collective-permute-start(f32[32,128]{1,0:T(8,128)S(1)} %get-tuple-element.17.refs_1_.refs_8_), channel_id=1, source_target_pairs={{0,2},{1,3},{2,0},{3,1},{4,6},{5,7},{6,4},{7,5},{8,10},{9,11},{10,... | collective-permute-start | bytes 49160 | tf_op jit(solution)/shard_map/ppermute | solution.py:288
  40.0 3.7 %collective-permute-start.9 = (f32[32,128]{1,0:T(8,128)S(1)}, f32[32,128]{1,0:T(8,128)S(1)}, u32[]{:S(2)}, u32[]{:S(2)}) collective-permute-start(f32[32,128]{1,0:T(8,128)S(1)} %get-tuple-element.17.refs_1_.refs_8_), channel_id=1, source_target_pairs={{0,3},{1,0},{2,1},{3,2},{4,7},{5,4},{6,5},{7,6},{8,11},{9,8},{10,9... | collective-permute-start | bytes 49160 | tf_op jit(solution)/shard_map/ppermute | solution.py:288
  46.1 5.7 %collective-permute-start.10 = (f32[32,128]{1,0:T(8,128)S(1)}, f32[32,128]{1,0:T(8,128)S(1)}, u32[]{:S(2)}, u32[]{:S(2)}) collective-permute-start(f32[32,128]{1,0:T(8,128)S(1)} %col_pass.2.refs_2_), channel_id=1, source_target_pairs={{0,4},{4,8},{8,12},{12,16},{16,20},{20,24},{24,28},{28,0},{1,5},{5... | collective-permute-start | bytes 49160 | tf_op jit(solution)/shard_map/ppermute | solution.py:288
  46.1 6.8 %collective-permute-start.11 = (f32[32,128]{1,0:T(8,128)S(1)}, f32[32,128]{1,0:T(8,128)S(1)}, u32[]{:S(2)}, u32[]{:S(2)}) collective-permute-start(f32[32,128]{1,0:T(8,128)S(1)} %col_pass.2.refs_2_), channel_id=1, source_target_pairs={{0,8},{4,12},{8,16},{12,20},{16,24},{20,28},{24,0},{28,4},{1,9},{5... | collective-permute-start | bytes 49160 | tf_op jit(solution)/shard_map/ppermute | solution.py:288
  46.9 6.7 %collective-permute-start.12 = (f32[32,128]{1,0:T(8,128)S(1)}, f32[32,128]{1,0:T(8,128)S(1)}, u32[]{:S(2)}, u32[]{:S(2)}) collective-permute-start(f32[32,128]{1,0:T(8,128)S(1)} %col_pass.2.refs_2_), channel_id=1, source_target_pairs={{0,12},{4,16},{8,20},{12,24},{16,28},{20,0},{24,4},{28,8},{1,13},{... | collective-permute-start | bytes 49160 | tf_op jit(solution)/shard_map/ppermute | solution.py:288
  49.3 4.6 %collective-permute-start.13 = (f32[32,128]{1,0:T(8,128)S(1)}, f32[32,128]{1,0:T(8,128)S(1)}, u32[]{:S(2)}, u32[]{:S(2)}) collective-permute-start(f32[32,128]{1,0:T(8,128)S(1)} %col_pass.2.refs_2_), channel_id=1, source_target_pairs={{0,16},{4,20},{8,24},{12,28},{16,0},{20,4},{24,8},{28,12},{1,17},{... | collective-permute-start | bytes 49160 | tf_op jit(solution)/shard_map/ppermute | solution.py:288
  50.6 3.4 %collective-permute-start.14 = (f32[32,128]{1,0:T(8,128)S(1)}, f32[32,128]{1,0:T(8,128)S(1)}, u32[]{:S(2)}, u32[]{:S(2)}) collective-permute-start(f32[32,128]{1,0:T(8,128)S(1)} %col_pass.2.refs_2_), channel_id=1, source_target_pairs={{0,20},{4,24},{8,28},{12,0},{16,4},{20,8},{24,12},{28,16},{1,21},{... | collective-permute-start | bytes 49160 | tf_op jit(solution)/shard_map/ppermute | solution.py:288
  51.8 3.7 %collective-permute-start.15 = (f32[32,128]{1,0:T(8,128)S(1)}, f32[32,128]{1,0:T(8,128)S(1)}, u32[]{:S(2)}, u32[]{:S(2)}) collective-permute-start(f32[32,128]{1,0:T(8,128)S(1)} %col_pass.2.refs_2_), channel_id=1, source_target_pairs={{0,24},{4,28},{8,0},{12,4},{16,8},{20,12},{24,16},{28,20},{1,25},{... | collective-permute-start | bytes 49160 | tf_op jit(solution)/shard_map/ppermute | solution.py:288
  58.9 4.5 %collective-permute-start.17 = (f32[16,128]{1,0:T(8,128)S(1)}, f32[16,128]{1,0:T(8,128)S(1)}, u32[]{:S(2)}, u32[]{:S(2)}) collective-permute-start(f32[16,128]{1,0:T(8,128)S(1)} %get-tuple-element.18.refs_1_), channel_id=1, source_target_pairs={{0,1},{1,2},{2,3},{3,0},{4,5},{5,6},{6,7},{7,4},{8,9},{9,10},{10,1... | collective-permute-start | bytes 24584 | tf_op jit(solution)/shard_map/ppermute | solution.py:288
  60.3 3.7 %collective-permute-start.18 = (f32[16,128]{1,0:T(8,128)S(1)}, f32[16,128]{1,0:T(8,128)S(1)}, u32[]{:S(2)}, u32[]{:S(2)}) collective-permute-start(f32[16,128]{1,0:T(8,128)S(1)} %get-tuple-element.18.refs_1_), channel_id=1, source_target_pairs={{0,2},{1,3},{2,0},{3,1},{4,6},{5,7},{6,4},{7,5},{8,10},{9,11},{10,... | collective-permute-start | bytes 24584 | tf_op jit(solution)/shard_map/ppermute | solution.py:288
  61.8 3.7 %collective-permute-start.19 = (f32[16,128]{1,0:T(8,128)S(1)}, f32[16,128]{1,0:T(8,128)S(1)}, u32[]{:S(2)}, u32[]{:S(2)}) collective-permute-start(f32[16,128]{1,0:T(8,128)S(1)} %get-tuple-element.18.refs_1_), channel_id=1, source_target_pairs={{0,3},{1,0},{2,1},{3,2},{4,7},{5,4},{6,5},{7,6},{8,11},{9,8},{10,9... | collective-permute-start | bytes 24584 | tf_op jit(solution)/shard_map/ppermute | solution.py:288
  67.8 6.1 %collective-permute-start.20 = (f32[32,128]{1,0:T(8,128)S(1)}, f32[32,128]{1,0:T(8,128)S(1)}, u32[]{:S(2)}, u32[]{:S(2)}) collective-permute-start(f32[32,128]{1,0:T(8,128)S(1)} %col_pass.3.refs_2_), channel_id=1, source_target_pairs={{0,4},{4,8},{8,12},{12,16},{16,20},{20,24},{24,28},{28,0},{1,5},{5... | collective-permute-start | bytes 49160 | tf_op jit(solution)/shard_map/ppermute | solution.py:288
  67.9 7.1 %collective-permute-start.21 = (f32[32,128]{1,0:T(8,128)S(1)}, f32[32,128]{1,0:T(8,128)S(1)}, u32[]{:S(2)}, u32[]{:S(2)}) collective-permute-start(f32[32,128]{1,0:T(8,128)S(1)} %col_pass.3.refs_2_), channel_id=1, source_target_pairs={{0,8},{4,12},{8,16},{12,20},{16,24},{20,28},{24,0},{28,4},{1,9},{5... | collective-permute-start | bytes 49160 | tf_op jit(solution)/shard_map/ppermute | solution.py:288
  69.1 7.3 %collective-permute-start.22 = (f32[32,128]{1,0:T(8,128)S(1)}, f32[32,128]{1,0:T(8,128)S(1)}, u32[]{:S(2)}, u32[]{:S(2)}) collective-permute-start(f32[32,128]{1,0:T(8,128)S(1)} %col_pass.3.refs_2_), channel_id=1, source_target_pairs={{0,12},{4,16},{8,20},{12,24},{16,28},{20,0},{24,4},{28,8},{1,13},{... | collective-permute-start | bytes 49160 | tf_op jit(solution)/shard_map/ppermute | solution.py:288
  71.5 4.9 %collective-permute-start.23 = (f32[32,128]{1,0:T(8,128)S(1)}, f32[32,128]{1,0:T(8,128)S(1)}, u32[]{:S(2)}, u32[]{:S(2)}) collective-permute-start(f32[32,128]{1,0:T(8,128)S(1)} %col_pass.3.refs_2_), channel_id=1, source_target_pairs={{0,16},{4,20},{8,24},{12,28},{16,0},{20,4},{24,8},{28,12},{1,17},{... | collective-permute-start | bytes 49160 | tf_op jit(solution)/shard_map/ppermute | solution.py:288
  72.9 3.5 %collective-permute-start.24 = (f32[32,128]{1,0:T(8,128)S(1)}, f32[32,128]{1,0:T(8,128)S(1)}, u32[]{:S(2)}, u32[]{:S(2)}) collective-permute-start(f32[32,128]{1,0:T(8,128)S(1)} %col_pass.3.refs_2_), channel_id=1, source_target_pairs={{0,20},{4,24},{8,28},{12,0},{16,4},{20,8},{24,12},{28,16},{1,21},{... | collective-permute-start | bytes 49160 | tf_op jit(solution)/shard_map/ppermute | solution.py:288
  73.9 3.7 %collective-permute-start.25 = (f32[32,128]{1,0:T(8,128)S(1)}, f32[32,128]{1,0:T(8,128)S(1)}, u32[]{:S(2)}, u32[]{:S(2)}) collective-permute-start(f32[32,128]{1,0:T(8,128)S(1)} %col_pass.3.refs_2_), channel_id=1, source_target_pairs={{0,24},{4,28},{8,0},{12,4},{16,8},{20,12},{24,16},{28,20},{1,25},{... | collective-permute-start | bytes 49160 | tf_op jit(solution)/shard_map/ppermute | solution.py:288
  81.4 4.5 %collective-permute-start.27 = (f32[16,128]{1,0:T(8,128)S(1)}, f32[16,128]{1,0:T(8,128)S(1)}, u32[]{:S(2)}, u32[]{:S(2)}) collective-permute-start(f32[16,128]{1,0:T(8,128)S(1)} %get-tuple-element.22.refs_4_), channel_id=1, source_target_pairs={{0,1},{1,2},{2,3},{3,0},{4,5},{5,6},{6,7},{7,4},{8,9},{9,10},{10,1... | collective-permute-start | bytes 24584 | tf_op jit(solution)/shard_map/ppermute | solution.py:288
  82.9 3.7 %collective-permute-start.28 = (f32[16,128]{1,0:T(8,128)S(1)}, f32[16,128]{1,0:T(8,128)S(1)}, u32[]{:S(2)}, u32[]{:S(2)}) collective-permute-start(f32[16,128]{1,0:T(8,128)S(1)} %get-tuple-element.22.refs_4_), channel_id=1, source_target_pairs={{0,2},{1,3},{2,0},{3,1},{4,6},{5,7},{6,4},{7,5},{8,10},{9,11},{10,... | collective-permute-start | bytes 24584 | tf_op jit(solution)/shard_map/ppermute | solution.py:288
  83.4 3.7 %collective-permute-start.29 = (f32[16,128]{1,0:T(8,128)S(1)}, f32[16,128]{1,0:T(8,128)S(1)}, u32[]{:S(2)}, u32[]{:S(2)}) collective-permute-start(f32[16,128]{1,0:T(8,128)S(1)} %get-tuple-element.22.refs_4_), channel_id=1, source_target_pairs={{0,3},{1,0},{2,1},{3,2},{4,7},{5,4},{6,5},{7,6},{8,11},{9,8},{10,9... | collective-permute-start | bytes 24584 | tf_op jit(solution)/shard_map/ppermute | solution.py:288
  105.0 74.5 %reduce-scatter.3.cloned.1.call-start = ((), (), s32[]{:S(2)}) async-start(), calls=%async_computation.2 | async-start | bytes 2359296 | tf_op jit(solution)/shard_map/reduce_scatter | solution.py:324
  105.8 117.0 %all-gather.5.cloned.1.call-start = ((), (), s32[]{:S(2)}) async-start(), calls=%async_computation.5 | async-start | bytes 2621440 | tf_op jit(solution)/shard_map/all_gather | solution.py:344
  144.8 102.9 %all-gather.3.cloned.1.call-start = ((), (), s32[]{:S(2)}) async-start(), calls=%async_computation.3 | async-start | bytes 2359296 | tf_op jit(solution)/shard_map/all_gather | solution.py:343
  (16 other events, 56.0 us)
Sparse Core Ops, SparseCore 0:
  105.1 35.5 reduce-scatter.4
  143.7 35.7 reduce-scatter.2
  182.1 34.2 all-gather.4
  218.5 29.1 all-gather.2

commit v2 on v1

--- a/solution.py
+++ b/solution.py
@@ -205,13 +205,14 @@
     )(pltpu.with_memory_space_constraint(t, pltpu.VMEM), *row_parts)
 
 
-def grad_kernel(parts, *refs):
-    t_ref, r_ref, ubt_ref, cb_ref = refs[:4]
+def grad_kernel(parts, batch_count, *refs):
+    me_ref, t_ref, r_ref, ubt_ref = refs[:4]
     row_parts = refs[4 : 4 + parts]
     den_parts = refs[4 + parts : 4 + 2 * parts]
-    dc_ref, du_ref, g_s, code_s, prob_s = refs[4 + 2 * parts :]
+    send_ref, keep_ref, g_ref, code_s, prob_s = refs[4 + 2 * parts :]
     clips, count = t_ref.shape[1:]
     groups, lines = clips // LANES, count // LANES
+    width = count // batch_count
     total = row_parts[0][...]
     for part in row_parts[1:]:
         total = total + part[...]
@@ -227,58 +228,157 @@
             code_s[v, rows, :] = to_columns(code[line : line + 1, :])
             prob_s[v, rows, :] = to_columns(prob[line : line + 1, :])
 
-    def chunk(j, _):
-        first = pl.multiple_of(j * 256, 256)
-        for h in range(2):
+    def chunk(m, out_ref, slot):
+        which = jnp.bitwise_xor(me_ref[0], m)
+        first = pl.multiple_of(which * width, width)
+        for h in range(width // LANES):
             span = pl.ds(first + h * LANES, LANES)
-            scale = [r_ref[pl.ds(v * lines + j * 2 + h, 1), :] for v in range(2)]
+            line = which * (width // LANES) + h
+            scale = [r_ref[pl.ds(v * lines + line, 1), :] for v in range(2)]
             for i in range(groups):
                 rows = slice(i * LANES, (i + 1) * LANES)
                 t = [t_ref[v, rows, span] for v in range(2)]
                 q = [t[v] * t[v] * scale[v] * code_s[v, rows, :] for v in range(2)]
                 for v in range(2):
                     g = t[v] * prob_s[v, rows, :] - q[1 - v]
-                    g_s[v, rows, span] = g.astype(jnp.bfloat16)
-        cols = pl.ds(first, 256)
-        dct = jnp.dot(ubt_ref[0], g_s[0, :, cols], preferred_element_type=jnp.float32)
-        dct = dct + jnp.dot(ubt_ref[1], g_s[1, :, cols], preferred_element_type=jnp.float32)
-        dc_ref[cols, :] = dct.T
+                    g_ref[v, rows, span] = g.astype(jnp.bfloat16)
+        cols = pl.ds(first, width)
+        dct = jnp.dot(ubt_ref[0], g_ref[0, :, cols], preferred_element_type=jnp.float32)
+        dct = dct + jnp.dot(ubt_ref[1], g_ref[1, :, cols], preferred_element_type=jnp.float32)
+        out_ref[slot] = dct.T
+
+    def pair(i, _):
+        chunk(2 * i + 1, send_ref, i)
+        chunk(2 * i, keep_ref, i)
         return 0
 
-    lax.fori_loop(0, count // 256, chunk, 0)
-    for v in range(2):
-
-        def rows_step(i, _, v=v):
-            rows = pl.ds(pl.multiple_of(i * 256, 256), 256)
-            du_ref[rows, v * cb_ref.shape[1] : (v + 1) * cb_ref.shape[1]] = jnp.dot(
-                g_s[v, rows, :], cb_ref[...], preferred_element_type=jnp.float32
-            )
-            return 0
-
-        lax.fori_loop(0, clips // 256, rows_step, 0)
-
-
-def gradients(t, r, ubt, cb, row_parts, den_parts):
+    lax.fori_loop(0, batch_count // 2, pair, 0)
+
+
+def proto_gradients(me, t, r, ubt, row_parts, den_parts, batch_count):
     clips, count = t.shape[1:]
-    feats = cb.shape[1]
-    return pl.pallas_call(
-        functools.partial(grad_kernel, len(row_parts)),
-        out_shape=(
-            jax.ShapeDtypeStruct((count, feats), jnp.float32),
-            jax.ShapeDtypeStruct((clips, 2 * feats), jnp.float32),
-        ),
-        in_specs=[vmem_spec()] * (4 + 2 * len(row_parts)),
-        out_specs=(vmem_spec(),) * 2,
+    feats = ubt.shape[1]
+    share = jax.ShapeDtypeStruct(
+        (batch_count // 2, count // batch_count, feats), jnp.float32
+    )
+    return pl.pallas_call(
+        functools.partial(grad_kernel, len(row_parts), batch_count),
+        out_shape=(share, share, pltpu.VMEM((2, clips, count), jnp.bfloat16)),
+        in_specs=[pl.BlockSpec(memory_space=pltpu.SMEM)] + [vmem_spec()] * (3 + 2 * len(row_parts)),
+        out_specs=(vmem_spec(),) * 3,
         scratch_shapes=[
-            pltpu.VMEM((2, clips, count), jnp.bfloat16),
             pltpu.VMEM((2, clips, LANES), jnp.float32),
             pltpu.VMEM((2, clips, LANES), jnp.float32),
         ],
-        compiler_params=params(40),
-        name="gradients",
+        compiler_params=params(32),
+        cost_estimate=pl.CostEstimate(
+            flops=4 * clips * count * feats, bytes_accessed=8 * MIB, transcendentals=0
+        ),
+        name="proto_gradients",
     )(
-        pltpu.with_memory_space_constraint(t, pltpu.VMEM), r, ubt, cb, *row_parts, *den_parts
+        me, pltpu.with_memory_space_constraint(t, pltpu.VMEM), r, ubt, *row_parts, *den_parts
     )
+
+
+def piece_of(position, order):
+    steps = len(order)
+    return sum(((position >> (steps - 1 - j)) & 1) << bit for j, bit in enumerate(order))
+
+
+def embed_grad_kernel(orders, me_ref, g_ref, cb_ref, *outs):
+    clips = g_ref.shape[1]
+    pieces = 1 << len(orders[0])
+    size = clips // pieces
+    for v in range(2):
+        for place in range(pieces):
+            which = jnp.bitwise_xor(me_ref[0], piece_of(place, orders[v]))
+            rows = pl.ds(pl.multiple_of(which * size, size), size)
+            out_ref = outs[2 * v + (0 if place >= pieces // 2 else 1)]
+            out_ref[place % (pieces // 2)] = jnp.dot(
+                g_ref[v, rows, :], cb_ref[...], preferred_element_type=jnp.float32
+            )
+
+
+def embed_gradients(me, g, cb, orders):
+    clips, count = g.shape[1:]
+    feats = cb.shape[1]
+    pieces = 1 << len(orders[0])
+    share = jax.ShapeDtypeStruct((pieces // 2, clips // pieces, feats), jnp.float32)
+    return pl.pallas_call(
+        functools.partial(embed_grad_kernel, orders),
+        out_shape=(share,) * 4,
+        in_specs=[pl.BlockSpec(memory_space=pltpu.SMEM)] + [vmem_spec()] * 2,
+        out_specs=(vmem_spec(),) * 4,
+        compiler_params=params(24),
+        cost_estimate=pl.CostEstimate(
+            flops=4 * clips * count * feats, bytes_accessed=8 * MIB, transcendentals=0
+        ),
+        name="embed_gradients",
+    )(me, pltpu.with_memory_space_constraint(g, pltpu.VMEM), cb)
+
+
+def share_kernel(counts, raw_count, *refs):
+    raws = refs[:raw_count]
+    terms = refs[raw_count : raw_count + sum(counts)]
+    outs = refs[raw_count + sum(counts) :]
+    square = jnp.zeros((8, LANES), jnp.float32)
+    place = 0
+    for n, (raw, count) in enumerate(zip(raws, counts)):
+        x = raw[...].astype(jnp.float32)
+        length = jnp.sqrt(jnp.sum(x * x, axis=-1, keepdims=True) + 1e-12)
+        unit = x / length
+        grad = terms[place][...]
+        for term in terms[place + 1 : place + count]:
+            grad = grad + term[...]
+        place += count
+        along = jnp.sum(unit * grad, axis=-1, keepdims=True)
+        grad = (grad - unit * along) / length
+        outs[n][...] = grad
+        square = square + row_fold(lane_sum(grad * grad))
+    total = jnp.sum(jnp.sum(square, axis=0, keepdims=True), axis=1, keepdims=True)
+    outs[-1][...] = jnp.broadcast_to(total, (8, LANES))
+
+
+def project_shares(raws, groups):
+    terms = [term for group in groups for term in group]
+    return pl.pallas_call(
+        functools.partial(share_kernel, [len(group) for group in groups], len(raws)),
+        out_shape=tuple(jax.ShapeDtypeStruct(raw.shape, jnp.float32) for raw in raws)
+        + (jax.ShapeDtypeStruct((8, LANES), jnp.float32),),
+        in_specs=[vmem_spec()] * (len(raws) + len(terms)),
+        out_specs=(vmem_spec(),) * (len(raws) + 1),
+        compiler_params=params(8),
+        name="project_shares",
+    )(*raws, *terms)
+
+
+def finish_kernel(entries, counts, me_ref, square_ref, *refs):
+    ins, outs = refs[: sum(counts)], refs[sum(counts) :]
+    place = 0
+    for n, count in enumerate(counts):
+        mean = square_ref[n, 0:1, 0:1] / entries[n]
+        factor = lax.rsqrt(mean + NORM_EPS)
+        for m in range(count):
+            src = ins[place + m]
+            size = src.shape[0]
+            which = jnp.bitwise_xor(me_ref[n], m)
+            outs[n][pl.ds(pl.multiple_of(which * size, size), size), :] = src[...] * factor
+        place += count
+
+
+def finish(me, squares, groups, entries):
+    pieces = [piece for group in groups for piece in group]
+    return pl.pallas_call(
+        functools.partial(finish_kernel, entries, [len(group) for group in groups]),
+        out_shape=tuple(
+            jax.ShapeDtypeStruct((len(group) * group[0].shape[0], group[0].shape[1]), jnp.float32)
+            for group in groups
+        ),
+        in_specs=[pl.BlockSpec(memory_space=pltpu.SMEM)] + [vmem_spec()] * (1 + len(pieces)),
+        out_specs=(vmem_spec(),) * len(groups),
+        compiler_params=params(24),
+        name="finish",
+    )(me, squares, *pieces)
 
 
 def all_parts(own, axis):
@@ -289,14 +389,47 @@
     return parts
 
 
-def normalize(raw_rows):
-    lengths = jnp.sqrt(jnp.sum(raw_rows * raw_rows, axis=-1, keepdims=True) + 1e-12)
-    return (raw_rows / lengths, lengths)
-
-
-def project_back(grad_unit, unit_vec, lengths):
-    along = jnp.sum(unit_vec * grad_unit, axis=-1, keepdims=True)
-    return (grad_unit - unit_vec * along) / lengths
+def swap(own, axis, bit):
+    return lax.ppermute(own, axis, [(i, i ^ (1 << bit)) for i in range(lax.axis_size(axis))])
+
+
+def bits_of(axis):
+    count = lax.axis_size(axis)
+    bits = count.bit_length() - 1
+    if count != 1 << bits:
+        raise ValueError("axis size")
+    return bits
+
+
+def scatter_batch(send, keep):
+    bits = bits_of("batch")
+    recv = swap(send, "batch", 0)
+    pieces = {m: [keep[m], recv[m]] for m in range(1 << (bits - 1))}
+    for bit in range(bits - 1):
+        for m in sorted((m for m in pieces if m >> bit & 1), reverse=True):
+            terms = pieces.pop(m)
+            total = terms[0]
+            for term in terms[1:]:
+                total = total + term
+            pieces[m ^ (1 << bit)].append(swap(total, "batch", bit + 1))
+    return pieces[0]
+
+
+def scatter_proto(send, keep, order):
+    for bit in order[:-1]:
+        recv = swap(send, "proto", bit)
+        half = keep.shape[0] // 2
+        send = keep[half:] + recv[half:]
+        keep = keep[:half] + recv[:half]
+    return [keep[0], swap(send, "proto", order[-1])[0]]
+
+
+def gather_bits(own, axis, order):
+    pieces = {0: own}
+    for bit in order:
+        for m in list(pieces):
+            pieces[m | 1 << bit] = swap(pieces[m], axis, bit)
+    return [pieces[m] for m in range(len(pieces))]
 
 
 def body(slow_embed, fast_embed, prototypes):
@@ -308,6 +441,11 @@
     protos_all = proto_dev * proto_count
     proto_entries = float(protos_all * feat_width)
     embed_entries = float(2 * clips_all * feat_width)
+    batch_bits, proto_bits = bits_of("batch"), bits_of("proto")
+    me_batch, me_proto = lax.axis_index("batch"), lax.axis_index("proto")
+    me = jnp.stack([me_batch, me_proto, me_proto]).astype(jnp.int32)
+    me_first = me[:1]
+    me_second = me[1:2]
 
     t, col, den, unit_b, unit_bt, proto_b = scores(slow_embed, fast_embed, prototypes)
     for iteration in range(ITERS):
@@ -317,40 +455,38 @@
             den_parts = row_parts
         if iteration + 1 < ITERS:
             col = col_pass(t, row_parts, clips_all)
-    dc, du = gradients(t, r, unit_bt, proto_b, row_parts, den_parts)
+
+    orders = (tuple(range(proto_bits)), tuple(reversed(range(proto_bits))))
+    send, keep, g = proto_gradients(
+        me_first, t, r, unit_bt, row_parts, den_parts, batch_count
+    )
+    sends = embed_gradients(me_second, g, proto_b, orders)
 
     proto_rows = proto_dev // batch_count
     clip_rows = clip_dev // proto_count
-    dc_share = lax.psum_scatter(dc, "batch", scatter_dimension=0, tiled=True)
-    du_share = lax.psum_scatter(du, "proto", scatter_dimension=0, tiled=True)
-    proto_first = lax.axis_index("batch") * proto_rows
-    unit_share, len_share = normalize(
-        lax.dynamic_slice_in_dim(prototypes, proto_first, proto_rows, 0)
-    )
-    grad_proto = project_back(dc_share, unit_share, len_share)
-    clip_first = lax.axis_index("proto") * clip_rows
-    views = [
-        lax.dynamic_slice_in_dim(x, clip_first, clip_rows, 0).astype(jnp.float32)
+    raw_protos = lax.dynamic_slice_in_dim(prototypes, me_batch * proto_rows, proto_rows, 0)
+    raw_views = [
+        lax.dynamic_slice_in_dim(x, me_proto * clip_rows, clip_rows, 0)
         for x in (slow_embed, fast_embed)
     ]
-    grad_embed = []
-    for v in range(2):
-        unit, length = normalize(views[v])
-        grad_embed.append(
-            project_back(du_share[:, v * feat_width : (v + 1) * feat_width], unit, length)
-        )
-    grad_embed = jnp.concatenate(grad_embed, axis=1)
-    proto_all = lax.all_gather(grad_proto, "batch", axis=0, tiled=True)
-    embed_all = lax.all_gather(grad_embed, "proto", axis=0, tiled=True)
-    proto_square = jnp.sum(grad_proto * grad_proto)
-    embed_square = jnp.sum(grad_embed * grad_embed)
-    totals = lax.psum((proto_square, embed_square), ("batch", "proto"))
-    proto_factor = lax.rsqrt(totals[0] / proto_entries + NORM_EPS)
-    embed_factor = lax.rsqrt(totals[1] / embed_entries + NORM_EPS)
-    return (
-        proto_all * proto_factor,
-        embed_all[:, :feat_width] * embed_factor,
-        embed_all[:, feat_width:] * embed_factor,
+    proto_terms = scatter_batch(send, keep)
+    view_terms = [scatter_proto(sends[2 * v], sends[2 * v + 1], orders[v]) for v in range(2)]
+    grad_proto, proto_square = project_shares([raw_protos], [proto_terms])
+    grad_slow, grad_fast, embed_square = project_shares(raw_views, view_terms)
+
+    proto_pieces = gather_bits(grad_proto, "batch", tuple(reversed(range(batch_bits))))
+    slow_pieces = gather_bits(grad_slow, "proto", orders[1])
+    fast_pieces = gather_bits(grad_fast, "proto", orders[0])
+    squares = jnp.stack([proto_square, embed_square, embed_square])
+    for bit in range(proto_bits):
+        squares = squares + swap(squares, "proto", bit)
+    for bit in range(batch_bits):
+        squares = squares + swap(squares, "batch", bit)
+    return finish(
+        me,
+        squares,
+        (proto_pieces, slow_pieces, fast_pieces),
+        (proto_entries, embed_entries, embed_entries),
     )
 
 

time: 258 us -> 175 us (0.68)
  waiting for transfers between devices: 103 us -> 45.1 us
  blocking collectives: 38.2 us -> 0 us
  starting transfers between devices: 38.2 us -> 64 us
  between operations: 15.3 us -> 0.83 us
  local copies, waits for them, and re-layouts: 2.99 us -> 17.1 us
  other arithmetic: 15 us -> 1.8 us
    reduce_scatter x2 -> x0, waiting for transfers between devices: 67.9 us -> none  [the longest x1 34.4 us: body(): du_share = lax.psum_scatter(du, 'proto', scatter_dimension=0, tiled=True)]
    psum x1 -> x0, blocking collectives: 38.2 us -> none  [body(): totals = lax.psum((proto_square, embed_square), ('batch', 'proto'))]
    ppermute x0 -> x26, waiting for transfers between devices: none -> 32.4 us  [swap(): lax.ppermute(own, axis, [(i, i ^ 1 << bit) for i in range(lax.axis_size(a...]
    ppermute x0 -> x26, starting transfers between devices: none -> 25.9 us  [swap(): lax.ppermute(own, axis, [(i, i ^ 1 << bit) for i in range(lax.axis_size(a...]
    all_gather x2 -> x0, waiting for transfers between devices: 21.9 us -> none  [the longest x1 21.9 us: body(): proto_all = lax.all_gather(grad_proto, 'batch', axis=0, tiled=True)]
    unnamed x28 -> x36, local copies, waits for them, and re-layouts: 2.99 us -> 15.2 us
    reduce_sum x5 -> x0, other arithmetic: 6.18 us -> none  [the longest x2 2.49 us: project_back(): along = jnp.sum(unit_vec * grad_unit, axis=-1, keepdims=True)]
    mul x2 -> x0, other arithmetic: 6.04 us -> none  [the longest x1 3.05 us: body(): proto_all * proto_factor]
  transfers between devices with their start and end apart: 34 -> 56, of which waited for: 18 -> 29; matrix products, arithmetic and copies ran while one was open for 5% -> 2% of each run, Pallas kernels for 0% -> 2%
where the time goes in v2:
time: 175 us; the launch traced here: 174 us
  starting transfers between devices  64 us (37%)
  Pallas kernels  45.5 us (26%)
  waiting for transfers between devices  45.1 us (26%)
  local copies, waits for them, and re-layouts  17.1 us (10%)
  other arithmetic  1.8 us (1%)
    ppermute x30, starting transfers between devices, all_parts(): lax.ppermute(own, axis, [(i, (i + shift) % count) for i in range(count)])  38.1 us
    ppermute x26, waiting for transfers between devices, swap(): lax.ppermute(own, axis, [(i, i ^ 1 << bit) for i in range(lax.axis_size(a...  32.4 us
    ppermute x26, starting transfers between devices, swap(): lax.ppermute(own, axis, [(i, i ^ 1 << bit) for i in range(lax.axis_size(a...  25.9 us
    unnamed x36, local copies, waits for them, and re-layouts  15.2 us
    pallas_call x1, Pallas kernels, proto_gradients(): pl.pallas_call(functools.partial(grad_kernel, len(row_parts), batch_count...  12.7 us
    ppermute x30, waiting for transfers between devices, all_parts(): lax.ppermute(own, axis, [(i, (i + shift) % count) for i in range(count)])  12.7 us
    pallas_call x1, Pallas kernels, scores(): pl.pallas_call(score_kernel, out_shape=(pltpu.VMEM((2, clips, count), jnp...  12.5 us
    pallas_call x3, Pallas kernels, row_pass(): pl.pallas_call(functools.partial(row_kernel, protos_all, extra, len(col_p...  9.76 us
  transfers between devices with their start and end apart: 56, of which 29 were waited for; matrix products, arithmetic and copies ran while one was open for 2% of the time, Pallas kernels for 2%

profile of v2, /device:TPU:0, one launch (start us, length us, event | category | flops | bytes accessed | tf_op | source)
XLA Modules:
  0.0 174.3 jit_solution(16020627069355710404)
XLA Ops:
  0.6 12.5 %scores.1 = (f32[2,1024,2048]{2,1,0:T(8,128)S(1)}, f32[32,128]{1,0:T(8,128)}, f32[16,128]{1,0:T(8,128)}, bf16[2,1024,256]{2,1,0:T(8,128)(2,1)}, bf16[2,256,1024]...) custom-call(bf16[1024,256]{1,0:T(8,128)(2,1)} %slow.1, bf16[1024,256]{1,0:T(8,128)(2,1)} %fast.1, f32[2048,256]{1,0:T(8,128)} %protos.1), custom_call_target="tpu_custom_call" | custom-call | tf_op jit(solution)/shard_map/scores/pallas_call | solution.py:103
  13.5 2.6 %collective-permute-start.1 = (f32[32,128]{1,0:T(8,128)}, f32[32,128]{1,0:T(8,128)S(1)}, u32[]{:S(2)}, u32[]{:S(2)}) collective-permute-start(f32[32,128]{1,0:T(8,128)} %get-tuple-element.26.refs_2_), channel_id=1, source_target_pairs={{0,8},{4,12},{8,16},{12,20},{16,24},{20,28},{24,0},{28,4},{1,9},{5... | collective-permute-start | bytes 49160 | tf_op jit(solution)/shard_map/ppermute | solution.py:388
  16.2 2.5 %collective-permute-start.2 = (f32[32,128]{1,0:T(8,128)}, f32[32,128]{1,0:T(8,128)S(1)}, u32[]{:S(2)}, u32[]{:S(2)}) collective-permute-start(f32[32,128]{1,0:T(8,128)} %get-tuple-element.26.refs_2_), channel_id=1, source_target_pairs={{0,12},{4,16},{8,20},{12,24},{16,28},{20,0},{24,4},{28,8},{1,13},{... | collective-permute-start | bytes 49160 | tf_op jit(solution)/shard_map/ppermute | solution.py:388
  27.0 3.4 %row_pass.3 = (f32[32,128]{1,0:T(8,128)S(1)}, f32[32,128]{1,0:T(8,128)}) custom-call(f32[2,1024,2048]{2,1,0:T(8,128)S(1)} %get-tuple-element.24.refs_0_.refs_1_, f32[16,128]{1,0:T(8,128)S(1)} %copy-done.5, f32[32,128]{1,0:T(8,128)S(1)} %copy-done.12, f32[32,128]{1,0:T(8,128)S(1)} %collective-permute-done.refs_3_, ...), custom_call_target="tpu_custom_call" | custom-call | tf_op jit(solution)/shard_map/row_pass/pallas_call | solution.py:150
  37.1 2.3 %col_pass.2.refs_2_ = f32[32,128]{1,0:T(8,128)S(1)} custom-call(f32[2,1024,2048]{2,1,0:T(8,128)S(1)} %get-tuple-element.24.refs_0_.refs_1_, f32[32,128]{1,0:T(8,128)S(1)} %get-tuple-element.27.refs_1_.refs_8_, f32[32,128]{1,0:T(8,128)S(1)} %collective-permute-done.7.refs_2_.refs_9_, f32[32,128]{1,0:T(8,128)S(1)} %collective-permute-done.8.refs_3_.refs_10_, ...), custom_call_target="tpu_custom_call" | custom-call | tf_op jit(solution)/shard_map/col_pass/pallas_call | solution.py:194
  40.3 2.5 %collective-permute-start.12 = (f32[32,128]{1,0:T(8,128)S(1)}, f32[32,128]{1,0:T(8,128)S(1)}, u32[]{:S(2)}, u32[]{:S(2)}) collective-permute-start(f32[32,128]{1,0:T(8,128)S(1)} %col_pass.2.refs_2_), channel_id=1, source_target_pairs={{0,12},{4,16},{8,20},{12,24},{16,28},{20,0},{24,4},{28,8},{1,13},{... | collective-permute-start | bytes 49160 | tf_op jit(solution)/shard_map/ppermute | solution.py:388
  47.4 1.5 collective-permute-done.15.refs_8_
  49.0 3.4 %row_pass.4 = (f32[16,128]{1,0:T(8,128)S(1)}, f32[32,128]{1,0:T(8,128)}) custom-call(f32[2,1024,2048]{2,1,0:T(8,128)S(1)} %get-tuple-element.24.refs_0_.refs_1_, f32[16,128]{1,0:T(8,128)S(1)} %copy-done.6, f32[32,128]{1,0:T(8,128)S(1)} %col_pass.2.refs_2_, f32[32,128]{1,0:T(8,128)S(1)} %collective-permute-done.10.refs_3_, ...), custom_call_target="tpu_custom_call" | custom-call | tf_op jit(solution)/shard_map/row_pass/pallas_call | solution.py:150
  58.9 2.3 %col_pass.3.refs_2_ = f32[32,128]{1,0:T(8,128)S(1)} custom-call(f32[2,1024,2048]{2,1,0:T(8,128)S(1)} %get-tuple-element.24.refs_0_.refs_1_, f32[16,128]{1,0:T(8,128)S(1)} %get-tuple-element.28.refs_1_, f32[16,128]{1,0:T(8,128)S(1)} %collective-permute-done.17.refs_2_, f32[16,128]{1,0:T(8,128)S(1)} %collective-permute-done.18.refs_3_, ...), custom_call_target="tpu_custom_call" | custom-call | tf_op jit(solution)/shard_map/col_pass/pallas_call | solution.py:194
  62.5 2.4 %collective-permute-start.22 = (f32[32,128]{1,0:T(8,128)S(1)}, f32[32,128]{1,0:T(8,128)S(1)}, u32[]{:S(2)}, u32[]{:S(2)}) collective-permute-start(f32[32,128]{1,0:T(8,128)S(1)} %col_pass.3.refs_2_), channel_id=1, source_target_pairs={{0,12},{4,16},{8,20},{12,24},{16,28},{20,0},{24,4},{28,8},{1,13},{... | collective-permute-start | bytes 49160 | tf_op jit(solution)/shard_map/ppermute | solution.py:388
  71.2 3.0 %row_pass.5 = (f32[16,128]{1,0:T(8,128)S(1)}, f32[32,128]{1,0:T(8,128)S(1)}) custom-call(f32[2,1024,2048]{2,1,0:T(8,128)S(1)} %get-tuple-element.24.refs_0_.refs_1_, f32[16,128]{1,0:T(8,128)S(1)} %copy-done.6, f32[32,128]{1,0:T(8,128)S(1)} %col_pass.3.refs_2_, f32[32,128]{1,0:T(8,128)S(1)} %collective-permute-done.20.refs_3_, ...), custom_call_target="tpu_custom_call" | custom-call | tf_op jit(solution)/shard_map/row_pass/pallas_call | solution.py:150
  81.0 5.8 %copy-done.1 = f32[2,1024,2048]{2,1,0:T(8,128)S(1)} copy-done((f32[2,1024,2048]{2,1,0:T(8,128)S(1)}, f32[2,1024,2048]{2,1,0:T(8,128)}, u32[]{:S(2)}) %copy-start.1) | copy-done | bytes 16777240
  86.8 12.7 %proto_gradients.1 = (f32[4,256,256]{2,1,0:T(8,128)}, f32[4,256,256]{2,1,0:T(8,128)}, bf16[2,1024,2048]{2,1,0:T(8,128)(2,1)S(1)}) custom-call(s32[1]{0:T(128)} %bitcast.refs_0_, f32[2,1024,2048]{2,1,0:T(8,128)S(1)} %copy-done.1, f32[32,128]{1,0:T(8,128)} %copy-done.11, bf16[2,256,1024]{2,1,0:T(8,128)(2,1)} %get-tuple-element.30.refs_3_, ...), custom_call_target="tpu_custom_call" | custom-call | flops 2147483648 | bytes 8388608 | tf_op jit(solution)/shard_map/proto_gradients/pallas_call | solution.py:264
  99.6 3.4 %copy-done.2 = bf16[2,1024,2048]{2,1,0:T(8,128)(2,1)} copy-done((bf16[2,1024,2048]{2,1,0:T(8,128)(2,1)}, bf16[2,1024,2048]{2,1,0:T(8,128)(2,1)S(1)}, u32[]{:S(2)}) %copy-start.2) | copy-done | bytes 8388632
  102.9 3.4 %copy-done.3 = bf16[2,1024,2048]{2,1,0:T(8,128)(2,1)S(1)} copy-done((bf16[2,1024,2048]{2,1,0:T(8,128)(2,1)S(1)}, bf16[2,1024,2048]{2,1,0:T(8,128)(2,1)}, u32[]{:S(2)}) %copy-start.3) | copy-done | bytes 8388632
  106.3 2.3 %embed_gradients.1 = (f32[2,256,256]{2,1,0:T(8,128)S(1)}, f32[2,256,256]{2,1,0:T(8,128)S(1)}, f32[2,256,256]{2,1,0:T(8,128)S(1)}, f32[2,256,256]{2,1,0:T(8,128)S(1)}) custom-call(s32[1]{0:T(128)} %bitcast.1.me_ref, bf16[2,1024,2048]{2,1,0:T(8,128)(2,1)S(1)} %copy-done.3, bf16[2048,256]{1,0:T(8,128)(2,1)S(1)} %copy-done.4), custom_call_target="tpu_custom_call" | custom-call | flops 2147483648 | bytes 8388608 | tf_op jit(solution)/shard_map/embed_gradients/pallas_call | solution.py:307
  108.6 1.6 collective-permute-start.36
  112.8 10.2 %collective-permute-done.36 = f32[2,256,256]{2,1,0:T(8,128)S(1)} collective-permute-done((f32[2,256,256]{2,1,0:T(8,128)S(1)}, f32[2,256,256]{2,1,0:T(8,128)S(1)}, u32[]{:S(2)}, u32[]{:S(2)}) %collective-permute-start.36) | collective-permute-done | bytes 524320 | tf_op jit(solution)/shard_map/ppermute | solution.py:393
  123.1 2.5 %collective-permute-start.37 = (f32[1,256,256]{2,1,0:T(8,128)S(1)}, f32[1,256,256]{2,1,0:T(8,128)S(1)}, u32[]{:S(2)}, u32[]{:S(2)}) collective-permute-start(f32[1,256,256]{2,1,0:T(8,128)S(1)} %get-tuple-element.49), channel_id=1, source_target_pairs={{0,1},{1,0},{2,3},{3,2},{4,5},{5,4},{6,7},{7,6},{8,9},{9,8},{10,11... | collective-permute-start | bytes 786440 | tf_op jit(solution)/shard_map/ppermute | solution.py:393
  128.6 2.3 %collective-permute-start.33 = (f32[256,256]{1,0:T(8,128)}, f32[256,256]{1,0:T(8,128)S(1)}, u32[]{:S(2)}, u32[]{:S(2)}) collective-permute-start(f32[256,256]{1,0:T(8,128)} %fusion.4), channel_id=1, source_target_pairs={{0,16},{4,20},{8,24},{12,28},{16,0},{20,4},{24,8},{28,12},{1,17},{... | collective-permute-start | bytes 786440 | tf_op jit(solution)/shard_map/ppermute | solution.py:393
  134.6 3.6 %collective-permute-done.31.refs_3_ = f32[256,256]{1,0:T(8,128)S(1)} collective-permute-done((f32[256,256]{1,0:T(8,128)S(1)}, f32[256,256]{1,0:T(8,128)S(1)}, u32[]{:S(2)}, u32[]{:S(2)}) %collective-permute-start.31) | collective-permute-done | bytes 262176 | tf_op jit(solution)/shard_map/ppermute | solution.py:393
  138.3 4.2 %collective-permute-done.33.refs_4_ = f32[256,256]{1,0:T(8,128)S(1)} collective-permute-done((f32[256,256]{1,0:T(8,128)}, f32[256,256]{1,0:T(8,128)S(1)}, u32[]{:S(2)}, u32[]{:S(2)}) %collective-permute-start.33) | collective-permute-done | bytes 262176 | tf_op jit(solution)/shard_map/ppermute | solution.py:393
  144.7 1.7 collective-permute-start.53
  146.5 1.5 collective-permute-start.39
  148.1 2.3 %collective-permute-done.39 = f32[3,8,128]{2,1,0:T(8,128)S(1)} collective-permute-done((f32[3,8,128]{2,1,0:T(8,128)S(1)}, f32[3,8,128]{2,1,0:T(8,128)S(1)}, u32[]{:S(2)}, u32[]{:S(2)}) %collective-permute-start.39) | collective-permute-done | bytes 12320 | tf_op jit(solution)/shard_map/ppermute | solution.py:393
  151.6 2.2 %collective-permute-start.41 = (f32[3,8,128]{2,1,0:T(8,128)S(1)}, f32[3,8,128]{2,1,0:T(8,128)S(1)}, u32[]{:S(2)}, u32[]{:S(2)}) collective-permute-start(f32[3,8,128]{2,1,0:T(8,128)S(1)} %add.70), channel_id=1, source_target_pairs={{0,8},{4,12},{8,0},{12,4},{16,24},{20,28},{24,16},{28,20},{1,9},{5... | collective-permute-start | bytes 36872 | tf_op jit(solution)/shard_map/ppermute | solution.py:393
  155.8 1.7 collective-permute-start.44
  157.9 1.8 %collective-permute-done.50.refs_9_ = f32[256,256]{1,0:T(8,128)S(1)} collective-permute-done((f32[256,256]{1,0:T(8,128)S(1)}, f32[256,256]{1,0:T(8,128)S(1)}, u32[]{:S(2)}, u32[]{:S(2)}) %collective-permute-start.50) | collective-permute-done | bytes 262176 | tf_op jit(solution)/shard_map/ppermute | solution.py:393
  159.6 2.6 %collective-permute-start.42 = (f32[3,8,128]{2,1,0:T(8,128)S(1)}, f32[3,8,128]{2,1,0:T(8,128)S(1)}, u32[]{:S(2)}, u32[]{:S(2)}) collective-permute-start(f32[3,8,128]{2,1,0:T(8,128)S(1)} %add.71), channel_id=1, source_target_pairs={{0,16},{4,20},{8,24},{12,28},{16,0},{20,4},{24,8},{28,12},{1,17},{... | collective-permute-start | bytes 36872 | tf_op jit(solution)/shard_map/ppermute | solution.py:393
  162.7 2.1 %collective-permute-done.52.refs_11_ = f32[256,256]{1,0:T(8,128)S(1)} collective-permute-done((f32[256,256]{1,0:T(8,128)S(1)}, f32[256,256]{1,0:T(8,128)S(1)}, u32[]{:S(2)}, u32[]{:S(2)}) %collective-permute-start.52) | collective-permute-done | bytes 262176 | tf_op jit(solution)/shard_map/ppermute | solution.py:393
  164.8 3.7 %collective-permute-done.42 = f32[3,8,128]{2,1,0:T(8,128)S(1)} collective-permute-done((f32[3,8,128]{2,1,0:T(8,128)S(1)}, f32[3,8,128]{2,1,0:T(8,128)S(1)}, u32[]{:S(2)}, u32[]{:S(2)}) %collective-permute-start.42) | collective-permute-done | bytes 12320 | tf_op jit(solution)/shard_map/ppermute | solution.py:393
  171.5 2.8 %finish.1 = (f32[2048,256]{1,0:T(8,128)}, f32[1024,256]{1,0:T(8,128)}, f32[1024,256]{1,0:T(8,128)}) custom-call(s32[3]{0:T(128)S(1)} %pad_add_fusion.me_ref, f32[3,8,128]{2,1,0:T(8,128)S(1)} %add.72.square_ref, f32[256,256]{1,0:T(8,128)S(1)} %get-tuple-element.42.refs_0_, f32[256,256]{1,0:T(8,128)S(1)} %collective-permute-done.43.refs_1_, ...), custom_call_target="tpu_custom_call" | custom-call | tf_op jit(solution)/shard_map/finish/pallas_call | solution.py:371
  (140 shorter events, 60.5 us)
Async XLA Ops:
  13.1 8.0 %collective-permute-start = (f32[32,128]{1,0:T(8,128)}, f32[32,128]{1,0:T(8,128)S(1)}, u32[]{:S(2)}, u32[]{:S(2)}) collective-permute-start(f32[32,128]{1,0:T(8,128)} %get-tuple-element.26.refs_2_), channel_id=1, source_target_pairs={{0,4},{4,8},{8,12},{12,16},{16,20},{20,24},{24,28},{28,0},{1,5},{5... | collective-permute-start | bytes 49160 | tf_op jit(solution)/shard_map/ppermute | solution.py:388
  13.5 8.9 %collective-permute-start.1 = (f32[32,128]{1,0:T(8,128)}, f32[32,128]{1,0:T(8,128)S(1)}, u32[]{:S(2)}, u32[]{:S(2)}) collective-permute-start(f32[32,128]{1,0:T(8,128)} %get-tuple-element.26.refs_2_), channel_id=1, source_target_pairs={{0,8},{4,12},{8,16},{12,20},{16,24},{20,28},{24,0},{28,4},{1,9},{5... | collective-permute-start | bytes 49160 | tf_op jit(solution)/shard_map/ppermute | solution.py:388
  16.2 7.7 %collective-permute-start.2 = (f32[32,128]{1,0:T(8,128)}, f32[32,128]{1,0:T(8,128)S(1)}, u32[]{:S(2)}, u32[]{:S(2)}) collective-permute-start(f32[32,128]{1,0:T(8,128)} %get-tuple-element.26.refs_2_), channel_id=1, source_target_pairs={{0,12},{4,16},{8,20},{12,24},{16,28},{20,0},{24,4},{28,8},{1,13},{... | collective-permute-start | bytes 49160 | tf_op jit(solution)/shard_map/ppermute | solution.py:388
  18.7 5.2 %collective-permute-start.3 = (f32[32,128]{1,0:T(8,128)}, f32[32,128]{1,0:T(8,128)S(1)}, u32[]{:S(2)}, u32[]{:S(2)}) collective-permute-start(f32[32,128]{1,0:T(8,128)} %get-tuple-element.26.refs_2_), channel_id=1, source_target_pairs={{0,16},{4,20},{8,24},{12,28},{16,0},{20,4},{24,8},{28,12},{1,17},{... | collective-permute-start | bytes 49160 | tf_op jit(solution)/shard_map/ppermute | solution.py:388
  30.4 4.6 %collective-permute-start.7 = (f32[32,128]{1,0:T(8,128)S(1)}, f32[32,128]{1,0:T(8,128)S(1)}, u32[]{:S(2)}, u32[]{:S(2)}) collective-permute-start(f32[32,128]{1,0:T(8,128)S(1)} %get-tuple-element.27.refs_1_.refs_8_), channel_id=1, source_target_pairs={{0,1},{1,2},{2,3},{3,0},{4,5},{5,6},{6,7},{7,4},{8,9},{9,10},{10,1... | collective-permute-start | bytes 49160 | tf_op jit(solution)/shard_map/ppermute | solution.py:388
  39.5 5.7 %collective-permute-start.10 = (f32[32,128]{1,0:T(8,128)S(1)}, f32[32,128]{1,0:T(8,128)S(1)}, u32[]{:S(2)}, u32[]{:S(2)}) collective-permute-start(f32[32,128]{1,0:T(8,128)S(1)} %col_pass.2.refs_2_), channel_id=1, source_target_pairs={{0,4},{4,8},{8,12},{12,16},{16,20},{20,24},{24,28},{28,0},{1,5},{5... | collective-permute-start | bytes 49160 | tf_op jit(solution)/shard_map/ppermute | solution.py:388
  39.6 6.8 %collective-permute-start.11 = (f32[32,128]{1,0:T(8,128)S(1)}, f32[32,128]{1,0:T(8,128)S(1)}, u32[]{:S(2)}, u32[]{:S(2)}) collective-permute-start(f32[32,128]{1,0:T(8,128)S(1)} %col_pass.2.refs_2_), channel_id=1, source_target_pairs={{0,8},{4,12},{8,16},{12,20},{16,24},{20,28},{24,0},{28,4},{1,9},{5... | collective-permute-start | bytes 49160 | tf_op jit(solution)/shard_map/ppermute | solution.py:388
  40.3 6.7 %collective-permute-start.12 = (f32[32,128]{1,0:T(8,128)S(1)}, f32[32,128]{1,0:T(8,128)S(1)}, u32[]{:S(2)}, u32[]{:S(2)}) collective-permute-start(f32[32,128]{1,0:T(8,128)S(1)} %col_pass.2.refs_2_), channel_id=1, source_target_pairs={{0,12},{4,16},{8,20},{12,24},{16,28},{20,0},{24,4},{28,8},{1,13},{... | collective-permute-start | bytes 49160 | tf_op jit(solution)/shard_map/ppermute | solution.py:388
  42.8 4.6 %collective-permute-start.13 = (f32[32,128]{1,0:T(8,128)S(1)}, f32[32,128]{1,0:T(8,128)S(1)}, u32[]{:S(2)}, u32[]{:S(2)}) collective-permute-start(f32[32,128]{1,0:T(8,128)S(1)} %col_pass.2.refs_2_), channel_id=1, source_target_pairs={{0,16},{4,20},{8,24},{12,28},{16,0},{20,4},{24,8},{28,12},{1,17},{... | collective-permute-start | bytes 49160 | tf_op jit(solution)/shard_map/ppermute | solution.py:388
  61.3 6.1 %collective-permute-start.20 = (f32[32,128]{1,0:T(8,128)S(1)}, f32[32,128]{1,0:T(8,128)S(1)}, u32[]{:S(2)}, u32[]{:S(2)}) collective-permute-start(f32[32,128]{1,0:T(8,128)S(1)} %col_pass.3.refs_2_), channel_id=1, source_target_pairs={{0,4},{4,8},{8,12},{12,16},{16,20},{20,24},{24,28},{28,0},{1,5},{5... | collective-permute-start | bytes 49160 | tf_op jit(solution)/shard_map/ppermute | solution.py:388
  61.3 7.1 %collective-permute-start.21 = (f32[32,128]{1,0:T(8,128)S(1)}, f32[32,128]{1,0:T(8,128)S(1)}, u32[]{:S(2)}, u32[]{:S(2)}) collective-permute-start(f32[32,128]{1,0:T(8,128)S(1)} %col_pass.3.refs_2_), channel_id=1, source_target_pairs={{0,8},{4,12},{8,16},{12,20},{16,24},{20,28},{24,0},{28,4},{1,9},{5... | collective-permute-start | bytes 49160 | tf_op jit(solution)/shard_map/ppermute | solution.py:388
  62.5 7.3 %collective-permute-start.22 = (f32[32,128]{1,0:T(8,128)S(1)}, f32[32,128]{1,0:T(8,128)S(1)}, u32[]{:S(2)}, u32[]{:S(2)}) collective-permute-start(f32[32,128]{1,0:T(8,128)S(1)} %col_pass.3.refs_2_), channel_id=1, source_target_pairs={{0,12},{4,16},{8,20},{12,24},{16,28},{20,0},{24,4},{28,8},{1,13},{... | collective-permute-start | bytes 49160 | tf_op jit(solution)/shard_map/ppermute | solution.py:388
  64.9 4.8 %collective-permute-start.23 = (f32[32,128]{1,0:T(8,128)S(1)}, f32[32,128]{1,0:T(8,128)S(1)}, u32[]{:S(2)}, u32[]{:S(2)}) collective-permute-start(f32[32,128]{1,0:T(8,128)S(1)} %col_pass.3.refs_2_), channel_id=1, source_target_pairs={{0,16},{4,20},{8,24},{12,28},{16,0},{20,4},{24,8},{28,12},{1,17},{... | collective-permute-start | bytes 49160 | tf_op jit(solution)/shard_map/ppermute | solution.py:388
  102.9 8.7 %collective-permute-start.30 = (f32[4,256,256]{2,1,0:T(8,128)}, f32[4,256,256]{2,1,0:T(8,128)S(1)}, u32[]{:S(2)}, u32[]{:S(2)}) collective-permute-start(f32[4,256,256]{2,1,0:T(8,128)} %get-tuple-element.33), channel_id=1, source_target_pairs={{0,4},{4,0},{8,12},{12,8},{16,20},{20,16},{24,28},{28,24},{1,5},{5... | collective-permute-start | bytes 3145736 | tf_op jit(solution)/shard_map/ppermute | solution.py:393
  108.6 14.4 %collective-permute-start.36 = (f32[2,256,256]{2,1,0:T(8,128)S(1)}, f32[2,256,256]{2,1,0:T(8,128)S(1)}, u32[]{:S(2)}, u32[]{:S(2)}) collective-permute-start(f32[2,256,256]{2,1,0:T(8,128)S(1)} %get-tuple-element.40), channel_id=1, source_target_pairs={{0,2},{1,3},{2,0},{3,1},{4,6},{5,7},{6,4},{7,5},{8,10},{9,11},{10,... | collective-permute-start | bytes 1572872 | tf_op jit(solution)/shard_map/ppermute | solution.py:393
  110.2 15.3 %collective-permute-start.34 = (f32[2,256,256]{2,1,0:T(8,128)S(1)}, f32[2,256,256]{2,1,0:T(8,128)S(1)}, u32[]{:S(2)}, u32[]{:S(2)}) collective-permute-start(f32[2,256,256]{2,1,0:T(8,128)S(1)} %get-tuple-element.38), channel_id=1, source_target_pairs={{0,1},{1,0},{2,3},{3,2},{4,5},{5,4},{6,7},{7,6},{8,9},{9,8},{10,11... | collective-permute-start | bytes 1572872 | tf_op jit(solution)/shard_map/ppermute | solution.py:393
  111.7 16.2 %collective-permute-start.32 = (f32[256,256]{1,0:T(8,128)S(1)}, f32[256,256]{1,0:T(8,128)S(1)}, u32[]{:S(2)}, u32[]{:S(2)}) collective-permute-start(f32[256,256]{1,0:T(8,128)S(1)} %get-tuple-element.45), channel_id=1, source_target_pairs={{0,8},{4,12},{8,0},{12,4},{16,24},{20,28},{24,16},{28,20},{1,9},{5... | collective-permute-start | bytes 786440 | tf_op jit(solution)/shard_map/ppermute | solution.py:393
  123.1 9.8 %collective-permute-start.37 = (f32[1,256,256]{2,1,0:T(8,128)S(1)}, f32[1,256,256]{2,1,0:T(8,128)S(1)}, u32[]{:S(2)}, u32[]{:S(2)}) collective-permute-start(f32[1,256,256]{2,1,0:T(8,128)S(1)} %get-tuple-element.49), channel_id=1, source_target_pairs={{0,1},{1,0},{2,3},{3,2},{4,5},{5,4},{6,7},{7,6},{8,9},{9,8},{10,11... | collective-permute-start | bytes 786440 | tf_op jit(solution)/shard_map/ppermute | solution.py:393
  126.3 7.9 %collective-permute-start.35 = (f32[1,256,256]{2,1,0:T(8,128)}, f32[1,256,256]{2,1,0:T(8,128)S(1)}, u32[]{:S(2)}, u32[]{:S(2)}) collective-permute-start(f32[1,256,256]{2,1,0:T(8,128)} %get-tuple-element.51), channel_id=1, source_target_pairs={{0,2},{1,3},{2,0},{3,1},{4,6},{5,7},{6,4},{7,5},{8,10},{9,11},{10,... | collective-permute-start | bytes 786440 | tf_op jit(solution)/shard_map/ppermute | solution.py:393
  126.8 11.4 %collective-permute-start.31 = (f32[256,256]{1,0:T(8,128)S(1)}, f32[256,256]{1,0:T(8,128)S(1)}, u32[]{:S(2)}, u32[]{:S(2)}) collective-permute-start(f32[256,256]{1,0:T(8,128)S(1)} %get-tuple-element.46), channel_id=1, source_target_pairs={{0,8},{4,12},{8,0},{12,4},{16,24},{20,28},{24,16},{28,20},{1,9},{5... | collective-permute-start | bytes 786440 | tf_op jit(solution)/shard_map/ppermute | solution.py:393
  128.6 13.9 %collective-permute-start.33 = (f32[256,256]{1,0:T(8,128)}, f32[256,256]{1,0:T(8,128)S(1)}, u32[]{:S(2)}, u32[]{:S(2)}) collective-permute-start(f32[256,256]{1,0:T(8,128)} %fusion.4), channel_id=1, source_target_pairs={{0,16},{4,20},{8,24},{12,28},{16,0},{20,4},{24,8},{28,12},{1,17},{... | collective-permute-start | bytes 786440 | tf_op jit(solution)/shard_map/ppermute | solution.py:393
  143.9 9.9 %collective-permute-start.51 = (f32[256,256]{1,0:T(8,128)S(1)}, f32[256,256]{1,0:T(8,128)S(1)}, u32[]{:S(2)}, u32[]{:S(2)}) collective-permute-start(f32[256,256]{1,0:T(8,128)S(1)} %get-tuple-element.43.refs_8_), channel_id=1, source_target_pairs={{0,2},{1,3},{2,0},{3,1},{4,6},{5,7},{6,4},{7,5},{8,10},{9,11},{10,... | collective-permute-start | bytes 786440 | tf_op jit(solution)/shard_map/ppermute | solution.py:393
  144.7 9.7 %collective-permute-start.53 = (f32[256,256]{1,0:T(8,128)S(1)}, f32[256,256]{1,0:T(8,128)S(1)}, u32[]{:S(2)}, u32[]{:S(2)}) collective-permute-start(f32[256,256]{1,0:T(8,128)S(1)} %get-tuple-element.44.refs_12_), channel_id=1, source_target_pairs={{0,1},{1,0},{2,3},{3,2},{4,5},{5,4},{6,7},{7,6},{8,9},{9,8},{10,11... | collective-permute-start | bytes 786440 | tf_op jit(solution)/shard_map/ppermute | solution.py:393
  146.4 11.1 %collective-permute-start.46 = (f32[256,256]{1,0:T(8,128)S(1)}, f32[256,256]{1,0:T(8,128)S(1)}, u32[]{:S(2)}, u32[]{:S(2)}) collective-permute-start(f32[256,256]{1,0:T(8,128)S(1)} %get-tuple-element.42.refs_0_), channel_id=1, source_target_pairs={{0,16},{4,20},{8,24},{12,28},{16,0},{20,4},{24,8},{28,12},{1,17},{... | collective-permute-start | bytes 786440 | tf_op jit(solution)/shard_map/ppermute | solution.py:393
  150.5 9.2 %collective-permute-start.50 = (f32[256,256]{1,0:T(8,128)S(1)}, f32[256,256]{1,0:T(8,128)S(1)}, u32[]{:S(2)}, u32[]{:S(2)}) collective-permute-start(f32[256,256]{1,0:T(8,128)S(1)} %get-tuple-element.43.refs_8_), channel_id=1, source_target_pairs={{0,1},{1,0},{2,3},{3,2},{4,5},{5,4},{6,7},{7,6},{8,9},{9,8},{10,11... | collective-permute-start | bytes 786440 | tf_op jit(solution)/shard_map/ppermute | solution.py:393
  153.9 8.4 %collective-permute-start.54 = (f32[256,256]{1,0:T(8,128)S(1)}, f32[256,256]{1,0:T(8,128)S(1)}, u32[]{:S(2)}, u32[]{:S(2)}) collective-permute-start(f32[256,256]{1,0:T(8,128)S(1)} %get-tuple-element.44.refs_12_), channel_id=1, source_target_pairs={{0,2},{1,3},{2,0},{3,1},{4,6},{5,7},{6,4},{7,5},{8,10},{9,11},{10,... | collective-permute-start | bytes 786440 | tf_op jit(solution)/shard_map/ppermute | solution.py:393
  154.4 10.4 %collective-permute-start.52 = (f32[256,256]{1,0:T(8,128)S(1)}, f32[256,256]{1,0:T(8,128)S(1)}, u32[]{:S(2)}, u32[]{:S(2)}) collective-permute-start(f32[256,256]{1,0:T(8,128)S(1)} %collective-permute-done.51.refs_10_), channel_id=1, source_target_pairs={{0,1},{1,0},{2,3},{3,2},{4,5},{5,4},{6,7},{7,6},{8,9},{9,8},{10,11... | collective-permute-start | bytes 786440 | tf_op jit(solution)/shard_map/ppermute | solution.py:393
  155.8 12.7 %collective-permute-start.44 = (f32[256,256]{1,0:T(8,128)S(1)}, f32[256,256]{1,0:T(8,128)S(1)}, u32[]{:S(2)}, u32[]{:S(2)}) collective-permute-start(f32[256,256]{1,0:T(8,128)S(1)} %get-tuple-element.42.refs_0_), channel_id=1, source_target_pairs={{0,8},{4,12},{8,0},{12,4},{16,24},{20,28},{24,16},{28,20},{1,9},{5... | collective-permute-start | bytes 786440 | tf_op jit(solution)/shard_map/ppermute | solution.py:393
  157.6 12.4 %collective-permute-start.48 = (f32[256,256]{1,0:T(8,128)S(1)}, f32[256,256]{1,0:T(8,128)S(1)}, u32[]{:S(2)}, u32[]{:S(2)}) collective-permute-start(f32[256,256]{1,0:T(8,128)S(1)} %collective-permute-done.46.refs_4_), channel_id=1, source_target_pairs={{0,8},{4,12},{8,0},{12,4},{16,24},{20,28},{24,16},{28,20},{1,9},{5... | collective-permute-start | bytes 786440 | tf_op jit(solution)/shard_map/ppermute | solution.py:393
  159.6 8.9 %collective-permute-start.42 = (f32[3,8,128]{2,1,0:T(8,128)S(1)}, f32[3,8,128]{2,1,0:T(8,128)S(1)}, u32[]{:S(2)}, u32[]{:S(2)}) collective-permute-start(f32[3,8,128]{2,1,0:T(8,128)S(1)} %add.71), channel_id=1, source_target_pairs={{0,16},{4,20},{8,24},{12,28},{16,0},{20,4},{24,8},{28,12},{1,17},{... | collective-permute-start | bytes 36872 | tf_op jit(solution)/shard_map/ppermute | solution.py:393
  162.2 7.8 %collective-permute-start.55 = (f32[256,256]{1,0:T(8,128)S(1)}, f32[256,256]{1,0:T(8,128)S(1)}, u32[]{:S(2)}, u32[]{:S(2)}) collective-permute-start(f32[256,256]{1,0:T(8,128)S(1)} %collective-permute-done.53.refs_13_), channel_id=1, source_target_pairs={{0,2},{1,3},{2,0},{3,1},{4,6},{5,7},{6,4},{7,5},{8,10},{9,11},{10,... | collective-permute-start | bytes 786440 | tf_op jit(solution)/shard_map/ppermute | solution.py:393
  164.8 5.3 %collective-permute-start.43 = (f32[256,256]{1,0:T(8,128)S(1)}, f32[256,256]{1,0:T(8,128)S(1)}, u32[]{:S(2)}, u32[]{:S(2)}) collective-permute-start(f32[256,256]{1,0:T(8,128)S(1)} %get-tuple-element.42.refs_0_), channel_id=1, source_target_pairs={{0,4},{4,0},{8,12},{12,8},{16,20},{20,16},{24,28},{28,24},{1,5},{5... | collective-permute-start | bytes 786440 | tf_op jit(solution)/shard_map/ppermute | solution.py:393
  (42 other events, 220.9 us)

commit v3 on v2

--- a/solution.py
+++ b/solution.py
@@ -44,7 +44,12 @@
     return jnp.sum(block.reshape(block.shape[0] // 8, 8, block.shape[1]), axis=0)
 
 
-def score_kernel(slow, fast, protos, t_ref, col_ref, den_ref, ub_ref, ubt_ref, cb_ref, den_s):
+def copies(out_ref, src_ref):
+    for i in range(out_ref.shape[0]):
+        out_ref[i] = src_ref[...]
+
+
+def score_kernel(slow, fast, protos, t_ref, out_ref, den_ref, ubt_ref, cb_ref, ub_ref, den_s, col_ref):
     clips, feats = slow.shape
     count = protos.shape[0]
     for v, src in enumerate((slow, fast)):
@@ -95,39 +100,45 @@
     for v in range(2):
         for i in range(groups):
             den_ref[pl.ds(v * groups + i, 1), :] = to_line(den_s[v, i * LANES : (i + 1) * LANES, :])
-
-
-def scores(slow, fast, protos):
+    copies(out_ref, col_ref)
+
+
+def scores(slow, fast, protos, peers):
     clips, feats = slow.shape
     count = protos.shape[0]
     return pl.pallas_call(
         score_kernel,
         out_shape=(
             pltpu.VMEM((2, clips, count), jnp.float32),
-            jax.ShapeDtypeStruct((2 * count // LANES, LANES), jnp.float32),
+            jax.ShapeDtypeStruct((peers, 2 * count // LANES, LANES), jnp.float32),
             jax.ShapeDtypeStruct((2 * clips // LANES, LANES), jnp.float32),
-            jax.ShapeDtypeStruct((2, clips, feats), jnp.bfloat16),
             jax.ShapeDtypeStruct((2, feats, clips), jnp.bfloat16),
             jax.ShapeDtypeStruct((count, feats), jnp.bfloat16),
         ),
         in_specs=[vmem_spec()] * 3,
-        out_specs=(vmem_spec(),) * 6,
-        scratch_shapes=[pltpu.VMEM((2, clips, LANES), jnp.float32)],
-        compiler_params=params(40),
+        out_specs=(vmem_spec(),) * 5,
+        scratch_shapes=[
+            pltpu.VMEM((2, clips, feats), jnp.bfloat16),
+            pltpu.VMEM((2, clips, LANES), jnp.float32),
+            pltpu.VMEM((2 * count // LANES, LANES), jnp.float32),
+        ],
+        compiler_params=params(14),
         name="scores",
     )(slow, fast, protos)
 
 
-def row_kernel(protos_all, extra, parts, *refs):
-    t_ref, den_ref = refs[0], refs[1]
-    col_parts = refs[2 : 2 + parts]
-    row_ref, r_ref = refs[2 + parts :]
+def stack_sum(ref, first=0, size=None):
+    size = ref.shape[1] if size is None else size
+    total = ref[0, first : first + size, :]
+    for i in range(1, ref.shape[0]):
+        total = total + ref[i, first : first + size, :]
+    return total
+
+
+def row_kernel(protos_all, extra, t_ref, den_ref, col_ref, out_ref, r_ref, row_ref):
     clips, count = t_ref.shape[1:]
     groups, lines = clips // LANES, count // LANES
-    total = col_parts[0][...]
-    for part in col_parts[1:]:
-        total = total + part[...]
-    r_ref[...] = 1.0 / (float(protos_all) * total)
+    r_ref[...] = 1.0 / (float(protos_all) * stack_sum(col_ref))
     if extra:
         row_ref[2 * groups :, :] = den_ref[...]
     for v in range(2):
@@ -142,34 +153,30 @@
             return 0
 
         lax.fori_loop(0, groups, step, 0)
-
-
-def row_pass(t, den, col_parts, protos_all, extra):
+    copies(out_ref, row_ref)
+
+
+def row_pass(t, den, col_parts, protos_all, extra, peers):
     clips, count = t.shape[1:]
-    lines = 2 * clips // LANES
-    return pl.pallas_call(
-        functools.partial(row_kernel, protos_all, extra, len(col_parts)),
+    lines = 2 * clips // LANES * (2 if extra else 1)
+    return pl.pallas_call(
+        functools.partial(row_kernel, protos_all, extra),
         out_shape=(
-            jax.ShapeDtypeStruct((lines * (2 if extra else 1), LANES), jnp.float32),
+            jax.ShapeDtypeStruct((peers, lines, LANES), jnp.float32),
             jax.ShapeDtypeStruct((2 * count // LANES, LANES), jnp.float32),
         ),
-        in_specs=[vmem_spec()] * (2 + len(col_parts)),
+        in_specs=[vmem_spec()] * 3,
         out_specs=(vmem_spec(),) * 2,
-        compiler_params=params(16),
+        scratch_shapes=[pltpu.VMEM((lines, LANES), jnp.float32)],
+        compiler_params=params(8),
         name="row_pass",
-    )(pltpu.with_memory_space_constraint(t, pltpu.VMEM), den, *col_parts)
-
-
-def col_kernel(clips_all, parts, *refs):
-    t_ref = refs[0]
-    row_parts = refs[1 : 1 + parts]
-    col_ref, acc_s, s_s = refs[1 + parts :]
+    )(pltpu.with_memory_space_constraint(t, pltpu.VMEM), den, col_parts)
+
+
+def col_kernel(clips_all, t_ref, row_ref, out_ref, acc_s, s_s, col_ref):
     clips, count = t_ref.shape[1:]
     groups, lines = clips // LANES, count // LANES
-    total = row_parts[0][: 2 * groups, :]
-    for part in row_parts[1:]:
-        total = total + part[: 2 * groups, :]
-    s_s[...] = 1.0 / (float(clips_all) * total)
+    s_s[...] = 1.0 / (float(clips_all) * stack_sum(row_ref, 0, 2 * groups))
     acc_s[...] = jnp.zeros_like(acc_s)
     for v in range(2):
 
@@ -187,40 +194,33 @@
             col_ref[v * lines + j : v * lines + j + 1, :] = jnp.sum(
                 acc_s[v, :, j * LANES : (j + 1) * LANES], axis=0, keepdims=True
             )
-
-
-def col_pass(t, row_parts, clips_all):
+    copies(out_ref, col_ref)
+
+
+def col_pass(t, row_parts, clips_all, peers):
     clips, count = t.shape[1:]
     return pl.pallas_call(
-        functools.partial(col_kernel, clips_all, len(row_parts)),
-        out_shape=jax.ShapeDtypeStruct((2 * count // LANES, LANES), jnp.float32),
-        in_specs=[vmem_spec()] * (1 + len(row_parts)),
+        functools.partial(col_kernel, clips_all),
+        out_shape=jax.ShapeDtypeStruct((peers, 2 * count // LANES, LANES), jnp.float32),
+        in_specs=[vmem_spec()] * 2,
         out_specs=vmem_spec(),
         scratch_shapes=[
             pltpu.VMEM((2, 8, count), jnp.float32),
             pltpu.VMEM((2 * clips // LANES, LANES), jnp.float32),
+            pltpu.VMEM((2 * count // LANES, LANES), jnp.float32),
         ],
-        compiler_params=params(16),
+        compiler_params=params(8),
         name="col_pass",
-    )(pltpu.with_memory_space_constraint(t, pltpu.VMEM), *row_parts)
-
-
-def grad_kernel(parts, batch_count, *refs):
-    me_ref, t_ref, r_ref, ubt_ref = refs[:4]
-    row_parts = refs[4 : 4 + parts]
-    den_parts = refs[4 + parts : 4 + 2 * parts]
-    send_ref, keep_ref, g_ref, code_s, prob_s = refs[4 + 2 * parts :]
+    )(pltpu.with_memory_space_constraint(t, pltpu.VMEM), row_parts)
+
+
+def grad_kernel(batch_count, me_ref, t_ref, r_ref, ubt_ref, row_ref, den_ref, *outs):
+    send_ref, keep_ref, g_ref, code_s, prob_s = outs
     clips, count = t_ref.shape[1:]
     groups, lines = clips // LANES, count // LANES
     width = count // batch_count
-    total = row_parts[0][...]
-    for part in row_parts[1:]:
-        total = total + part[...]
-    code = (1.0 / TEMPER) / total
-    total = den_parts[0][2 * groups :, :]
-    for part in den_parts[1:]:
-        total = total + part[2 * groups :, :]
-    prob = (1.0 / TEMPER) / total
+    code = (1.0 / TEMPER) / stack_sum(row_ref, 0, 2 * groups)
+    prob = (1.0 / TEMPER) / stack_sum(den_ref, 2 * groups, 2 * groups)
     for v in range(2):
         for i in range(groups):
             line = v * groups + i
@@ -262,21 +262,21 @@
         (batch_count // 2, count // batch_count, feats), jnp.float32
     )
     return pl.pallas_call(
-        functools.partial(grad_kernel, len(row_parts), batch_count),
+        functools.partial(grad_kernel, batch_count),
         out_shape=(share, share, pltpu.VMEM((2, clips, count), jnp.bfloat16)),
-        in_specs=[pl.BlockSpec(memory_space=pltpu.SMEM)] + [vmem_spec()] * (3 + 2 * len(row_parts)),
+        in_specs=[pl.BlockSpec(memory_space=pltpu.SMEM)] + [vmem_spec()] * 5,
         out_specs=(vmem_spec(),) * 3,
         scratch_shapes=[
             pltpu.VMEM((2, clips, LANES), jnp.float32),
             pltpu.VMEM((2, clips, LANES), jnp.float32),
         ],
-        compiler_params=params(32),
+        compiler_params=params(14),
         cost_estimate=pl.CostEstimate(
             flops=4 * clips * count * feats, bytes_accessed=8 * MIB, transcendentals=0
         ),
         name="proto_gradients",
     )(
-        me, pltpu.with_memory_space_constraint(t, pltpu.VMEM), r, ubt, *row_parts, *den_parts
+        me, pltpu.with_memory_space_constraint(t, pltpu.VMEM), r, ubt, row_parts, den_parts
     )
 
 
@@ -309,7 +309,7 @@
         out_shape=(share,) * 4,
         in_specs=[pl.BlockSpec(memory_space=pltpu.SMEM)] + [vmem_spec()] * 2,
         out_specs=(vmem_spec(),) * 4,
-        compiler_params=params(24),
+        compiler_params=params(10),
         cost_estimate=pl.CostEstimate(
             flops=4 * clips * count * feats, bytes_accessed=8 * MIB, transcendentals=0
         ),
@@ -381,12 +381,8 @@
     )(me, squares, *pieces)
 
 
-def all_parts(own, axis):
-    count = lax.axis_size(axis)
-    parts = [own]
-    for shift in range(1, count):
-        parts.append(lax.ppermute(own, axis, [(i, (i + shift) % count) for i in range(count)]))
-    return parts
+def exchange(copied, axis):
+    return lax.all_to_all(copied, axis, split_axis=0, concat_axis=0, tiled=True)
 
 
 def swap(own, axis, bit):
@@ -447,14 +443,16 @@
     me_first = me[:1]
     me_second = me[1:2]
 
-    t, col, den, unit_b, unit_bt, proto_b = scores(slow_embed, fast_embed, prototypes)
+    t, col, den, unit_bt, proto_b = scores(slow_embed, fast_embed, prototypes, batch_count)
     for iteration in range(ITERS):
-        rows, r = row_pass(t, den, all_parts(col, "batch"), protos_all, iteration == 0)
-        row_parts = all_parts(rows, "proto")
+        rows, r = row_pass(
+            t, den, exchange(col, "batch"), protos_all, iteration == 0, proto_count
+        )
+        row_parts = exchange(rows, "proto")
         if iteration == 0:
             den_parts = row_parts
         if iteration + 1 < ITERS:
-            col = col_pass(t, row_parts, clips_all)
+            col = col_pass(t, row_parts, clips_all, batch_count)
 
     orders = (tuple(range(proto_bits)), tuple(reversed(range(proto_bits))))
     send, keep, g = proto_gradients(

time: 175 us -> 176 us (level)
  blocking collectives: 0 us -> 46.9 us
  starting transfers between devices: 64 us -> 21.7 us
  Pallas kernels: 45.5 us -> 41.6 us
  waiting for transfers between devices: 45.1 us -> 42.1 us
  other arithmetic: 1.8 us -> 4.56 us
    all_to_all x0 -> x5, blocking collectives: none -> 46.9 us  [exchange(): return lax.all_to_all(copied, axis, split_axis=0, concat_axis=0, tiled=True)]
    ppermute x30 -> x0, starting transfers between devices: 38.1 us -> none  [all_parts(): lax.ppermute(own, axis, [(i, (i + shift) % count) for i in range(count)])]
    ppermute x30 -> x0, waiting for transfers between devices: 12.7 us -> none  [all_parts(): lax.ppermute(own, axis, [(i, (i + shift) % count) for i in range(count)])]
    ppermute x26, starting transfers between devices: 25.9 us -> 18.2 us  [swap(): lax.ppermute(own, axis, [(i, i ^ 1 << bit) for i in range(lax.axis_size(a...]
    ppermute x26, waiting for transfers between devices: 32.4 us -> 37.5 us  [swap(): lax.ppermute(own, axis, [(i, i ^ 1 << bit) for i in range(lax.axis_size(a...]
    all_to_all x0 -> x1, waiting for transfers between devices: none -> 4.54 us  [exchange(): return lax.all_to_all(copied, axis, split_axis=0, concat_axis=0, tiled=True)]
    all_to_all x0 -> x1, starting transfers between devices: none -> 3.44 us  [exchange(): return lax.all_to_all(copied, axis, split_axis=0, concat_axis=0, tiled=True)]
    pallas_call x1, Pallas kernels: 12.5 us -> 9.41 us  [scores(): pl.pallas_call(score_kernel, out_shape=(pltpu.VMEM((2, clips, count), jnp...]
  transfers between devices with their start and end apart: 56 -> 27, of which waited for: 29 -> 15; matrix products, arithmetic and copies ran while one was open for 2% -> 4% of each run, Pallas kernels for 2% -> 2%
where the time goes in v3:
time: 176 us
  blocking collectives  46.9 us (27%)
  waiting for transfers between devices  42.1 us (24%)
  Pallas kernels  41.6 us (24%)
  starting transfers between devices  21.7 us (12%)
  local copies, waits for them, and re-layouts  18.1 us (10%)
  other arithmetic  4.56 us (3%)
    all_to_all x5, blocking collectives, exchange(): return lax.all_to_all(copied, axis, split_axis=0, concat_axis=0, tiled=True)  46.9 us
    ppermute x26, waiting for transfers between devices, swap(): lax.ppermute(own, axis, [(i, i ^ 1 << bit) for i in range(lax.axis_size(a...  37.5 us
    ppermute x26, starting transfers between devices, swap(): lax.ppermute(own, axis, [(i, i ^ 1 << bit) for i in range(lax.axis_size(a...  18.2 us
    unnamed x14, local copies, waits for them, and re-layouts  16.1 us
    pallas_call x1, Pallas kernels, proto_gradients(): pl.pallas_call(functools.partial(grad_kernel, batch_count), out_shape=(sh...  11.1 us
    pallas_call x3, Pallas kernels, row_pass(): pl.pallas_call(functools.partial(row_kernel, protos_all, extra), out_shap...  10.6 us
    pallas_call x1, Pallas kernels, scores(): pl.pallas_call(score_kernel, out_shape=(pltpu.VMEM((2, clips, count), jnp...  9.41 us
    pallas_call x2, Pallas kernels, col_pass(): pl.pallas_call(functools.partial(col_kernel, clips_all), out_shape=jax.Sh...  4.71 us
  transfers between devices with their start and end apart: 27, of which 15 were waited for; matrix products, arithmetic and copies ran while one was open for 4% of the time, Pallas kernels for 2%

profile of v3, /device:TPU:0, one launch (start us, length us, event | category | flops | bytes accessed | tf_op | source)
XLA Modules:
  0.0 175.7 jit_solution(15904668665064712956)
XLA Ops:
  0.6 1.6 copy-done.4
  4.3 9.4 %scores.1 = (f32[2,1024,2048]{2,1,0:T(8,128)S(1)}, f32[8,32,128]{2,1,0:T(8,128)S(1)}, f32[16,128]{1,0:T(8,128)S(1)}, bf16[2,256,1024]{2,1,0:T(8,128)(2,1)S(1)}, bf16[2048,256]{1,0:T(8,128)(2,1)S(1)}) custom-call(bf16[1024,256]{1,0:T(8,128)(2,1)S(1)} %copy-done.6, bf16[1024,256]{1,0:T(8,128)(2,1)S(1)} %copy-done.5, f32[2048,256]{1,0:T(8,128)S(1)} %copy-done.4), custom_call_target="tpu_custom_call" | custom-call | tf_op jit(solution)/shard_map/scores/pallas_call | solution.py:109
  13.7 12.9 %all_to_all.30.col_ref = f32[8,32,128]{2,1,0:T(8,128)S(1)} all-to-all(f32[8,32,128]{2,1,0:T(8,128)S(1)} %get-tuple-element.26), channel_id=1, replica_groups=mesh['batch'=8,'proto'=4] {'batch'}, dimensions={0} | all-to-all | bytes 262144 | tf_op jit(solution)/shard_map/all_to_all | solution.py:385
  26.6 3.5 %row_pass.3 = (f32[4,32,128]{2,1,0:T(8,128)S(1)}, f32[32,128]{1,0:T(8,128)}) custom-call(f32[2,1024,2048]{2,1,0:T(8,128)S(1)} %get-tuple-element.24.t_ref, f32[16,128]{1,0:T(8,128)S(1)} %get-tuple-element.25.den_ref, f32[8,32,128]{2,1,0:T(8,128)S(1)} %all_to_all.30.col_ref), custom_call_target="tpu_custom_call" | custom-call | tf_op jit(solution)/shard_map/row_pass/pallas_call | solution.py:162
  30.1 8.4 %all_to_all.31.row_ref.den_ref = f32[4,32,128]{2,1,0:T(8,128)S(1)} all-to-all(f32[4,32,128]{2,1,0:T(8,128)S(1)} %get-tuple-element.27), channel_id=1, replica_groups=mesh['batch'=8,'proto'=4] {'proto'}, dimensions={0} | all-to-all | bytes 131072 | tf_op jit(solution)/shard_map/all_to_all | solution.py:385
  38.5 2.4 %col_pass.2 = f32[8,32,128]{2,1,0:T(8,128)S(1)} custom-call(f32[2,1024,2048]{2,1,0:T(8,128)S(1)} %get-tuple-element.24.t_ref, f32[4,32,128]{2,1,0:T(8,128)S(1)} %all_to_all.31.row_ref.den_ref), custom_call_target="tpu_custom_call" | custom-call | tf_op jit(solution)/shard_map/col_pass/pallas_call | solution.py:202
  40.8 9.3 %all_to_all.32.col_ref = f32[8,32,128]{2,1,0:T(8,128)S(1)} all-to-all(f32[8,32,128]{2,1,0:T(8,128)S(1)} %col_pass.2), channel_id=1, replica_groups=mesh['batch'=8,'proto'=4] {'batch'}, dimensions={0} | all-to-all | bytes 262144 | tf_op jit(solution)/shard_map/all_to_all | solution.py:385
  50.1 3.4 %row_pass.4 = (f32[4,16,128]{2,1,0:T(8,128)S(1)}, f32[32,128]{1,0:T(8,128)}) custom-call(f32[2,1024,2048]{2,1,0:T(8,128)S(1)} %get-tuple-element.24.t_ref, f32[16,128]{1,0:T(8,128)S(1)} %get-tuple-element.25.den_ref, f32[8,32,128]{2,1,0:T(8,128)S(1)} %all_to_all.32.col_ref), custom_call_target="tpu_custom_call" | custom-call | tf_op jit(solution)/shard_map/row_pass/pallas_call | solution.py:162
  53.5 7.1 %all_to_all.33.row_ref = f32[4,16,128]{2,1,0:T(8,128)S(1)} all-to-all(f32[4,16,128]{2,1,0:T(8,128)S(1)} %get-tuple-element.28), channel_id=1, replica_groups=mesh['batch'=8,'proto'=4] {'proto'}, dimensions={0} | all-to-all | bytes 65536 | tf_op jit(solution)/shard_map/all_to_all | solution.py:385
  60.6 2.4 %col_pass.3 = f32[8,32,128]{2,1,0:T(8,128)S(1)} custom-call(f32[2,1024,2048]{2,1,0:T(8,128)S(1)} %get-tuple-element.24.t_ref, f32[4,16,128]{2,1,0:T(8,128)S(1)} %all_to_all.33.row_ref), custom_call_target="tpu_custom_call" | custom-call | tf_op jit(solution)/shard_map/col_pass/pallas_call | solution.py:202
  63.0 9.3 %all_to_all.34.col_ref = f32[8,32,128]{2,1,0:T(8,128)S(1)} all-to-all(f32[8,32,128]{2,1,0:T(8,128)S(1)} %col_pass.3), channel_id=1, replica_groups=mesh['batch'=8,'proto'=4] {'batch'}, dimensions={0} | all-to-all | bytes 262144 | tf_op jit(solution)/shard_map/all_to_all | solution.py:385
  72.3 3.7 %row_pass.5 = (f32[4,16,128]{2,1,0:T(8,128)}, f32[32,128]{1,0:T(8,128)S(1)}) custom-call(f32[2,1024,2048]{2,1,0:T(8,128)S(1)} %get-tuple-element.24.t_ref, f32[16,128]{1,0:T(8,128)S(1)} %get-tuple-element.25.den_ref, f32[8,32,128]{2,1,0:T(8,128)S(1)} %all_to_all.34.col_ref), custom_call_target="tpu_custom_call" | custom-call | tf_op jit(solution)/shard_map/row_pass/pallas_call | solution.py:162
  75.9 3.4 %all-to-all-start.5 = ((f32[4,16,128]{2,1,0:T(8,128)}), f32[4,16,128]{2,1,0:T(8,128)S(1)}, u32[]{:S(2)}, u32[]{:S(2)}) async-start(f32[4,16,128]{2,1,0:T(8,128)} %get-tuple-element.31), calls=%async_computation.5 | async-start | bytes 65536 | tf_op jit(solution)/shard_map/all_to_all | solution.py:385
  79.4 4.5 %all-to-all-done.5.row_ref = f32[4,16,128]{2,1,0:T(8,128)S(1)} async-done(((f32[4,16,128]{2,1,0:T(8,128)}), f32[4,16,128]{2,1,0:T(8,128)S(1)}, u32[]{:S(2)}, u32[]{:S(2)}) %all-to-all-start.5) | async-done | bytes 32800 | tf_op jit(solution)/shard_map/all_to_all | solution.py:385
  83.9 5.8 %copy-done.1 = f32[2,1024,2048]{2,1,0:T(8,128)S(1)} copy-done((f32[2,1024,2048]{2,1,0:T(8,128)S(1)}, f32[2,1024,2048]{2,1,0:T(8,128)}, u32[]{:S(2)}) %copy-start.1) | copy-done | bytes 16777240
  89.7 11.1 %proto_gradients.1 = (f32[4,256,256]{2,1,0:T(8,128)}, f32[4,256,256]{2,1,0:T(8,128)S(1)}, bf16[2,1024,2048]{2,1,0:T(8,128)(2,1)S(1)}) custom-call(s32[1]{0:T(128)} %bitcast.me_ref, f32[2,1024,2048]{2,1,0:T(8,128)S(1)} %copy-done.1, f32[32,128]{1,0:T(8,128)S(1)} %get-tuple-element.29.r_ref, bf16[2,256,1024]{2,1,0:T(8,128)(2,1)S(1)} %get-tuple-element.30.ubt_ref, ...), custom_call_target="tpu_custom_call" | custom-call | flops 2147483648 | bytes 8388608 | tf_op jit(solution)/shard_map/proto_gradients/pallas_call | solution.py:264
  100.7 3.3 %copy-done.2 = bf16[2,1024,2048]{2,1,0:T(8,128)(2,1)} copy-done((bf16[2,1024,2048]{2,1,0:T(8,128)(2,1)}, bf16[2,1024,2048]{2,1,0:T(8,128)(2,1)S(1)}, u32[]{:S(2)}) %copy-start.2) | copy-done | bytes 8388632
  104.0 3.4 %copy-done.3 = bf16[2,1024,2048]{2,1,0:T(8,128)(2,1)S(1)} copy-done((bf16[2,1024,2048]{2,1,0:T(8,128)(2,1)S(1)}, bf16[2,1024,2048]{2,1,0:T(8,128)(2,1)}, u32[]{:S(2)}) %copy-start.3) | copy-done | bytes 8388632
  107.4 2.3 %embed_gradients.1 = (f32[2,256,256]{2,1,0:T(8,128)S(1)}, f32[2,256,256]{2,1,0:T(8,128)S(1)}, f32[2,256,256]{2,1,0:T(8,128)S(1)}, f32[2,256,256]{2,1,0:T(8,128)S(1)}) custom-call(s32[1]{0:T(128)} %bitcast.1.me_ref, bf16[2,1024,2048]{2,1,0:T(8,128)(2,1)S(1)} %copy-done.3, bf16[2048,256]{1,0:T(8,128)(2,1)S(1)} %get-tuple-element.36.cb_ref), custom_call_target="tpu_custom_call" | custom-call | flops 2147483648 | bytes 8388608 | tf_op jit(solution)/shard_map/embed_gradients/pallas_call | solution.py:307
  113.1 11.0 %collective-permute-done.6 = f32[2,256,256]{2,1,0:T(8,128)S(1)} collective-permute-done((f32[2,256,256]{2,1,0:T(8,128)S(1)}, f32[2,256,256]{2,1,0:T(8,128)S(1)}, u32[]{:S(2)}, u32[]{:S(2)}) %collective-permute-start.6) | collective-permute-done | bytes 524320 | tf_op jit(solution)/shard_map/ppermute | solution.py:389
  127.7 1.7 fusion.4
  134.6 1.6 collective-permute-done.1.refs_3_
  136.2 7.0 %collective-permute-done.3.refs_4_ = f32[256,256]{1,0:T(8,128)S(1)} collective-permute-done((f32[256,256]{1,0:T(8,128)}, f32[256,256]{1,0:T(8,128)S(1)}, u32[]{:S(2)}, u32[]{:S(2)}) %collective-permute-start.3) | collective-permute-done | bytes 262176 | tf_op jit(solution)/shard_map/ppermute | solution.py:389
  147.3 1.6 collective-permute-start.9
  148.9 3.1 %collective-permute-done.9 = f32[3,8,128]{2,1,0:T(8,128)S(1)} collective-permute-done((f32[3,8,128]{2,1,0:T(8,128)S(1)}, f32[3,8,128]{2,1,0:T(8,128)S(1)}, u32[]{:S(2)}, u32[]{:S(2)}) %collective-permute-start.9) | collective-permute-done | bytes 12320 | tf_op jit(solution)/shard_map/ppermute | solution.py:389
  157.6 1.6 collective-permute-start.18
  159.2 2.0 %collective-permute-done.20.refs_9_ = f32[256,256]{1,0:T(8,128)S(1)} collective-permute-done((f32[256,256]{1,0:T(8,128)S(1)}, f32[256,256]{1,0:T(8,128)S(1)}, u32[]{:S(2)}, u32[]{:S(2)}) %collective-permute-start.20) | collective-permute-done | bytes 262176 | tf_op jit(solution)/shard_map/ppermute | solution.py:389
  161.3 1.7 collective-permute-start.12
  163.5 3.0 %collective-permute-done.22.refs_11_ = f32[256,256]{1,0:T(8,128)S(1)} collective-permute-done((f32[256,256]{1,0:T(8,128)S(1)}, f32[256,256]{1,0:T(8,128)S(1)}, u32[]{:S(2)}, u32[]{:S(2)}) %collective-permute-start.22) | collective-permute-done | bytes 262176 | tf_op jit(solution)/shard_map/ppermute | solution.py:389
  166.4 2.7 %collective-permute-done.12 = f32[3,8,128]{2,1,0:T(8,128)S(1)} collective-permute-done((f32[3,8,128]{2,1,0:T(8,128)S(1)}, f32[3,8,128]{2,1,0:T(8,128)S(1)}, u32[]{:S(2)}, u32[]{:S(2)}) %collective-permute-start.12) | collective-permute-done | bytes 12320 | tf_op jit(solution)/shard_map/ppermute | solution.py:389
  169.7 1.7 collective-permute-done.18.refs_6_
  172.9 2.8 %finish.1 = (f32[2048,256]{1,0:T(8,128)}, f32[1024,256]{1,0:T(8,128)}, f32[1024,256]{1,0:T(8,128)}) custom-call(s32[3]{0:T(128)S(1)} %pad_add_fusion.me_ref, f32[3,8,128]{2,1,0:T(8,128)S(1)} %add.72.square_ref, f32[256,256]{1,0:T(8,128)S(1)} %get-tuple-element.42.refs_0_, f32[256,256]{1,0:T(8,128)S(1)} %collective-permute-done.13.refs_1_, ...), custom_call_target="tpu_custom_call" | custom-call | tf_op jit(solution)/shard_map/finish/pallas_call | solution.py:371
  (65 shorter events, 26.3 us)
Async XLA Ops:
  0.6 1.6 copy-start.4
  13.7 58.5 %copy-start = (f32[2,1024,2048]{2,1,0:T(8,128)}, f32[2,1024,2048]{2,1,0:T(8,128)S(1)}, u32[]{:S(2)}) copy-start(f32[2,1024,2048]{2,1,0:T(8,128)S(1)} %get-tuple-element.24.t_ref) | copy-start | bytes 50331652
  75.9 8.0 %all-to-all-start.5 = ((f32[4,16,128]{2,1,0:T(8,128)}), f32[4,16,128]{2,1,0:T(8,128)S(1)}, u32[]{:S(2)}, u32[]{:S(2)}) async-start(f32[4,16,128]{2,1,0:T(8,128)} %get-tuple-element.31), calls=%async_computation.5 | async-start | bytes 65536 | tf_op jit(solution)/shard_map/all_to_all | solution.py:385
  83.9 5.8 %copy-start.1 = (f32[2,1024,2048]{2,1,0:T(8,128)S(1)}, f32[2,1024,2048]{2,1,0:T(8,128)}, u32[]{:S(2)}) copy-start(f32[2,1024,2048]{2,1,0:T(8,128)} %copy-done) | copy-start | bytes 50331652
  100.7 3.3 %copy-start.2 = (bf16[2,1024,2048]{2,1,0:T(8,128)(2,1)}, bf16[2,1024,2048]{2,1,0:T(8,128)(2,1)S(1)}, u32[]{:S(2)}) copy-start(bf16[2,1024,2048]{2,1,0:T(8,128)(2,1)S(1)} %get-tuple-element.35.g_ref) | copy-start | bytes 25165828
  104.0 6.9 %collective-permute-start = (f32[4,256,256]{2,1,0:T(8,128)}, f32[4,256,256]{2,1,0:T(8,128)}, u32[]{:S(2)}, u32[]{:S(2)}) collective-permute-start(f32[4,256,256]{2,1,0:T(8,128)} %get-tuple-element.33), channel_id=1, source_target_pairs={{0,4},{4,0},{8,12},{12,8},{16,20},{20,16},{24,28},{28,24},{1,5},{5... | collective-permute-start | bytes 3145736 | tf_op jit(solution)/shard_map/ppermute | solution.py:389
  104.0 3.4 %copy-start.3 = (bf16[2,1024,2048]{2,1,0:T(8,128)(2,1)S(1)}, bf16[2,1024,2048]{2,1,0:T(8,128)(2,1)}, u32[]{:S(2)}) copy-start(bf16[2,1024,2048]{2,1,0:T(8,128)(2,1)} %copy-done.2) | copy-start | bytes 25165828
  109.7 14.4 %collective-permute-start.6 = (f32[2,256,256]{2,1,0:T(8,128)S(1)}, f32[2,256,256]{2,1,0:T(8,128)S(1)}, u32[]{:S(2)}, u32[]{:S(2)}) collective-permute-start(f32[2,256,256]{2,1,0:T(8,128)S(1)} %get-tuple-element.40), channel_id=1, source_target_pairs={{0,2},{1,3},{2,0},{3,1},{4,6},{5,7},{6,4},{7,5},{8,10},{9,11},{10,... | collective-permute-start | bytes 1572872 | tf_op jit(solution)/shard_map/ppermute | solution.py:389
  110.5 15.1 %collective-permute-start.4 = (f32[2,256,256]{2,1,0:T(8,128)S(1)}, f32[2,256,256]{2,1,0:T(8,128)S(1)}, u32[]{:S(2)}, u32[]{:S(2)}) collective-permute-start(f32[2,256,256]{2,1,0:T(8,128)S(1)} %get-tuple-element.38), channel_id=1, source_target_pairs={{0,1},{1,0},{2,3},{3,2},{4,5},{5,4},{6,7},{7,6},{8,9},{9,8},{10,11... | collective-permute-start | bytes 1572872 | tf_op jit(solution)/shard_map/ppermute | solution.py:389
  112.2 15.6 %collective-permute-start.2 = (f32[256,256]{1,0:T(8,128)S(1)}, f32[256,256]{1,0:T(8,128)S(1)}, u32[]{:S(2)}, u32[]{:S(2)}) collective-permute-start(f32[256,256]{1,0:T(8,128)S(1)} %get-tuple-element.45), channel_id=1, source_target_pairs={{0,8},{4,12},{8,0},{12,4},{16,24},{20,28},{24,16},{28,20},{1,9},{5... | collective-permute-start | bytes 786440 | tf_op jit(solution)/shard_map/ppermute | solution.py:389
  124.9 8.1 %collective-permute-start.7 = (f32[1,256,256]{2,1,0:T(8,128)}, f32[1,256,256]{2,1,0:T(8,128)S(1)}, u32[]{:S(2)}, u32[]{:S(2)}) collective-permute-start(f32[1,256,256]{2,1,0:T(8,128)} %get-tuple-element.49), channel_id=1, source_target_pairs={{0,1},{1,0},{2,3},{3,2},{4,5},{5,4},{6,7},{7,6},{8,9},{9,8},{10,11... | collective-permute-start | bytes 786440 | tf_op jit(solution)/shard_map/ppermute | solution.py:389
  126.3 7.9 %collective-permute-start.5 = (f32[1,256,256]{2,1,0:T(8,128)}, f32[1,256,256]{2,1,0:T(8,128)S(1)}, u32[]{:S(2)}, u32[]{:S(2)}) collective-permute-start(f32[1,256,256]{2,1,0:T(8,128)} %get-tuple-element.51), channel_id=1, source_target_pairs={{0,2},{1,3},{2,0},{3,1},{4,6},{5,7},{6,4},{7,5},{8,10},{9,11},{10,... | collective-permute-start | bytes 786440 | tf_op jit(solution)/shard_map/ppermute | solution.py:389
  126.8 9.4 %collective-permute-start.1 = (f32[256,256]{1,0:T(8,128)S(1)}, f32[256,256]{1,0:T(8,128)S(1)}, u32[]{:S(2)}, u32[]{:S(2)}) collective-permute-start(f32[256,256]{1,0:T(8,128)S(1)} %get-tuple-element.46), channel_id=1, source_target_pairs={{0,8},{4,12},{8,0},{12,4},{16,24},{20,28},{24,16},{28,20},{1,9},{5... | collective-permute-start | bytes 786440 | tf_op jit(solution)/shard_map/ppermute | solution.py:389
  129.4 13.8 %collective-permute-start.3 = (f32[256,256]{1,0:T(8,128)}, f32[256,256]{1,0:T(8,128)S(1)}, u32[]{:S(2)}, u32[]{:S(2)}) collective-permute-start(f32[256,256]{1,0:T(8,128)} %fusion.4), channel_id=1, source_target_pairs={{0,16},{4,20},{8,24},{12,28},{16,0},{20,4},{24,8},{28,12},{1,17},{... | collective-permute-start | bytes 786440 | tf_op jit(solution)/shard_map/ppermute | solution.py:389
  143.6 3.7 %collective-permute-start.8 = (f32[3,8,128]{2,1,0:T(8,128)S(1)}, f32[3,8,128]{2,1,0:T(8,128)S(1)}, u32[]{:S(2)}, u32[]{:S(2)}) collective-permute-start(f32[3,8,128]{2,1,0:T(8,128)S(1)} %pad_maximum_fusion), channel_id=1, source_target_pairs={{0,1},{1,0},{2,3},{3,2},{4,5},{5,4},{6,7},{7,6},{8,9},{9,8},{10,11... | collective-permute-start | bytes 36872 | tf_op jit(solution)/shard_map/ppermute | solution.py:389
  145.2 8.7 %collective-permute-start.21 = (f32[256,256]{1,0:T(8,128)S(1)}, f32[256,256]{1,0:T(8,128)S(1)}, u32[]{:S(2)}, u32[]{:S(2)}) collective-permute-start(f32[256,256]{1,0:T(8,128)S(1)} %get-tuple-element.43.refs_8_), channel_id=1, source_target_pairs={{0,2},{1,3},{2,0},{3,1},{4,6},{5,7},{6,4},{7,5},{8,10},{9,11},{10,... | collective-permute-start | bytes 786440 | tf_op jit(solution)/shard_map/ppermute | solution.py:389
  146.6 8.2 %collective-permute-start.23 = (f32[256,256]{1,0:T(8,128)S(1)}, f32[256,256]{1,0:T(8,128)S(1)}, u32[]{:S(2)}, u32[]{:S(2)}) collective-permute-start(f32[256,256]{1,0:T(8,128)S(1)} %get-tuple-element.44.refs_12_), channel_id=1, source_target_pairs={{0,1},{1,0},{2,3},{3,2},{4,5},{5,4},{6,7},{7,6},{8,9},{9,8},{10,11... | collective-permute-start | bytes 786440 | tf_op jit(solution)/shard_map/ppermute | solution.py:389
  147.2 10.4 %collective-permute-start.16 = (f32[256,256]{1,0:T(8,128)S(1)}, f32[256,256]{1,0:T(8,128)S(1)}, u32[]{:S(2)}, u32[]{:S(2)}) collective-permute-start(f32[256,256]{1,0:T(8,128)S(1)} %get-tuple-element.42.refs_0_), channel_id=1, source_target_pairs={{0,16},{4,20},{8,24},{12,28},{16,0},{20,4},{24,8},{28,12},{1,17},{... | collective-permute-start | bytes 786440 | tf_op jit(solution)/shard_map/ppermute | solution.py:389
  147.3 4.8 %collective-permute-start.9 = (f32[3,8,128]{2,1,0:T(8,128)S(1)}, f32[3,8,128]{2,1,0:T(8,128)S(1)}, u32[]{:S(2)}, u32[]{:S(2)}) collective-permute-start(f32[3,8,128]{2,1,0:T(8,128)S(1)} %fusion.6), channel_id=1, source_target_pairs={{0,2},{1,3},{2,0},{3,1},{4,6},{5,7},{6,4},{7,5},{8,10},{9,11},{10,... | collective-permute-start | bytes 36872 | tf_op jit(solution)/shard_map/ppermute | solution.py:389
  152.1 1.2 collective-permute-start.10
  152.1 9.2 %collective-permute-start.20 = (f32[256,256]{1,0:T(8,128)S(1)}, f32[256,256]{1,0:T(8,128)S(1)}, u32[]{:S(2)}, u32[]{:S(2)}) collective-permute-start(f32[256,256]{1,0:T(8,128)S(1)} %get-tuple-element.43.refs_8_), channel_id=1, source_target_pairs={{0,1},{1,0},{2,3},{3,2},{4,5},{5,4},{6,7},{7,6},{8,9},{9,8},{10,11... | collective-permute-start | bytes 786440 | tf_op jit(solution)/shard_map/ppermute | solution.py:389
  153.3 3.9 %collective-permute-start.11 = (f32[3,8,128]{2,1,0:T(8,128)S(1)}, f32[3,8,128]{2,1,0:T(8,128)S(1)}, u32[]{:S(2)}, u32[]{:S(2)}) collective-permute-start(f32[3,8,128]{2,1,0:T(8,128)S(1)} %add.70), channel_id=1, source_target_pairs={{0,8},{4,12},{8,0},{12,4},{16,24},{20,28},{24,16},{28,20},{1,9},{5... | collective-permute-start | bytes 36872 | tf_op jit(solution)/shard_map/ppermute | solution.py:389
  153.8 9.1 %collective-permute-start.24 = (f32[256,256]{1,0:T(8,128)S(1)}, f32[256,256]{1,0:T(8,128)S(1)}, u32[]{:S(2)}, u32[]{:S(2)}) collective-permute-start(f32[256,256]{1,0:T(8,128)S(1)} %get-tuple-element.44.refs_12_), channel_id=1, source_target_pairs={{0,2},{1,3},{2,0},{3,1},{4,6},{5,7},{6,4},{7,5},{8,10},{9,11},{10,... | collective-permute-start | bytes 786440 | tf_op jit(solution)/shard_map/ppermute | solution.py:389
  154.7 11.7 %collective-permute-start.22 = (f32[256,256]{1,0:T(8,128)S(1)}, f32[256,256]{1,0:T(8,128)S(1)}, u32[]{:S(2)}, u32[]{:S(2)}) collective-permute-start(f32[256,256]{1,0:T(8,128)S(1)} %collective-permute-done.21.refs_10_), channel_id=1, source_target_pairs={{0,1},{1,0},{2,3},{3,2},{4,5},{5,4},{6,7},{7,6},{8,9},{9,8},{10,11... | collective-permute-start | bytes 786440 | tf_op jit(solution)/shard_map/ppermute | solution.py:389
  157.2 11.9 %collective-permute-start.14 = (f32[256,256]{1,0:T(8,128)S(1)}, f32[256,256]{1,0:T(8,128)S(1)}, u32[]{:S(2)}, u32[]{:S(2)}) collective-permute-start(f32[256,256]{1,0:T(8,128)S(1)} %get-tuple-element.42.refs_0_), channel_id=1, source_target_pairs={{0,8},{4,12},{8,0},{12,4},{16,24},{20,28},{24,16},{28,20},{1,9},{5... | collective-permute-start | bytes 786440 | tf_op jit(solution)/shard_map/ppermute | solution.py:389
  157.6 13.7 %collective-permute-start.18 = (f32[256,256]{1,0:T(8,128)S(1)}, f32[256,256]{1,0:T(8,128)S(1)}, u32[]{:S(2)}, u32[]{:S(2)}) collective-permute-start(f32[256,256]{1,0:T(8,128)S(1)} %collective-permute-done.16.refs_4_), channel_id=1, source_target_pairs={{0,8},{4,12},{8,0},{12,4},{16,24},{20,28},{24,16},{28,20},{1,9},{5... | collective-permute-start | bytes 786440 | tf_op jit(solution)/shard_map/ppermute | solution.py:389
  161.3 7.9 %collective-permute-start.12 = (f32[3,8,128]{2,1,0:T(8,128)S(1)}, f32[3,8,128]{2,1,0:T(8,128)S(1)}, u32[]{:S(2)}, u32[]{:S(2)}) collective-permute-start(f32[3,8,128]{2,1,0:T(8,128)S(1)} %add.71), channel_id=1, source_target_pairs={{0,16},{4,20},{8,24},{12,28},{16,0},{20,4},{24,8},{28,12},{1,17},{... | collective-permute-start | bytes 36872 | tf_op jit(solution)/shard_map/ppermute | solution.py:389
  163.0 8.4 %collective-permute-start.25 = (f32[256,256]{1,0:T(8,128)S(1)}, f32[256,256]{1,0:T(8,128)S(1)}, u32[]{:S(2)}, u32[]{:S(2)}) collective-permute-start(f32[256,256]{1,0:T(8,128)S(1)} %collective-permute-done.23.refs_13_), channel_id=1, source_target_pairs={{0,2},{1,3},{2,0},{3,1},{4,6},{5,7},{6,4},{7,5},{8,10},{9,11},{10,... | collective-permute-start | bytes 786440 | tf_op jit(solution)/shard_map/ppermute | solution.py:389
  166.4 5.0 %collective-permute-start.13 = (f32[256,256]{1,0:T(8,128)S(1)}, f32[256,256]{1,0:T(8,128)S(1)}, u32[]{:S(2)}, u32[]{:S(2)}) collective-permute-start(f32[256,256]{1,0:T(8,128)S(1)} %get-tuple-element.42.refs_0_), channel_id=1, source_target_pairs={{0,4},{4,0},{8,12},{12,8},{16,20},{20,16},{24,28},{28,24},{1,5},{5... | collective-permute-start | bytes 786440 | tf_op jit(solution)/shard_map/ppermute | solution.py:389
  169.1 2.3 %collective-permute-start.17 = (f32[256,256]{1,0:T(8,128)S(1)}, f32[256,256]{1,0:T(8,128)S(1)}, u32[]{:S(2)}, u32[]{:S(2)}) collective-permute-start(f32[256,256]{1,0:T(8,128)S(1)} %collective-permute-done.16.refs_4_), channel_id=1, source_target_pairs={{0,4},{4,0},{8,12},{12,8},{16,20},{20,16},{24,28},{28,24},{1,5},{5... | collective-permute-start | bytes 786440 | tf_op jit(solution)/shard_map/ppermute | solution.py:389
  169.1 2.3 %collective-permute-start.15 = (f32[256,256]{1,0:T(8,128)S(1)}, f32[256,256]{1,0:T(8,128)S(1)}, u32[]{:S(2)}, u32[]{:S(2)}) collective-permute-start(f32[256,256]{1,0:T(8,128)S(1)} %collective-permute-done.14.refs_2_), channel_id=1, source_target_pairs={{0,4},{4,0},{8,12},{12,8},{16,20},{20,16},{24,28},{28,24},{1,5},{5... | collective-permute-start | bytes 786440 | tf_op jit(solution)/shard_map/ppermute | solution.py:389
  171.3 1.5 collective-permute-start.19
  (2 other events, 2.1 us)

commit v4 on v1

v4 whole, which is shorter than its diff:
```python
import functools

import jax
import jax.numpy as jnp
from jax import lax
from jax.experimental import pallas as pl
from jax.experimental.pallas import tpu as pltpu
from jax.sharding import PartitionSpec as P

ITERS = 3


CODE_EPS = 0.05
TEMPER = 0.1
NORM_EPS = 1e-06
LANES = 128
MIB = 1024 * 1024


def vmem_spec():
    return pl.BlockSpec(memory_space=pltpu.VMEM)


def params(limit):
    return pltpu.CompilerParams(vmem_limit_bytes=limit * MIB)


def to_columns(line):
    return jnp.broadcast_to(line, (LANES, LANES)).T


def to_line(partial):
    return jnp.sum(partial.T, axis=0, keepdims=True)


def lane_sum(block):
    total = block[:, :LANES]
    for j in range(1, block.shape[1] // LANES):
        total = total + block[:, j * LANES : (j + 1) * LANES]
    return total


def row_fold(block):
    return jnp.sum(block.reshape(block.shape[0] // 8, 8, block.shape[1]), axis=0)


def sum_of(refs, first=0, size=None):
    size = refs[0].shape[0] if size is None else size
    total = refs[0][first : first + size, :]
    for ref in refs[1:]:
        total = total + ref[first : first + size, :]
    return total


LOG2E = 1.4426950408889634


def score_kernel(slow, fast, protos, t_ref, col_ref, den_ref, ubt_ref, cb_ref, raw_s, w_s, ub_s, den_s, sems):
    clips, feats = slow.shape
    count = protos.shape[0]
    loads = []
    for v, src in enumerate((slow, fast)):
        loads.append(pltpu.make_async_copy(src, raw_s.at[v], sems.at[v]))
    loads.append(pltpu.make_async_copy(protos, w_s, sems.at[2]))
    for load in loads:
        load.start()
    for v in range(2):
        loads[v].wait()
        for first in range(0, clips, 256):
            rows = pl.ds(first, 256)
            x = raw_s[v, rows, :].astype(jnp.float32)
            length = jnp.sqrt(jnp.sum(x * x, axis=-1, keepdims=True) + 1e-12)
            u = x / length
            ub_s[v, rows, :] = u.astype(jnp.bfloat16)
            ubt_ref[:, v * clips + first : v * clips + first + 256] = u.T.astype(jnp.bfloat16)
    den_s[...] = jnp.zeros_like(den_s)
    loads[2].wait()

    def chunk(j, _):
        first = pl.multiple_of(j * 256, 256)
        w = w_s[pl.ds(first, 256), :]
        length = jnp.sqrt(jnp.sum(w * w, axis=-1, keepdims=True) + 1e-12)
        c = w / length
        cb_ref[pl.ds(first, 256), :] = c.astype(jnp.bfloat16)
        weights = c.T.astype(jnp.bfloat16)
        for v in range(2):
            cols = jnp.zeros((8, 256), jnp.float32)
            for r in range(0, clips, 512):
                s = jnp.dot(
                    ub_s[v, r : r + 512, :], weights, preferred_element_type=jnp.float32
                )
                for q in range(0, 512, 64):
                    rows = pl.ds(r + q, 64)
                    t = jnp.exp2(s[q : q + 64] * (LOG2E / TEMPER))
                    t_ref[v, rows, pl.ds(first, 256)] = t
                    cols = cols + row_fold(t * t)
                    den_s[v, rows, :] += lane_sum(t)
            line = jnp.sum(cols, axis=0, keepdims=True)
            for h in range(2):
                col_ref[pl.ds(v * (count // LANES) + j * 2 + h, 1), :] = line[
                    :, h * LANES : (h + 1) * LANES
                ]
        return 0

    lax.fori_loop(0, count // 256, chunk, 0)
    groups = clips // LANES
    for v in range(2):
        for i in range(groups):
            den_ref[pl.ds(v * groups + i, 1), :] = to_line(den_s[v, i * LANES : (i + 1) * LANES, :])


def scores(slow, fast, protos):
    clips, feats = slow.shape
    count = protos.shape[0]
    return pl.pallas_call(
        score_kernel,
        out_shape=(
            pltpu.VMEM((2, clips, count), jnp.float32),
            jax.ShapeDtypeStruct((2 * count // LANES, LANES), jnp.float32),
            jax.ShapeDtypeStruct((2 * clips // LANES, LANES), jnp.float32),
            jax.ShapeDtypeStruct((feats, 2 * clips), jnp.bfloat16),
            jax.ShapeDtypeStruct((count, feats), jnp.bfloat16),
        ),
        in_specs=[pl.BlockSpec(memory_space=pl.ANY)] * 3,
        out_specs=(vmem_spec(),) * 5,
        scratch_shapes=[
            pltpu.VMEM((2, clips, feats), jnp.bfloat16),
            pltpu.VMEM((count, feats), jnp.float32),
            pltpu.VMEM((2, clips, feats), jnp.bfloat16),
            pltpu.VMEM((2, clips, LANES), jnp.float32),
            pltpu.SemaphoreType.DMA((3,)),
        ],
        compiler_params=params(20),
        name="scores",
    )(slow, fast, protos)


def row_kernel(protos_all, extra, t_ref, den_ref, *refs):
    col_parts, (row_ref, r_ref) = refs[:-2], refs[-2:]
    clips, count = t_ref.shape[1:]
    groups, lines = clips // LANES, count // LANES
    r_ref[...] = 1.0 / (float(protos_all) * sum_of(col_parts))
    if extra:
        row_ref[2 * groups :, :] = den_ref[...]
    for v in range(2):

        def step(i, _, v=v):
            rows = pl.ds(pl.multiple_of(i * LANES, LANES), LANES)
            acc = jnp.zeros((LANES, LANES), jnp.float32)
            for j in range(lines):
                t = t_ref[v, rows, j * LANES : (j + 1) * LANES]
                acc = acc + t * t * r_ref[v * lines + j : v * lines + j + 1, :]
            row_ref[pl.ds(v * groups + i, 1), :] = to_line(acc)
            return 0

        lax.fori_loop(0, groups, step, 0)


def row_pass(t, den, col_parts, protos_all, extra):
    clips, count = t.shape[1:]
    lines = 2 * clips // LANES * (2 if extra else 1)
    return pl.pallas_call(
        functools.partial(row_kernel, protos_all, extra),
        out_shape=(
            jax.ShapeDtypeStruct((lines, LANES), jnp.float32),
            jax.ShapeDtypeStruct((2 * count // LANES, LANES), jnp.float32),
        ),
        in_specs=[vmem_spec()] * (2 + len(col_parts)),
        out_specs=(vmem_spec(),) * 2,
        compiler_params=params(8),
        name="row_pass",
    )(pltpu.with_memory_space_constraint(t, pltpu.VMEM), den, *col_parts)


def col_kernel(clips_all, t_ref, *refs):
    row_parts, (col_ref, acc_s, s_s) = refs[:-3], refs[-3:]
    clips, count = t_ref.shape[1:]
    groups, lines = clips // LANES, count // LANES
    s_s[...] = 1.0 / (float(clips_all) * sum_of(row_parts, 0, 2 * groups))
    acc_s[...] = jnp.zeros_like(acc_s)
    for v in range(2):

        def step(i, _, v=v):
            rows = pl.ds(pl.multiple_of(i * LANES, LANES), LANES)
            scale = to_columns(s_s[pl.ds(v * groups + i, 1), :])
            for j in range(lines):
                span = slice(j * LANES, (j + 1) * LANES)
                t = t_ref[v, rows, span]
                acc_s[v, :, span] += row_fold(t * t * scale)
            return 0

        lax.fori_loop(0, groups, step, 0)
        for j in range(lines):
            col_ref[v * lines + j : v * lines + j + 1, :] = jnp.sum(
                acc_s[v, :, j * LANES : (j + 1) * LANES], axis=0, keepdims=True
            )


def col_pass(t, row_parts, clips_all):
    clips, count = t.shape[1:]
    return pl.pallas_call(
        functools.partial(col_kernel, clips_all),
        out_shape=jax.ShapeDtypeStruct((2 * count // LANES, LANES), jnp.float32),
        in_specs=[vmem_spec()] * (1 + len(row_parts)),
        out_specs=vmem_spec(),
        scratch_shapes=[
            pltpu.VMEM((2, 8, count), jnp.float32),
            pltpu.VMEM((2 * clips // LANES, LANES), jnp.float32),
        ],
        compiler_params=params(8),
        name="col_pass",
    )(pltpu.with_memory_space_constraint(t, pltpu.VMEM), *row_parts)


def piece_of(position, order):
    steps = len(order)
    return sum(((position >> (steps - 1 - j)) & 1) << bit for j, bit in enumerate(order))


def place_of(piece, order):
    steps = len(order)
    return sum(((piece >> bit) & 1) << (steps - 1 - j) for j, bit in enumerate(order))


def grad_kernel(batch_orders, proto_orders, parts, me_ref, t_ref, r_ref, ubt_ref, cb_ref, *refs):
    row_parts, den_parts = refs[:parts], refs[parts : 2 * parts]
    send_ref, keep_ref = refs[2 * parts : 2 * parts + 2]
    du_refs = refs[2 * parts + 2 : 2 * parts + 6]
    g_s, odd_s, even_s, code_s, prob_s = refs[2 * parts + 6 :]
    clips, count = t_ref.shape[1:]
    groups, lines = clips // LANES, count // LANES
    pieces = 1 << len(batch_orders[0])
    width = count // (2 * pieces)
    half = width // 2
    code = (1.0 / TEMPER) / sum_of(row_parts, 0, 2 * groups)
    prob = (1.0 / TEMPER) / sum_of(den_parts, 2 * groups, 2 * groups)
    for v in range(2):
        for i in range(groups):
            line = v * groups + i
            rows = slice(i * LANES, (i + 1) * LANES)
            code_s[v, rows, :] = to_columns(code[line : line + 1, :])
            prob_s[v, rows, :] = to_columns(prob[line : line + 1, :])

    def score_grads(m, chunk_s):
        which = jnp.bitwise_xor(me_ref[0], m)
        first = pl.multiple_of(which * width, width)
        for i in range(0, clips, 32):
            rows = slice(i, i + 32)
            codes = [code_s[v, rows, :] for v in range(2)]
            probs = [prob_s[v, rows, :] for v in range(2)]
            for h in range(width // LANES):
                span = pl.ds(first + h * LANES, LANES)
                line = which * (width // LANES) + h
                t = [t_ref[v, rows, span] for v in range(2)]
                q = [
                    t[v] * t[v] * r_ref[pl.ds(v * lines + line, 1), :] * codes[v]
                    for v in range(2)
                ]
                for v in range(2):
                    g = (t[v] * probs[v] - q[1 - v]).astype(jnp.bfloat16)
                    g_s[v, rows, span] = g
                    chunk_s[v * clips + i : v * clips + i + 32, h * LANES : (h + 1) * LANES] = g

    def proto_grads(i, chunk_s, out_ref):
        dct = jnp.dot(ubt_ref[...], chunk_s[...], preferred_element_type=jnp.float32)
        dc = dct.T
        for h in range(2):
            place = place_of(i, batch_orders[h])
            out_ref[h, place] = dc[h * half : (h + 1) * half]

    even_s[...] = jnp.zeros_like(even_s)

    def pair(i, _):
        score_grads(2 * i + 1, odd_s)
        proto_grads(jnp.maximum(i - 1, 0), even_s, keep_ref)
        score_grads(2 * i, even_s)
        proto_grads(i, odd_s, send_ref)
        return 0

    lax.fori_loop(0, pieces, pair, 0)
    proto_grads(pieces - 1, even_s, keep_ref)

    peers = 1 << len(proto_orders[0])
    size = clips // peers
    for v in range(2):
        for place in range(peers):
            which = jnp.bitwise_xor(me_ref[1], piece_of(place, proto_orders[v]))
            rows = pl.ds(pl.multiple_of(which * size, size), size)
            out_ref = du_refs[2 * v + (0 if place >= peers // 2 else 1)]
            out_ref[place % (peers // 2)] = jnp.dot(
                g_s[v, rows, :], cb_ref[...], preferred_element_type=jnp.float32
            )


def gradients(me, t, r, ubt, cb, row_parts, den_parts, batch_orders, proto_orders):
    clips, count = t.shape[1:]
    feats = cb.shape[1]
    pieces, peers = 1 << len(batch_orders[0]), 1 << len(proto_orders[0])
    width = count // (2 * pieces)
    proto_share = jax.ShapeDtypeStruct((2, pieces, width // 2, feats), jnp.float32)
    embed_share = jax.ShapeDtypeStruct((peers // 2, clips // peers, feats), jnp.float32)
    return pl.pallas_call(
        functools.partial(grad_kernel, batch_orders, proto_orders, len(row_parts)),
        out_shape=(proto_share,) * 2 + (embed_share,) * 4,
        in_specs=[pl.BlockSpec(memory_space=pltpu.SMEM)] + [vmem_spec()] * (4 + 2 * len(row_parts)),
        out_specs=(vmem_spec(),) * 6,
        scratch_shapes=[
            pltpu.VMEM((2, clips, count), jnp.bfloat16),
            pltpu.VMEM((2 * clips, width), jnp.bfloat16),
            pltpu.VMEM((2 * clips, width), jnp.bfloat16),
            pltpu.VMEM((2, clips, LANES), jnp.float32),
            pltpu.VMEM((2, clips, LANES), jnp.float32),
        ],
        compiler_params=params(28),
        name="gradients",
    )(
        me,
        pltpu.with_memory_space_constraint(t, pltpu.VMEM),
        r,
        ubt,
        cb,
        *row_parts,
        *den_parts,
    )


def split_add_kernel(plan, inputs, *refs):
    ins, outs = refs[:inputs], refs[inputs:]
    for n, (keep_place, recv_place, part) in enumerate(plan):
        keep, recv = ins[keep_place], ins[recv_place]
        if part is not None:
            keep, recv = keep.at[part], recv.at[part]
        send_out, keep_out = outs[2 * n : 2 * n + 2]
        half = keep_out.shape[0]
        keep_out[...] = keep[:half] + recv[:half]
        send_out[...] = keep[half:] + recv[half:]


def split_add(arrays, plan):
    halves = []
    for place, _, part in plan:
        shape = arrays[place].shape if part is None else arrays[place].shape[1:]
        halves += [jax.ShapeDtypeStruct((shape[0] // 2,) + shape[1:], jnp.float32)] * 2
    outs = pl.pallas_call(
        functools.partial(split_add_kernel, plan, len(arrays)),
        out_shape=tuple(halves),
        in_specs=[vmem_spec()] * len(arrays),
        out_specs=(vmem_spec(),) * len(halves),
        compiler_params=params(12),
        name="split_add",
    )(*arrays)
    return [(outs[2 * n], outs[2 * n + 1]) for n in range(len(plan))]


def share_kernel(proto_raw, slow_raw, fast_raw, *refs):
    terms, (proto_out, embed_out, square_out) = refs[:-3], refs[-3:]
    half = proto_raw.shape[0] // 2
    jobs = [(proto_raw, slice(h * half, (h + 1) * half), None) for h in range(2)]
    jobs += [(raw, slice(None), v) for v, raw in enumerate((slow_raw, fast_raw))]
    squares = [jnp.zeros((8, LANES), jnp.float32)] * 2
    for n, (raw, rows, view) in enumerate(jobs):
        x = raw[rows, :].astype(jnp.float32)
        length = jnp.sqrt(jnp.sum(x * x, axis=-1, keepdims=True) + 1e-12)
        unit = x / length
        grad = terms[2 * n][0] + terms[2 * n + 1][0]
        along = jnp.sum(unit * grad, axis=-1, keepdims=True)
        grad = (grad - unit * along) / length
        if view is None:
            proto_out[rows, :] = grad
        else:
            embed_out[view] = grad
        kind = 0 if view is None else 1
        squares[kind] = squares[kind] + row_fold(lane_sum(grad * grad))
    for kind in range(2):
        total = jnp.sum(jnp.sum(squares[kind], axis=0, keepdims=True), axis=1, keepdims=True)
        square_out[kind] = jnp.broadcast_to(total, (8, LANES))


def project_shares(raws, terms):
    rows, feats = raws[1].shape
    return pl.pallas_call(
        share_kernel,
        out_shape=(
            jax.ShapeDtypeStruct(raws[0].shape, jnp.float32),
            jax.ShapeDtypeStruct((2, rows, feats), jnp.float32),
            jax.ShapeDtypeStruct((2, 8, LANES), jnp.float32),
        ),
        in_specs=[vmem_spec()] * (len(raws) + len(terms)),
        out_specs=(vmem_spec(),) * 3,
        compiler_params=params(10),
        name="project_shares",
    )(*raws, *terms)


def finish_kernel(entries, plan, inputs, me_ref, square_ref, *refs):
    ins, outs = refs[:inputs], refs[inputs:]
    for n, pieces in enumerate(plan):
        kind = min(n, 1)
        mean = square_ref[kind, 0:1, 0:1] / entries[kind]
        factor = lax.rsqrt(mean + NORM_EPS)
        for m, (place, view) in enumerate(pieces):
            src = ins[place][...] if view is None else ins[place][view]
            size = src.shape[0]
            which = jnp.bitwise_xor(me_ref[kind], m)
            outs[n][pl.ds(pl.multiple_of(which * size, size), size), :] = src * factor


def finish(me, squares, groups, entries):
    arrays, plan, outs = [], [], []
    for group in groups:
        pieces = []
        for array, view in group:
            place = next((i for i, other in enumerate(arrays) if other is array), None)
            if place is None:
                place = len(arrays)
                arrays.append(array)
            pieces.append((place, view))
        plan.append(pieces)
        rows, feats = group[0][0].shape[-2:]
        outs.append(jax.ShapeDtypeStruct((len(group) * rows, feats), jnp.float32))
    return pl.pallas_call(
        functools.partial(finish_kernel, entries, plan, len(arrays)),
        out_shape=tuple(outs),
        in_specs=[pl.BlockSpec(memory_space=pltpu.SMEM)] + [vmem_spec()] * (1 + len(arrays)),
        out_specs=(vmem_spec(),) * len(groups),
        compiler_params=params(16),
        name="finish",
    )(me, squares, *arrays)


def swap(own, axis, mask):
    return lax.ppermute(own, axis, [(i, i ^ mask) for i in range(lax.axis_size(axis))])


def bits_of(axis):
    count = lax.axis_size(axis)
    bits = count.bit_length() - 1
    if count != 1 << bits:
        raise ValueError("axis size")
    return bits


def proto_parts(own):
    return [own] + [swap(own, "proto", m) for m in range(1, lax.axis_size("proto"))]


def batch_parts(own):
    pair = own + swap(own, "batch", 1)
    return [pair] + [swap(pair, "batch", 2 * m) for m in range(1, lax.axis_size("batch") // 2)]


def scatter_sums(groups):
    stage, terms = 0, [None] * len(groups)
    state = list(groups)
    while any(term is None for term in terms):
        live = [n for n in range(len(state)) if terms[n] is None]
        recvs = {}
        for n in live:
            axis, order, send, keep = state[n]
            recvs[n] = swap(send, axis, 1 << order[stage])
        going = []
        for n in live:
            axis, order, send, keep = state[n]
            if stage + 1 == len(order):
                terms[n] = (keep, recvs[n])
            else:
                going.append(n)
        if going:
            arrays = [x for n in going for x in (state[n][3], recvs[n])]
            split = split_add(arrays, [(2 * i, 2 * i + 1, None) for i in range(len(going))])
            for n, (send, keep) in zip(going, split):
                state[n] = (state[n][0], state[n][1], send, keep)
        stage += 1
    return [x for term in terms for x in term]


def gather_batch(own):
    bits = list(reversed(range(lax.axis_size("batch").bit_length() - 1)))
    pieces = {0: own}
    first = {bit: swap(own, "batch", 1 << bit) for bit in bits}
    for bit in bits:
        for m in list(pieces):
            pieces[m | 1 << bit] = first[bit] if m == 0 else swap(pieces[m], "batch", 1 << bit)
    return [(pieces[m], None) for m in range(len(pieces))]


def gather_views(own, orders):
    first = {bit: swap(own, "proto", 1 << bit) for bit in sorted(orders[0])}
    groups = []
    for v, order in enumerate(orders):
        pieces = {0: (own, v)}
        for bit in order:
            for m in list(pieces):
                if m == 0:
                    pieces[1 << bit] = (first[bit], v)
                else:
                    array, view = pieces[m]
                    piece = array if view is None else array[view]
                    pieces[m | 1 << bit] = (swap(piece, "proto", 1 << bit), None)
        groups.append([pieces[m] for m in range(len(pieces))])
    return groups


def body(slow_embed, fast_embed, prototypes):
    clip_dev, feat_width = slow_embed.shape
    proto_dev = prototypes.shape[0]
    batch_count = lax.axis_size("batch")
    proto_count = lax.axis_size("proto")
    clips_all = clip_dev * batch_count
    protos_all = proto_dev * proto_count
    proto_entries = float(protos_all * feat_width)
    embed_entries = float(2 * clips_all * feat_width)
    batch_bits, proto_bits = bits_of("batch"), bits_of("proto")
    me_batch, me_proto = lax.axis_index("batch"), lax.axis_index("proto")
    me = jnp.stack([me_batch, me_proto]).astype(jnp.int32)

    t, col, den, unit_bt, proto_b = scores(slow_embed, fast_embed, prototypes)
    for iteration in range(ITERS):
        rows, r = row_pass(t, den, batch_parts(col), protos_all, iteration == 0)
        row_parts = proto_parts(rows)
        if iteration == 0:
            den_parts = row_parts
        if iteration + 1 < ITERS:
            col = col_pass(t, row_parts, clips_all)

    near = tuple(range(batch_bits - 1))
    batch_orders = (near, tuple(reversed(near)))
    proto_orders = (tuple(range(proto_bits)), tuple(reversed(range(proto_bits))))
    send, keep, *shares = gradients(
        me, t, r, unit_bt, proto_b, row_parts, den_parts, batch_orders, proto_orders
    )

    proto_rows = proto_dev // batch_count
    clip_rows = clip_dev // proto_count
    raws = [lax.dynamic_slice_in_dim(prototypes, me_batch * proto_rows, proto_rows, 0)]
    for x in (slow_embed, fast_embed):
        raws.append(lax.dynamic_slice_in_dim(x, me_proto * clip_rows, clip_rows, 0))
    recv = swap(send, "batch", 1)
    halves = split_add([keep, recv], [(0, 1, h) for h in range(2)])
    groups = []
    for h in range(2):
        order = tuple(bit + 1 for bit in batch_orders[h])
        groups.append(("batch", order) + tuple(halves[h]))
    for v in range(2):
        groups.append(("proto", proto_orders[v], shares[2 * v], shares[2 * v + 1]))
    grad_proto, grad_embed, squares = project_shares(raws, scatter_sums(groups))

    proto_pieces = gather_batch(grad_proto)
    view_pieces = gather_views(grad_embed, (proto_orders[1], proto_orders[0]))
    for bit in range(proto_bits):
        squares = squares + swap(squares, "proto", 1 << bit)
    for bit in range(batch_bits):
        squares = squares + swap(squares, "batch", 1 << bit)
    return finish(me, squares, [proto_pieces] + view_pieces, (proto_entries, embed_entries))


def solution(mesh):
    placed = (P("batch", None), P("batch", None), P("proto", None))
    return jax.shard_map(
        body,
        mesh=mesh,
        in_specs=placed,
        out_specs=(P("proto", None), P("batch", None), P("batch", None)),
        check_vma=False,
    )
```

time: 258 us -> 164 us (0.64)
  blocking collectives: 38.2 us -> 0 us
  waiting for transfers between devices: 103 us -> 69.3 us
  other arithmetic: 15 us -> 0.1 us
  between operations: 15.3 us -> 0.8 us
  local copies, waits for them, and re-layouts: 2.99 us -> 11.4 us
  Pallas kernels: 44.2 us -> 38.1 us
  starting transfers between devices: 38.2 us -> 44.3 us
    reduce_scatter x2 -> x0, waiting for transfers between devices: 67.9 us -> none  [the longest x1 34.4 us: body(): du_share = lax.psum_scatter(du, 'proto', scatter_dimension=0, tiled=True)]
    ppermute x30 -> x46, waiting for transfers between devices: 12.7 us -> 69.3 us  [swap(): lax.ppermute(own, axis, [(i, i ^ mask) for i in range(lax.axis_size(axis))])]
    psum x1 -> x0, blocking collectives: 38.2 us -> none  [body(): totals = lax.psum((proto_square, embed_square), ('batch', 'proto'))]
    all_gather x2 -> x0, waiting for transfers between devices: 21.9 us -> none  [the longest x1 21.9 us: body(): proto_all = lax.all_gather(grad_proto, 'batch', axis=0, tiled=True)]
    unnamed x28 -> x12, local copies, waits for them, and re-layouts: 2.99 us -> 9.45 us
    ppermute x30 -> x46, starting transfers between devices: 38.1 us -> 44.3 us  [swap(): lax.ppermute(own, axis, [(i, i ^ mask) for i in range(lax.axis_size(axis))])]
    reduce_sum x5 -> x0, other arithmetic: 6.18 us -> none  [the longest x2 2.49 us: project_back(): along = jnp.sum(unit_vec * grad_unit, axis=-1, keepdims=True)]
    mul x2 -> x0, other arithmetic: 6.04 us -> none  [the longest x1 3.05 us: body(): proto_all * proto_factor]
  transfers between devices with their start and end apart: 34 -> 46, of which waited for: 18 -> 32; matrix products, arithmetic and copies ran while one was open for 5% -> 1% of each run, Pallas kernels for 0% -> 0%
where the time goes in v4:
time: 164 us
  waiting for transfers between devices  69.3 us (42%)
  starting transfers between devices  44.3 us (27%)
  Pallas kernels  38.1 us (23%)
  local copies, waits for them, and re-layouts  11.4 us (7%)
    ppermute x46, waiting for transfers between devices, swap(): lax.ppermute(own, axis, [(i, i ^ mask) for i in range(lax.axis_size(axis))])  69.3 us
    ppermute x46, starting transfers between devices, swap(): lax.ppermute(own, axis, [(i, i ^ mask) for i in range(lax.axis_size(axis))])  44.3 us
    pallas_call x1, Pallas kernels, gradients(): pl.pallas_call(functools.partial(grad_kernel, batch_orders, proto_orders,...  12.1 us
    pallas_call x3, Pallas kernels, row_pass(): pl.pallas_call(functools.partial(row_kernel, protos_all, extra), out_shap...  9.92 us
    unnamed x12, local copies, waits for them, and re-layouts  9.45 us
    pallas_call x1, Pallas kernels, scores(): pl.pallas_call(score_kernel, out_shape=(pltpu.VMEM((2, clips, count), jnp...  7.75 us
    pallas_call x2, Pallas kernels, col_pass(): pl.pallas_call(functools.partial(col_kernel, clips_all), out_shape=jax.Sh...  4.69 us
  transfers between devices with their start and end apart: 46, of which 32 were waited for; matrix products, arithmetic and copies ran while one was open for 1% of the time, Pallas kernels for 0%

profile of v4, /device:TPU:0, one launch (start us, length us, event | category | flops | bytes accessed | tf_op | source)
XLA Modules:
  0.0 164.1 jit_solution(16148683498280699016)
XLA Ops:
  0.6 1.6 copy-done.3
  4.3 7.8 %scores.1 = (f32[2,1024,2048]{2,1,0:T(8,128)S(1)}, f32[32,128]{1,0:T(8,128)S(1)}, f32[16,128]{1,0:T(8,128)S(1)}, bf16[256,2048]{1,0:T(8,128)(2,1)S(1)}, bf16[2048,256]{1,0:T(8,128)(2,1)S(1)}) custom-call(bf16[1024,256]{1,0:T(8,128)(2,1)S(1)} %copy-done.5, bf16[1024,256]{1,0:T(8,128)(2,1)S(1)} %copy-done.4, f32[2048,256]{1,0:T(8,128)S(1)} %copy-done.3), custom_call_target="tpu_custom_call" | custom-call | tf_op jit(solution)/shard_map/scores/pallas_call | solution.py:115
  13.4 2.9 %collective-permute-start.1 = (f32[32,128]{1,0:T(8,128)S(1)}, f32[32,128]{1,0:T(8,128)S(1)}, u32[]{:S(2)}, u32[]{:S(2)}) collective-permute-start(f32[32,128]{1,0:T(8,128)S(1)} %add.33.refs_0_), channel_id=1, source_target_pairs={{0,8},{4,12},{8,0},{12,4},{16,24},{20,28},{24,16},{28,20},{1,9},{5... | collective-permute-start | bytes 49160 | tf_op jit(solution)/shard_map/ppermute | solution.py:432
  16.4 2.6 %collective-permute-start.2 = (f32[32,128]{1,0:T(8,128)S(1)}, f32[32,128]{1,0:T(8,128)S(1)}, u32[]{:S(2)}, u32[]{:S(2)}) collective-permute-start(f32[32,128]{1,0:T(8,128)S(1)} %add.33.refs_0_), channel_id=1, source_target_pairs={{0,16},{4,20},{8,24},{12,28},{16,0},{20,4},{24,8},{28,12},{1,17},{... | collective-permute-start | bytes 49160 | tf_op jit(solution)/shard_map/ppermute | solution.py:432
  19.0 2.0 %collective-permute-done.2.refs_2_ = f32[32,128]{1,0:T(8,128)S(1)} collective-permute-done((f32[32,128]{1,0:T(8,128)S(1)}, f32[32,128]{1,0:T(8,128)S(1)}, u32[]{:S(2)}, u32[]{:S(2)}) %collective-permute-start.2) | collective-permute-done | bytes 16416 | tf_op jit(solution)/shard_map/ppermute | solution.py:432
  21.0 3.5 %collective-permute-done.3.refs_3_ = f32[32,128]{1,0:T(8,128)S(1)} collective-permute-done((f32[32,128]{1,0:T(8,128)S(1)}, f32[32,128]{1,0:T(8,128)S(1)}, u32[]{:S(2)}, u32[]{:S(2)}) %collective-permute-start.3) | collective-permute-done | bytes 16416 | tf_op jit(solution)/shard_map/ppermute | solution.py:432
  24.5 3.5 %row_pass.3 = (f32[32,128]{1,0:T(8,128)S(1)}, f32[32,128]{1,0:T(8,128)}) custom-call(f32[2,1024,2048]{2,1,0:T(8,128)S(1)} %get-tuple-element.33.t_ref, f32[16,128]{1,0:T(8,128)S(1)} %get-tuple-element.34.den_ref, f32[32,128]{1,0:T(8,128)S(1)} %add.33.refs_0_, f32[32,128]{1,0:T(8,128)S(1)} %collective-permute-done.1.refs_1_, ...), custom_call_target="tpu_custom_call" | custom-call | tf_op jit(solution)/shard_map/row_pass/pallas_call | solution.py:162
  33.2 2.4 %collective-permute-done.6.refs_3_.refs_7_ = f32[32,128]{1,0:T(8,128)S(1)} collective-permute-done((f32[32,128]{1,0:T(8,128)S(1)}, f32[32,128]{1,0:T(8,128)S(1)}, u32[]{:S(2)}, u32[]{:S(2)}) %collective-permute-start.6) | collective-permute-done | bytes 16416 | tf_op jit(solution)/shard_map/ppermute | solution.py:432
  35.6 2.3 %col_pass.2 = f32[32,128]{1,0:T(8,128)S(1)} custom-call(f32[2,1024,2048]{2,1,0:T(8,128)S(1)} %get-tuple-element.33.t_ref, f32[32,128]{1,0:T(8,128)S(1)} %get-tuple-element.36.refs_0_.refs_4_, f32[32,128]{1,0:T(8,128)S(1)} %collective-permute-done.4.refs_1_.refs_5_, f32[32,128]{1,0:T(8,128)S(1)} %collective-permute-done.5.refs_2_.refs_6_, ...), custom_call_target="tpu_custom_call" | custom-call | tf_op jit(solution)/shard_map/col_pass/pallas_call | solution.py:201
  39.4 4.2 %collective-permute-start.9 = (f32[32,128]{1,0:T(8,128)S(1)}, f32[32,128]{1,0:T(8,128)S(1)}, u32[]{:S(2)}, u32[]{:S(2)}) collective-permute-start(f32[32,128]{1,0:T(8,128)S(1)} %add.34.refs_0_), channel_id=1, source_target_pairs={{0,16},{4,20},{8,24},{12,28},{16,0},{20,4},{24,8},{28,12},{1,17},{... | collective-permute-start | bytes 49160 | tf_op jit(solution)/shard_map/ppermute | solution.py:432
  45.3 3.5 %row_pass.4 = (f32[16,128]{1,0:T(8,128)S(1)}, f32[32,128]{1,0:T(8,128)}) custom-call(f32[2,1024,2048]{2,1,0:T(8,128)S(1)} %get-tuple-element.33.t_ref, f32[16,128]{1,0:T(8,128)S(1)} %get-tuple-element.34.den_ref, f32[32,128]{1,0:T(8,128)S(1)} %add.34.refs_0_, f32[32,128]{1,0:T(8,128)S(1)} %collective-permute-done.8.refs_1_, ...), custom_call_target="tpu_custom_call" | custom-call | tf_op jit(solution)/shard_map/row_pass/pallas_call | solution.py:162
  49.8 2.4 %collective-permute-start.13 = (f32[16,128]{1,0:T(8,128)S(1)}, f32[16,128]{1,0:T(8,128)S(1)}, u32[]{:S(2)}, u32[]{:S(2)}) collective-permute-start(f32[16,128]{1,0:T(8,128)S(1)} %get-tuple-element.37.refs_0_), channel_id=1, source_target_pairs={{0,3},{1,2},{2,1},{3,0},{4,7},{5,6},{6,5},{7,4},{8,11},{9,10},{10,... | collective-permute-start | bytes 24584 | tf_op jit(solution)/shard_map/ppermute | solution.py:432
  54.3 2.3 %col_pass.3 = f32[32,128]{1,0:T(8,128)S(1)} custom-call(f32[2,1024,2048]{2,1,0:T(8,128)S(1)} %get-tuple-element.33.t_ref, f32[16,128]{1,0:T(8,128)S(1)} %get-tuple-element.37.refs_0_, f32[16,128]{1,0:T(8,128)S(1)} %collective-permute-done.11.refs_1_, f32[16,128]{1,0:T(8,128)S(1)} %collective-permute-done.12.refs_2_, ...), custom_call_target="tpu_custom_call" | custom-call | tf_op jit(solution)/shard_map/col_pass/pallas_call | solution.py:201
  58.7 2.3 %collective-permute-start.16 = (f32[32,128]{1,0:T(8,128)S(1)}, f32[32,128]{1,0:T(8,128)S(1)}, u32[]{:S(2)}, u32[]{:S(2)}) collective-permute-start(f32[32,128]{1,0:T(8,128)S(1)} %add.35.refs_0_), channel_id=1, source_target_pairs={{0,16},{4,20},{8,24},{12,28},{16,0},{20,4},{24,8},{28,12},{1,17},{... | collective-permute-start | bytes 49160 | tf_op jit(solution)/shard_map/ppermute | solution.py:432
  63.3 3.1 %collective-permute-done.17.refs_3_ = f32[32,128]{1,0:T(8,128)S(1)} collective-permute-done((f32[32,128]{1,0:T(8,128)S(1)}, f32[32,128]{1,0:T(8,128)S(1)}, u32[]{:S(2)}, u32[]{:S(2)}) %collective-permute-start.17) | collective-permute-done | bytes 16416 | tf_op jit(solution)/shard_map/ppermute | solution.py:432
  66.5 5.8 %copy-done.1 = f32[2,1024,2048]{2,1,0:T(8,128)S(1)} copy-done((f32[2,1024,2048]{2,1,0:T(8,128)S(1)}, f32[2,1024,2048]{2,1,0:T(8,128)}, u32[]{:S(2)}) %copy-start.1) | copy-done | bytes 16777240
  72.3 3.0 %row_pass.5 = (f32[16,128]{1,0:T(8,128)S(1)}, f32[32,128]{1,0:T(8,128)S(1)}) custom-call(f32[2,1024,2048]{2,1,0:T(8,128)S(1)} %copy-done.1, f32[16,128]{1,0:T(8,128)S(1)} %get-tuple-element.34.den_ref, f32[32,128]{1,0:T(8,128)S(1)} %add.35.refs_0_, f32[32,128]{1,0:T(8,128)S(1)} %collective-permute-done.15.refs_1_, ...), custom_call_target="tpu_custom_call" | custom-call | tf_op jit(solution)/shard_map/row_pass/pallas_call | solution.py:162
  80.5 2.4 %collective-permute-done.20.refs_3_ = f32[16,128]{1,0:T(8,128)S(1)} collective-permute-done((f32[16,128]{1,0:T(8,128)S(1)}, f32[16,128]{1,0:T(8,128)S(1)}, u32[]{:S(2)}, u32[]{:S(2)}) %collective-permute-start.20) | collective-permute-done | bytes 8224 | tf_op jit(solution)/shard_map/ppermute | solution.py:432
  82.9 12.1 %gradients.1 = (f32[2,4,128,256]{3,2,1,0:T(8,128)S(1)}, f32[2,4,128,256]{3,2,1,0:T(8,128)S(1)}, f32[2,256,256]{2,1,0:T(8,128)S(1)}, f32[2,256,256]{2,1,0:T(8,128...) custom-call(s32[2]{0:T(128)S(1)} %pad_add_fusion.me_ref, f32[2,1024,2048]{2,1,0:T(8,128)S(1)} %copy-done.2, ...), custom_call_target="tpu_custom_call" | custom-call | tf_op jit(solution)/shard_map/gradients/pallas_call | solution.py:302
  98.1 1.8 %collective-permute-start.23 = (f32[2,128,256]{2,1,0:T(8,128)S(1)}, f32[2,128,256]{2,1,0:T(8,128)S(1)}, u32[]{:S(2)}, u32[]{:S(2)}) collective-permute-start(f32[2,128,256]{2,1,0:T(8,128)S(1)} %get-tuple-element.47), channel_id=1, source_target_pairs={{0,16},{4,20},{8,24},{12,28},{16,0},{20,4},{24,8},{28,12},{1,17},{... | collective-permute-start | bytes 786440 | tf_op jit(solution)/shard_map/ppermute | solution.py:432
  99.9 9.6 %collective-permute-done.24.refs_5_ = f32[2,256,256]{2,1,0:T(8,128)S(1)} collective-permute-done((f32[2,256,256]{2,1,0:T(8,128)S(1)}, f32[2,256,256]{2,1,0:T(8,128)S(1)}, u32[]{:S(2)}, u32[]{:S(2)}) %collective-permute-start.24) | collective-permute-done | bytes 524320 | tf_op jit(solution)/shard_map/ppermute | solution.py:432
  110.6 2.3 %collective-permute-done.23.refs_3_ = f32[2,128,256]{2,1,0:T(8,128)S(1)} collective-permute-done((f32[2,128,256]{2,1,0:T(8,128)S(1)}, f32[2,128,256]{2,1,0:T(8,128)S(1)}, u32[]{:S(2)}, u32[]{:S(2)}) %collective-permute-start.23) | collective-permute-done | bytes 262176 | tf_op jit(solution)/shard_map/ppermute | solution.py:432
  114.6 1.7 %collective-permute-start.27 = (f32[1,128,256]{2,1,0:T(8,128)S(1)}, f32[1,128,256]{2,1,0:T(8,128)S(1)}, u32[]{:S(2)}, u32[]{:S(2)}) collective-permute-start(f32[1,128,256]{2,1,0:T(8,128)S(1)} %get-tuple-element.55), channel_id=1, source_target_pairs={{0,8},{4,12},{8,0},{12,4},{16,24},{20,28},{24,16},{28,20},{1,9},{5... | collective-permute-start | bytes 393224 | tf_op jit(solution)/shard_map/ppermute | solution.py:432
  118.3 2.8 %collective-permute-done.26.refs_1_ = f32[1,128,256]{2,1,0:T(8,128)S(1)} collective-permute-done((f32[1,128,256]{2,1,0:T(8,128)S(1)}, f32[1,128,256]{2,1,0:T(8,128)S(1)}, u32[]{:S(2)}, u32[]{:S(2)}) %collective-permute-start.26) | collective-permute-done | bytes 131104 | tf_op jit(solution)/shard_map/ppermute | solution.py:432
  121.8 1.7 %collective-permute-start.43 = (f32[2,256,256]{2,1,0:T(8,128)S(1)}, f32[2,256,256]{2,1,0:T(8,128)S(1)}, u32[]{:S(2)}, u32[]{:S(2)}) collective-permute-start(f32[2,256,256]{2,1,0:T(8,128)S(1)} %get-tuple-element.62.refs_8_), channel_id=1, source_target_pairs={{0,2},{1,3},{2,0},{3,1},{4,6},{5,7},{6,4},{7,5},{8,10},{9,11},{10,... | collective-permute-start | bytes 1572872 | tf_op jit(solution)/shard_map/ppermute | solution.py:432
  126.3 10.1 %collective-permute-done.30 = f32[2,8,128]{2,1,0:T(8,128)S(1)} collective-permute-done((f32[2,8,128]{2,1,0:T(8,128)S(1)}, f32[2,8,128]{2,1,0:T(8,128)S(1)}, u32[]{:S(2)}, u32[]{:S(2)}) %collective-permute-start.30) | collective-permute-done | bytes 8224 | tf_op jit(solution)/shard_map/ppermute | solution.py:432
  136.9 2.0 %collective-permute-start.40 = (f32[256,256]{1,0:T(8,128)S(1)}, f32[256,256]{1,0:T(8,128)S(1)}, u32[]{:S(2)}, u32[]{:S(2)}) collective-permute-start(f32[256,256]{1,0:T(8,128)S(1)} %collective-permute-done.38.refs_4_), channel_id=1, source_target_pairs={{0,8},{4,12},{8,0},{12,4},{16,24},{20,28},{24,16},{28,20},{1,9},{5... | collective-permute-start | bytes 786440 | tf_op jit(solution)/shard_map/ppermute | solution.py:432
  141.3 6.5 %collective-permute-done.33 = f32[2,8,128]{2,1,0:T(8,128)S(1)} collective-permute-done((f32[2,8,128]{2,1,0:T(8,128)S(1)}, f32[2,8,128]{2,1,0:T(8,128)S(1)}, u32[]{:S(2)}, u32[]{:S(2)}) %collective-permute-start.33) | collective-permute-done | bytes 8224 | tf_op jit(solution)/shard_map/ppermute | solution.py:432
  150.1 2.3 %collective-permute-done.34 = f32[2,8,128]{2,1,0:T(8,128)S(1)} collective-permute-done((f32[2,8,128]{2,1,0:T(8,128)S(1)}, f32[2,8,128]{2,1,0:T(8,128)S(1)}, u32[]{:S(2)}, u32[]{:S(2)}) %collective-permute-start.34) | collective-permute-done | bytes 8224 | tf_op jit(solution)/shard_map/ppermute | solution.py:432
  152.3 1.7 %collective-permute-start.44 = (f32[256,256]{1,0:T(8,128)S(1)}, f32[256,256]{1,0:T(8,128)S(1)}, u32[]{:S(2)}, u32[]{:S(2)}) collective-permute-start(f32[256,256]{1,0:T(8,128)S(1)} %slice_bitcast_fusion.1), channel_id=1, source_target_pairs={{0,1},{1,0},{2,3},{3,2},{4,5},{5,4},{6,7},{7,6},{8,9},{9,8},{10,11... | collective-permute-start | bytes 786440 | tf_op jit(solution)/shard_map/ppermute | solution.py:432
  155.6 4.3 %collective-permute-done.44.refs_11_ = f32[256,256]{1,0:T(8,128)S(1)} collective-permute-done((f32[256,256]{1,0:T(8,128)S(1)}, f32[256,256]{1,0:T(8,128)S(1)}, u32[]{:S(2)}, u32[]{:S(2)}) %collective-permute-start.44) | collective-permute-done | bytes 262176 | tf_op jit(solution)/shard_map/ppermute | solution.py:432
  161.3 2.8 %finish.1 = (f32[2048,256]{1,0:T(8,128)}, f32[1024,256]{1,0:T(8,128)}, f32[1024,256]{1,0:T(8,128)}) custom-call(s32[2]{0:T(128)S(1)} %pad_add_fusion.me_ref, f32[2,8,128]{2,1,0:T(8,128)S(1)} %add.40.square_ref, f32[256,256]{1,0:T(8,128)S(1)} %get-tuple-element.61.refs_0_, f32[256,256]{1,0:T(8,128)S(1)} %collective-permute-done.35.refs_1_, ...), custom_call_target="tpu_custom_call" | custom-call | tf_op jit(solution)/shard_map/finish/pallas_call | solution.py:421
  (96 shorter events, 44.1 us)
Async XLA Ops:
  13.4 5.5 %collective-permute-start.1 = (f32[32,128]{1,0:T(8,128)S(1)}, f32[32,128]{1,0:T(8,128)S(1)}, u32[]{:S(2)}, u32[]{:S(2)}) collective-permute-start(f32[32,128]{1,0:T(8,128)S(1)} %add.33.refs_0_), channel_id=1, source_target_pairs={{0,8},{4,12},{8,0},{12,4},{16,24},{20,28},{24,16},{28,20},{1,9},{5... | collective-permute-start | bytes 49160 | tf_op jit(solution)/shard_map/ppermute | solution.py:432
  16.4 4.6 %collective-permute-start.2 = (f32[32,128]{1,0:T(8,128)S(1)}, f32[32,128]{1,0:T(8,128)S(1)}, u32[]{:S(2)}, u32[]{:S(2)}) collective-permute-start(f32[32,128]{1,0:T(8,128)S(1)} %add.33.refs_0_), channel_id=1, source_target_pairs={{0,16},{4,20},{8,24},{12,28},{16,0},{20,4},{24,8},{28,12},{1,17},{... | collective-permute-start | bytes 49160 | tf_op jit(solution)/shard_map/ppermute | solution.py:432
  18.9 5.5 %collective-permute-start.3 = (f32[32,128]{1,0:T(8,128)S(1)}, f32[32,128]{1,0:T(8,128)S(1)}, u32[]{:S(2)}, u32[]{:S(2)}) collective-permute-start(f32[32,128]{1,0:T(8,128)S(1)} %add.33.refs_0_), channel_id=1, source_target_pairs={{0,24},{4,28},{8,16},{12,20},{16,8},{20,12},{24,0},{28,4},{1,25},{... | collective-permute-start | bytes 49160 | tf_op jit(solution)/shard_map/ppermute | solution.py:432
  31.0 4.6 %collective-permute-start.6 = (f32[32,128]{1,0:T(8,128)S(1)}, f32[32,128]{1,0:T(8,128)S(1)}, u32[]{:S(2)}, u32[]{:S(2)}) collective-permute-start(f32[32,128]{1,0:T(8,128)S(1)} %get-tuple-element.36.refs_0_.refs_4_), channel_id=1, source_target_pairs={{0,3},{1,2},{2,1},{3,0},{4,7},{5,6},{6,5},{7,4},{8,11},{9,10},{10,... | collective-permute-start | bytes 49160 | tf_op jit(solution)/shard_map/ppermute | solution.py:432
  39.2 5.5 %collective-permute-start.10 = (f32[32,128]{1,0:T(8,128)S(1)}, f32[32,128]{1,0:T(8,128)S(1)}, u32[]{:S(2)}, u32[]{:S(2)}) collective-permute-start(f32[32,128]{1,0:T(8,128)S(1)} %add.34.refs_0_), channel_id=1, source_target_pairs={{0,24},{4,28},{8,16},{12,20},{16,8},{20,12},{24,0},{28,4},{1,25},{... | collective-permute-start | bytes 49160 | tf_op jit(solution)/shard_map/ppermute | solution.py:432
  39.4 5.3 %collective-permute-start.8 = (f32[32,128]{1,0:T(8,128)S(1)}, f32[32,128]{1,0:T(8,128)S(1)}, u32[]{:S(2)}, u32[]{:S(2)}) collective-permute-start(f32[32,128]{1,0:T(8,128)S(1)} %add.34.refs_0_), channel_id=1, source_target_pairs={{0,8},{4,12},{8,0},{12,4},{16,24},{20,28},{24,16},{28,20},{1,9},{5... | collective-permute-start | bytes 49160 | tf_op jit(solution)/shard_map/ppermute | solution.py:432
  39.4 5.9 %collective-permute-start.9 = (f32[32,128]{1,0:T(8,128)S(1)}, f32[32,128]{1,0:T(8,128)S(1)}, u32[]{:S(2)}, u32[]{:S(2)}) collective-permute-start(f32[32,128]{1,0:T(8,128)S(1)} %add.34.refs_0_), channel_id=1, source_target_pairs={{0,16},{4,20},{8,24},{12,28},{16,0},{20,4},{24,8},{28,12},{1,17},{... | collective-permute-start | bytes 49160 | tf_op jit(solution)/shard_map/ppermute | solution.py:432
  49.8 4.5 %collective-permute-start.13 = (f32[16,128]{1,0:T(8,128)S(1)}, f32[16,128]{1,0:T(8,128)S(1)}, u32[]{:S(2)}, u32[]{:S(2)}) collective-permute-start(f32[16,128]{1,0:T(8,128)S(1)} %get-tuple-element.37.refs_0_), channel_id=1, source_target_pairs={{0,3},{1,2},{2,1},{3,0},{4,7},{5,6},{6,5},{7,4},{8,11},{9,10},{10,... | collective-permute-start | bytes 24584 | tf_op jit(solution)/shard_map/ppermute | solution.py:432
  58.7 4.6 %collective-permute-start.16 = (f32[32,128]{1,0:T(8,128)S(1)}, f32[32,128]{1,0:T(8,128)S(1)}, u32[]{:S(2)}, u32[]{:S(2)}) collective-permute-start(f32[32,128]{1,0:T(8,128)S(1)} %add.35.refs_0_), channel_id=1, source_target_pairs={{0,16},{4,20},{8,24},{12,28},{16,0},{20,4},{24,8},{28,12},{1,17},{... | collective-permute-start | bytes 49160 | tf_op jit(solution)/shard_map/ppermute | solution.py:432
  60.9 5.5 %collective-permute-start.17 = (f32[32,128]{1,0:T(8,128)S(1)}, f32[32,128]{1,0:T(8,128)S(1)}, u32[]{:S(2)}, u32[]{:S(2)}) collective-permute-start(f32[32,128]{1,0:T(8,128)S(1)} %add.35.refs_0_), channel_id=1, source_target_pairs={{0,24},{4,28},{8,16},{12,20},{16,8},{20,12},{24,0},{28,4},{1,25},{... | collective-permute-start | bytes 49160 | tf_op jit(solution)/shard_map/ppermute | solution.py:432
  95.1 14.3 %collective-permute-start.24 = (f32[2,256,256]{2,1,0:T(8,128)S(1)}, f32[2,256,256]{2,1,0:T(8,128)S(1)}, u32[]{:S(2)}, u32[]{:S(2)}) collective-permute-start(f32[2,256,256]{2,1,0:T(8,128)S(1)} %get-tuple-element.49), channel_id=1, source_target_pairs={{0,1},{1,0},{2,3},{3,2},{4,5},{5,4},{6,7},{7,6},{8,9},{9,8},{10,11... | collective-permute-start | bytes 1572872 | tf_op jit(solution)/shard_map/ppermute | solution.py:432
  95.7 14.0 %collective-permute-start.25 = (f32[2,256,256]{2,1,0:T(8,128)S(1)}, f32[2,256,256]{2,1,0:T(8,128)S(1)}, u32[]{:S(2)}, u32[]{:S(2)}) collective-permute-start(f32[2,256,256]{2,1,0:T(8,128)S(1)} %get-tuple-element.51), channel_id=1, source_target_pairs={{0,2},{1,3},{2,0},{3,1},{4,6},{5,7},{6,4},{7,5},{8,10},{9,11},{10,... | collective-permute-start | bytes 1572872 | tf_op jit(solution)/shard_map/ppermute | solution.py:432
  97.9 12.8 %collective-permute-start.22 = (f32[2,128,256]{2,1,0:T(8,128)S(1)}, f32[2,128,256]{2,1,0:T(8,128)S(1)}, u32[]{:S(2)}, u32[]{:S(2)}) collective-permute-start(f32[2,128,256]{2,1,0:T(8,128)S(1)} %get-tuple-element.45), channel_id=1, source_target_pairs={{0,8},{4,12},{8,0},{12,4},{16,24},{20,28},{24,16},{28,20},{1,9},{5... | collective-permute-start | bytes 786440 | tf_op jit(solution)/shard_map/ppermute | solution.py:432
  98.1 14.8 %collective-permute-start.23 = (f32[2,128,256]{2,1,0:T(8,128)S(1)}, f32[2,128,256]{2,1,0:T(8,128)S(1)}, u32[]{:S(2)}, u32[]{:S(2)}) collective-permute-start(f32[2,128,256]{2,1,0:T(8,128)S(1)} %get-tuple-element.47), channel_id=1, source_target_pairs={{0,16},{4,20},{8,24},{12,28},{16,0},{20,4},{24,8},{28,12},{1,17},{... | collective-permute-start | bytes 786440 | tf_op jit(solution)/shard_map/ppermute | solution.py:432
  113.1 8.2 %collective-permute-start.28 = (f32[1,256,256]{2,1,0:T(8,128)S(1)}, f32[1,256,256]{2,1,0:T(8,128)S(1)}, u32[]{:S(2)}, u32[]{:S(2)}) collective-permute-start(f32[1,256,256]{2,1,0:T(8,128)S(1)} %get-tuple-element.57), channel_id=1, source_target_pairs={{0,2},{1,3},{2,0},{3,1},{4,6},{5,7},{6,4},{7,5},{8,10},{9,11},{10,... | collective-permute-start | bytes 786440 | tf_op jit(solution)/shard_map/ppermute | solution.py:432
  113.7 7.6 %collective-permute-start.29 = (f32[1,256,256]{2,1,0:T(8,128)S(1)}, f32[1,256,256]{2,1,0:T(8,128)S(1)}, u32[]{:S(2)}, u32[]{:S(2)}) collective-permute-start(f32[1,256,256]{2,1,0:T(8,128)S(1)} %get-tuple-element.59), channel_id=1, source_target_pairs={{0,1},{1,0},{2,3},{3,2},{4,5},{5,4},{6,7},{7,6},{8,9},{9,8},{10,11... | collective-permute-start | bytes 786440 | tf_op jit(solution)/shard_map/ppermute | solution.py:432
  114.4 6.7 %collective-permute-start.26 = (f32[1,128,256]{2,1,0:T(8,128)S(1)}, f32[1,128,256]{2,1,0:T(8,128)S(1)}, u32[]{:S(2)}, u32[]{:S(2)}) collective-permute-start(f32[1,128,256]{2,1,0:T(8,128)S(1)} %get-tuple-element.53), channel_id=1, source_target_pairs={{0,16},{4,20},{8,24},{12,28},{16,0},{20,4},{24,8},{28,12},{1,17},{... | collective-permute-start | bytes 393224 | tf_op jit(solution)/shard_map/ppermute | solution.py:432
  114.6 6.6 %collective-permute-start.27 = (f32[1,128,256]{2,1,0:T(8,128)S(1)}, f32[1,128,256]{2,1,0:T(8,128)S(1)}, u32[]{:S(2)}, u32[]{:S(2)}) collective-permute-start(f32[1,128,256]{2,1,0:T(8,128)S(1)} %get-tuple-element.55), channel_id=1, source_target_pairs={{0,8},{4,12},{8,0},{12,4},{16,24},{20,28},{24,16},{28,20},{1,9},{5... | collective-permute-start | bytes 393224 | tf_op jit(solution)/shard_map/ppermute | solution.py:432
  121.8 25.9 %collective-permute-start.43 = (f32[2,256,256]{2,1,0:T(8,128)S(1)}, f32[2,256,256]{2,1,0:T(8,128)S(1)}, u32[]{:S(2)}, u32[]{:S(2)}) collective-permute-start(f32[2,256,256]{2,1,0:T(8,128)S(1)} %get-tuple-element.62.refs_8_), channel_id=1, source_target_pairs={{0,2},{1,3},{2,0},{3,1},{4,6},{5,7},{6,4},{7,5},{8,10},{9,11},{10,... | collective-permute-start | bytes 1572872 | tf_op jit(solution)/shard_map/ppermute | solution.py:432
  123.5 13.4 %collective-permute-start.38 = (f32[256,256]{1,0:T(8,128)S(1)}, f32[256,256]{1,0:T(8,128)S(1)}, u32[]{:S(2)}, u32[]{:S(2)}) collective-permute-start(f32[256,256]{1,0:T(8,128)S(1)} %get-tuple-element.61.refs_0_), channel_id=1, source_target_pairs={{0,16},{4,20},{8,24},{12,28},{16,0},{20,4},{24,8},{28,12},{1,17},{... | collective-permute-start | bytes 786440 | tf_op jit(solution)/shard_map/ppermute | solution.py:432
  124.3 25.6 %collective-permute-start.42 = (f32[2,256,256]{2,1,0:T(8,128)S(1)}, f32[2,256,256]{2,1,0:T(8,128)S(1)}, u32[]{:S(2)}, u32[]{:S(2)}) collective-permute-start(f32[2,256,256]{2,1,0:T(8,128)S(1)} %get-tuple-element.62.refs_8_), channel_id=1, source_target_pairs={{0,1},{1,0},{2,3},{3,2},{4,5},{5,4},{6,7},{7,6},{8,9},{9,8},{10,11... | collective-permute-start | bytes 1572872 | tf_op jit(solution)/shard_map/ppermute | solution.py:432
  125.7 10.7 %collective-permute-start.30 = (f32[2,8,128]{2,1,0:T(8,128)S(1)}, f32[2,8,128]{2,1,0:T(8,128)S(1)}, u32[]{:S(2)}, u32[]{:S(2)}) collective-permute-start(f32[2,8,128]{2,1,0:T(8,128)S(1)} %get-tuple-element.60), channel_id=1, source_target_pairs={{0,1},{1,0},{2,3},{3,2},{4,5},{5,4},{6,7},{7,6},{8,9},{9,8},{10,11... | collective-permute-start | bytes 24584 | tf_op jit(solution)/shard_map/ppermute | solution.py:432
  136.9 12.4 %collective-permute-start.36 = (f32[256,256]{1,0:T(8,128)S(1)}, f32[256,256]{1,0:T(8,128)S(1)}, u32[]{:S(2)}, u32[]{:S(2)}) collective-permute-start(f32[256,256]{1,0:T(8,128)S(1)} %get-tuple-element.61.refs_0_), channel_id=1, source_target_pairs={{0,8},{4,12},{8,0},{12,4},{16,24},{20,28},{24,16},{28,20},{1,9},{5... | collective-permute-start | bytes 786440 | tf_op jit(solution)/shard_map/ppermute | solution.py:432
  136.9 12.6 %collective-permute-start.40 = (f32[256,256]{1,0:T(8,128)S(1)}, f32[256,256]{1,0:T(8,128)S(1)}, u32[]{:S(2)}, u32[]{:S(2)}) collective-permute-start(f32[256,256]{1,0:T(8,128)S(1)} %collective-permute-done.38.refs_4_), channel_id=1, source_target_pairs={{0,8},{4,12},{8,0},{12,4},{16,24},{20,28},{24,16},{28,20},{1,9},{5... | collective-permute-start | bytes 786440 | tf_op jit(solution)/shard_map/ppermute | solution.py:432
  141.3 6.5 %collective-permute-start.33 = (f32[2,8,128]{2,1,0:T(8,128)S(1)}, f32[2,8,128]{2,1,0:T(8,128)S(1)}, u32[]{:S(2)}, u32[]{:S(2)}) collective-permute-start(f32[2,8,128]{2,1,0:T(8,128)S(1)} %add.38), channel_id=1, source_target_pairs={{0,8},{4,12},{8,0},{12,4},{16,24},{20,28},{24,16},{28,20},{1,9},{5... | collective-permute-start | bytes 24584 | tf_op jit(solution)/shard_map/ppermute | solution.py:432
  147.7 6.3 %collective-permute-start.35 = (f32[256,256]{1,0:T(8,128)S(1)}, f32[256,256]{1,0:T(8,128)S(1)}, u32[]{:S(2)}, u32[]{:S(2)}) collective-permute-start(f32[256,256]{1,0:T(8,128)S(1)} %get-tuple-element.61.refs_0_), channel_id=1, source_target_pairs={{0,4},{4,0},{8,12},{12,8},{16,20},{20,16},{24,28},{28,24},{1,5},{5... | collective-permute-start | bytes 786440 | tf_op jit(solution)/shard_map/ppermute | solution.py:432
  147.7 4.6 %collective-permute-start.34 = (f32[2,8,128]{2,1,0:T(8,128)S(1)}, f32[2,8,128]{2,1,0:T(8,128)S(1)}, u32[]{:S(2)}, u32[]{:S(2)}) collective-permute-start(f32[2,8,128]{2,1,0:T(8,128)S(1)} %add.39), channel_id=1, source_target_pairs={{0,16},{4,20},{8,24},{12,28},{16,0},{20,4},{24,8},{28,12},{1,17},{... | collective-permute-start | bytes 24584 | tf_op jit(solution)/shard_map/ppermute | solution.py:432
  149.3 6.2 %collective-permute-start.39 = (f32[256,256]{1,0:T(8,128)S(1)}, f32[256,256]{1,0:T(8,128)S(1)}, u32[]{:S(2)}, u32[]{:S(2)}) collective-permute-start(f32[256,256]{1,0:T(8,128)S(1)} %collective-permute-done.38.refs_4_), channel_id=1, source_target_pairs={{0,4},{4,0},{8,12},{12,8},{16,20},{20,16},{24,28},{28,24},{1,5},{5... | collective-permute-start | bytes 786440 | tf_op jit(solution)/shard_map/ppermute | solution.py:432
  149.5 6.0 %collective-permute-start.37 = (f32[256,256]{1,0:T(8,128)S(1)}, f32[256,256]{1,0:T(8,128)S(1)}, u32[]{:S(2)}, u32[]{:S(2)}) collective-permute-start(f32[256,256]{1,0:T(8,128)S(1)} %collective-permute-done.36.refs_2_), channel_id=1, source_target_pairs={{0,4},{4,0},{8,12},{12,8},{16,20},{20,16},{24,28},{28,24},{1,5},{5... | collective-permute-start | bytes 786440 | tf_op jit(solution)/shard_map/ppermute | solution.py:432
  149.9 5.6 %collective-permute-start.41 = (f32[256,256]{1,0:T(8,128)S(1)}, f32[256,256]{1,0:T(8,128)S(1)}, u32[]{:S(2)}, u32[]{:S(2)}) collective-permute-start(f32[256,256]{1,0:T(8,128)S(1)} %collective-permute-done.40.refs_6_), channel_id=1, source_target_pairs={{0,4},{4,0},{8,12},{12,8},{16,20},{20,16},{24,28},{28,24},{1,5},{5... | collective-permute-start | bytes 786440 | tf_op jit(solution)/shard_map/ppermute | solution.py:432
  152.3 7.5 %collective-permute-start.44 = (f32[256,256]{1,0:T(8,128)S(1)}, f32[256,256]{1,0:T(8,128)S(1)}, u32[]{:S(2)}, u32[]{:S(2)}) collective-permute-start(f32[256,256]{1,0:T(8,128)S(1)} %slice_bitcast_fusion.1), channel_id=1, source_target_pairs={{0,1},{1,0},{2,3},{3,2},{4,5},{5,4},{6,7},{7,6},{8,9},{9,8},{10,11... | collective-permute-start | bytes 786440 | tf_op jit(solution)/shard_map/ppermute | solution.py:432
  154.0 7.2 %collective-permute-start.45 = (f32[256,256]{1,0:T(8,128)S(1)}, f32[256,256]{1,0:T(8,128)S(1)}, u32[]{:S(2)}, u32[]{:S(2)}) collective-permute-start(f32[256,256]{1,0:T(8,128)S(1)} %slice_bitcast_fusion), channel_id=1, source_target_pairs={{0,2},{1,3},{2,0},{3,1},{4,6},{5,7},{6,4},{7,5},{8,10},{9,11},{10,... | collective-permute-start | bytes 786440 | tf_op jit(solution)/shard_map/ppermute | solution.py:432
  (20 other events, 104.9 us)

commit v5 on v4

--- a/solution.py
+++ b/solution.py
@@ -121,7 +121,7 @@
             jax.ShapeDtypeStruct((feats, 2 * clips), jnp.bfloat16),
             jax.ShapeDtypeStruct((count, feats), jnp.bfloat16),
         ),
-        in_specs=[pl.BlockSpec(memory_space=pl.ANY)] * 3,
+        in_specs=[pl.BlockSpec(memory_space=pltpu.HBM)] * 3,
         out_specs=(vmem_spec(),) * 5,
         scratch_shapes=[
             pltpu.VMEM((2, clips, feats), jnp.bfloat16),
@@ -130,7 +130,7 @@
             pltpu.VMEM((2, clips, LANES), jnp.float32),
             pltpu.SemaphoreType.DMA((3,)),
         ],
-        compiler_params=params(20),
+        compiler_params=params(24),
         name="scores",
     )(slow, fast, protos)
 
@@ -222,7 +222,7 @@
     return sum(((piece >> bit) & 1) << (steps - 1 - j) for j, bit in enumerate(order))
 
 
-def grad_kernel(batch_orders, proto_orders, parts, me_ref, t_ref, r_ref, ubt_ref, cb_ref, *refs):
+def grad_kernel(batch_orders, proto_orders, parts, t_ref, r_ref, ubt_ref, cb_ref, *refs):
     row_parts, den_parts = refs[:parts], refs[parts : 2 * parts]
     send_ref, keep_ref = refs[2 * parts : 2 * parts + 2]
     du_refs = refs[2 * parts + 2 : 2 * parts + 6]
@@ -242,7 +242,7 @@
             prob_s[v, rows, :] = to_columns(prob[line : line + 1, :])
 
     def score_grads(m, chunk_s):
-        which = jnp.bitwise_xor(me_ref[0], m)
+        which = jnp.bitwise_xor(lax.axis_index("batch"), m)
         first = pl.multiple_of(which * width, width)
         for i in range(0, clips, 32):
             rows = slice(i, i + 32)
@@ -284,7 +284,7 @@
     size = clips // peers
     for v in range(2):
         for place in range(peers):
-            which = jnp.bitwise_xor(me_ref[1], piece_of(place, proto_orders[v]))
+            which = jnp.bitwise_xor(lax.axis_index("proto"), piece_of(place, proto_orders[v]))
             rows = pl.ds(pl.multiple_of(which * size, size), size)
             out_ref = du_refs[2 * v + (0 if place >= peers // 2 else 1)]
             out_ref[place % (peers // 2)] = jnp.dot(
@@ -292,7 +292,7 @@
             )
 
 
-def gradients(me, t, r, ubt, cb, row_parts, den_parts, batch_orders, proto_orders):
+def gradients(t, r, ubt, cb, row_parts, den_parts, batch_orders, proto_orders):
     clips, count = t.shape[1:]
     feats = cb.shape[1]
     pieces, peers = 1 << len(batch_orders[0]), 1 << len(proto_orders[0])
@@ -302,7 +302,7 @@
     return pl.pallas_call(
         functools.partial(grad_kernel, batch_orders, proto_orders, len(row_parts)),
         out_shape=(proto_share,) * 2 + (embed_share,) * 4,
-        in_specs=[pl.BlockSpec(memory_space=pltpu.SMEM)] + [vmem_spec()] * (4 + 2 * len(row_parts)),
+        in_specs=[vmem_spec()] * (4 + 2 * len(row_parts)),
         out_specs=(vmem_spec(),) * 6,
         scratch_shapes=[
             pltpu.VMEM((2, clips, count), jnp.bfloat16),
@@ -311,10 +311,9 @@
             pltpu.VMEM((2, clips, LANES), jnp.float32),
             pltpu.VMEM((2, clips, LANES), jnp.float32),
         ],
-        compiler_params=params(28),
+        compiler_params=params(24),
         name="gradients",
     )(
-        me,
         pltpu.with_memory_space_constraint(t, pltpu.VMEM),
         r,
         ubt,
@@ -352,65 +351,101 @@
     return [(outs[2 * n], outs[2 * n + 1]) for n in range(len(plan))]
 
 
+def project(raw, terms):
+    x = raw.astype(jnp.float32)
+    length = jnp.sqrt(jnp.sum(x * x, axis=-1, keepdims=True) + 1e-12)
+    unit = x / length
+    grad = terms[0][0] + terms[1][0]
+    along = jnp.sum(unit * grad, axis=-1, keepdims=True)
+    return (grad - unit * along) / length
+
+
 def share_kernel(proto_raw, slow_raw, fast_raw, *refs):
-    terms, (proto_out, embed_out, square_out) = refs[:-3], refs[-3:]
+    terms, (proto_out, square_out) = refs[:-2], refs[-2:]
     half = proto_raw.shape[0] // 2
-    jobs = [(proto_raw, slice(h * half, (h + 1) * half), None) for h in range(2)]
-    jobs += [(raw, slice(None), v) for v, raw in enumerate((slow_raw, fast_raw))]
     squares = [jnp.zeros((8, LANES), jnp.float32)] * 2
-    for n, (raw, rows, view) in enumerate(jobs):
-        x = raw[rows, :].astype(jnp.float32)
-        length = jnp.sqrt(jnp.sum(x * x, axis=-1, keepdims=True) + 1e-12)
-        unit = x / length
-        grad = terms[2 * n][0] + terms[2 * n + 1][0]
-        along = jnp.sum(unit * grad, axis=-1, keepdims=True)
-        grad = (grad - unit * along) / length
-        if view is None:
-            proto_out[rows, :] = grad
-        else:
-            embed_out[view] = grad
-        kind = 0 if view is None else 1
-        squares[kind] = squares[kind] + row_fold(lane_sum(grad * grad))
+    for h in range(2):
+        rows = slice(h * half, (h + 1) * half)
+        grad = project(proto_raw[rows, :], terms[2 * h : 2 * h + 2])
+        proto_out[rows, :] = grad
+        squares[0] = squares[0] + row_fold(lane_sum(grad * grad))
+    for v, raw in enumerate((slow_raw, fast_raw)):
+        grad = project(raw[...], terms[4 + 2 * v : 6 + 2 * v])
+        squares[1] = squares[1] + row_fold(lane_sum(grad * grad))
     for kind in range(2):
         total = jnp.sum(jnp.sum(squares[kind], axis=0, keepdims=True), axis=1, keepdims=True)
         square_out[kind] = jnp.broadcast_to(total, (8, LANES))
 
 
-def project_shares(raws, terms):
-    rows, feats = raws[1].shape
+def project_protos(raws, terms):
     return pl.pallas_call(
         share_kernel,
         out_shape=(
             jax.ShapeDtypeStruct(raws[0].shape, jnp.float32),
-            jax.ShapeDtypeStruct((2, rows, feats), jnp.float32),
             jax.ShapeDtypeStruct((2, 8, LANES), jnp.float32),
         ),
         in_specs=[vmem_spec()] * (len(raws) + len(terms)),
-        out_specs=(vmem_spec(),) * 3,
+        out_specs=(vmem_spec(),) * 2,
         compiler_params=params(10),
-        name="project_shares",
+        name="project_protos",
     )(*raws, *terms)
 
 
-def finish_kernel(entries, plan, inputs, me_ref, square_ref, *refs):
+def embed_kernel(square_ref, other_ref, slow_raw, fast_raw, *refs):
+    terms, (embed_out, square_out) = refs[:-2], refs[-2:]
+    square_out[...] = square_ref[...] + other_ref[...]
+    for v, raw in enumerate((slow_raw, fast_raw)):
+        embed_out[v] = project(raw[...], terms[2 * v : 2 * v + 2])
+
+
+def project_embeds(square, other, raws, terms):
+    rows, feats = raws[0].shape
+    return pl.pallas_call(
+        embed_kernel,
+        out_shape=(
+            jax.ShapeDtypeStruct((2, rows, feats), jnp.float32),
+            jax.ShapeDtypeStruct(square.shape, jnp.float32),
+        ),
+        in_specs=[vmem_spec()] * (2 + len(raws) + len(terms)),
+        out_specs=(vmem_spec(),) * 2,
+        compiler_params=params(10),
+        name="project_embeds",
+    )(square, other, *raws, *terms)
+
+
+def add_kernel(x_ref, y_ref, *refs):
+    refs[-1][...] = x_ref[...] + y_ref[...]
+
+
+def add_after(x, y, arrived):
+    return pl.pallas_call(
+        add_kernel,
+        out_shape=jax.ShapeDtypeStruct(x.shape, x.dtype),
+        in_specs=[vmem_spec()] * 2 + [pl.BlockSpec(memory_space=pl.ANY)] * len(arrived),
+        out_specs=vmem_spec(),
+        compiler_params=params(4),
+        name="add_after",
+    )(x, y, *arrived)
+
+
+def finish_kernel(axis, kind, entries, plan, inputs, square_ref, other_ref, *refs):
     ins, outs = refs[:inputs], refs[inputs:]
+    square = square_ref[kind, 0:1, 0:1] + other_ref[kind, 0:1, 0:1]
+    factor = lax.rsqrt(square / entries + NORM_EPS)
     for n, pieces in enumerate(plan):
-        kind = min(n, 1)
-        mean = square_ref[kind, 0:1, 0:1] / entries[kind]
-        factor = lax.rsqrt(mean + NORM_EPS)
         for m, (place, view) in enumerate(pieces):
             src = ins[place][...] if view is None else ins[place][view]
             size = src.shape[0]
-            which = jnp.bitwise_xor(me_ref[kind], m)
+            which = jnp.bitwise_xor(lax.axis_index(axis), m)
             outs[n][pl.ds(pl.multiple_of(which * size, size), size), :] = src * factor
 
 
-def finish(me, squares, groups, entries):
+def finish(axis, kind, entries, square, other, groups):
     arrays, plan, outs = [], [], []
     for group in groups:
         pieces = []
         for array, view in group:
-            place = next((i for i, other in enumerate(arrays) if other is array), None)
+            place = next((i for i, known in enumerate(arrays) if known is array), None)
             if place is None:
                 place = len(arrays)
                 arrays.append(array)
@@ -419,13 +454,13 @@
         rows, feats = group[0][0].shape[-2:]
         outs.append(jax.ShapeDtypeStruct((len(group) * rows, feats), jnp.float32))
     return pl.pallas_call(
-        functools.partial(finish_kernel, entries, plan, len(arrays)),
+        functools.partial(finish_kernel, axis, kind, entries, plan, len(arrays)),
         out_shape=tuple(outs),
-        in_specs=[pl.BlockSpec(memory_space=pltpu.SMEM)] + [vmem_spec()] * (1 + len(arrays)),
+        in_specs=[vmem_spec()] * (2 + len(arrays)),
         out_specs=(vmem_spec(),) * len(groups),
-        compiler_params=params(16),
+        compiler_params=params(12),
         name="finish",
-    )(me, squares, *arrays)
+    )(square, other, *arrays)
 
 
 def swap(own, axis, mask):
@@ -512,7 +547,6 @@
     embed_entries = float(2 * clips_all * feat_width)
     batch_bits, proto_bits = bits_of("batch"), bits_of("proto")
     me_batch, me_proto = lax.axis_index("batch"), lax.axis_index("proto")
-    me = jnp.stack([me_batch, me_proto]).astype(jnp.int32)
 
     t, col, den, unit_bt, proto_b = scores(slow_embed, fast_embed, prototypes)
     for iteration in range(ITERS):
@@ -527,7 +561,7 @@
     batch_orders = (near, tuple(reversed(near)))
     proto_orders = (tuple(range(proto_bits)), tuple(reversed(range(proto_bits))))
     send, keep, *shares = gradients(
-        me, t, r, unit_bt, proto_b, row_parts, den_parts, batch_orders, proto_orders
+        t, r, unit_bt, proto_b, row_parts, den_parts, batch_orders, proto_orders
     )
 
     proto_rows = proto_dev // batch_count
@@ -543,15 +577,22 @@
         groups.append(("batch", order) + tuple(halves[h]))
     for v in range(2):
         groups.append(("proto", proto_orders[v], shares[2 * v], shares[2 * v + 1]))
-    grad_proto, grad_embed, squares = project_shares(raws, scatter_sums(groups))
-
+    terms = scatter_sums(groups)
+    grad_proto, square = project_protos(raws, terms)
     proto_pieces = gather_batch(grad_proto)
+    for bit in range(proto_bits - 1):
+        square = square + swap(square, "proto", 1 << bit)
+    other = swap(square, "proto", 1 << (proto_bits - 1))
+    grad_embed, square = project_embeds(square, other, raws[1:], terms[4:])
     view_pieces = gather_views(grad_embed, (proto_orders[1], proto_orders[0]))
-    for bit in range(proto_bits):
-        squares = squares + swap(squares, "proto", 1 << bit)
-    for bit in range(batch_bits):
-        squares = squares + swap(squares, "batch", 1 << bit)
-    return finish(me, squares, [proto_pieces] + view_pieces, (proto_entries, embed_entries))
+    arrived = [proto_pieces[1 << bit][0] for bit in range(1, batch_bits)]
+    square = add_after(square, swap(square, "batch", 1), arrived)
+    for bit in range(1, batch_bits - 1):
+        square = square + swap(square, "batch", 1 << bit)
+    other = swap(square, "batch", 1 << (batch_bits - 1))
+    (proto_grad,) = finish("batch", 0, proto_entries, square, other, [proto_pieces])
+    slow_grad, fast_grad = finish("proto", 1, embed_entries, square, other, view_pieces)
+    return proto_grad, slow_grad, fast_grad
 
 
 def solution(mesh):

time: 164 us -> 157 us (0.957)
  local copies, waits for them, and re-layouts: 11.4 us -> 5.66 us
  starting transfers between devices: 44.3 us -> 42.5 us
    unnamed x12 -> x6, local copies, waits for them, and re-layouts: 9.45 us -> 3.67 us
    ppermute x46, starting transfers between devices: 44.3 us -> 42.5 us  [swap(): lax.ppermute(own, axis, [(i, i ^ mask) for i in range(lax.axis_size(axis))])]
    pallas_call x2 -> x5, Pallas kernels: 3.36 us -> 3.87 us  [the longest x2 2.97 us: finish(): pl.pallas_call(functools.partial(finish_kernel, axis, kind, entries, plan...]
  transfers between devices with their start and end apart: 46 -> 46, of which waited for: 32 -> 34; matrix products, arithmetic and copies ran while one was open for 1% -> 1% of each run, Pallas kernels for 0% -> 1%
where the time goes in v5:
time: 157 us; the launch traced here: 156 us
  waiting for transfers between devices  69.4 us (44%)
  starting transfers between devices  42.5 us (27%)
  Pallas kernels  38.1 us (24%)
  local copies, waits for them, and re-layouts  5.66 us (4%)
    ppermute x46, waiting for transfers between devices, swap(): lax.ppermute(own, axis, [(i, i ^ mask) for i in range(lax.axis_size(axis))])  69.4 us
    ppermute x46, starting transfers between devices, swap(): lax.ppermute(own, axis, [(i, i ^ mask) for i in range(lax.axis_size(axis))])  42.5 us
    pallas_call x1, Pallas kernels, gradients(): pl.pallas_call(functools.partial(grad_kernel, batch_orders, proto_orders,...  11.7 us
    pallas_call x3, Pallas kernels, row_pass(): pl.pallas_call(functools.partial(row_kernel, protos_all, extra), out_shap...  9.79 us
    pallas_call x1, Pallas kernels, scores(): pl.pallas_call(score_kernel, out_shape=(pltpu.VMEM((2, clips, count), jnp...  7.75 us
    pallas_call x2, Pallas kernels, col_pass(): pl.pallas_call(functools.partial(col_kernel, clips_all), out_shape=jax.Sh...  4.65 us
    unnamed x6, local copies, waits for them, and re-layouts  3.67 us
  transfers between devices with their start and end apart: 46, of which 34 were waited for; matrix products, arithmetic and copies ran while one was open for 1% of the time, Pallas kernels for 1%

profile of v5, /device:TPU:0, one launch (start us, length us, event | category | flops | bytes accessed | tf_op | source)
XLA Modules:
  0.0 156.5 jit_solution(8952760966108383447)
XLA Ops:
  4.3 7.8 %scores.1 = (f32[2,1024,2048]{2,1,0:T(8,128)S(1)}, f32[32,128]{1,0:T(8,128)S(1)}, f32[16,128]{1,0:T(8,128)S(1)}, bf16[256,2048]{1,0:T(8,128)(2,1)S(1)}, bf16[2048,256]{1,0:T(8,128)(2,1)S(1)}) custom-call(bf16[1024,256]{1,0:T(8,128)(2,1)S(1)} %copy-done.2, bf16[1024,256]{1,0:T(8,128)(2,1)S(1)} %copy-done.1, f32[2048,256]{1,0:T(8,128)S(1)} %copy-done), custom_call_target="tpu_custom_call" | custom-call | tf_op jit(solution)/shard_map/scores/pallas_call | solution.py:115
  13.4 2.9 %collective-permute-start.1 = (f32[32,128]{1,0:T(8,128)S(1)}, f32[32,128]{1,0:T(8,128)S(1)}, u32[]{:S(2)}, u32[]{:S(2)}) collective-permute-start(f32[32,128]{1,0:T(8,128)S(1)} %add.24.refs_0_), channel_id=1, source_target_pairs={{0,8},{4,12},{8,0},{12,4},{16,24},{20,28},{24,16},{28,20},{1,9},{5... | collective-permute-start | bytes 49160 | tf_op jit(solution)/shard_map/ppermute | solution.py:467
  16.3 2.6 %collective-permute-start.2 = (f32[32,128]{1,0:T(8,128)S(1)}, f32[32,128]{1,0:T(8,128)S(1)}, u32[]{:S(2)}, u32[]{:S(2)}) collective-permute-start(f32[32,128]{1,0:T(8,128)S(1)} %add.24.refs_0_), channel_id=1, source_target_pairs={{0,16},{4,20},{8,24},{12,28},{16,0},{20,4},{24,8},{28,12},{1,17},{... | collective-permute-start | bytes 49160 | tf_op jit(solution)/shard_map/ppermute | solution.py:467
  18.9 2.0 %collective-permute-done.2.refs_2_ = f32[32,128]{1,0:T(8,128)S(1)} collective-permute-done((f32[32,128]{1,0:T(8,128)S(1)}, f32[32,128]{1,0:T(8,128)S(1)}, u32[]{:S(2)}, u32[]{:S(2)}) %collective-permute-start.2) | collective-permute-done | bytes 16416 | tf_op jit(solution)/shard_map/ppermute | solution.py:467
  21.0 3.5 %collective-permute-done.3.refs_3_ = f32[32,128]{1,0:T(8,128)S(1)} collective-permute-done((f32[32,128]{1,0:T(8,128)S(1)}, f32[32,128]{1,0:T(8,128)S(1)}, u32[]{:S(2)}, u32[]{:S(2)}) %collective-permute-start.3) | collective-permute-done | bytes 16416 | tf_op jit(solution)/shard_map/ppermute | solution.py:467
  24.5 3.4 %row_pass.3 = (f32[32,128]{1,0:T(8,128)S(1)}, f32[32,128]{1,0:T(8,128)}) custom-call(f32[2,1024,2048]{2,1,0:T(8,128)S(1)} %get-tuple-element.36.t_ref, f32[16,128]{1,0:T(8,128)S(1)} %get-tuple-element.37.den_ref, f32[32,128]{1,0:T(8,128)S(1)} %add.24.refs_0_, f32[32,128]{1,0:T(8,128)S(1)} %collective-permute-done.1.refs_1_, ...), custom_call_target="tpu_custom_call" | custom-call | tf_op jit(solution)/shard_map/row_pass/pallas_call | solution.py:162
  33.1 2.4 %collective-permute-done.6.refs_3_.refs_7_ = f32[32,128]{1,0:T(8,128)S(1)} collective-permute-done((f32[32,128]{1,0:T(8,128)S(1)}, f32[32,128]{1,0:T(8,128)S(1)}, u32[]{:S(2)}, u32[]{:S(2)}) %collective-permute-start.6) | collective-permute-done | bytes 16416 | tf_op jit(solution)/shard_map/ppermute | solution.py:467
  35.5 2.3 %col_pass.2 = f32[32,128]{1,0:T(8,128)S(1)} custom-call(f32[2,1024,2048]{2,1,0:T(8,128)S(1)} %get-tuple-element.36.t_ref, f32[32,128]{1,0:T(8,128)S(1)} %get-tuple-element.39.refs_0_.refs_4_, f32[32,128]{1,0:T(8,128)S(1)} %collective-permute-done.4.refs_1_.refs_5_, f32[32,128]{1,0:T(8,128)S(1)} %collective-permute-done.5.refs_2_.refs_6_, ...), custom_call_target="tpu_custom_call" | custom-call | tf_op jit(solution)/shard_map/col_pass/pallas_call | solution.py:201
  39.3 4.2 %collective-permute-start.9 = (f32[32,128]{1,0:T(8,128)S(1)}, f32[32,128]{1,0:T(8,128)S(1)}, u32[]{:S(2)}, u32[]{:S(2)}) collective-permute-start(f32[32,128]{1,0:T(8,128)S(1)} %add.25.refs_0_), channel_id=1, source_target_pairs={{0,16},{4,20},{8,24},{12,28},{16,0},{20,4},{24,8},{28,12},{1,17},{... | collective-permute-start | bytes 49160 | tf_op jit(solution)/shard_map/ppermute | solution.py:467
  45.2 3.4 %row_pass.4 = (f32[16,128]{1,0:T(8,128)S(1)}, f32[32,128]{1,0:T(8,128)}) custom-call(f32[2,1024,2048]{2,1,0:T(8,128)S(1)} %get-tuple-element.36.t_ref, f32[16,128]{1,0:T(8,128)S(1)} %get-tuple-element.37.den_ref, f32[32,128]{1,0:T(8,128)S(1)} %add.25.refs_0_, f32[32,128]{1,0:T(8,128)S(1)} %collective-permute-done.8.refs_1_, ...), custom_call_target="tpu_custom_call" | custom-call | tf_op jit(solution)/shard_map/row_pass/pallas_call | solution.py:162
  49.6 2.4 %collective-permute-start.13 = (f32[16,128]{1,0:T(8,128)S(1)}, f32[16,128]{1,0:T(8,128)S(1)}, u32[]{:S(2)}, u32[]{:S(2)}) collective-permute-start(f32[16,128]{1,0:T(8,128)S(1)} %get-tuple-element.40.refs_0_), channel_id=1, source_target_pairs={{0,3},{1,2},{2,1},{3,0},{4,7},{5,6},{6,5},{7,4},{8,11},{9,10},{10,... | collective-permute-start | bytes 24584 | tf_op jit(solution)/shard_map/ppermute | solution.py:467
  54.2 2.3 %col_pass.3 = f32[32,128]{1,0:T(8,128)S(1)} custom-call(f32[2,1024,2048]{2,1,0:T(8,128)S(1)} %get-tuple-element.36.t_ref, f32[16,128]{1,0:T(8,128)S(1)} %get-tuple-element.40.refs_0_, f32[16,128]{1,0:T(8,128)S(1)} %collective-permute-done.11.refs_1_, f32[16,128]{1,0:T(8,128)S(1)} %collective-permute-done.12.refs_2_, ...), custom_call_target="tpu_custom_call" | custom-call | tf_op jit(solution)/shard_map/col_pass/pallas_call | solution.py:201
  58.5 2.3 %collective-permute-start.16 = (f32[32,128]{1,0:T(8,128)S(1)}, f32[32,128]{1,0:T(8,128)S(1)}, u32[]{:S(2)}, u32[]{:S(2)}) collective-permute-start(f32[32,128]{1,0:T(8,128)S(1)} %add.26.refs_0_), channel_id=1, source_target_pairs={{0,16},{4,20},{8,24},{12,28},{16,0},{20,4},{24,8},{28,12},{1,17},{... | collective-permute-start | bytes 49160 | tf_op jit(solution)/shard_map/ppermute | solution.py:467
  63.2 3.1 %collective-permute-done.17.refs_3_ = f32[32,128]{1,0:T(8,128)S(1)} collective-permute-done((f32[32,128]{1,0:T(8,128)S(1)}, f32[32,128]{1,0:T(8,128)S(1)}, u32[]{:S(2)}, u32[]{:S(2)}) %collective-permute-start.17) | collective-permute-done | bytes 16416 | tf_op jit(solution)/shard_map/ppermute | solution.py:467
  66.3 3.0 %row_pass.5 = (f32[16,128]{1,0:T(8,128)S(1)}, f32[32,128]{1,0:T(8,128)S(1)}) custom-call(f32[2,1024,2048]{2,1,0:T(8,128)S(1)} %get-tuple-element.36.t_ref, f32[16,128]{1,0:T(8,128)S(1)} %get-tuple-element.37.den_ref, f32[32,128]{1,0:T(8,128)S(1)} %add.26.refs_0_, f32[32,128]{1,0:T(8,128)S(1)} %collective-permute-done.15.refs_1_, ...), custom_call_target="tpu_custom_call" | custom-call | tf_op jit(solution)/shard_map/row_pass/pallas_call | solution.py:162
  74.5 2.4 %collective-permute-done.20.refs_3_ = f32[16,128]{1,0:T(8,128)S(1)} collective-permute-done((f32[16,128]{1,0:T(8,128)S(1)}, f32[16,128]{1,0:T(8,128)S(1)}, u32[]{:S(2)}, u32[]{:S(2)}) %collective-permute-start.20) | collective-permute-done | bytes 8224 | tf_op jit(solution)/shard_map/ppermute | solution.py:467
  77.0 11.7 %gradients.1 = (f32[2,4,128,256]{3,2,1,0:T(8,128)S(1)}, f32[2,4,128,256]{3,2,1,0:T(8,128)S(1)}, f32[2,256,256]{2,1,0:T(8,128)S(1)}, f32[2,256,256]{2,1,0:T(8,128...) custom-call(f32[2,1024,2048]{2,1,0:T(8,128)S(1)} %get-tuple-element.36.t_ref, ...), custom_call_target="tpu_custom_call" | custom-call | tf_op jit(solution)/shard_map/gradients/pallas_call | solution.py:302
  91.8 1.8 %collective-permute-start.23 = (f32[2,128,256]{2,1,0:T(8,128)S(1)}, f32[2,128,256]{2,1,0:T(8,128)S(1)}, u32[]{:S(2)}, u32[]{:S(2)}) collective-permute-start(f32[2,128,256]{2,1,0:T(8,128)S(1)} %get-tuple-element.50), channel_id=1, source_target_pairs={{0,16},{4,20},{8,24},{12,28},{16,0},{20,4},{24,8},{28,12},{1,17},{... | collective-permute-start | bytes 786440 | tf_op jit(solution)/shard_map/ppermute | solution.py:467
  93.6 9.6 %collective-permute-done.24.refs_5_ = f32[2,256,256]{2,1,0:T(8,128)S(1)} collective-permute-done((f32[2,256,256]{2,1,0:T(8,128)S(1)}, f32[2,256,256]{2,1,0:T(8,128)S(1)}, u32[]{:S(2)}, u32[]{:S(2)}) %collective-permute-start.24) | collective-permute-done | bytes 524320 | tf_op jit(solution)/shard_map/ppermute | solution.py:467
  104.3 2.3 %collective-permute-done.23.refs_3_ = f32[2,128,256]{2,1,0:T(8,128)S(1)} collective-permute-done((f32[2,128,256]{2,1,0:T(8,128)S(1)}, f32[2,128,256]{2,1,0:T(8,128)S(1)}, u32[]{:S(2)}, u32[]{:S(2)}) %collective-permute-start.23) | collective-permute-done | bytes 262176 | tf_op jit(solution)/shard_map/ppermute | solution.py:467
  108.3 1.7 %collective-permute-start.27 = (f32[1,128,256]{2,1,0:T(8,128)S(1)}, f32[1,128,256]{2,1,0:T(8,128)S(1)}, u32[]{:S(2)}, u32[]{:S(2)}) collective-permute-start(f32[1,128,256]{2,1,0:T(8,128)S(1)} %get-tuple-element.58), channel_id=1, source_target_pairs={{0,8},{4,12},{8,0},{12,4},{16,24},{20,28},{24,16},{28,20},{1,9},{5... | collective-permute-start | bytes 393224 | tf_op jit(solution)/shard_map/ppermute | solution.py:467
  112.0 2.8 %collective-permute-done.26.refs_1_ = f32[1,128,256]{2,1,0:T(8,128)S(1)} collective-permute-done((f32[1,128,256]{2,1,0:T(8,128)S(1)}, f32[1,128,256]{2,1,0:T(8,128)S(1)}, u32[]{:S(2)}, u32[]{:S(2)}) %collective-permute-start.26) | collective-permute-done | bytes 131104 | tf_op jit(solution)/shard_map/ppermute | solution.py:467
  117.2 2.0 %collective-permute-done.30 = f32[2,8,128]{2,1,0:T(8,128)S(1)} collective-permute-done((f32[2,8,128]{2,1,0:T(8,128)S(1)}, f32[2,8,128]{2,1,0:T(8,128)S(1)}, u32[]{:S(2)}, u32[]{:S(2)}) %collective-permute-start.30) | collective-permute-done | bytes 8224 | tf_op jit(solution)/shard_map/ppermute | solution.py:467
  119.1 1.7 %collective-permute-start.31 = (f32[2,8,128]{2,1,0:T(8,128)S(1)}, f32[2,8,128]{2,1,0:T(8,128)S(1)}, u32[]{:S(2)}, u32[]{:S(2)}) collective-permute-start(f32[2,8,128]{2,1,0:T(8,128)S(1)} %add.27.square_ref), channel_id=1, source_target_pairs={{0,2},{1,3},{2,0},{3,1},{4,6},{5,7},{6,4},{7,5},{8,10},{9,11},{10,... | collective-permute-start | bytes 24584 | tf_op jit(solution)/shard_map/ppermute | solution.py:467
  120.8 2.0 %collective-permute-done.31.other_ref = f32[2,8,128]{2,1,0:T(8,128)S(1)} collective-permute-done((f32[2,8,128]{2,1,0:T(8,128)S(1)}, f32[2,8,128]{2,1,0:T(8,128)S(1)}, u32[]{:S(2)}, u32[]{:S(2)}) %collective-permute-start.31) | collective-permute-done | bytes 8224 | tf_op jit(solution)/shard_map/ppermute | solution.py:467
  123.2 1.8 %collective-permute-start.43 = (f32[2,256,256]{2,1,0:T(8,128)S(1)}, f32[2,256,256]{2,1,0:T(8,128)S(1)}, u32[]{:S(2)}, u32[]{:S(2)}) collective-permute-start(f32[2,256,256]{2,1,0:T(8,128)S(1)} %get-tuple-element.66.refs_0_), channel_id=1, source_target_pairs={{0,2},{1,3},{2,0},{3,1},{4,6},{5,7},{6,4},{7,5},{8,10},{9,11},{10,... | collective-permute-start | bytes 1572872 | tf_op jit(solution)/shard_map/ppermute | solution.py:467
  128.6 6.4 %collective-permute-done.34.refs_1_.refs_4_ = f32[256,256]{1,0:T(8,128)S(1)} collective-permute-done((f32[256,256]{1,0:T(8,128)S(1)}, f32[256,256]{1,0:T(8,128)S(1)}, u32[]{:S(2)}, u32[]{:S(2)}) %collective-permute-start.34) | collective-permute-done | bytes 262176 | tf_op jit(solution)/shard_map/ppermute | solution.py:467
  136.2 2.9 %collective-permute-done.33.refs_0_.refs_2_ = f32[256,256]{1,0:T(8,128)S(1)} collective-permute-done((f32[256,256]{1,0:T(8,128)S(1)}, f32[256,256]{1,0:T(8,128)S(1)}, u32[]{:S(2)}, u32[]{:S(2)}) %collective-permute-start.33) | collective-permute-done | bytes 262176 | tf_op jit(solution)/shard_map/ppermute | solution.py:467
  139.1 3.6 %collective-permute-done.35 = f32[2,8,128]{2,1,0:T(8,128)S(1)} collective-permute-done((f32[2,8,128]{2,1,0:T(8,128)S(1)}, f32[2,8,128]{2,1,0:T(8,128)S(1)}, u32[]{:S(2)}, u32[]{:S(2)}) %collective-permute-start.35) | collective-permute-done | bytes 8224 | tf_op jit(solution)/shard_map/ppermute | solution.py:467
  144.3 3.5 %collective-permute-done.36.other_ref = f32[2,8,128]{2,1,0:T(8,128)S(1)} collective-permute-done((f32[2,8,128]{2,1,0:T(8,128)S(1)}, f32[2,8,128]{2,1,0:T(8,128)S(1)}, u32[]{:S(2)}, u32[]{:S(2)}) %collective-permute-start.36) | collective-permute-done | bytes 8224 | tf_op jit(solution)/shard_map/ppermute | solution.py:467
  149.7 2.5 %collective-permute-done.44.refs_3_ = f32[256,256]{1,0:T(8,128)S(1)} collective-permute-done((f32[256,256]{1,0:T(8,128)S(1)}, f32[256,256]{1,0:T(8,128)S(1)}, u32[]{:S(2)}, u32[]{:S(2)}) %collective-permute-start.44) | collective-permute-done | bytes 262176 | tf_op jit(solution)/shard_map/ppermute | solution.py:467
  152.2 2.8 %collective-permute-done.45.refs_4_ = f32[256,256]{1,0:T(8,128)S(1)} collective-permute-done((f32[256,256]{1,0:T(8,128)S(1)}, f32[256,256]{1,0:T(8,128)S(1)}, u32[]{:S(2)}, u32[]{:S(2)}) %collective-permute-start.45) | collective-permute-done | bytes 262176 | tf_op jit(solution)/shard_map/ppermute | solution.py:467
  (89 shorter events, 46.5 us)
Async XLA Ops:
  13.4 5.5 %collective-permute-start.1 = (f32[32,128]{1,0:T(8,128)S(1)}, f32[32,128]{1,0:T(8,128)S(1)}, u32[]{:S(2)}, u32[]{:S(2)}) collective-permute-start(f32[32,128]{1,0:T(8,128)S(1)} %add.24.refs_0_), channel_id=1, source_target_pairs={{0,8},{4,12},{8,0},{12,4},{16,24},{20,28},{24,16},{28,20},{1,9},{5... | collective-permute-start | bytes 49160 | tf_op jit(solution)/shard_map/ppermute | solution.py:467
  16.3 4.6 %collective-permute-start.2 = (f32[32,128]{1,0:T(8,128)S(1)}, f32[32,128]{1,0:T(8,128)S(1)}, u32[]{:S(2)}, u32[]{:S(2)}) collective-permute-start(f32[32,128]{1,0:T(8,128)S(1)} %add.24.refs_0_), channel_id=1, source_target_pairs={{0,16},{4,20},{8,24},{12,28},{16,0},{20,4},{24,8},{28,12},{1,17},{... | collective-permute-start | bytes 49160 | tf_op jit(solution)/shard_map/ppermute | solution.py:467
  18.9 5.5 %collective-permute-start.3 = (f32[32,128]{1,0:T(8,128)S(1)}, f32[32,128]{1,0:T(8,128)S(1)}, u32[]{:S(2)}, u32[]{:S(2)}) collective-permute-start(f32[32,128]{1,0:T(8,128)S(1)} %add.24.refs_0_), channel_id=1, source_target_pairs={{0,24},{4,28},{8,16},{12,20},{16,8},{20,12},{24,0},{28,4},{1,25},{... | collective-permute-start | bytes 49160 | tf_op jit(solution)/shard_map/ppermute | solution.py:467
  30.9 4.6 %collective-permute-start.6 = (f32[32,128]{1,0:T(8,128)S(1)}, f32[32,128]{1,0:T(8,128)S(1)}, u32[]{:S(2)}, u32[]{:S(2)}) collective-permute-start(f32[32,128]{1,0:T(8,128)S(1)} %get-tuple-element.39.refs_0_.refs_4_), channel_id=1, source_target_pairs={{0,3},{1,2},{2,1},{3,0},{4,7},{5,6},{6,5},{7,4},{8,11},{9,10},{10,... | collective-permute-start | bytes 49160 | tf_op jit(solution)/shard_map/ppermute | solution.py:467
  39.1 5.5 %collective-permute-start.10 = (f32[32,128]{1,0:T(8,128)S(1)}, f32[32,128]{1,0:T(8,128)S(1)}, u32[]{:S(2)}, u32[]{:S(2)}) collective-permute-start(f32[32,128]{1,0:T(8,128)S(1)} %add.25.refs_0_), channel_id=1, source_target_pairs={{0,24},{4,28},{8,16},{12,20},{16,8},{20,12},{24,0},{28,4},{1,25},{... | collective-permute-start | bytes 49160 | tf_op jit(solution)/shard_map/ppermute | solution.py:467
  39.3 5.3 %collective-permute-start.8 = (f32[32,128]{1,0:T(8,128)S(1)}, f32[32,128]{1,0:T(8,128)S(1)}, u32[]{:S(2)}, u32[]{:S(2)}) collective-permute-start(f32[32,128]{1,0:T(8,128)S(1)} %add.25.refs_0_), channel_id=1, source_target_pairs={{0,8},{4,12},{8,0},{12,4},{16,24},{20,28},{24,16},{28,20},{1,9},{5... | collective-permute-start | bytes 49160 | tf_op jit(solution)/shard_map/ppermute | solution.py:467
  39.3 5.9 %collective-permute-start.9 = (f32[32,128]{1,0:T(8,128)S(1)}, f32[32,128]{1,0:T(8,128)S(1)}, u32[]{:S(2)}, u32[]{:S(2)}) collective-permute-start(f32[32,128]{1,0:T(8,128)S(1)} %add.25.refs_0_), channel_id=1, source_target_pairs={{0,16},{4,20},{8,24},{12,28},{16,0},{20,4},{24,8},{28,12},{1,17},{... | collective-permute-start | bytes 49160 | tf_op jit(solution)/shard_map/ppermute | solution.py:467
  49.6 4.5 %collective-permute-start.13 = (f32[16,128]{1,0:T(8,128)S(1)}, f32[16,128]{1,0:T(8,128)S(1)}, u32[]{:S(2)}, u32[]{:S(2)}) collective-permute-start(f32[16,128]{1,0:T(8,128)S(1)} %get-tuple-element.40.refs_0_), channel_id=1, source_target_pairs={{0,3},{1,2},{2,1},{3,0},{4,7},{5,6},{6,5},{7,4},{8,11},{9,10},{10,... | collective-permute-start | bytes 24584 | tf_op jit(solution)/shard_map/ppermute | solution.py:467
  57.8 4.4 %collective-permute-start.15 = (f32[32,128]{1,0:T(8,128)S(1)}, f32[32,128]{1,0:T(8,128)S(1)}, u32[]{:S(2)}, u32[]{:S(2)}) collective-permute-start(f32[32,128]{1,0:T(8,128)S(1)} %add.26.refs_0_), channel_id=1, source_target_pairs={{0,8},{4,12},{8,0},{12,4},{16,24},{20,28},{24,16},{28,20},{1,9},{5... | collective-permute-start | bytes 49160 | tf_op jit(solution)/shard_map/ppermute | solution.py:467
  58.5 4.6 %collective-permute-start.16 = (f32[32,128]{1,0:T(8,128)S(1)}, f32[32,128]{1,0:T(8,128)S(1)}, u32[]{:S(2)}, u32[]{:S(2)}) collective-permute-start(f32[32,128]{1,0:T(8,128)S(1)} %add.26.refs_0_), channel_id=1, source_target_pairs={{0,16},{4,20},{8,24},{12,28},{16,0},{20,4},{24,8},{28,12},{1,17},{... | collective-permute-start | bytes 49160 | tf_op jit(solution)/shard_map/ppermute | solution.py:467
  60.8 5.5 %collective-permute-start.17 = (f32[32,128]{1,0:T(8,128)S(1)}, f32[32,128]{1,0:T(8,128)S(1)}, u32[]{:S(2)}, u32[]{:S(2)}) collective-permute-start(f32[32,128]{1,0:T(8,128)S(1)} %add.26.refs_0_), channel_id=1, source_target_pairs={{0,24},{4,28},{8,16},{12,20},{16,8},{20,12},{24,0},{28,4},{1,25},{... | collective-permute-start | bytes 49160 | tf_op jit(solution)/shard_map/ppermute | solution.py:467
  72.4 4.5 %collective-permute-start.20 = (f32[16,128]{1,0:T(8,128)S(1)}, f32[16,128]{1,0:T(8,128)S(1)}, u32[]{:S(2)}, u32[]{:S(2)}) collective-permute-start(f32[16,128]{1,0:T(8,128)S(1)} %get-tuple-element.44.refs_0_), channel_id=1, source_target_pairs={{0,3},{1,2},{2,1},{3,0},{4,7},{5,6},{6,5},{7,4},{8,11},{9,10},{10,... | collective-permute-start | bytes 24584 | tf_op jit(solution)/shard_map/ppermute | solution.py:467
  88.8 14.3 %collective-permute-start.24 = (f32[2,256,256]{2,1,0:T(8,128)S(1)}, f32[2,256,256]{2,1,0:T(8,128)S(1)}, u32[]{:S(2)}, u32[]{:S(2)}) collective-permute-start(f32[2,256,256]{2,1,0:T(8,128)S(1)} %get-tuple-element.52), channel_id=1, source_target_pairs={{0,1},{1,0},{2,3},{3,2},{4,5},{5,4},{6,7},{7,6},{8,9},{9,8},{10,11... | collective-permute-start | bytes 1572872 | tf_op jit(solution)/shard_map/ppermute | solution.py:467
  89.4 14.0 %collective-permute-start.25 = (f32[2,256,256]{2,1,0:T(8,128)S(1)}, f32[2,256,256]{2,1,0:T(8,128)S(1)}, u32[]{:S(2)}, u32[]{:S(2)}) collective-permute-start(f32[2,256,256]{2,1,0:T(8,128)S(1)} %get-tuple-element.54), channel_id=1, source_target_pairs={{0,2},{1,3},{2,0},{3,1},{4,6},{5,7},{6,4},{7,5},{8,10},{9,11},{10,... | collective-permute-start | bytes 1572872 | tf_op jit(solution)/shard_map/ppermute | solution.py:467
  91.5 12.8 %collective-permute-start.22 = (f32[2,128,256]{2,1,0:T(8,128)S(1)}, f32[2,128,256]{2,1,0:T(8,128)S(1)}, u32[]{:S(2)}, u32[]{:S(2)}) collective-permute-start(f32[2,128,256]{2,1,0:T(8,128)S(1)} %get-tuple-element.48), channel_id=1, source_target_pairs={{0,8},{4,12},{8,0},{12,4},{16,24},{20,28},{24,16},{28,20},{1,9},{5... | collective-permute-start | bytes 786440 | tf_op jit(solution)/shard_map/ppermute | solution.py:467
  91.8 14.8 %collective-permute-start.23 = (f32[2,128,256]{2,1,0:T(8,128)S(1)}, f32[2,128,256]{2,1,0:T(8,128)S(1)}, u32[]{:S(2)}, u32[]{:S(2)}) collective-permute-start(f32[2,128,256]{2,1,0:T(8,128)S(1)} %get-tuple-element.50), channel_id=1, source_target_pairs={{0,16},{4,20},{8,24},{12,28},{16,0},{20,4},{24,8},{28,12},{1,17},{... | collective-permute-start | bytes 786440 | tf_op jit(solution)/shard_map/ppermute | solution.py:467
  106.7 8.2 %collective-permute-start.28 = (f32[1,256,256]{2,1,0:T(8,128)S(1)}, f32[1,256,256]{2,1,0:T(8,128)S(1)}, u32[]{:S(2)}, u32[]{:S(2)}) collective-permute-start(f32[1,256,256]{2,1,0:T(8,128)S(1)} %get-tuple-element.60), channel_id=1, source_target_pairs={{0,2},{1,3},{2,0},{3,1},{4,6},{5,7},{6,4},{7,5},{8,10},{9,11},{10,... | collective-permute-start | bytes 786440 | tf_op jit(solution)/shard_map/ppermute | solution.py:467
  107.3 7.6 %collective-permute-start.29 = (f32[1,256,256]{2,1,0:T(8,128)S(1)}, f32[1,256,256]{2,1,0:T(8,128)S(1)}, u32[]{:S(2)}, u32[]{:S(2)}) collective-permute-start(f32[1,256,256]{2,1,0:T(8,128)S(1)} %get-tuple-element.62), channel_id=1, source_target_pairs={{0,1},{1,0},{2,3},{3,2},{4,5},{5,4},{6,7},{7,6},{8,9},{9,8},{10,11... | collective-permute-start | bytes 786440 | tf_op jit(solution)/shard_map/ppermute | solution.py:467
  108.0 6.7 %collective-permute-start.26 = (f32[1,128,256]{2,1,0:T(8,128)S(1)}, f32[1,128,256]{2,1,0:T(8,128)S(1)}, u32[]{:S(2)}, u32[]{:S(2)}) collective-permute-start(f32[1,128,256]{2,1,0:T(8,128)S(1)} %get-tuple-element.56), channel_id=1, source_target_pairs={{0,16},{4,20},{8,24},{12,28},{16,0},{20,4},{24,8},{28,12},{1,17},{... | collective-permute-start | bytes 393224 | tf_op jit(solution)/shard_map/ppermute | solution.py:467
  108.3 6.6 %collective-permute-start.27 = (f32[1,128,256]{2,1,0:T(8,128)S(1)}, f32[1,128,256]{2,1,0:T(8,128)S(1)}, u32[]{:S(2)}, u32[]{:S(2)}) collective-permute-start(f32[1,128,256]{2,1,0:T(8,128)S(1)} %get-tuple-element.58), channel_id=1, source_target_pairs={{0,8},{4,12},{8,0},{12,4},{16,24},{20,28},{24,16},{28,20},{1,9},{5... | collective-permute-start | bytes 393224 | tf_op jit(solution)/shard_map/ppermute | solution.py:467
  123.2 19.5 %collective-permute-start.43 = (f32[2,256,256]{2,1,0:T(8,128)S(1)}, f32[2,256,256]{2,1,0:T(8,128)S(1)}, u32[]{:S(2)}, u32[]{:S(2)}) collective-permute-start(f32[2,256,256]{2,1,0:T(8,128)S(1)} %get-tuple-element.66.refs_0_), channel_id=1, source_target_pairs={{0,2},{1,3},{2,0},{3,1},{4,6},{5,7},{6,4},{7,5},{8,10},{9,11},{10,... | collective-permute-start | bytes 1572872 | tf_op jit(solution)/shard_map/ppermute | solution.py:467
  125.0 10.0 %collective-permute-start.34 = (f32[256,256]{1,0:T(8,128)S(1)}, f32[256,256]{1,0:T(8,128)S(1)}, u32[]{:S(2)}, u32[]{:S(2)}) collective-permute-start(f32[256,256]{1,0:T(8,128)S(1)} %get-tuple-element.65.refs_0_), channel_id=1, source_target_pairs={{0,16},{4,20},{8,24},{12,28},{16,0},{20,4},{24,8},{28,12},{1,17},{... | collective-permute-start | bytes 786440 | tf_op jit(solution)/shard_map/ppermute | solution.py:467
  125.6 17.7 %collective-permute-start.42 = (f32[2,256,256]{2,1,0:T(8,128)S(1)}, f32[2,256,256]{2,1,0:T(8,128)S(1)}, u32[]{:S(2)}, u32[]{:S(2)}) collective-permute-start(f32[2,256,256]{2,1,0:T(8,128)S(1)} %get-tuple-element.66.refs_0_), channel_id=1, source_target_pairs={{0,1},{1,0},{2,3},{3,2},{4,5},{5,4},{6,7},{7,6},{8,9},{9,8},{10,11... | collective-permute-start | bytes 1572872 | tf_op jit(solution)/shard_map/ppermute | solution.py:467
  127.1 11.9 %collective-permute-start.33 = (f32[256,256]{1,0:T(8,128)S(1)}, f32[256,256]{1,0:T(8,128)S(1)}, u32[]{:S(2)}, u32[]{:S(2)}) collective-permute-start(f32[256,256]{1,0:T(8,128)S(1)} %get-tuple-element.65.refs_0_), channel_id=1, source_target_pairs={{0,8},{4,12},{8,0},{12,4},{16,24},{20,28},{24,16},{28,20},{1,9},{5... | collective-permute-start | bytes 786440 | tf_op jit(solution)/shard_map/ppermute | solution.py:467
  135.0 8.2 %collective-permute-start.40 = (f32[256,256]{1,0:T(8,128)S(1)}, f32[256,256]{1,0:T(8,128)S(1)}, u32[]{:S(2)}, u32[]{:S(2)}) collective-permute-start(f32[256,256]{1,0:T(8,128)S(1)} %collective-permute-done.34.refs_1_.refs_4_), channel_id=1, source_target_pairs={{0,8},{4,12},{8,0},{12,4},{16,24},{20,28},{24,16},{28,20},{1,9},{5... | collective-permute-start | bytes 786440 | tf_op jit(solution)/shard_map/ppermute | solution.py:467
  139.0 4.4 %collective-permute-start.37 = (f32[256,256]{1,0:T(8,128)S(1)}, f32[256,256]{1,0:T(8,128)S(1)}, u32[]{:S(2)}, u32[]{:S(2)}) collective-permute-start(f32[256,256]{1,0:T(8,128)S(1)} %get-tuple-element.65.refs_0_), channel_id=1, source_target_pairs={{0,4},{4,0},{8,12},{12,8},{16,20},{20,16},{24,28},{28,24},{1,5},{5... | collective-permute-start | bytes 786440 | tf_op jit(solution)/shard_map/ppermute | solution.py:467
  142.7 5.5 %collective-permute-start.38 = (f32[256,256]{1,0:T(8,128)S(1)}, f32[256,256]{1,0:T(8,128)S(1)}, u32[]{:S(2)}, u32[]{:S(2)}) collective-permute-start(f32[256,256]{1,0:T(8,128)S(1)} %collective-permute-done.33.refs_0_.refs_2_), channel_id=1, source_target_pairs={{0,4},{4,0},{8,12},{12,8},{16,20},{20,16},{24,28},{28,24},{1,5},{5... | collective-permute-start | bytes 786440 | tf_op jit(solution)/shard_map/ppermute | solution.py:467
  142.7 5.5 %collective-permute-start.39 = (f32[256,256]{1,0:T(8,128)S(1)}, f32[256,256]{1,0:T(8,128)S(1)}, u32[]{:S(2)}, u32[]{:S(2)}) collective-permute-start(f32[256,256]{1,0:T(8,128)S(1)} %collective-permute-done.34.refs_1_.refs_4_), channel_id=1, source_target_pairs={{0,4},{4,0},{8,12},{12,8},{16,20},{20,16},{24,28},{28,24},{1,5},{5... | collective-permute-start | bytes 786440 | tf_op jit(solution)/shard_map/ppermute | solution.py:467
  143.2 4.6 %collective-permute-start.36 = (f32[2,8,128]{2,1,0:T(8,128)S(1)}, f32[2,8,128]{2,1,0:T(8,128)S(1)}, u32[]{:S(2)}, u32[]{:S(2)}) collective-permute-start(f32[2,8,128]{2,1,0:T(8,128)S(1)} %add.28.square_ref), channel_id=1, source_target_pairs={{0,16},{4,20},{8,24},{12,28},{16,0},{20,4},{24,8},{28,12},{1,17},{... | collective-permute-start | bytes 24584 | tf_op jit(solution)/shard_map/ppermute | solution.py:467
  143.3 4.9 %collective-permute-start.41 = (f32[256,256]{1,0:T(8,128)S(1)}, f32[256,256]{1,0:T(8,128)S(1)}, u32[]{:S(2)}, u32[]{:S(2)}) collective-permute-start(f32[256,256]{1,0:T(8,128)S(1)} %collective-permute-done.40.refs_6_), channel_id=1, source_target_pairs={{0,4},{4,0},{8,12},{12,8},{16,20},{20,16},{24,28},{28,24},{1,5},{5... | collective-permute-start | bytes 786440 | tf_op jit(solution)/shard_map/ppermute | solution.py:467
  143.5 8.7 %collective-permute-start.44 = (f32[256,256]{1,0:T(8,128)S(1)}, f32[256,256]{1,0:T(8,128)S(1)}, u32[]{:S(2)}, u32[]{:S(2)}) collective-permute-start(f32[256,256]{1,0:T(8,128)S(1)} %slice_bitcast_fusion.1), channel_id=1, source_target_pairs={{0,1},{1,0},{2,3},{3,2},{4,5},{5,4},{6,7},{7,6},{8,9},{9,8},{10,11... | collective-permute-start | bytes 786440 | tf_op jit(solution)/shard_map/ppermute | solution.py:467
  147.9 7.1 %collective-permute-start.45 = (f32[256,256]{1,0:T(8,128)S(1)}, f32[256,256]{1,0:T(8,128)S(1)}, u32[]{:S(2)}, u32[]{:S(2)}) collective-permute-start(f32[256,256]{1,0:T(8,128)S(1)} %slice_bitcast_fusion), channel_id=1, source_target_pairs={{0,2},{1,3},{2,0},{3,1},{4,6},{5,7},{6,4},{7,5},{8,10},{9,11},{10,... | collective-permute-start | bytes 786440 | tf_op jit(solution)/shard_map/ppermute | solution.py:467
  (17 other events, 44.7 us)

commit v6 on v5

--- a/solution.py
+++ b/solution.py
@@ -132,11 +132,11 @@
         ],
         compiler_params=params(24),
         name="scores",
-    )(slow, fast, protos)
+    )(*[pltpu.with_memory_space_constraint(x, pltpu.HBM) for x in (slow, fast, protos)])
 
 
 def row_kernel(protos_all, extra, t_ref, den_ref, *refs):
-    col_parts, (row_ref, r_ref) = refs[:-2], refs[-2:]
+    col_parts, (row_ref, r_ref, acc_s) = refs[:-3], refs[-3:]
     clips, count = t_ref.shape[1:]
     groups, lines = clips // LANES, count // LANES
     r_ref[...] = 1.0 / (float(protos_all) * sum_of(col_parts))
@@ -150,10 +150,12 @@
             for j in range(lines):
                 t = t_ref[v, rows, j * LANES : (j + 1) * LANES]
                 acc = acc + t * t * r_ref[v * lines + j : v * lines + j + 1, :]
-            row_ref[pl.ds(v * groups + i, 1), :] = to_line(acc)
+            acc_s[pl.ds(pl.multiple_of((v * groups + i) * LANES, LANES), LANES), :] = acc
             return 0
 
         lax.fori_loop(0, groups, step, 0)
+    for line in range(2 * groups):
+        row_ref[line : line + 1, :] = to_line(acc_s[line * LANES : (line + 1) * LANES, :])
 
 
 def row_pass(t, den, col_parts, protos_all, extra):
@@ -167,6 +169,7 @@
         ),
         in_specs=[vmem_spec()] * (2 + len(col_parts)),
         out_specs=(vmem_spec(),) * 2,
+        scratch_shapes=[pltpu.VMEM((2 * clips, LANES), jnp.float32)],
         compiler_params=params(8),
         name="row_pass",
     )(pltpu.with_memory_space_constraint(t, pltpu.VMEM), den, *col_parts)
@@ -360,8 +363,11 @@
     return (grad - unit * along) / length
 
 
+EXTRA = 8
+
+
 def share_kernel(proto_raw, slow_raw, fast_raw, *refs):
-    terms, (proto_out, square_out) = refs[:-2], refs[-2:]
+    terms, (proto_out, embed_out, square_out) = refs[:-3], refs[-3:]
     half = proto_raw.shape[0] // 2
     squares = [jnp.zeros((8, LANES), jnp.float32)] * 2
     for h in range(2):
@@ -371,96 +377,118 @@
         squares[0] = squares[0] + row_fold(lane_sum(grad * grad))
     for v, raw in enumerate((slow_raw, fast_raw)):
         grad = project(raw[...], terms[4 + 2 * v : 6 + 2 * v])
+        embed_out[v] = grad
         squares[1] = squares[1] + row_fold(lane_sum(grad * grad))
     for kind in range(2):
         total = jnp.sum(jnp.sum(squares[kind], axis=0, keepdims=True), axis=1, keepdims=True)
         square_out[kind] = jnp.broadcast_to(total, (8, LANES))
 
 
-def project_protos(raws, terms):
+def project_shares(raws, terms):
+    rows, feats = raws[1].shape
     return pl.pallas_call(
         share_kernel,
         out_shape=(
             jax.ShapeDtypeStruct(raws[0].shape, jnp.float32),
+            jax.ShapeDtypeStruct((2, rows, feats), jnp.float32),
             jax.ShapeDtypeStruct((2, 8, LANES), jnp.float32),
         ),
         in_specs=[vmem_spec()] * (len(raws) + len(terms)),
+        out_specs=(vmem_spec(),) * 3,
+        compiler_params=params(10),
+        name="project_shares",
+    )(*raws, *terms)
+
+
+def tree_sum(terms):
+    while len(terms) > 1:
+        terms = [terms[i] + terms[i + 1] for i in range(0, len(terms), 2)]
+    return terms[0]
+
+
+def pack_kernel(proto_ref, embed_ref, *refs):
+    squares, (proto_out, embed_out) = refs[:-2], refs[-2:]
+    rows = proto_ref.shape[0]
+    total = tree_sum([square[...] for square in squares])
+    proto_out[:rows, :] = proto_ref[...]
+    for kind in range(2):
+        proto_out[rows:, kind * LANES : (kind + 1) * LANES] = total[kind]
+    embed_out[...] = embed_ref[...]
+
+
+def pack_shares(grad_proto, grad_embed, squares):
+    rows, feats = grad_proto.shape
+    return pl.pallas_call(
+        pack_kernel,
+        out_shape=(
+            jax.ShapeDtypeStruct((rows + EXTRA, feats), jnp.float32),
+            jax.ShapeDtypeStruct(grad_embed.shape, jnp.float32),
+        ),
+        in_specs=[vmem_spec()] * (2 + len(squares)),
         out_specs=(vmem_spec(),) * 2,
         compiler_params=params(10),
-        name="project_protos",
-    )(*raws, *terms)
-
-
-def embed_kernel(square_ref, other_ref, slow_raw, fast_raw, *refs):
-    terms, (embed_out, square_out) = refs[:-2], refs[-2:]
-    square_out[...] = square_ref[...] + other_ref[...]
-    for v, raw in enumerate((slow_raw, fast_raw)):
-        embed_out[v] = project(raw[...], terms[2 * v : 2 * v + 2])
-
-
-def project_embeds(square, other, raws, terms):
-    rows, feats = raws[0].shape
-    return pl.pallas_call(
-        embed_kernel,
-        out_shape=(
-            jax.ShapeDtypeStruct((2, rows, feats), jnp.float32),
-            jax.ShapeDtypeStruct(square.shape, jnp.float32),
-        ),
-        in_specs=[vmem_spec()] * (2 + len(raws) + len(terms)),
-        out_specs=(vmem_spec(),) * 2,
-        compiler_params=params(10),
-        name="project_embeds",
-    )(square, other, *raws, *terms)
-
-
-def add_kernel(x_ref, y_ref, *refs):
-    refs[-1][...] = x_ref[...] + y_ref[...]
-
-
-def add_after(x, y, arrived):
-    return pl.pallas_call(
-        add_kernel,
-        out_shape=jax.ShapeDtypeStruct(x.shape, x.dtype),
-        in_specs=[vmem_spec()] * 2 + [pl.BlockSpec(memory_space=pl.ANY)] * len(arrived),
+        name="pack_shares",
+    )(grad_proto, grad_embed, *squares)
+
+
+def total_square(refs, kind):
+    lanes = slice(kind * LANES, (kind + 1) * LANES)
+    return tree_sum([ref[ref.shape[0] - EXTRA :, lanes] for ref in refs])[0:1, 0:1]
+
+
+def finish_protos_kernel(entries, *refs):
+    pieces, out_ref = refs[:-1], refs[-1]
+    factor = lax.rsqrt(total_square(pieces, 0) / entries + NORM_EPS)
+    size = pieces[0].shape[0] - EXTRA
+    for m, piece in enumerate(pieces):
+        which = jnp.bitwise_xor(lax.axis_index("batch"), m)
+        out_ref[pl.ds(pl.multiple_of(which * size, size), size), :] = piece[:size, :] * factor
+
+
+def finish_protos(entries, pieces):
+    rows, feats = pieces[0].shape
+    return pl.pallas_call(
+        functools.partial(finish_protos_kernel, entries),
+        out_shape=jax.ShapeDtypeStruct((len(pieces) * (rows - EXTRA), feats), jnp.float32),
+        in_specs=[vmem_spec()] * len(pieces),
         out_specs=vmem_spec(),
-        compiler_params=params(4),
-        name="add_after",
-    )(x, y, *arrived)
-
-
-def finish_kernel(axis, kind, entries, plan, inputs, square_ref, other_ref, *refs):
-    ins, outs = refs[:inputs], refs[inputs:]
-    square = square_ref[kind, 0:1, 0:1] + other_ref[kind, 0:1, 0:1]
-    factor = lax.rsqrt(square / entries + NORM_EPS)
-    for n, pieces in enumerate(plan):
-        for m, (place, view) in enumerate(pieces):
+        compiler_params=params(12),
+        name="finish_protos",
+    )(*pieces)
+
+
+def finish_embeds_kernel(entries, plan, count, *refs):
+    pieces, ins, outs = refs[:count], refs[count:-2], refs[-2:]
+    factor = lax.rsqrt(total_square(pieces, 1) / entries + NORM_EPS)
+    for v, places in enumerate(plan):
+        for m, (place, view) in enumerate(places):
             src = ins[place][...] if view is None else ins[place][view]
             size = src.shape[0]
-            which = jnp.bitwise_xor(lax.axis_index(axis), m)
-            outs[n][pl.ds(pl.multiple_of(which * size, size), size), :] = src * factor
-
-
-def finish(axis, kind, entries, square, other, groups):
+            which = jnp.bitwise_xor(lax.axis_index("proto"), m)
+            outs[v][pl.ds(pl.multiple_of(which * size, size), size), :] = src * factor
+
+
+def finish_embeds(entries, pieces, groups):
     arrays, plan, outs = [], [], []
     for group in groups:
-        pieces = []
+        places = []
         for array, view in group:
             place = next((i for i, known in enumerate(arrays) if known is array), None)
             if place is None:
                 place = len(arrays)
                 arrays.append(array)
-            pieces.append((place, view))
-        plan.append(pieces)
+            places.append((place, view))
+        plan.append(places)
         rows, feats = group[0][0].shape[-2:]
         outs.append(jax.ShapeDtypeStruct((len(group) * rows, feats), jnp.float32))
     return pl.pallas_call(
-        functools.partial(finish_kernel, axis, kind, entries, plan, len(arrays)),
+        functools.partial(finish_embeds_kernel, entries, plan, len(pieces)),
         out_shape=tuple(outs),
-        in_specs=[vmem_spec()] * (2 + len(arrays)),
+        in_specs=[vmem_spec()] * (len(pieces) + len(arrays)),
         out_specs=(vmem_spec(),) * len(groups),
         compiler_params=params(12),
-        name="finish",
-    )(square, other, *arrays)
+        name="finish_embeds",
+    )(*pieces, *arrays)
 
 
 def swap(own, axis, mask):
@@ -516,7 +544,7 @@
     for bit in bits:
         for m in list(pieces):
             pieces[m | 1 << bit] = first[bit] if m == 0 else swap(pieces[m], "batch", 1 << bit)
-    return [(pieces[m], None) for m in range(len(pieces))]
+    return [pieces[m] for m in range(len(pieces))]
 
 
 def gather_views(own, orders):
@@ -578,20 +606,12 @@
     for v in range(2):
         groups.append(("proto", proto_orders[v], shares[2 * v], shares[2 * v + 1]))
     terms = scatter_sums(groups)
-    grad_proto, square = project_protos(raws, terms)
-    proto_pieces = gather_batch(grad_proto)
-    for bit in range(proto_bits - 1):
-        square = square + swap(square, "proto", 1 << bit)
-    other = swap(square, "proto", 1 << (proto_bits - 1))
-    grad_embed, square = project_embeds(square, other, raws[1:], terms[4:])
+    grad_proto, grad_embed, square = project_shares(raws, terms)
+    packed, grad_embed = pack_shares(grad_proto, grad_embed, proto_parts(square))
+    proto_pieces = gather_batch(packed)
     view_pieces = gather_views(grad_embed, (proto_orders[1], proto_orders[0]))
-    arrived = [proto_pieces[1 << bit][0] for bit in range(1, batch_bits)]
-    square = add_after(square, swap(square, "batch", 1), arrived)
-    for bit in range(1, batch_bits - 1):
-        square = square + swap(square, "batch", 1 << bit)
-    other = swap(square, "batch", 1 << (batch_bits - 1))
-    (proto_grad,) = finish("batch", 0, proto_entries, square, other, [proto_pieces])
-    slow_grad, fast_grad = finish("proto", 1, embed_entries, square, other, view_pieces)
+    proto_grad = finish_protos(proto_entries, proto_pieces)
+    slow_grad, fast_grad = finish_embeds(embed_entries, proto_pieces, view_pieces)
     return proto_grad, slow_grad, fast_grad
 
 

time: 157 us -> 146 us (0.930)
  waiting for transfers between devices: 69.4 us -> 63.6 us
  local copies, waits for them, and re-layouts: 5.66 us -> 1.99 us
  Pallas kernels: 38.1 us -> 35.7 us
    ppermute x46 -> x44, waiting for transfers between devices: 69.4 us -> 63.6 us  [swap(): lax.ppermute(own, axis, [(i, i ^ mask) for i in range(lax.axis_size(axis))])]
    unnamed x6 -> x0, local copies, waits for them, and re-layouts: 3.67 us -> none
    pallas_call x3, Pallas kernels: 9.79 us -> 6.88 us  [row_pass(): pl.pallas_call(functools.partial(row_kernel, protos_all, extra), out_shap...]
    ppermute x46 -> x44, starting transfers between devices: 42.5 us -> 43.6 us  [swap(): lax.ppermute(own, axis, [(i, i ^ mask) for i in range(lax.axis_size(axis))])]
    pallas_call x5 -> x4, Pallas kernels: 3.87 us -> 3.61 us  [the longest x1 1.51 us: finish_protos(): pl.pallas_call(functools.partial(finish_protos_kernel, entries), out_shap...]
  transfers between devices with their start and end apart: 46 -> 44, of which waited for: 34 -> 33; matrix products, arithmetic and copies ran while one was open for 1% -> 1% of each run, Pallas kernels for 1% -> 1%
where the time goes in v6:
time: 146 us
  waiting for transfers between devices  63.6 us (44%)
  starting transfers between devices  43.6 us (30%)
  Pallas kernels  35.7 us (24%)
  local copies, waits for them, and re-layouts  1.99 us (1%)
    ppermute x44, waiting for transfers between devices, swap(): lax.ppermute(own, axis, [(i, i ^ mask) for i in range(lax.axis_size(axis))])  63.6 us
    ppermute x44, starting transfers between devices, swap(): lax.ppermute(own, axis, [(i, i ^ mask) for i in range(lax.axis_size(axis))])  43.6 us
    pallas_call x1, Pallas kernels, gradients(): pl.pallas_call(functools.partial(grad_kernel, batch_orders, proto_orders,...  11.7 us
    pallas_call x1, Pallas kernels, scores(): pl.pallas_call(score_kernel, out_shape=(pltpu.VMEM((2, clips, count), jnp...  8.59 us
    pallas_call x3, Pallas kernels, row_pass(): pl.pallas_call(functools.partial(row_kernel, protos_all, extra), out_shap...  6.88 us
    pallas_call x2, Pallas kernels, col_pass(): pl.pallas_call(functools.partial(col_kernel, clips_all), out_shape=jax.Sh...  4.65 us
  transfers between devices with their start and end apart: 44, of which 33 were waited for; matrix products, arithmetic and copies ran while one was open for 1% of the time, Pallas kernels for 1%

profile of v6, /device:TPU:0, one launch (start us, length us, event | category | flops | bytes accessed | tf_op | source)
XLA Modules:
  0.0 145.8 jit_solution(11370890251668217038)
XLA Ops:
  0.6 8.6 %scores.1 = (f32[2,1024,2048]{2,1,0:T(8,128)S(1)}, f32[32,128]{1,0:T(8,128)S(1)}, f32[16,128]{1,0:T(8,128)S(1)}, bf16[256,2048]{1,0:T(8,128)(2,1)S(1)}, bf16[2048,256]{1,0:T(8,128)(2,1)S(1)}) custom-call(bf16[1024,256]{1,0:T(8,128)(2,1)} %slow.1, bf16[1024,256]{1,0:T(8,128)(2,1)} %fast.1, f32[2048,256]{1,0:T(8,128)} %protos.1), custom_call_target="tpu_custom_call" | custom-call | tf_op jit(solution)/shard_map/scores/pallas_call | solution.py:115
  10.6 2.9 %collective-permute-start.1 = (f32[32,128]{1,0:T(8,128)S(1)}, f32[32,128]{1,0:T(8,128)S(1)}, u32[]{:S(2)}, u32[]{:S(2)}) collective-permute-start(f32[32,128]{1,0:T(8,128)S(1)} %add.18.refs_0_), channel_id=1, source_target_pairs={{0,8},{4,12},{8,0},{12,4},{16,24},{20,28},{24,16},{28,20},{1,9},{5... | collective-permute-start | bytes 49160 | tf_op jit(solution)/shard_map/ppermute | solution.py:495
  13.5 2.6 %collective-permute-start.2 = (f32[32,128]{1,0:T(8,128)S(1)}, f32[32,128]{1,0:T(8,128)S(1)}, u32[]{:S(2)}, u32[]{:S(2)}) collective-permute-start(f32[32,128]{1,0:T(8,128)S(1)} %add.18.refs_0_), channel_id=1, source_target_pairs={{0,16},{4,20},{8,24},{12,28},{16,0},{20,4},{24,8},{28,12},{1,17},{... | collective-permute-start | bytes 49160 | tf_op jit(solution)/shard_map/ppermute | solution.py:495
  16.1 2.0 %collective-permute-done.2.refs_2_ = f32[32,128]{1,0:T(8,128)S(1)} collective-permute-done((f32[32,128]{1,0:T(8,128)S(1)}, f32[32,128]{1,0:T(8,128)S(1)}, u32[]{:S(2)}, u32[]{:S(2)}) %collective-permute-start.2) | collective-permute-done | bytes 16416 | tf_op jit(solution)/shard_map/ppermute | solution.py:495
  18.1 3.5 %collective-permute-done.3.refs_3_ = f32[32,128]{1,0:T(8,128)S(1)} collective-permute-done((f32[32,128]{1,0:T(8,128)S(1)}, f32[32,128]{1,0:T(8,128)S(1)}, u32[]{:S(2)}, u32[]{:S(2)}) %collective-permute-start.3) | collective-permute-done | bytes 16416 | tf_op jit(solution)/shard_map/ppermute | solution.py:495
  21.6 2.4 %row_pass.3 = (f32[32,128]{1,0:T(8,128)S(1)}, f32[32,128]{1,0:T(8,128)}) custom-call(f32[2,1024,2048]{2,1,0:T(8,128)S(1)} %get-tuple-element.37.t_ref, f32[16,128]{1,0:T(8,128)S(1)} %get-tuple-element.38.den_ref, f32[32,128]{1,0:T(8,128)S(1)} %add.18.refs_0_, f32[32,128]{1,0:T(8,128)S(1)} %collective-permute-done.1.refs_1_, ...), custom_call_target="tpu_custom_call" | custom-call | tf_op jit(solution)/shard_map/row_pass/pallas_call | solution.py:164
  29.2 2.4 %collective-permute-done.6.refs_3_.refs_7_ = f32[32,128]{1,0:T(8,128)S(1)} collective-permute-done((f32[32,128]{1,0:T(8,128)S(1)}, f32[32,128]{1,0:T(8,128)S(1)}, u32[]{:S(2)}, u32[]{:S(2)}) %collective-permute-start.6) | collective-permute-done | bytes 16416 | tf_op jit(solution)/shard_map/ppermute | solution.py:495
  31.6 2.3 %col_pass.2 = f32[32,128]{1,0:T(8,128)S(1)} custom-call(f32[2,1024,2048]{2,1,0:T(8,128)S(1)} %get-tuple-element.37.t_ref, f32[32,128]{1,0:T(8,128)S(1)} %get-tuple-element.40.refs_0_.refs_4_, f32[32,128]{1,0:T(8,128)S(1)} %collective-permute-done.4.refs_1_.refs_5_, f32[32,128]{1,0:T(8,128)S(1)} %collective-permute-done.5.refs_2_.refs_6_, ...), custom_call_target="tpu_custom_call" | custom-call | tf_op jit(solution)/shard_map/col_pass/pallas_call | solution.py:204
  35.4 4.2 %collective-permute-start.9 = (f32[32,128]{1,0:T(8,128)S(1)}, f32[32,128]{1,0:T(8,128)S(1)}, u32[]{:S(2)}, u32[]{:S(2)}) collective-permute-start(f32[32,128]{1,0:T(8,128)S(1)} %add.19.refs_0_), channel_id=1, source_target_pairs={{0,16},{4,20},{8,24},{12,28},{16,0},{20,4},{24,8},{28,12},{1,17},{... | collective-permute-start | bytes 49160 | tf_op jit(solution)/shard_map/ppermute | solution.py:495
  41.3 2.4 %row_pass.4 = (f32[16,128]{1,0:T(8,128)S(1)}, f32[32,128]{1,0:T(8,128)}) custom-call(f32[2,1024,2048]{2,1,0:T(8,128)S(1)} %get-tuple-element.37.t_ref, f32[16,128]{1,0:T(8,128)S(1)} %get-tuple-element.38.den_ref, f32[32,128]{1,0:T(8,128)S(1)} %add.19.refs_0_, f32[32,128]{1,0:T(8,128)S(1)} %collective-permute-done.8.refs_1_, ...), custom_call_target="tpu_custom_call" | custom-call | tf_op jit(solution)/shard_map/row_pass/pallas_call | solution.py:164
  44.7 2.4 %collective-permute-start.13 = (f32[16,128]{1,0:T(8,128)S(1)}, f32[16,128]{1,0:T(8,128)S(1)}, u32[]{:S(2)}, u32[]{:S(2)}) collective-permute-start(f32[16,128]{1,0:T(8,128)S(1)} %get-tuple-element.41.refs_0_), channel_id=1, source_target_pairs={{0,3},{1,2},{2,1},{3,0},{4,7},{5,6},{6,5},{7,4},{8,11},{9,10},{10,... | collective-permute-start | bytes 24584 | tf_op jit(solution)/shard_map/ppermute | solution.py:495
  49.3 2.3 %col_pass.3 = f32[32,128]{1,0:T(8,128)S(1)} custom-call(f32[2,1024,2048]{2,1,0:T(8,128)S(1)} %get-tuple-element.37.t_ref, f32[16,128]{1,0:T(8,128)S(1)} %get-tuple-element.41.refs_0_, f32[16,128]{1,0:T(8,128)S(1)} %collective-permute-done.11.refs_1_, f32[16,128]{1,0:T(8,128)S(1)} %collective-permute-done.12.refs_2_, ...), custom_call_target="tpu_custom_call" | custom-call | tf_op jit(solution)/shard_map/col_pass/pallas_call | solution.py:204
  53.6 2.3 %collective-permute-start.16 = (f32[32,128]{1,0:T(8,128)S(1)}, f32[32,128]{1,0:T(8,128)S(1)}, u32[]{:S(2)}, u32[]{:S(2)}) collective-permute-start(f32[32,128]{1,0:T(8,128)S(1)} %add.20.refs_0_), channel_id=1, source_target_pairs={{0,16},{4,20},{8,24},{12,28},{16,0},{20,4},{24,8},{28,12},{1,17},{... | collective-permute-start | bytes 49160 | tf_op jit(solution)/shard_map/ppermute | solution.py:495
  58.3 3.1 %collective-permute-done.17.refs_3_ = f32[32,128]{1,0:T(8,128)S(1)} collective-permute-done((f32[32,128]{1,0:T(8,128)S(1)}, f32[32,128]{1,0:T(8,128)S(1)}, u32[]{:S(2)}, u32[]{:S(2)}) %collective-permute-start.17) | collective-permute-done | bytes 16416 | tf_op jit(solution)/shard_map/ppermute | solution.py:495
  61.4 2.2 %row_pass.5 = (f32[16,128]{1,0:T(8,128)S(1)}, f32[32,128]{1,0:T(8,128)S(1)}) custom-call(f32[2,1024,2048]{2,1,0:T(8,128)S(1)} %get-tuple-element.37.t_ref, f32[16,128]{1,0:T(8,128)S(1)} %get-tuple-element.38.den_ref, f32[32,128]{1,0:T(8,128)S(1)} %add.20.refs_0_, f32[32,128]{1,0:T(8,128)S(1)} %collective-permute-done.15.refs_1_, ...), custom_call_target="tpu_custom_call" | custom-call | tf_op jit(solution)/shard_map/row_pass/pallas_call | solution.py:164
  63.6 1.6 %collective-permute-start.18 = (f32[16,128]{1,0:T(8,128)S(1)}, f32[16,128]{1,0:T(8,128)S(1)}, u32[]{:S(2)}, u32[]{:S(2)}) collective-permute-start(f32[16,128]{1,0:T(8,128)S(1)} %get-tuple-element.45.refs_0_), channel_id=1, source_target_pairs={{0,1},{1,0},{2,3},{3,2},{4,5},{5,4},{6,7},{7,6},{8,9},{9,8},{10,11... | collective-permute-start | bytes 24584 | tf_op jit(solution)/shard_map/ppermute | solution.py:495
  68.8 2.4 %collective-permute-done.20.refs_3_ = f32[16,128]{1,0:T(8,128)S(1)} collective-permute-done((f32[16,128]{1,0:T(8,128)S(1)}, f32[16,128]{1,0:T(8,128)S(1)}, u32[]{:S(2)}, u32[]{:S(2)}) %collective-permute-start.20) | collective-permute-done | bytes 8224 | tf_op jit(solution)/shard_map/ppermute | solution.py:495
  71.2 11.7 %gradients.1 = (f32[2,4,128,256]{3,2,1,0:T(8,128)S(1)}, f32[2,4,128,256]{3,2,1,0:T(8,128)S(1)}, f32[2,256,256]{2,1,0:T(8,128)S(1)}, f32[2,256,256]{2,1,0:T(8,128...) custom-call(f32[2,1024,2048]{2,1,0:T(8,128)S(1)} %get-tuple-element.37.t_ref, ...), custom_call_target="tpu_custom_call" | custom-call | tf_op jit(solution)/shard_map/gradients/pallas_call | solution.py:305
  84.1 1.5 %collective-permute-done.21.refs_1_ = f32[2,4,128,256]{3,2,1,0:T(8,128)S(1)} collective-permute-done((f32[2,4,128,256]{3,2,1,0:T(8,128)S(1)}, f32[2,4,128,256]{3,2,1,0:T(8,128)S(1)}, u32[]{:S(2)}, u32[]{:S(2)}) %collective-permute-start.21) | collective-permute-done | bytes 1048608 | tf_op jit(solution)/shard_map/ppermute | solution.py:495
  86.0 1.8 %collective-permute-start.23 = (f32[2,128,256]{2,1,0:T(8,128)S(1)}, f32[2,128,256]{2,1,0:T(8,128)S(1)}, u32[]{:S(2)}, u32[]{:S(2)}) collective-permute-start(f32[2,128,256]{2,1,0:T(8,128)S(1)} %get-tuple-element.51), channel_id=1, source_target_pairs={{0,16},{4,20},{8,24},{12,28},{16,0},{20,4},{24,8},{28,12},{1,17},{... | collective-permute-start | bytes 786440 | tf_op jit(solution)/shard_map/ppermute | solution.py:495
  87.8 9.6 %collective-permute-done.24.refs_5_ = f32[2,256,256]{2,1,0:T(8,128)S(1)} collective-permute-done((f32[2,256,256]{2,1,0:T(8,128)S(1)}, f32[2,256,256]{2,1,0:T(8,128)S(1)}, u32[]{:S(2)}, u32[]{:S(2)}) %collective-permute-start.24) | collective-permute-done | bytes 524320 | tf_op jit(solution)/shard_map/ppermute | solution.py:495
  98.5 2.3 %collective-permute-done.23.refs_3_ = f32[2,128,256]{2,1,0:T(8,128)S(1)} collective-permute-done((f32[2,128,256]{2,1,0:T(8,128)S(1)}, f32[2,128,256]{2,1,0:T(8,128)S(1)}, u32[]{:S(2)}, u32[]{:S(2)}) %collective-permute-start.23) | collective-permute-done | bytes 262176 | tf_op jit(solution)/shard_map/ppermute | solution.py:495
  102.6 1.7 %collective-permute-start.27 = (f32[1,128,256]{2,1,0:T(8,128)S(1)}, f32[1,128,256]{2,1,0:T(8,128)S(1)}, u32[]{:S(2)}, u32[]{:S(2)}) collective-permute-start(f32[1,128,256]{2,1,0:T(8,128)S(1)} %get-tuple-element.59), channel_id=1, source_target_pairs={{0,8},{4,12},{8,0},{12,4},{16,24},{20,28},{24,16},{28,20},{1,9},{5... | collective-permute-start | bytes 393224 | tf_op jit(solution)/shard_map/ppermute | solution.py:495
  106.2 2.8 %collective-permute-done.26.refs_1_ = f32[1,128,256]{2,1,0:T(8,128)S(1)} collective-permute-done((f32[1,128,256]{2,1,0:T(8,128)S(1)}, f32[1,128,256]{2,1,0:T(8,128)S(1)}, u32[]{:S(2)}, u32[]{:S(2)}) %collective-permute-start.26) | collective-permute-done | bytes 131104 | tf_op jit(solution)/shard_map/ppermute | solution.py:495
  109.8 1.7 %collective-permute-start.30 = (f32[2,8,128]{2,1,0:T(8,128)S(1)}, f32[2,8,128]{2,1,0:T(8,128)S(1)}, u32[]{:S(2)}, u32[]{:S(2)}) collective-permute-start(f32[2,8,128]{2,1,0:T(8,128)S(1)} %get-tuple-element.66.refs_0_), channel_id=1, source_target_pairs={{0,1},{1,0},{2,3},{3,2},{4,5},{5,4},{6,7},{7,6},{8,9},{9,8},{10,11... | collective-permute-start | bytes 24584 | tf_op jit(solution)/shard_map/ppermute | solution.py:495
  113.5 1.6 %collective-permute-done.31.refs_2_ = f32[2,8,128]{2,1,0:T(8,128)S(1)} collective-permute-done((f32[2,8,128]{2,1,0:T(8,128)S(1)}, f32[2,8,128]{2,1,0:T(8,128)S(1)}, u32[]{:S(2)}, u32[]{:S(2)}) %collective-permute-start.31) | collective-permute-done | bytes 8224 | tf_op jit(solution)/shard_map/ppermute | solution.py:495
  115.1 2.5 %collective-permute-done.32.refs_3_ = f32[2,8,128]{2,1,0:T(8,128)S(1)} collective-permute-done((f32[2,8,128]{2,1,0:T(8,128)S(1)}, f32[2,8,128]{2,1,0:T(8,128)S(1)}, u32[]{:S(2)}, u32[]{:S(2)}) %collective-permute-start.32) | collective-permute-done | bytes 8224 | tf_op jit(solution)/shard_map/ppermute | solution.py:495
  121.0 7.9 %collective-permute-done.36.refs_4_ = f32[264,256]{1,0:T(8,128)S(1)} collective-permute-done((f32[264,256]{1,0:T(8,128)S(1)}, f32[264,256]{1,0:T(8,128)S(1)}, u32[]{:S(2)}, u32[]{:S(2)}) %collective-permute-start.36) | collective-permute-done | bytes 270368 | tf_op jit(solution)/shard_map/ppermute | solution.py:495
  130.9 2.8 %collective-permute-start.42 = (f32[256,256]{1,0:T(8,128)S(1)}, f32[256,256]{1,0:T(8,128)S(1)}, u32[]{:S(2)}, u32[]{:S(2)}) collective-permute-start(f32[256,256]{1,0:T(8,128)S(1)} %slice_bitcast_fusion.1), channel_id=1, source_target_pairs={{0,1},{1,0},{2,3},{3,2},{4,5},{5,4},{6,7},{7,6},{8,9},{9,8},{10,11... | collective-permute-start | bytes 786440 | tf_op jit(solution)/shard_map/ppermute | solution.py:495
  133.6 1.9 %collective-permute-done.38.refs_6_ = f32[264,256]{1,0:T(8,128)S(1)} collective-permute-done((f32[264,256]{1,0:T(8,128)S(1)}, f32[264,256]{1,0:T(8,128)S(1)}, u32[]{:S(2)}, u32[]{:S(2)}) %collective-permute-start.38) | collective-permute-done | bytes 270368 | tf_op jit(solution)/shard_map/ppermute | solution.py:495
  135.6 1.6 %collective-permute-start.43 = (f32[256,256]{1,0:T(8,128)S(1)}, f32[256,256]{1,0:T(8,128)S(1)}, u32[]{:S(2)}, u32[]{:S(2)}) collective-permute-start(f32[256,256]{1,0:T(8,128)S(1)} %slice_bitcast_fusion), channel_id=1, source_target_pairs={{0,2},{1,3},{2,0},{3,1},{4,6},{5,7},{6,4},{7,5},{8,10},{9,11},{10,... | collective-permute-start | bytes 786440 | tf_op jit(solution)/shard_map/ppermute | solution.py:495
  140.1 4.2 %collective-permute-done.43.refs_12_ = f32[256,256]{1,0:T(8,128)S(1)} collective-permute-done((f32[256,256]{1,0:T(8,128)S(1)}, f32[256,256]{1,0:T(8,128)S(1)}, u32[]{:S(2)}, u32[]{:S(2)}) %collective-permute-start.43) | collective-permute-done | bytes 262176 | tf_op jit(solution)/shard_map/ppermute | solution.py:495
  (76 shorter events, 39.9 us)
Async XLA Ops:
  10.6 5.5 %collective-permute-start.1 = (f32[32,128]{1,0:T(8,128)S(1)}, f32[32,128]{1,0:T(8,128)S(1)}, u32[]{:S(2)}, u32[]{:S(2)}) collective-permute-start(f32[32,128]{1,0:T(8,128)S(1)} %add.18.refs_0_), channel_id=1, source_target_pairs={{0,8},{4,12},{8,0},{12,4},{16,24},{20,28},{24,16},{28,20},{1,9},{5... | collective-permute-start | bytes 49160 | tf_op jit(solution)/shard_map/ppermute | solution.py:495
  13.5 4.6 %collective-permute-start.2 = (f32[32,128]{1,0:T(8,128)S(1)}, f32[32,128]{1,0:T(8,128)S(1)}, u32[]{:S(2)}, u32[]{:S(2)}) collective-permute-start(f32[32,128]{1,0:T(8,128)S(1)} %add.18.refs_0_), channel_id=1, source_target_pairs={{0,16},{4,20},{8,24},{12,28},{16,0},{20,4},{24,8},{28,12},{1,17},{... | collective-permute-start | bytes 49160 | tf_op jit(solution)/shard_map/ppermute | solution.py:495
  16.1 5.5 %collective-permute-start.3 = (f32[32,128]{1,0:T(8,128)S(1)}, f32[32,128]{1,0:T(8,128)S(1)}, u32[]{:S(2)}, u32[]{:S(2)}) collective-permute-start(f32[32,128]{1,0:T(8,128)S(1)} %add.18.refs_0_), channel_id=1, source_target_pairs={{0,24},{4,28},{8,16},{12,20},{16,8},{20,12},{24,0},{28,4},{1,25},{... | collective-permute-start | bytes 49160 | tf_op jit(solution)/shard_map/ppermute | solution.py:495
  24.0 3.8 %collective-permute-start.4 = (f32[32,128]{1,0:T(8,128)S(1)}, f32[32,128]{1,0:T(8,128)S(1)}, u32[]{:S(2)}, u32[]{:S(2)}) collective-permute-start(f32[32,128]{1,0:T(8,128)S(1)} %get-tuple-element.40.refs_0_.refs_4_), channel_id=1, source_target_pairs={{0,1},{1,0},{2,3},{3,2},{4,5},{5,4},{6,7},{7,6},{8,9},{9,8},{10,11... | collective-permute-start | bytes 49160 | tf_op jit(solution)/shard_map/ppermute | solution.py:495
  27.0 4.6 %collective-permute-start.6 = (f32[32,128]{1,0:T(8,128)S(1)}, f32[32,128]{1,0:T(8,128)S(1)}, u32[]{:S(2)}, u32[]{:S(2)}) collective-permute-start(f32[32,128]{1,0:T(8,128)S(1)} %get-tuple-element.40.refs_0_.refs_4_), channel_id=1, source_target_pairs={{0,3},{1,2},{2,1},{3,0},{4,7},{5,6},{6,5},{7,4},{8,11},{9,10},{10,... | collective-permute-start | bytes 49160 | tf_op jit(solution)/shard_map/ppermute | solution.py:495
  35.2 5.5 %collective-permute-start.10 = (f32[32,128]{1,0:T(8,128)S(1)}, f32[32,128]{1,0:T(8,128)S(1)}, u32[]{:S(2)}, u32[]{:S(2)}) collective-permute-start(f32[32,128]{1,0:T(8,128)S(1)} %add.19.refs_0_), channel_id=1, source_target_pairs={{0,24},{4,28},{8,16},{12,20},{16,8},{20,12},{24,0},{28,4},{1,25},{... | collective-permute-start | bytes 49160 | tf_op jit(solution)/shard_map/ppermute | solution.py:495
  35.4 5.3 %collective-permute-start.8 = (f32[32,128]{1,0:T(8,128)S(1)}, f32[32,128]{1,0:T(8,128)S(1)}, u32[]{:S(2)}, u32[]{:S(2)}) collective-permute-start(f32[32,128]{1,0:T(8,128)S(1)} %add.19.refs_0_), channel_id=1, source_target_pairs={{0,8},{4,12},{8,0},{12,4},{16,24},{20,28},{24,16},{28,20},{1,9},{5... | collective-permute-start | bytes 49160 | tf_op jit(solution)/shard_map/ppermute | solution.py:495
  35.4 5.9 %collective-permute-start.9 = (f32[32,128]{1,0:T(8,128)S(1)}, f32[32,128]{1,0:T(8,128)S(1)}, u32[]{:S(2)}, u32[]{:S(2)}) collective-permute-start(f32[32,128]{1,0:T(8,128)S(1)} %add.19.refs_0_), channel_id=1, source_target_pairs={{0,16},{4,20},{8,24},{12,28},{16,0},{20,4},{24,8},{28,12},{1,17},{... | collective-permute-start | bytes 49160 | tf_op jit(solution)/shard_map/ppermute | solution.py:495
  44.7 4.5 %collective-permute-start.13 = (f32[16,128]{1,0:T(8,128)S(1)}, f32[16,128]{1,0:T(8,128)S(1)}, u32[]{:S(2)}, u32[]{:S(2)}) collective-permute-start(f32[16,128]{1,0:T(8,128)S(1)} %get-tuple-element.41.refs_0_), channel_id=1, source_target_pairs={{0,3},{1,2},{2,1},{3,0},{4,7},{5,6},{6,5},{7,4},{8,11},{9,10},{10,... | collective-permute-start | bytes 24584 | tf_op jit(solution)/shard_map/ppermute | solution.py:495
  52.9 4.4 %collective-permute-start.15 = (f32[32,128]{1,0:T(8,128)S(1)}, f32[32,128]{1,0:T(8,128)S(1)}, u32[]{:S(2)}, u32[]{:S(2)}) collective-permute-start(f32[32,128]{1,0:T(8,128)S(1)} %add.20.refs_0_), channel_id=1, source_target_pairs={{0,8},{4,12},{8,0},{12,4},{16,24},{20,28},{24,16},{28,20},{1,9},{5... | collective-permute-start | bytes 49160 | tf_op jit(solution)/shard_map/ppermute | solution.py:495
  53.6 4.6 %collective-permute-start.16 = (f32[32,128]{1,0:T(8,128)S(1)}, f32[32,128]{1,0:T(8,128)S(1)}, u32[]{:S(2)}, u32[]{:S(2)}) collective-permute-start(f32[32,128]{1,0:T(8,128)S(1)} %add.20.refs_0_), channel_id=1, source_target_pairs={{0,16},{4,20},{8,24},{12,28},{16,0},{20,4},{24,8},{28,12},{1,17},{... | collective-permute-start | bytes 49160 | tf_op jit(solution)/shard_map/ppermute | solution.py:495
  55.9 5.5 %collective-permute-start.17 = (f32[32,128]{1,0:T(8,128)S(1)}, f32[32,128]{1,0:T(8,128)S(1)}, u32[]{:S(2)}, u32[]{:S(2)}) collective-permute-start(f32[32,128]{1,0:T(8,128)S(1)} %add.20.refs_0_), channel_id=1, source_target_pairs={{0,24},{4,28},{8,16},{12,20},{16,8},{20,12},{24,0},{28,4},{1,25},{... | collective-permute-start | bytes 49160 | tf_op jit(solution)/shard_map/ppermute | solution.py:495
  66.6 4.5 %collective-permute-start.20 = (f32[16,128]{1,0:T(8,128)S(1)}, f32[16,128]{1,0:T(8,128)S(1)}, u32[]{:S(2)}, u32[]{:S(2)}) collective-permute-start(f32[16,128]{1,0:T(8,128)S(1)} %get-tuple-element.45.refs_0_), channel_id=1, source_target_pairs={{0,3},{1,2},{2,1},{3,0},{4,7},{5,6},{6,5},{7,4},{8,11},{9,10},{10,... | collective-permute-start | bytes 24584 | tf_op jit(solution)/shard_map/ppermute | solution.py:495
  83.0 14.3 %collective-permute-start.24 = (f32[2,256,256]{2,1,0:T(8,128)S(1)}, f32[2,256,256]{2,1,0:T(8,128)S(1)}, u32[]{:S(2)}, u32[]{:S(2)}) collective-permute-start(f32[2,256,256]{2,1,0:T(8,128)S(1)} %get-tuple-element.53), channel_id=1, source_target_pairs={{0,1},{1,0},{2,3},{3,2},{4,5},{5,4},{6,7},{7,6},{8,9},{9,8},{10,11... | collective-permute-start | bytes 1572872 | tf_op jit(solution)/shard_map/ppermute | solution.py:495
  83.6 14.0 %collective-permute-start.25 = (f32[2,256,256]{2,1,0:T(8,128)S(1)}, f32[2,256,256]{2,1,0:T(8,128)S(1)}, u32[]{:S(2)}, u32[]{:S(2)}) collective-permute-start(f32[2,256,256]{2,1,0:T(8,128)S(1)} %get-tuple-element.55), channel_id=1, source_target_pairs={{0,2},{1,3},{2,0},{3,1},{4,6},{5,7},{6,4},{7,5},{8,10},{9,11},{10,... | collective-permute-start | bytes 1572872 | tf_op jit(solution)/shard_map/ppermute | solution.py:495
  85.8 12.8 %collective-permute-start.22 = (f32[2,128,256]{2,1,0:T(8,128)S(1)}, f32[2,128,256]{2,1,0:T(8,128)S(1)}, u32[]{:S(2)}, u32[]{:S(2)}) collective-permute-start(f32[2,128,256]{2,1,0:T(8,128)S(1)} %get-tuple-element.49), channel_id=1, source_target_pairs={{0,8},{4,12},{8,0},{12,4},{16,24},{20,28},{24,16},{28,20},{1,9},{5... | collective-permute-start | bytes 786440 | tf_op jit(solution)/shard_map/ppermute | solution.py:495
  86.0 14.8 %collective-permute-start.23 = (f32[2,128,256]{2,1,0:T(8,128)S(1)}, f32[2,128,256]{2,1,0:T(8,128)S(1)}, u32[]{:S(2)}, u32[]{:S(2)}) collective-permute-start(f32[2,128,256]{2,1,0:T(8,128)S(1)} %get-tuple-element.51), channel_id=1, source_target_pairs={{0,16},{4,20},{8,24},{12,28},{16,0},{20,4},{24,8},{28,12},{1,17},{... | collective-permute-start | bytes 786440 | tf_op jit(solution)/shard_map/ppermute | solution.py:495
  101.0 8.2 %collective-permute-start.28 = (f32[1,256,256]{2,1,0:T(8,128)S(1)}, f32[1,256,256]{2,1,0:T(8,128)S(1)}, u32[]{:S(2)}, u32[]{:S(2)}) collective-permute-start(f32[1,256,256]{2,1,0:T(8,128)S(1)} %get-tuple-element.61), channel_id=1, source_target_pairs={{0,2},{1,3},{2,0},{3,1},{4,6},{5,7},{6,4},{7,5},{8,10},{9,11},{10,... | collective-permute-start | bytes 786440 | tf_op jit(solution)/shard_map/ppermute | solution.py:495
  101.6 7.6 %collective-permute-start.29 = (f32[1,256,256]{2,1,0:T(8,128)S(1)}, f32[1,256,256]{2,1,0:T(8,128)S(1)}, u32[]{:S(2)}, u32[]{:S(2)}) collective-permute-start(f32[1,256,256]{2,1,0:T(8,128)S(1)} %get-tuple-element.63), channel_id=1, source_target_pairs={{0,1},{1,0},{2,3},{3,2},{4,5},{5,4},{6,7},{7,6},{8,9},{9,8},{10,11... | collective-permute-start | bytes 786440 | tf_op jit(solution)/shard_map/ppermute | solution.py:495
  102.3 6.7 %collective-permute-start.26 = (f32[1,128,256]{2,1,0:T(8,128)S(1)}, f32[1,128,256]{2,1,0:T(8,128)S(1)}, u32[]{:S(2)}, u32[]{:S(2)}) collective-permute-start(f32[1,128,256]{2,1,0:T(8,128)S(1)} %get-tuple-element.57), channel_id=1, source_target_pairs={{0,16},{4,20},{8,24},{12,28},{16,0},{20,4},{24,8},{28,12},{1,17},{... | collective-permute-start | bytes 393224 | tf_op jit(solution)/shard_map/ppermute | solution.py:495
  102.6 6.6 %collective-permute-start.27 = (f32[1,128,256]{2,1,0:T(8,128)S(1)}, f32[1,128,256]{2,1,0:T(8,128)S(1)}, u32[]{:S(2)}, u32[]{:S(2)}) collective-permute-start(f32[1,128,256]{2,1,0:T(8,128)S(1)} %get-tuple-element.59), channel_id=1, source_target_pairs={{0,8},{4,12},{8,0},{12,4},{16,24},{20,28},{24,16},{28,20},{1,9},{5... | collective-permute-start | bytes 393224 | tf_op jit(solution)/shard_map/ppermute | solution.py:495
  113.0 4.7 %collective-permute-start.32 = (f32[2,8,128]{2,1,0:T(8,128)S(1)}, f32[2,8,128]{2,1,0:T(8,128)S(1)}, u32[]{:S(2)}, u32[]{:S(2)}) collective-permute-start(f32[2,8,128]{2,1,0:T(8,128)S(1)} %get-tuple-element.66.refs_0_), channel_id=1, source_target_pairs={{0,3},{1,2},{2,1},{3,0},{4,7},{5,6},{6,5},{7,4},{8,11},{9,10},{10,... | collective-permute-start | bytes 24584 | tf_op jit(solution)/shard_map/ppermute | solution.py:495
  117.7 12.7 %collective-permute-start.41 = (f32[2,256,256]{2,1,0:T(8,128)S(1)}, f32[2,256,256]{2,1,0:T(8,128)S(1)}, u32[]{:S(2)}, u32[]{:S(2)}) collective-permute-start(f32[2,256,256]{2,1,0:T(8,128)S(1)} %get-tuple-element.68.refs_8_), channel_id=1, source_target_pairs={{0,2},{1,3},{2,0},{3,1},{4,6},{5,7},{6,4},{7,5},{8,10},{9,11},{10,... | collective-permute-start | bytes 1572872 | tf_op jit(solution)/shard_map/ppermute | solution.py:495
  118.3 10.7 %collective-permute-start.36 = (f32[264,256]{1,0:T(8,128)S(1)}, f32[264,256]{1,0:T(8,128)S(1)}, u32[]{:S(2)}, u32[]{:S(2)}) collective-permute-start(f32[264,256]{1,0:T(8,128)S(1)} %get-tuple-element.67.refs_0_), channel_id=1, source_target_pairs={{0,16},{4,20},{8,24},{12,28},{16,0},{20,4},{24,8},{28,12},{1,17},{... | collective-permute-start | bytes 811016 | tf_op jit(solution)/shard_map/ppermute | solution.py:495
  119.0 11.9 %collective-permute-start.40 = (f32[2,256,256]{2,1,0:T(8,128)S(1)}, f32[2,256,256]{2,1,0:T(8,128)S(1)}, u32[]{:S(2)}, u32[]{:S(2)}) collective-permute-start(f32[2,256,256]{2,1,0:T(8,128)S(1)} %get-tuple-element.68.refs_8_), channel_id=1, source_target_pairs={{0,1},{1,0},{2,3},{3,2},{4,5},{5,4},{6,7},{7,6},{8,9},{9,8},{10,11... | collective-permute-start | bytes 1572872 | tf_op jit(solution)/shard_map/ppermute | solution.py:495
  119.6 10.7 %collective-permute-start.34 = (f32[264,256]{1,0:T(8,128)S(1)}, f32[264,256]{1,0:T(8,128)S(1)}, u32[]{:S(2)}, u32[]{:S(2)}) collective-permute-start(f32[264,256]{1,0:T(8,128)S(1)} %get-tuple-element.67.refs_0_), channel_id=1, source_target_pairs={{0,8},{4,12},{8,0},{12,4},{16,24},{20,28},{24,16},{28,20},{1,9},{5... | collective-permute-start | bytes 811016 | tf_op jit(solution)/shard_map/ppermute | solution.py:495
  128.9 6.6 %collective-permute-start.38 = (f32[264,256]{1,0:T(8,128)S(1)}, f32[264,256]{1,0:T(8,128)S(1)}, u32[]{:S(2)}, u32[]{:S(2)}) collective-permute-start(f32[264,256]{1,0:T(8,128)S(1)} %collective-permute-done.36.refs_4_), channel_id=1, source_target_pairs={{0,8},{4,12},{8,0},{12,4},{16,24},{20,28},{24,16},{28,20},{1,9},{5... | collective-permute-start | bytes 811016 | tf_op jit(solution)/shard_map/ppermute | solution.py:495
  128.9 6.6 %collective-permute-start.33 = (f32[264,256]{1,0:T(8,128)S(1)}, f32[264,256]{1,0:T(8,128)S(1)}, u32[]{:S(2)}, u32[]{:S(2)}) collective-permute-start(f32[264,256]{1,0:T(8,128)S(1)} %get-tuple-element.67.refs_0_), channel_id=1, source_target_pairs={{0,4},{4,0},{8,12},{12,8},{16,20},{20,16},{24,28},{28,24},{1,5},{5... | collective-permute-start | bytes 811016 | tf_op jit(solution)/shard_map/ppermute | solution.py:495
  130.3 6.8 %collective-permute-start.37 = (f32[264,256]{1,0:T(8,128)S(1)}, f32[264,256]{1,0:T(8,128)S(1)}, u32[]{:S(2)}, u32[]{:S(2)}) collective-permute-start(f32[264,256]{1,0:T(8,128)S(1)} %collective-permute-done.36.refs_4_), channel_id=1, source_target_pairs={{0,4},{4,0},{8,12},{12,8},{16,20},{20,16},{24,28},{28,24},{1,5},{5... | collective-permute-start | bytes 811016 | tf_op jit(solution)/shard_map/ppermute | solution.py:495
  130.3 6.8 %collective-permute-start.35 = (f32[264,256]{1,0:T(8,128)S(1)}, f32[264,256]{1,0:T(8,128)S(1)}, u32[]{:S(2)}, u32[]{:S(2)}) collective-permute-start(f32[264,256]{1,0:T(8,128)S(1)} %collective-permute-done.34.refs_2_), channel_id=1, source_target_pairs={{0,4},{4,0},{8,12},{12,8},{16,20},{20,16},{24,28},{28,24},{1,5},{5... | collective-permute-start | bytes 811016 | tf_op jit(solution)/shard_map/ppermute | solution.py:495
  130.9 9.2 %collective-permute-start.42 = (f32[256,256]{1,0:T(8,128)S(1)}, f32[256,256]{1,0:T(8,128)S(1)}, u32[]{:S(2)}, u32[]{:S(2)}) collective-permute-start(f32[256,256]{1,0:T(8,128)S(1)} %slice_bitcast_fusion.1), channel_id=1, source_target_pairs={{0,1},{1,0},{2,3},{3,2},{4,5},{5,4},{6,7},{7,6},{8,9},{9,8},{10,11... | collective-permute-start | bytes 786440 | tf_op jit(solution)/shard_map/ppermute | solution.py:495
  135.6 8.8 %collective-permute-start.43 = (f32[256,256]{1,0:T(8,128)S(1)}, f32[256,256]{1,0:T(8,128)S(1)}, u32[]{:S(2)}, u32[]{:S(2)}) collective-permute-start(f32[256,256]{1,0:T(8,128)S(1)} %slice_bitcast_fusion), channel_id=1, source_target_pairs={{0,2},{1,3},{2,0},{3,1},{4,6},{5,7},{6,4},{7,5},{8,10},{9,11},{10,... | collective-permute-start | bytes 786440 | tf_op jit(solution)/shard_map/ppermute | solution.py:495
  (12 other events, 34.0 us)

commit v7 on v6

--- a/solution.py
+++ b/solution.py
@@ -225,16 +225,25 @@
     return sum(((piece >> bit) & 1) << (steps - 1 - j) for j, bit in enumerate(order))
 
 
-def grad_kernel(batch_orders, proto_orders, parts, t_ref, r_ref, ubt_ref, cb_ref, *refs):
+def chunk_span(m, width):
+    which = jnp.bitwise_xor(lax.axis_index("batch"), m)
+    return which, pl.multiple_of(which * width, width)
+
+
+def proto_grads(ubt, chunk, orders, i, out_ref):
+    dc = jnp.dot(ubt, chunk, preferred_element_type=jnp.float32).T
+    half = dc.shape[0] // 2
+    for h in range(2):
+        out_ref[h, place_of(i, orders[h])] = dc[h * half : (h + 1) * half]
+
+
+def send_kernel(orders, parts, t_ref, r_ref, ubt_ref, *refs):
     row_parts, den_parts = refs[:parts], refs[parts : 2 * parts]
-    send_ref, keep_ref = refs[2 * parts : 2 * parts + 2]
-    du_refs = refs[2 * parts + 2 : 2 * parts + 6]
-    g_s, odd_s, even_s, code_s, prob_s = refs[2 * parts + 6 :]
+    send_ref, g_ref, chunk_s, code_s, prob_s = refs[2 * parts :]
     clips, count = t_ref.shape[1:]
     groups, lines = clips // LANES, count // LANES
-    pieces = 1 << len(batch_orders[0])
+    pieces = 1 << len(orders[0])
     width = count // (2 * pieces)
-    half = width // 2
     code = (1.0 / TEMPER) / sum_of(row_parts, 0, 2 * groups)
     prob = (1.0 / TEMPER) / sum_of(den_parts, 2 * groups, 2 * groups)
     for v in range(2):
@@ -244,9 +253,8 @@
             code_s[v, rows, :] = to_columns(code[line : line + 1, :])
             prob_s[v, rows, :] = to_columns(prob[line : line + 1, :])
 
-    def score_grads(m, chunk_s):
-        which = jnp.bitwise_xor(lax.axis_index("batch"), m)
-        first = pl.multiple_of(which * width, width)
+    def score_grads(m, keep_chunk):
+        which, first = chunk_span(m, width)
         for i in range(0, clips, 32):
             rows = slice(i, i + 32)
             codes = [code_s[v, rows, :] for v in range(2)]
@@ -261,69 +269,105 @@
                 ]
                 for v in range(2):
                     g = (t[v] * probs[v] - q[1 - v]).astype(jnp.bfloat16)
-                    g_s[v, rows, span] = g
-                    chunk_s[v * clips + i : v * clips + i + 32, h * LANES : (h + 1) * LANES] = g
-
-    def proto_grads(i, chunk_s, out_ref):
-        dct = jnp.dot(ubt_ref[...], chunk_s[...], preferred_element_type=jnp.float32)
-        dc = dct.T
-        for h in range(2):
-            place = place_of(i, batch_orders[h])
-            out_ref[h, place] = dc[h * half : (h + 1) * half]
-
-    even_s[...] = jnp.zeros_like(even_s)
+                    own = slice(v * clips + i, v * clips + i + 32)
+                    g_ref[own, span] = g
+                    if keep_chunk:
+                        chunk_s[own, h * LANES : (h + 1) * LANES] = g
 
     def pair(i, _):
-        score_grads(2 * i + 1, odd_s)
-        proto_grads(jnp.maximum(i - 1, 0), even_s, keep_ref)
-        score_grads(2 * i, even_s)
-        proto_grads(i, odd_s, send_ref)
+        score_grads(2 * i + 1, True)
+        score_grads(2 * i, False)
+        proto_grads(ubt_ref[...], chunk_s[...], orders, i, send_ref)
         return 0
 
     lax.fori_loop(0, pieces, pair, 0)
-    proto_grads(pieces - 1, even_s, keep_ref)
-
-    peers = 1 << len(proto_orders[0])
-    size = clips // peers
-    for v in range(2):
-        for place in range(peers):
-            which = jnp.bitwise_xor(lax.axis_index("proto"), piece_of(place, proto_orders[v]))
-            rows = pl.ds(pl.multiple_of(which * size, size), size)
-            out_ref = du_refs[2 * v + (0 if place >= peers // 2 else 1)]
-            out_ref[place % (peers // 2)] = jnp.dot(
-                g_s[v, rows, :], cb_ref[...], preferred_element_type=jnp.float32
-            )
-
-
-def gradients(t, r, ubt, cb, row_parts, den_parts, batch_orders, proto_orders):
+
+
+def send_gradients(t, r, ubt, row_parts, den_parts, orders):
     clips, count = t.shape[1:]
-    feats = cb.shape[1]
-    pieces, peers = 1 << len(batch_orders[0]), 1 << len(proto_orders[0])
+    feats = ubt.shape[0]
+    pieces = 1 << len(orders[0])
     width = count // (2 * pieces)
-    proto_share = jax.ShapeDtypeStruct((2, pieces, width // 2, feats), jnp.float32)
-    embed_share = jax.ShapeDtypeStruct((peers // 2, clips // peers, feats), jnp.float32)
-    return pl.pallas_call(
-        functools.partial(grad_kernel, batch_orders, proto_orders, len(row_parts)),
-        out_shape=(proto_share,) * 2 + (embed_share,) * 4,
-        in_specs=[vmem_spec()] * (4 + 2 * len(row_parts)),
-        out_specs=(vmem_spec(),) * 6,
+    return pl.pallas_call(
+        functools.partial(send_kernel, orders, len(row_parts)),
+        out_shape=(
+            jax.ShapeDtypeStruct((2, pieces, width // 2, feats), jnp.float32),
+            pltpu.VMEM((2 * clips, count), jnp.bfloat16),
+        ),
+        in_specs=[vmem_spec()] * (3 + 2 * len(row_parts)),
+        out_specs=(vmem_spec(),) * 2,
         scratch_shapes=[
-            pltpu.VMEM((2, clips, count), jnp.bfloat16),
-            pltpu.VMEM((2 * clips, width), jnp.bfloat16),
             pltpu.VMEM((2 * clips, width), jnp.bfloat16),
             pltpu.VMEM((2, clips, LANES), jnp.float32),
             pltpu.VMEM((2, clips, LANES), jnp.float32),
         ],
-        compiler_params=params(24),
-        name="gradients",
-    )(
-        pltpu.with_memory_space_constraint(t, pltpu.VMEM),
-        r,
-        ubt,
-        cb,
-        *row_parts,
-        *den_parts,
-    )
+        compiler_params=params(14),
+        cost_estimate=pl.CostEstimate(
+            flops=2 * clips * count * feats, bytes_accessed=20 * MIB, transcendentals=0
+        ),
+        name="send_gradients",
+    )(pltpu.with_memory_space_constraint(t, pltpu.VMEM), r, ubt, *row_parts, *den_parts)
+
+
+def embed_grad_kernel(orders, g_ref, cb_ref, *outs):
+    clips = g_ref.shape[0] // 2
+    peers = 1 << len(orders[0])
+    size = clips // peers
+    for v in range(2):
+        for place in range(peers):
+            which = jnp.bitwise_xor(lax.axis_index("proto"), piece_of(place, orders[v]))
+            rows = pl.ds(pl.multiple_of(v * clips + which * size, size), size)
+            out_ref = outs[2 * v + (0 if place >= peers // 2 else 1)]
+            out_ref[place % (peers // 2)] = jnp.dot(
+                g_ref[rows, :], cb_ref[...], preferred_element_type=jnp.float32
+            )
+
+
+def embed_gradients(g, cb, orders):
+    clips, count = g.shape[0] // 2, g.shape[1]
+    feats = cb.shape[1]
+    peers = 1 << len(orders[0])
+    share = jax.ShapeDtypeStruct((peers // 2, clips // peers, feats), jnp.float32)
+    return pl.pallas_call(
+        functools.partial(embed_grad_kernel, orders),
+        out_shape=(share,) * 4,
+        in_specs=[vmem_spec()] * 2,
+        out_specs=(vmem_spec(),) * 4,
+        compiler_params=params(14),
+        cost_estimate=pl.CostEstimate(
+            flops=4 * clips * count * feats, bytes_accessed=11 * MIB, transcendentals=0
+        ),
+        name="embed_gradients",
+    )(pltpu.with_memory_space_constraint(g, pltpu.VMEM), cb)
+
+
+def keep_kernel(orders, g_ref, ubt_ref, after_ref, keep_ref):
+    pieces = 1 << len(orders[0])
+    width = g_ref.shape[1] // (2 * pieces)
+
+    def step(i, _):
+        _, first = chunk_span(2 * i, width)
+        proto_grads(ubt_ref[...], g_ref[:, pl.ds(first, width)], orders, i, keep_ref)
+        return 0
+
+    lax.fori_loop(0, pieces, step, 0)
+
+
+def keep_gradients(g, ubt, after, orders):
+    count = g.shape[1]
+    feats, clips = ubt.shape
+    pieces = 1 << len(orders[0])
+    return pl.pallas_call(
+        functools.partial(keep_kernel, orders),
+        out_shape=jax.ShapeDtypeStruct((2, pieces, count // (4 * pieces), feats), jnp.float32),
+        in_specs=[vmem_spec()] * 2 + [pl.BlockSpec(memory_space=pl.ANY)],
+        out_specs=vmem_spec(),
+        compiler_params=params(14),
+        cost_estimate=pl.CostEstimate(
+            flops=clips * count * feats, bytes_accessed=6 * MIB, transcendentals=0
+        ),
+        name="keep_gradients",
+    )(pltpu.with_memory_space_constraint(g, pltpu.VMEM), ubt, after)
 
 
 def split_add_kernel(plan, inputs, *refs):
@@ -367,8 +411,9 @@
 
 
 def share_kernel(proto_raw, slow_raw, fast_raw, *refs):
-    terms, (proto_out, embed_out, square_out) = refs[:-3], refs[-3:]
-    half = proto_raw.shape[0] // 2
+    terms, (proto_out, embed_out) = refs[:-2], refs[-2:]
+    count = proto_raw.shape[0]
+    half = count // 2
     squares = [jnp.zeros((8, LANES), jnp.float32)] * 2
     for h in range(2):
         rows = slice(h * half, (h + 1) * half)
@@ -381,20 +426,20 @@
         squares[1] = squares[1] + row_fold(lane_sum(grad * grad))
     for kind in range(2):
         total = jnp.sum(jnp.sum(squares[kind], axis=0, keepdims=True), axis=1, keepdims=True)
-        square_out[kind] = jnp.broadcast_to(total, (8, LANES))
+        proto_out[count:, kind * LANES : (kind + 1) * LANES] = jnp.broadcast_to(total, (EXTRA, LANES))
 
 
 def project_shares(raws, terms):
     rows, feats = raws[1].shape
+    count = raws[0].shape[0]
     return pl.pallas_call(
         share_kernel,
         out_shape=(
-            jax.ShapeDtypeStruct(raws[0].shape, jnp.float32),
+            jax.ShapeDtypeStruct((count + EXTRA, feats), jnp.float32),
             jax.ShapeDtypeStruct((2, rows, feats), jnp.float32),
-            jax.ShapeDtypeStruct((2, 8, LANES), jnp.float32),
         ),
         in_specs=[vmem_spec()] * (len(raws) + len(terms)),
-        out_specs=(vmem_spec(),) * 3,
+        out_specs=(vmem_spec(),) * 2,
         compiler_params=params(10),
         name="project_shares",
     )(*raws, *terms)
@@ -406,70 +451,57 @@
     return terms[0]
 
 
-def pack_kernel(proto_ref, embed_ref, *refs):
-    squares, (proto_out, embed_out) = refs[:-2], refs[-2:]
-    rows = proto_ref.shape[0]
-    total = tree_sum([square[...] for square in squares])
-    proto_out[:rows, :] = proto_ref[...]
+def squares_kernel(*refs):
+    pieces, out_ref = refs[:-1], refs[-1]
+    total = tree_sum([piece[piece.shape[0] - EXTRA :, :] for piece in pieces])
     for kind in range(2):
-        proto_out[rows:, kind * LANES : (kind + 1) * LANES] = total[kind]
-    embed_out[...] = embed_ref[...]
-
-
-def pack_shares(grad_proto, grad_embed, squares):
-    rows, feats = grad_proto.shape
-    return pl.pallas_call(
-        pack_kernel,
-        out_shape=(
-            jax.ShapeDtypeStruct((rows + EXTRA, feats), jnp.float32),
-            jax.ShapeDtypeStruct(grad_embed.shape, jnp.float32),
-        ),
-        in_specs=[vmem_spec()] * (2 + len(squares)),
-        out_specs=(vmem_spec(),) * 2,
-        compiler_params=params(10),
-        name="pack_shares",
-    )(grad_proto, grad_embed, *squares)
-
-
-def total_square(refs, kind):
-    lanes = slice(kind * LANES, (kind + 1) * LANES)
-    return tree_sum([ref[ref.shape[0] - EXTRA :, lanes] for ref in refs])[0:1, 0:1]
-
-
-def finish_protos_kernel(entries, *refs):
-    pieces, out_ref = refs[:-1], refs[-1]
-    factor = lax.rsqrt(total_square(pieces, 0) / entries + NORM_EPS)
-    size = pieces[0].shape[0] - EXTRA
-    for m, piece in enumerate(pieces):
-        which = jnp.bitwise_xor(lax.axis_index("batch"), m)
-        out_ref[pl.ds(pl.multiple_of(which * size, size), size), :] = piece[:size, :] * factor
-
-
-def finish_protos(entries, pieces):
-    rows, feats = pieces[0].shape
-    return pl.pallas_call(
-        functools.partial(finish_protos_kernel, entries),
-        out_shape=jax.ShapeDtypeStruct((len(pieces) * (rows - EXTRA), feats), jnp.float32),
+        out_ref[kind] = total[:, kind * LANES : (kind + 1) * LANES]
+
+
+def sum_squares(pieces):
+    return pl.pallas_call(
+        squares_kernel,
+        out_shape=jax.ShapeDtypeStruct((2, 8, LANES), jnp.float32),
         in_specs=[vmem_spec()] * len(pieces),
         out_specs=vmem_spec(),
-        compiler_params=params(12),
-        name="finish_protos",
+        compiler_params=params(8),
+        name="sum_squares",
     )(*pieces)
 
 
-def finish_embeds_kernel(entries, plan, count, *refs):
-    pieces, ins, outs = refs[:count], refs[count:-2], refs[-2:]
-    factor = lax.rsqrt(total_square(pieces, 1) / entries + NORM_EPS)
-    for v, places in enumerate(plan):
+def finish_kernel(entries, plan, counts, *refs):
+    squares, protos = refs[: counts[0]], refs[counts[0] : counts[0] + counts[1]]
+    ins, outs = refs[counts[0] + counts[1] : -7], refs[-7:-4]
+    proto_s, slow_s, fast_s, sems = refs[-4:]
+    total = tree_sum([square[...] for square in squares])
+    factors = [lax.rsqrt(total[k, 0:1, 0:1] / entries[k] + NORM_EPS) for k in range(2)]
+    size = protos[0].shape[0] - EXTRA
+    copies = []
+    for m, piece in enumerate(protos):
+        which = jnp.bitwise_xor(lax.axis_index("batch"), m)
+        rows = pl.ds(pl.multiple_of(which * size, size), size)
+        proto_s[m] = piece[:size, :] * factors[0]
+        copies.append(pltpu.make_async_copy(proto_s.at[m], outs[0].at[rows], sems.at[m]))
+        copies[-1].start()
+    for v, (places, scaled) in enumerate(zip(plan, (slow_s, fast_s))):
         for m, (place, view) in enumerate(places):
             src = ins[place][...] if view is None else ins[place][view]
             size = src.shape[0]
             which = jnp.bitwise_xor(lax.axis_index("proto"), m)
-            outs[v][pl.ds(pl.multiple_of(which * size, size), size), :] = src * factor
-
-
-def finish_embeds(entries, pieces, groups):
-    arrays, plan, outs = [], [], []
+            rows = pl.ds(pl.multiple_of(which * size, size), size)
+            scaled[m] = src * factors[1]
+            sem = sems.at[counts[1] + v * len(places) + m]
+            copies.append(pltpu.make_async_copy(scaled.at[m], outs[1 + v].at[rows], sem))
+            copies[-1].start()
+    for copy in copies:
+        copy.wait()
+
+
+def finish(entries, squares, protos, groups):
+    arrays, plan = [], []
+    rows, feats = protos[0].shape
+    scratch = [pltpu.VMEM((len(protos), rows - EXTRA, feats), jnp.float32)]
+    outs = [jax.ShapeDtypeStruct((len(protos) * (rows - EXTRA), feats), jnp.float32)]
     for group in groups:
         places = []
         for array, view in group:
@@ -480,15 +512,18 @@
             places.append((place, view))
         plan.append(places)
         rows, feats = group[0][0].shape[-2:]
+        scratch.append(pltpu.VMEM((len(group), rows, feats), jnp.float32))
         outs.append(jax.ShapeDtypeStruct((len(group) * rows, feats), jnp.float32))
-    return pl.pallas_call(
-        functools.partial(finish_embeds_kernel, entries, plan, len(pieces)),
+    count = len(protos) + sum(len(places) for places in plan)
+    return pl.pallas_call(
+        functools.partial(finish_kernel, entries, plan, (len(squares), len(protos))),
         out_shape=tuple(outs),
-        in_specs=[vmem_spec()] * (len(pieces) + len(arrays)),
-        out_specs=(vmem_spec(),) * len(groups),
+        in_specs=[vmem_spec()] * (len(squares) + len(protos) + len(arrays)),
+        out_specs=(pl.BlockSpec(memory_space=pltpu.HBM),) * len(outs),
+        scratch_shapes=scratch + [pltpu.SemaphoreType.DMA((count,))],
         compiler_params=params(12),
-        name="finish_embeds",
-    )(*pieces, *arrays)
+        name="finish",
+    )(*squares, *protos, *arrays)
 
 
 def swap(own, axis, mask):
@@ -588,9 +623,9 @@
     near = tuple(range(batch_bits - 1))
     batch_orders = (near, tuple(reversed(near)))
     proto_orders = (tuple(range(proto_bits)), tuple(reversed(range(proto_bits))))
-    send, keep, *shares = gradients(
-        t, r, unit_bt, proto_b, row_parts, den_parts, batch_orders, proto_orders
-    )
+    send, g = send_gradients(t, r, unit_bt, row_parts, den_parts, batch_orders)
+    shares = embed_gradients(g, proto_b, proto_orders)
+    keep = keep_gradients(g, unit_bt, shares[0], batch_orders)
 
     proto_rows = proto_dev // batch_count
     clip_rows = clip_dev // proto_count
@@ -606,13 +641,11 @@
     for v in range(2):
         groups.append(("proto", proto_orders[v], shares[2 * v], shares[2 * v + 1]))
     terms = scatter_sums(groups)
-    grad_proto, grad_embed, square = project_shares(raws, terms)
-    packed, grad_embed = pack_shares(grad_proto, grad_embed, proto_parts(square))
-    proto_pieces = gather_batch(packed)
+    grad_proto, grad_embed = project_shares(raws, terms)
+    proto_pieces = gather_batch(grad_proto)
     view_pieces = gather_views(grad_embed, (proto_orders[1], proto_orders[0]))
-    proto_grad = finish_protos(proto_entries, proto_pieces)
-    slow_grad, fast_grad = finish_embeds(embed_entries, proto_pieces, view_pieces)
-    return proto_grad, slow_grad, fast_grad
+    squares = proto_parts(sum_squares(proto_pieces))
+    return finish((proto_entries, embed_entries), squares, proto_pieces, view_pieces)
 
 
 def solution(mesh):

time: 146 us -> 142 us (0.973)
  waiting for transfers between devices: 63.6 us -> 59.1 us
    ppermute x44, waiting for transfers between devices: 63.6 us -> 59.1 us  [swap(): lax.ppermute(own, axis, [(i, i ^ mask) for i in range(lax.axis_size(axis))])]
    pallas_call x5 -> x6, Pallas kernels: 15.4 us -> 14.6 us  [the longest x1 7.3 us: send_gradients(): pl.pallas_call(functools.partial(send_kernel, orders, len(row_parts)), ou...]
  transfers between devices with their start and end apart: 44 -> 44, of which waited for: 33 -> 29; matrix products, arithmetic and copies ran while one was open for 1% -> 1% of each run, Pallas kernels for 1% -> 3%
where the time goes in v7:
time: 142 us; the launch traced here: 141 us
  waiting for transfers between devices  59.1 us (42%)
  starting transfers between devices  44.6 us (31%)
  Pallas kernels  34.9 us (25%)
  local copies, waits for them, and re-layouts  1.99 us (1%)
    ppermute x44, waiting for transfers between devices, swap(): lax.ppermute(own, axis, [(i, i ^ mask) for i in range(lax.axis_size(axis))])  59.1 us
    ppermute x44, starting transfers between devices, swap(): lax.ppermute(own, axis, [(i, i ^ mask) for i in range(lax.axis_size(axis))])  44.6 us
    pallas_call x1, Pallas kernels, scores(): pl.pallas_call(score_kernel, out_shape=(pltpu.VMEM((2, clips, count), jnp...  8.59 us
    pallas_call x1, Pallas kernels, send_gradients(): pl.pallas_call(functools.partial(send_kernel, orders, len(row_parts)), ou...  7.3 us
    pallas_call x3, Pallas kernels, row_pass(): pl.pallas_call(functools.partial(row_kernel, protos_all, extra), out_shap...  6.82 us
    pallas_call x2, Pallas kernels, col_pass(): pl.pallas_call(functools.partial(col_kernel, clips_all), out_shape=jax.Sh...  4.65 us
  transfers between devices with their start and end apart: 44, of which 29 were waited for; matrix products, arithmetic and copies ran while one was open for 1% of the time, Pallas kernels for 3%

profile of v7, /device:TPU:0, one launch (start us, length us, event | category | flops | bytes accessed | tf_op | source)
XLA Modules:
  0.0 141.4 jit_solution(9590849939197406703)
XLA Ops:
  0.6 8.6 %scores.1 = (f32[2,1024,2048]{2,1,0:T(8,128)S(1)}, f32[32,128]{1,0:T(8,128)S(1)}, f32[16,128]{1,0:T(8,128)S(1)}, bf16[256,2048]{1,0:T(8,128)(2,1)S(1)}, bf16[2048,256]{1,0:T(8,128)(2,1)S(1)}) custom-call(bf16[1024,256]{1,0:T(8,128)(2,1)} %slow.1, bf16[1024,256]{1,0:T(8,128)(2,1)} %fast.1, f32[2048,256]{1,0:T(8,128)} %protos.1), custom_call_target="tpu_custom_call" | custom-call | tf_op jit(solution)/shard_map/scores/pallas_call | solution.py:115
  10.6 2.9 %collective-permute-start.1 = (f32[32,128]{1,0:T(8,128)S(1)}, f32[32,128]{1,0:T(8,128)S(1)}, u32[]{:S(2)}, u32[]{:S(2)}) collective-permute-start(f32[32,128]{1,0:T(8,128)S(1)} %add.18.refs_0_), channel_id=1, source_target_pairs={{0,8},{4,12},{8,0},{12,4},{16,24},{20,28},{24,16},{28,20},{1,9},{5... | collective-permute-start | bytes 49160 | tf_op jit(solution)/shard_map/ppermute | solution.py:530
  13.5 2.6 %collective-permute-start.2 = (f32[32,128]{1,0:T(8,128)S(1)}, f32[32,128]{1,0:T(8,128)S(1)}, u32[]{:S(2)}, u32[]{:S(2)}) collective-permute-start(f32[32,128]{1,0:T(8,128)S(1)} %add.18.refs_0_), channel_id=1, source_target_pairs={{0,16},{4,20},{8,24},{12,28},{16,0},{20,4},{24,8},{28,12},{1,17},{... | collective-permute-start | bytes 49160 | tf_op jit(solution)/shard_map/ppermute | solution.py:530
  16.1 2.0 %collective-permute-done.2.refs_2_ = f32[32,128]{1,0:T(8,128)S(1)} collective-permute-done((f32[32,128]{1,0:T(8,128)S(1)}, f32[32,128]{1,0:T(8,128)S(1)}, u32[]{:S(2)}, u32[]{:S(2)}) %collective-permute-start.2) | collective-permute-done | bytes 16416 | tf_op jit(solution)/shard_map/ppermute | solution.py:530
  18.1 3.5 %collective-permute-done.3.refs_3_ = f32[32,128]{1,0:T(8,128)S(1)} collective-permute-done((f32[32,128]{1,0:T(8,128)S(1)}, f32[32,128]{1,0:T(8,128)S(1)}, u32[]{:S(2)}, u32[]{:S(2)}) %collective-permute-start.3) | collective-permute-done | bytes 16416 | tf_op jit(solution)/shard_map/ppermute | solution.py:530
  21.6 2.4 %row_pass.3 = (f32[32,128]{1,0:T(8,128)S(1)}, f32[32,128]{1,0:T(8,128)}) custom-call(f32[2,1024,2048]{2,1,0:T(8,128)S(1)} %get-tuple-element.32.t_ref, f32[16,128]{1,0:T(8,128)S(1)} %get-tuple-element.33.den_ref, f32[32,128]{1,0:T(8,128)S(1)} %add.18.refs_0_, f32[32,128]{1,0:T(8,128)S(1)} %collective-permute-done.1.refs_1_, ...), custom_call_target="tpu_custom_call" | custom-call | tf_op jit(solution)/shard_map/row_pass/pallas_call | solution.py:164
  29.2 2.4 %collective-permute-done.6.refs_3_.refs_7_ = f32[32,128]{1,0:T(8,128)S(1)} collective-permute-done((f32[32,128]{1,0:T(8,128)S(1)}, f32[32,128]{1,0:T(8,128)S(1)}, u32[]{:S(2)}, u32[]{:S(2)}) %collective-permute-start.6) | collective-permute-done | bytes 16416 | tf_op jit(solution)/shard_map/ppermute | solution.py:530
  31.6 2.3 %col_pass.2 = f32[32,128]{1,0:T(8,128)S(1)} custom-call(f32[2,1024,2048]{2,1,0:T(8,128)S(1)} %get-tuple-element.32.t_ref, f32[32,128]{1,0:T(8,128)S(1)} %get-tuple-element.35.refs_0_.refs_4_, f32[32,128]{1,0:T(8,128)S(1)} %collective-permute-done.4.refs_1_.refs_5_, f32[32,128]{1,0:T(8,128)S(1)} %collective-permute-done.5.refs_2_.refs_6_, ...), custom_call_target="tpu_custom_call" | custom-call | tf_op jit(solution)/shard_map/col_pass/pallas_call | solution.py:204
  35.4 4.2 %collective-permute-start.9 = (f32[32,128]{1,0:T(8,128)S(1)}, f32[32,128]{1,0:T(8,128)S(1)}, u32[]{:S(2)}, u32[]{:S(2)}) collective-permute-start(f32[32,128]{1,0:T(8,128)S(1)} %add.19.refs_0_), channel_id=1, source_target_pairs={{0,16},{4,20},{8,24},{12,28},{16,0},{20,4},{24,8},{28,12},{1,17},{... | collective-permute-start | bytes 49160 | tf_op jit(solution)/shard_map/ppermute | solution.py:530
  41.3 2.4 %row_pass.4 = (f32[16,128]{1,0:T(8,128)S(1)}, f32[32,128]{1,0:T(8,128)}) custom-call(f32[2,1024,2048]{2,1,0:T(8,128)S(1)} %get-tuple-element.32.t_ref, f32[16,128]{1,0:T(8,128)S(1)} %get-tuple-element.33.den_ref, f32[32,128]{1,0:T(8,128)S(1)} %add.19.refs_0_, f32[32,128]{1,0:T(8,128)S(1)} %collective-permute-done.8.refs_1_, ...), custom_call_target="tpu_custom_call" | custom-call | tf_op jit(solution)/shard_map/row_pass/pallas_call | solution.py:164
  44.7 2.4 %collective-permute-start.13 = (f32[16,128]{1,0:T(8,128)S(1)}, f32[16,128]{1,0:T(8,128)S(1)}, u32[]{:S(2)}, u32[]{:S(2)}) collective-permute-start(f32[16,128]{1,0:T(8,128)S(1)} %get-tuple-element.36.refs_0_), channel_id=1, source_target_pairs={{0,3},{1,2},{2,1},{3,0},{4,7},{5,6},{6,5},{7,4},{8,11},{9,10},{10,... | collective-permute-start | bytes 24584 | tf_op jit(solution)/shard_map/ppermute | solution.py:530
  49.3 2.3 %col_pass.3 = f32[32,128]{1,0:T(8,128)S(1)} custom-call(f32[2,1024,2048]{2,1,0:T(8,128)S(1)} %get-tuple-element.32.t_ref, f32[16,128]{1,0:T(8,128)S(1)} %get-tuple-element.36.refs_0_, f32[16,128]{1,0:T(8,128)S(1)} %collective-permute-done.11.refs_1_, f32[16,128]{1,0:T(8,128)S(1)} %collective-permute-done.12.refs_2_, ...), custom_call_target="tpu_custom_call" | custom-call | tf_op jit(solution)/shard_map/col_pass/pallas_call | solution.py:204
  53.6 2.3 %collective-permute-start.16 = (f32[32,128]{1,0:T(8,128)S(1)}, f32[32,128]{1,0:T(8,128)S(1)}, u32[]{:S(2)}, u32[]{:S(2)}) collective-permute-start(f32[32,128]{1,0:T(8,128)S(1)} %add.20.refs_0_), channel_id=1, source_target_pairs={{0,16},{4,20},{8,24},{12,28},{16,0},{20,4},{24,8},{28,12},{1,17},{... | collective-permute-start | bytes 49160 | tf_op jit(solution)/shard_map/ppermute | solution.py:530
  58.3 3.1 %collective-permute-done.17.refs_3_ = f32[32,128]{1,0:T(8,128)S(1)} collective-permute-done((f32[32,128]{1,0:T(8,128)S(1)}, f32[32,128]{1,0:T(8,128)S(1)}, u32[]{:S(2)}, u32[]{:S(2)}) %collective-permute-start.17) | collective-permute-done | bytes 16416 | tf_op jit(solution)/shard_map/ppermute | solution.py:530
  61.4 2.1 %row_pass.5 = (f32[16,128]{1,0:T(8,128)S(1)}, f32[32,128]{1,0:T(8,128)S(1)}) custom-call(f32[2,1024,2048]{2,1,0:T(8,128)S(1)} %get-tuple-element.32.t_ref, f32[16,128]{1,0:T(8,128)S(1)} %get-tuple-element.33.den_ref, f32[32,128]{1,0:T(8,128)S(1)} %add.20.refs_0_, f32[32,128]{1,0:T(8,128)S(1)} %collective-permute-done.15.refs_1_, ...), custom_call_target="tpu_custom_call" | custom-call | tf_op jit(solution)/shard_map/row_pass/pallas_call | solution.py:164
  63.5 1.6 %collective-permute-start.18 = (f32[16,128]{1,0:T(8,128)S(1)}, f32[16,128]{1,0:T(8,128)S(1)}, u32[]{:S(2)}, u32[]{:S(2)}) collective-permute-start(f32[16,128]{1,0:T(8,128)S(1)} %get-tuple-element.39.refs_0_), channel_id=1, source_target_pairs={{0,1},{1,0},{2,3},{3,2},{4,5},{5,4},{6,7},{7,6},{8,9},{9,8},{10,11... | collective-permute-start | bytes 24584 | tf_op jit(solution)/shard_map/ppermute | solution.py:530
  68.7 2.4 %collective-permute-done.20.refs_3_ = f32[16,128]{1,0:T(8,128)S(1)} collective-permute-done((f32[16,128]{1,0:T(8,128)S(1)}, f32[16,128]{1,0:T(8,128)S(1)}, u32[]{:S(2)}, u32[]{:S(2)}) %collective-permute-start.20) | collective-permute-done | bytes 8224 | tf_op jit(solution)/shard_map/ppermute | solution.py:530
  71.1 7.3 %send_gradients.1 = (f32[2,4,128,256]{3,2,1,0:T(8,128)S(1)}, bf16[2048,2048]{1,0:T(8,128)(2,1)S(1)}) custom-call(f32[2,1024,2048]{2,1,0:T(8,128)S(1)} %get-tuple-element.32.t_ref, f32[32,128]{1,0:T(8,128)S(1)} %get-tuple-element.37.r_ref, bf16[256,2048]{1,0:T(8,128)(2,1)S(1)} %get-tuple-element.38.ubt_ref, f32[16,128]{1,0:T(8,128)S(1)} %get-tuple-element.39.refs_0_, ...), custom_call_target="tpu_custom_call" | custom-call | flops 1073741824 | bytes 20971520 | tf_op jit(solution)/shard_map/send_gradients/pallas_call | solution.py:291
  78.5 2.3 %embed_gradients.1 = (f32[2,256,256]{2,1,0:T(8,128)S(1)}, f32[2,256,256]{2,1,0:T(8,128)S(1)}, f32[2,256,256]{2,1,0:T(8,128)S(1)}, f32[2,256,256]{2,1,0:T(8,128)S(1)}) custom-call(bf16[2048,2048]{1,0:T(8,128)(2,1)S(1)} %get-tuple-element.40.g_ref, bf16[2048,256]{1,0:T(8,128)(2,1)S(1)} %get-tuple-element.41.cb_ref), custom_call_target="tpu_custom_call" | custom-call | flops 2147483648 | bytes 11534336 | tf_op jit(solution)/shard_map/embed_gradients/pallas_call | solution.py:331
  82.0 2.2 %keep_gradients.1.refs_0_ = f32[2,4,128,256]{3,2,1,0:T(8,128)S(1)} custom-call(bf16[2048,2048]{1,0:T(8,128)(2,1)S(1)} %get-tuple-element.40.g_ref, bf16[256,2048]{1,0:T(8,128)(2,1)S(1)} %get-tuple-element.38.ubt_ref, f32[2,256,256]{2,1,0:T(8,128)S(1)} %get-tuple-element.42.after_ref), custom_call_target="tpu_custom_call" | custom-call | flops 1073741824 | bytes 6291456 | tf_op jit(solution)/shard_map/keep_gradients/pallas_call | solution.py:360
  84.5 1.8 %collective-permute-start.23 = (f32[2,128,256]{2,1,0:T(8,128)S(1)}, f32[2,128,256]{2,1,0:T(8,128)S(1)}, u32[]{:S(2)}, u32[]{:S(2)}) collective-permute-start(f32[2,128,256]{2,1,0:T(8,128)S(1)} %get-tuple-element.47), channel_id=1, source_target_pairs={{0,16},{4,20},{8,24},{12,28},{16,0},{20,4},{24,8},{28,12},{1,17},{... | collective-permute-start | bytes 786440 | tf_op jit(solution)/shard_map/ppermute | solution.py:530
  86.3 8.9 %collective-permute-done.24.refs_5_ = f32[2,256,256]{2,1,0:T(8,128)S(1)} collective-permute-done((f32[2,256,256]{2,1,0:T(8,128)S(1)}, f32[2,256,256]{2,1,0:T(8,128)S(1)}, u32[]{:S(2)}, u32[]{:S(2)}) %collective-permute-start.24) | collective-permute-done | bytes 524320 | tf_op jit(solution)/shard_map/ppermute | solution.py:530
  96.8 2.3 %collective-permute-done.23.refs_3_ = f32[2,128,256]{2,1,0:T(8,128)S(1)} collective-permute-done((f32[2,128,256]{2,1,0:T(8,128)S(1)}, f32[2,128,256]{2,1,0:T(8,128)S(1)}, u32[]{:S(2)}, u32[]{:S(2)}) %collective-permute-start.23) | collective-permute-done | bytes 262176 | tf_op jit(solution)/shard_map/ppermute | solution.py:530
  99.3 1.6 %collective-permute-start.28 = (f32[1,256,256]{2,1,0:T(8,128)S(1)}, f32[1,256,256]{2,1,0:T(8,128)S(1)}, u32[]{:S(2)}, u32[]{:S(2)}) collective-permute-start(f32[1,256,256]{2,1,0:T(8,128)S(1)} %get-tuple-element.56), channel_id=1, source_target_pairs={{0,2},{1,3},{2,0},{3,1},{4,6},{5,7},{6,4},{7,5},{8,10},{9,11},{10,... | collective-permute-start | bytes 786440 | tf_op jit(solution)/shard_map/ppermute | solution.py:530
  102.6 1.7 %collective-permute-start.27 = (f32[1,128,256]{2,1,0:T(8,128)S(1)}, f32[1,128,256]{2,1,0:T(8,128)S(1)}, u32[]{:S(2)}, u32[]{:S(2)}) collective-permute-start(f32[1,128,256]{2,1,0:T(8,128)S(1)} %get-tuple-element.54), channel_id=1, source_target_pairs={{0,8},{4,12},{8,0},{12,4},{16,24},{20,28},{24,16},{28,20},{1,9},{5... | collective-permute-start | bytes 393224 | tf_op jit(solution)/shard_map/ppermute | solution.py:530
  106.3 2.8 %collective-permute-done.26.refs_1_ = f32[1,128,256]{2,1,0:T(8,128)S(1)} collective-permute-done((f32[1,128,256]{2,1,0:T(8,128)S(1)}, f32[1,128,256]{2,1,0:T(8,128)S(1)}, u32[]{:S(2)}, u32[]{:S(2)}) %collective-permute-start.26) | collective-permute-done | bytes 131104 | tf_op jit(solution)/shard_map/ppermute | solution.py:530
  113.3 9.3 %collective-permute-done.33.refs_4_.refs_8_ = f32[264,256]{1,0:T(8,128)S(1)} collective-permute-done((f32[264,256]{1,0:T(8,128)S(1)}, f32[264,256]{1,0:T(8,128)S(1)}, u32[]{:S(2)}, u32[]{:S(2)}) %collective-permute-start.33) | collective-permute-done | bytes 270368 | tf_op jit(solution)/shard_map/ppermute | solution.py:530
  124.3 1.9 %collective-permute-start.42 = (f32[256,256]{1,0:T(8,128)S(1)}, f32[256,256]{1,0:T(8,128)S(1)}, u32[]{:S(2)}, u32[]{:S(2)}) collective-permute-start(f32[256,256]{1,0:T(8,128)S(1)} %slice_bitcast_fusion.1), channel_id=1, source_target_pairs={{0,1},{1,0},{2,3},{3,2},{4,5},{5,4},{6,7},{7,6},{8,9},{9,8},{10,11... | collective-permute-start | bytes 786440 | tf_op jit(solution)/shard_map/ppermute | solution.py:530
  126.2 3.8 %collective-permute-done.35.refs_6_.refs_10_ = f32[264,256]{1,0:T(8,128)S(1)} collective-permute-done((f32[264,256]{1,0:T(8,128)S(1)}, f32[264,256]{1,0:T(8,128)S(1)}, u32[]{:S(2)}, u32[]{:S(2)}) %collective-permute-start.35) | collective-permute-done | bytes 270368 | tf_op jit(solution)/shard_map/ppermute | solution.py:530
  130.1 1.6 %collective-permute-start.43 = (f32[256,256]{1,0:T(8,128)S(1)}, f32[256,256]{1,0:T(8,128)S(1)}, u32[]{:S(2)}, u32[]{:S(2)}) collective-permute-start(f32[256,256]{1,0:T(8,128)S(1)} %slice_bitcast_fusion), channel_id=1, source_target_pairs={{0,2},{1,3},{2,0},{3,1},{4,6},{5,7},{6,4},{7,5},{8,10},{9,11},{10,... | collective-permute-start | bytes 786440 | tf_op jit(solution)/shard_map/ppermute | solution.py:530
  135.3 3.9 %collective-permute-done.43.refs_16_ = f32[256,256]{1,0:T(8,128)S(1)} collective-permute-done((f32[256,256]{1,0:T(8,128)S(1)}, f32[256,256]{1,0:T(8,128)S(1)}, u32[]{:S(2)}, u32[]{:S(2)}) %collective-permute-start.43) | collective-permute-done | bytes 262176 | tf_op jit(solution)/shard_map/ppermute | solution.py:530
  139.2 2.2 %finish.1 = (f32[2048,256]{1,0:T(8,128)}, f32[1024,256]{1,0:T(8,128)}, f32[1024,256]{1,0:T(8,128)}) custom-call(f32[2,8,128]{2,1,0:T(8,128)S(1)} %sum_squares.1.refs_0_, f32[2,8,128]{2,1,0:T(8,128)S(1)} %collective-permute-done.37.refs_1_, f32[2,8,128]{2,1,0:T(8,128)S(1)} %collective-permute-done.38.refs_2_, ...), custom_call_target="tpu_custom_call" | custom-call | tf_op jit(solution)/shard_map/finish/pallas_call | solution.py:518
  (77 shorter events, 37.6 us)
Async XLA Ops:
  10.6 5.5 %collective-permute-start.1 = (f32[32,128]{1,0:T(8,128)S(1)}, f32[32,128]{1,0:T(8,128)S(1)}, u32[]{:S(2)}, u32[]{:S(2)}) collective-permute-start(f32[32,128]{1,0:T(8,128)S(1)} %add.18.refs_0_), channel_id=1, source_target_pairs={{0,8},{4,12},{8,0},{12,4},{16,24},{20,28},{24,16},{28,20},{1,9},{5... | collective-permute-start | bytes 49160 | tf_op jit(solution)/shard_map/ppermute | solution.py:530
  13.5 4.6 %collective-permute-start.2 = (f32[32,128]{1,0:T(8,128)S(1)}, f32[32,128]{1,0:T(8,128)S(1)}, u32[]{:S(2)}, u32[]{:S(2)}) collective-permute-start(f32[32,128]{1,0:T(8,128)S(1)} %add.18.refs_0_), channel_id=1, source_target_pairs={{0,16},{4,20},{8,24},{12,28},{16,0},{20,4},{24,8},{28,12},{1,17},{... | collective-permute-start | bytes 49160 | tf_op jit(solution)/shard_map/ppermute | solution.py:530
  16.1 5.5 %collective-permute-start.3 = (f32[32,128]{1,0:T(8,128)S(1)}, f32[32,128]{1,0:T(8,128)S(1)}, u32[]{:S(2)}, u32[]{:S(2)}) collective-permute-start(f32[32,128]{1,0:T(8,128)S(1)} %add.18.refs_0_), channel_id=1, source_target_pairs={{0,24},{4,28},{8,16},{12,20},{16,8},{20,12},{24,0},{28,4},{1,25},{... | collective-permute-start | bytes 49160 | tf_op jit(solution)/shard_map/ppermute | solution.py:530
  27.0 4.6 %collective-permute-start.6 = (f32[32,128]{1,0:T(8,128)S(1)}, f32[32,128]{1,0:T(8,128)S(1)}, u32[]{:S(2)}, u32[]{:S(2)}) collective-permute-start(f32[32,128]{1,0:T(8,128)S(1)} %get-tuple-element.35.refs_0_.refs_4_), channel_id=1, source_target_pairs={{0,3},{1,2},{2,1},{3,0},{4,7},{5,6},{6,5},{7,4},{8,11},{9,10},{10,... | collective-permute-start | bytes 49160 | tf_op jit(solution)/shard_map/ppermute | solution.py:530
  35.2 5.5 %collective-permute-start.10 = (f32[32,128]{1,0:T(8,128)S(1)}, f32[32,128]{1,0:T(8,128)S(1)}, u32[]{:S(2)}, u32[]{:S(2)}) collective-permute-start(f32[32,128]{1,0:T(8,128)S(1)} %add.19.refs_0_), channel_id=1, source_target_pairs={{0,24},{4,28},{8,16},{12,20},{16,8},{20,12},{24,0},{28,4},{1,25},{... | collective-permute-start | bytes 49160 | tf_op jit(solution)/shard_map/ppermute | solution.py:530
  35.4 5.3 %collective-permute-start.8 = (f32[32,128]{1,0:T(8,128)S(1)}, f32[32,128]{1,0:T(8,128)S(1)}, u32[]{:S(2)}, u32[]{:S(2)}) collective-permute-start(f32[32,128]{1,0:T(8,128)S(1)} %add.19.refs_0_), channel_id=1, source_target_pairs={{0,8},{4,12},{8,0},{12,4},{16,24},{20,28},{24,16},{28,20},{1,9},{5... | collective-permute-start | bytes 49160 | tf_op jit(solution)/shard_map/ppermute | solution.py:530
  35.4 5.9 %collective-permute-start.9 = (f32[32,128]{1,0:T(8,128)S(1)}, f32[32,128]{1,0:T(8,128)S(1)}, u32[]{:S(2)}, u32[]{:S(2)}) collective-permute-start(f32[32,128]{1,0:T(8,128)S(1)} %add.19.refs_0_), channel_id=1, source_target_pairs={{0,16},{4,20},{8,24},{12,28},{16,0},{20,4},{24,8},{28,12},{1,17},{... | collective-permute-start | bytes 49160 | tf_op jit(solution)/shard_map/ppermute | solution.py:530
  44.7 4.5 %collective-permute-start.13 = (f32[16,128]{1,0:T(8,128)S(1)}, f32[16,128]{1,0:T(8,128)S(1)}, u32[]{:S(2)}, u32[]{:S(2)}) collective-permute-start(f32[16,128]{1,0:T(8,128)S(1)} %get-tuple-element.36.refs_0_), channel_id=1, source_target_pairs={{0,3},{1,2},{2,1},{3,0},{4,7},{5,6},{6,5},{7,4},{8,11},{9,10},{10,... | collective-permute-start | bytes 24584 | tf_op jit(solution)/shard_map/ppermute | solution.py:530
  53.6 4.6 %collective-permute-start.16 = (f32[32,128]{1,0:T(8,128)S(1)}, f32[32,128]{1,0:T(8,128)S(1)}, u32[]{:S(2)}, u32[]{:S(2)}) collective-permute-start(f32[32,128]{1,0:T(8,128)S(1)} %add.20.refs_0_), channel_id=1, source_target_pairs={{0,16},{4,20},{8,24},{12,28},{16,0},{20,4},{24,8},{28,12},{1,17},{... | collective-permute-start | bytes 49160 | tf_op jit(solution)/shard_map/ppermute | solution.py:530
  55.9 5.5 %collective-permute-start.17 = (f32[32,128]{1,0:T(8,128)S(1)}, f32[32,128]{1,0:T(8,128)S(1)}, u32[]{:S(2)}, u32[]{:S(2)}) collective-permute-start(f32[32,128]{1,0:T(8,128)S(1)} %add.20.refs_0_), channel_id=1, source_target_pairs={{0,24},{4,28},{8,16},{12,20},{16,8},{20,12},{24,0},{28,4},{1,25},{... | collective-permute-start | bytes 49160 | tf_op jit(solution)/shard_map/ppermute | solution.py:530
  78.4 5.7 %collective-permute-start.21 = (f32[2,4,128,256]{3,2,1,0:T(8,128)S(1)}, f32[2,4,128,256]{3,2,1,0:T(8,128)S(1)}, u32[]{:S(2)}, u32[]{:S(2)}) collective-permute-start(f32[2,4,128,256]{3,2,1,0:T(8,128)S(1)} %get-tuple-element.43), channel_id=1, source_target_pairs={{0,4},{4,0},{8,12},{12,8},{16,20},{20,16},{24,28},{28,24},{1,5},{5... | collective-permute-start | bytes 3145736 | tf_op jit(solution)/shard_map/ppermute | solution.py:530
  80.9 14.4 %collective-permute-start.24 = (f32[2,256,256]{2,1,0:T(8,128)S(1)}, f32[2,256,256]{2,1,0:T(8,128)S(1)}, u32[]{:S(2)}, u32[]{:S(2)}) collective-permute-start(f32[2,256,256]{2,1,0:T(8,128)S(1)} %get-tuple-element.42.after_ref), channel_id=1, source_target_pairs={{0,1},{1,0},{2,3},{3,2},{4,5},{5,4},{6,7},{7,6},{8,9},{9,8},{10,11... | collective-permute-start | bytes 1572872 | tf_op jit(solution)/shard_map/ppermute | solution.py:530
  81.4 14.0 %collective-permute-start.25 = (f32[2,256,256]{2,1,0:T(8,128)S(1)}, f32[2,256,256]{2,1,0:T(8,128)S(1)}, u32[]{:S(2)}, u32[]{:S(2)}) collective-permute-start(f32[2,256,256]{2,1,0:T(8,128)S(1)} %get-tuple-element.50), channel_id=1, source_target_pairs={{0,2},{1,3},{2,0},{3,1},{4,6},{5,7},{6,4},{7,5},{8,10},{9,11},{10,... | collective-permute-start | bytes 1572872 | tf_op jit(solution)/shard_map/ppermute | solution.py:530
  84.3 12.6 %collective-permute-start.22 = (f32[2,128,256]{2,1,0:T(8,128)S(1)}, f32[2,128,256]{2,1,0:T(8,128)S(1)}, u32[]{:S(2)}, u32[]{:S(2)}) collective-permute-start(f32[2,128,256]{2,1,0:T(8,128)S(1)} %get-tuple-element.45), channel_id=1, source_target_pairs={{0,8},{4,12},{8,0},{12,4},{16,24},{20,28},{24,16},{28,20},{1,9},{5... | collective-permute-start | bytes 786440 | tf_op jit(solution)/shard_map/ppermute | solution.py:530
  84.5 14.6 %collective-permute-start.23 = (f32[2,128,256]{2,1,0:T(8,128)S(1)}, f32[2,128,256]{2,1,0:T(8,128)S(1)}, u32[]{:S(2)}, u32[]{:S(2)}) collective-permute-start(f32[2,128,256]{2,1,0:T(8,128)S(1)} %get-tuple-element.47), channel_id=1, source_target_pairs={{0,16},{4,20},{8,24},{12,28},{16,0},{20,4},{24,8},{28,12},{1,17},{... | collective-permute-start | bytes 786440 | tf_op jit(solution)/shard_map/ppermute | solution.py:530
  99.3 10.0 %collective-permute-start.28 = (f32[1,256,256]{2,1,0:T(8,128)S(1)}, f32[1,256,256]{2,1,0:T(8,128)S(1)}, u32[]{:S(2)}, u32[]{:S(2)}) collective-permute-start(f32[1,256,256]{2,1,0:T(8,128)S(1)} %get-tuple-element.56), channel_id=1, source_target_pairs={{0,2},{1,3},{2,0},{3,1},{4,6},{5,7},{6,4},{7,5},{8,10},{9,11},{10,... | collective-permute-start | bytes 786440 | tf_op jit(solution)/shard_map/ppermute | solution.py:530
  100.9 8.4 %collective-permute-start.29 = (f32[1,256,256]{2,1,0:T(8,128)S(1)}, f32[1,256,256]{2,1,0:T(8,128)S(1)}, u32[]{:S(2)}, u32[]{:S(2)}) collective-permute-start(f32[1,256,256]{2,1,0:T(8,128)S(1)} %get-tuple-element.58), channel_id=1, source_target_pairs={{0,1},{1,0},{2,3},{3,2},{4,5},{5,4},{6,7},{7,6},{8,9},{9,8},{10,11... | collective-permute-start | bytes 786440 | tf_op jit(solution)/shard_map/ppermute | solution.py:530
  102.4 6.7 %collective-permute-start.26 = (f32[1,128,256]{2,1,0:T(8,128)S(1)}, f32[1,128,256]{2,1,0:T(8,128)S(1)}, u32[]{:S(2)}, u32[]{:S(2)}) collective-permute-start(f32[1,128,256]{2,1,0:T(8,128)S(1)} %get-tuple-element.52), channel_id=1, source_target_pairs={{0,16},{4,20},{8,24},{12,28},{16,0},{20,4},{24,8},{28,12},{1,17},{... | collective-permute-start | bytes 393224 | tf_op jit(solution)/shard_map/ppermute | solution.py:530
  102.6 6.7 %collective-permute-start.27 = (f32[1,128,256]{2,1,0:T(8,128)S(1)}, f32[1,128,256]{2,1,0:T(8,128)S(1)}, u32[]{:S(2)}, u32[]{:S(2)}) collective-permute-start(f32[1,128,256]{2,1,0:T(8,128)S(1)} %get-tuple-element.54), channel_id=1, source_target_pairs={{0,8},{4,12},{8,0},{12,4},{16,24},{20,28},{24,16},{28,20},{1,9},{5... | collective-permute-start | bytes 393224 | tf_op jit(solution)/shard_map/ppermute | solution.py:530
  109.9 13.9 %collective-permute-start.41 = (f32[2,256,256]{2,1,0:T(8,128)S(1)}, f32[2,256,256]{2,1,0:T(8,128)S(1)}, u32[]{:S(2)}, u32[]{:S(2)}) collective-permute-start(f32[2,256,256]{2,1,0:T(8,128)S(1)} %get-tuple-element.60.refs_12_), channel_id=1, source_target_pairs={{0,2},{1,3},{2,0},{3,1},{4,6},{5,7},{6,4},{7,5},{8,10},{9,11},{10,... | collective-permute-start | bytes 1572872 | tf_op jit(solution)/shard_map/ppermute | solution.py:530
  110.4 12.2 %collective-permute-start.33 = (f32[264,256]{1,0:T(8,128)S(1)}, f32[264,256]{1,0:T(8,128)S(1)}, u32[]{:S(2)}, u32[]{:S(2)}) collective-permute-start(f32[264,256]{1,0:T(8,128)S(1)} %get-tuple-element.59.refs_0_.refs_4_), channel_id=1, source_target_pairs={{0,16},{4,20},{8,24},{12,28},{16,0},{20,4},{24,8},{28,12},{1,17},{... | collective-permute-start | bytes 811016 | tf_op jit(solution)/shard_map/ppermute | solution.py:530
  111.4 13.0 %collective-permute-start.40 = (f32[2,256,256]{2,1,0:T(8,128)S(1)}, f32[2,256,256]{2,1,0:T(8,128)S(1)}, u32[]{:S(2)}, u32[]{:S(2)}) collective-permute-start(f32[2,256,256]{2,1,0:T(8,128)S(1)} %get-tuple-element.60.refs_12_), channel_id=1, source_target_pairs={{0,1},{1,0},{2,3},{3,2},{4,5},{5,4},{6,7},{7,6},{8,9},{9,8},{10,11... | collective-permute-start | bytes 1572872 | tf_op jit(solution)/shard_map/ppermute | solution.py:530
  111.9 11.9 %collective-permute-start.31 = (f32[264,256]{1,0:T(8,128)S(1)}, f32[264,256]{1,0:T(8,128)S(1)}, u32[]{:S(2)}, u32[]{:S(2)}) collective-permute-start(f32[264,256]{1,0:T(8,128)S(1)} %get-tuple-element.59.refs_0_.refs_4_), channel_id=1, source_target_pairs={{0,8},{4,12},{8,0},{12,4},{16,24},{20,28},{24,16},{28,20},{1,9},{5... | collective-permute-start | bytes 811016 | tf_op jit(solution)/shard_map/ppermute | solution.py:530
  122.6 7.5 %collective-permute-start.35 = (f32[264,256]{1,0:T(8,128)S(1)}, f32[264,256]{1,0:T(8,128)S(1)}, u32[]{:S(2)}, u32[]{:S(2)}) collective-permute-start(f32[264,256]{1,0:T(8,128)S(1)} %collective-permute-done.33.refs_4_.refs_8_), channel_id=1, source_target_pairs={{0,8},{4,12},{8,0},{12,4},{16,24},{20,28},{24,16},{28,20},{1,9},{5... | collective-permute-start | bytes 811016 | tf_op jit(solution)/shard_map/ppermute | solution.py:530
  122.6 7.5 %collective-permute-start.30 = (f32[264,256]{1,0:T(8,128)S(1)}, f32[264,256]{1,0:T(8,128)S(1)}, u32[]{:S(2)}, u32[]{:S(2)}) collective-permute-start(f32[264,256]{1,0:T(8,128)S(1)} %get-tuple-element.59.refs_0_.refs_4_), channel_id=1, source_target_pairs={{0,4},{4,0},{8,12},{12,8},{16,20},{20,16},{24,28},{28,24},{1,5},{5... | collective-permute-start | bytes 811016 | tf_op jit(solution)/shard_map/ppermute | solution.py:530
  123.8 7.9 %collective-permute-start.34 = (f32[264,256]{1,0:T(8,128)S(1)}, f32[264,256]{1,0:T(8,128)S(1)}, u32[]{:S(2)}, u32[]{:S(2)}) collective-permute-start(f32[264,256]{1,0:T(8,128)S(1)} %collective-permute-done.33.refs_4_.refs_8_), channel_id=1, source_target_pairs={{0,4},{4,0},{8,12},{12,8},{16,20},{20,16},{24,28},{28,24},{1,5},{5... | collective-permute-start | bytes 811016 | tf_op jit(solution)/shard_map/ppermute | solution.py:530
  123.8 7.9 %collective-permute-start.32 = (f32[264,256]{1,0:T(8,128)S(1)}, f32[264,256]{1,0:T(8,128)S(1)}, u32[]{:S(2)}, u32[]{:S(2)}) collective-permute-start(f32[264,256]{1,0:T(8,128)S(1)} %collective-permute-done.31.refs_2_.refs_6_), channel_id=1, source_target_pairs={{0,4},{4,0},{8,12},{12,8},{16,20},{20,16},{24,28},{28,24},{1,5},{5... | collective-permute-start | bytes 811016 | tf_op jit(solution)/shard_map/ppermute | solution.py:530
  124.3 10.9 %collective-permute-start.42 = (f32[256,256]{1,0:T(8,128)S(1)}, f32[256,256]{1,0:T(8,128)S(1)}, u32[]{:S(2)}, u32[]{:S(2)}) collective-permute-start(f32[256,256]{1,0:T(8,128)S(1)} %slice_bitcast_fusion.1), channel_id=1, source_target_pairs={{0,1},{1,0},{2,3},{3,2},{4,5},{5,4},{6,7},{7,6},{8,9},{9,8},{10,11... | collective-permute-start | bytes 786440 | tf_op jit(solution)/shard_map/ppermute | solution.py:530
  130.1 9.0 %collective-permute-start.43 = (f32[256,256]{1,0:T(8,128)S(1)}, f32[256,256]{1,0:T(8,128)S(1)}, u32[]{:S(2)}, u32[]{:S(2)}) collective-permute-start(f32[256,256]{1,0:T(8,128)S(1)} %slice_bitcast_fusion), channel_id=1, source_target_pairs={{0,2},{1,3},{2,0},{3,1},{4,6},{5,7},{6,4},{7,5},{8,10},{9,11},{10,... | collective-permute-start | bytes 786440 | tf_op jit(solution)/shard_map/ppermute | solution.py:530
  131.7 7.5 %collective-permute-start.37 = (f32[2,8,128]{2,1,0:T(8,128)S(1)}, f32[2,8,128]{2,1,0:T(8,128)S(1)}, u32[]{:S(2)}, u32[]{:S(2)}) collective-permute-start(f32[2,8,128]{2,1,0:T(8,128)S(1)} %sum_squares.1.refs_0_), channel_id=1, source_target_pairs={{0,1},{1,0},{2,3},{3,2},{4,5},{5,4},{6,7},{7,6},{8,9},{9,8},{10,11... | collective-permute-start | bytes 24584 | tf_op jit(solution)/shard_map/ppermute | solution.py:530
  132.8 6.5 %collective-permute-start.38 = (f32[2,8,128]{2,1,0:T(8,128)S(1)}, f32[2,8,128]{2,1,0:T(8,128)S(1)}, u32[]{:S(2)}, u32[]{:S(2)}) collective-permute-start(f32[2,8,128]{2,1,0:T(8,128)S(1)} %sum_squares.1.refs_0_), channel_id=1, source_target_pairs={{0,2},{1,3},{2,0},{3,1},{4,6},{5,7},{6,4},{7,5},{8,10},{9,11},{10,... | collective-permute-start | bytes 24584 | tf_op jit(solution)/shard_map/ppermute | solution.py:530
  134.2 5.1 %collective-permute-start.39 = (f32[2,8,128]{2,1,0:T(8,128)S(1)}, f32[2,8,128]{2,1,0:T(8,128)S(1)}, u32[]{:S(2)}, u32[]{:S(2)}) collective-permute-start(f32[2,8,128]{2,1,0:T(8,128)S(1)} %sum_squares.1.refs_0_), channel_id=1, source_target_pairs={{0,3},{1,2},{2,1},{3,0},{4,7},{5,6},{6,5},{7,4},{8,11},{9,10},{10,... | collective-permute-start | bytes 24584 | tf_op jit(solution)/shard_map/ppermute | solution.py:530
  (12 other events, 36.6 us)

commit v8 on v7

--- a/solution.py
+++ b/solution.py
@@ -231,10 +231,10 @@
 
 
 def proto_grads(ubt, chunk, orders, i, out_ref):
-    dc = jnp.dot(ubt, chunk, preferred_element_type=jnp.float32).T
-    half = dc.shape[0] // 2
+    dct = jnp.dot(ubt, chunk, preferred_element_type=jnp.float32)
+    half = dct.shape[0] // 2
     for h in range(2):
-        out_ref[h, place_of(i, orders[h])] = dc[h * half : (h + 1) * half]
+        out_ref[h, place_of(i, orders[h])] = dct[h * half : (h + 1) * half]
 
 
 def send_kernel(orders, parts, t_ref, r_ref, ubt_ref, *refs):
@@ -291,7 +291,7 @@
     return pl.pallas_call(
         functools.partial(send_kernel, orders, len(row_parts)),
         out_shape=(
-            jax.ShapeDtypeStruct((2, pieces, width // 2, feats), jnp.float32),
+            jax.ShapeDtypeStruct((2, pieces, feats // 2, width), jnp.float32),
             pltpu.VMEM((2 * clips, count), jnp.bfloat16),
         ),
         in_specs=[vmem_spec()] * (3 + 2 * len(row_parts)),
@@ -359,7 +359,7 @@
     pieces = 1 << len(orders[0])
     return pl.pallas_call(
         functools.partial(keep_kernel, orders),
-        out_shape=jax.ShapeDtypeStruct((2, pieces, count // (4 * pieces), feats), jnp.float32),
+        out_shape=jax.ShapeDtypeStruct((2, pieces, feats // 2, count // (2 * pieces)), jnp.float32),
         in_specs=[vmem_spec()] * 2 + [pl.BlockSpec(memory_space=pl.ANY)],
         out_specs=vmem_spec(),
         compiler_params=params(14),
@@ -398,11 +398,10 @@
     return [(outs[2 * n], outs[2 * n + 1]) for n in range(len(plan))]
 
 
-def project(raw, terms):
+def project(raw, grad):
     x = raw.astype(jnp.float32)
     length = jnp.sqrt(jnp.sum(x * x, axis=-1, keepdims=True) + 1e-12)
     unit = x / length
-    grad = terms[0][0] + terms[1][0]
     along = jnp.sum(unit * grad, axis=-1, keepdims=True)
     return (grad - unit * along) / length
 
@@ -413,15 +412,13 @@
 def share_kernel(proto_raw, slow_raw, fast_raw, *refs):
     terms, (proto_out, embed_out) = refs[:-2], refs[-2:]
     count = proto_raw.shape[0]
-    half = count // 2
     squares = [jnp.zeros((8, LANES), jnp.float32)] * 2
-    for h in range(2):
-        rows = slice(h * half, (h + 1) * half)
-        grad = project(proto_raw[rows, :], terms[2 * h : 2 * h + 2])
-        proto_out[rows, :] = grad
-        squares[0] = squares[0] + row_fold(lane_sum(grad * grad))
+    halves = [terms[2 * h][0] + terms[2 * h + 1][0] for h in range(2)]
+    grad = project(proto_raw[...], jnp.concatenate(halves, axis=0).T)
+    proto_out[:count, :] = grad
+    squares[0] = row_fold(lane_sum(grad * grad))
     for v, raw in enumerate((slow_raw, fast_raw)):
-        grad = project(raw[...], terms[4 + 2 * v : 6 + 2 * v])
+        grad = project(raw[...], terms[4 + 2 * v][0] + terms[5 + 2 * v][0])
         embed_out[v] = grad
         squares[1] = squares[1] + row_fold(lane_sum(grad * grad))
     for kind in range(2):
@@ -451,79 +448,84 @@
     return terms[0]
 
 
-def squares_kernel(*refs):
-    pieces, out_ref = refs[:-1], refs[-1]
-    total = tree_sum([piece[piece.shape[0] - EXTRA :, :] for piece in pieces])
-    for kind in range(2):
-        out_ref[kind] = total[:, kind * LANES : (kind + 1) * LANES]
-
-
-def sum_squares(pieces):
-    return pl.pallas_call(
-        squares_kernel,
-        out_shape=jax.ShapeDtypeStruct((2, 8, LANES), jnp.float32),
-        in_specs=[vmem_spec()] * len(pieces),
-        out_specs=vmem_spec(),
-        compiler_params=params(8),
-        name="sum_squares",
-    )(*pieces)
-
-
-def finish_kernel(entries, plan, counts, *refs):
-    squares, protos = refs[: counts[0]], refs[counts[0] : counts[0] + counts[1]]
-    ins, outs = refs[counts[0] + counts[1] : -7], refs[-7:-4]
-    proto_s, slow_s, fast_s, sems = refs[-4:]
-    total = tree_sum([square[...] for square in squares])
-    factors = [lax.rsqrt(total[k, 0:1, 0:1] / entries[k] + NORM_EPS) for k in range(2)]
-    size = protos[0].shape[0] - EXTRA
-    copies = []
-    for m, piece in enumerate(protos):
-        which = jnp.bitwise_xor(lax.axis_index("batch"), m)
-        rows = pl.ds(pl.multiple_of(which * size, size), size)
-        proto_s[m] = piece[:size, :] * factors[0]
-        copies.append(pltpu.make_async_copy(proto_s.at[m], outs[0].at[rows], sems.at[m]))
-        copies[-1].start()
-    for v, (places, scaled) in enumerate(zip(plan, (slow_s, fast_s))):
-        for m, (place, view) in enumerate(places):
-            src = ins[place][...] if view is None else ins[place][view]
-            size = src.shape[0]
-            which = jnp.bitwise_xor(lax.axis_index("proto"), m)
-            rows = pl.ds(pl.multiple_of(which * size, size), size)
-            scaled[m] = src * factors[1]
-            sem = sems.at[counts[1] + v * len(places) + m]
-            copies.append(pltpu.make_async_copy(scaled.at[m], outs[1 + v].at[rows], sem))
-            copies[-1].start()
-    for copy in copies:
-        copy.wait()
-
-
-def finish(entries, squares, protos, groups):
+def distinct(groups):
     arrays, plan = [], []
-    rows, feats = protos[0].shape
-    scratch = [pltpu.VMEM((len(protos), rows - EXTRA, feats), jnp.float32)]
-    outs = [jax.ShapeDtypeStruct((len(protos) * (rows - EXTRA), feats), jnp.float32)]
     for group in groups:
         places = []
-        for array, view in group:
+        for array, part in group:
             place = next((i for i, known in enumerate(arrays) if known is array), None)
             if place is None:
                 place = len(arrays)
                 arrays.append(array)
-            places.append((place, view))
+            places.append((place, part))
         plan.append(places)
-        rows, feats = group[0][0].shape[-2:]
-        scratch.append(pltpu.VMEM((len(group), rows, feats), jnp.float32))
-        outs.append(jax.ShapeDtypeStruct((len(group) * rows, feats), jnp.float32))
-    count = len(protos) + sum(len(places) for places in plan)
-    return pl.pallas_call(
-        functools.partial(finish_kernel, entries, plan, (len(squares), len(protos))),
-        out_shape=tuple(outs),
-        in_specs=[vmem_spec()] * (len(squares) + len(protos) + len(arrays)),
+    return arrays, plan
+
+
+def piece_ref(ins, place, part):
+    return ins[place] if part is None else ins[place].at[part]
+
+
+def squares_kernel(plan, rows, *refs):
+    ins, out_ref = refs[:-1], refs[-1]
+    total = tree_sum([piece_ref(ins, *piece)[rows:, :] for piece in plan])
+    for kind in range(2):
+        out_ref[kind] = total[:, kind * LANES : (kind + 1) * LANES]
+
+
+def sum_squares(pieces, rows):
+    arrays, plan = distinct([pieces])
+    return pl.pallas_call(
+        functools.partial(squares_kernel, plan[0], rows),
+        out_shape=jax.ShapeDtypeStruct((2, 8, LANES), jnp.float32),
+        in_specs=[vmem_spec()] * len(arrays),
+        out_specs=vmem_spec(),
+        compiler_params=params(8),
+        cost_estimate=pl.CostEstimate(flops=8, bytes_accessed=8, transcendentals=0),
+        name="sum_squares",
+    )(*arrays)
+
+
+def finish_kernel(entries, plan, count, *refs):
+    squares, ins, outs = refs[:count], refs[count:-7], refs[-7:-4]
+    scratch, sems = refs[-4:-1], refs[-1]
+    total = tree_sum([square[...] for square in squares])
+    factors = [lax.rsqrt(total[k, 0:1, 0:1] / entries[k] + NORM_EPS) for k in range(2)]
+    copies = []
+    for n, pieces in enumerate(plan):
+        axis, kind = ("batch", 0) if n == 0 else ("proto", 1)
+        size = scratch[n].shape[1]
+        for m, piece in enumerate(pieces):
+            which = jnp.bitwise_xor(lax.axis_index(axis), m)
+            rows = pl.ds(pl.multiple_of(which * size, size), size)
+            scratch[n][m] = piece_ref(ins, *piece)[:size, :] * factors[kind]
+            sem = sems.at[len(copies)]
+            copies.append(pltpu.make_async_copy(scratch[n].at[m], outs[n].at[rows], sem))
+            copies[-1].start()
+    for copy in copies:
+        copy.wait()
+
+
+def finish(entries, squares, groups, sizes):
+    arrays, plan = distinct(groups)
+    feats = arrays[0].shape[-1]
+    scratch = [
+        pltpu.VMEM((len(group), size, feats), jnp.float32) for group, size in zip(groups, sizes)
+    ]
+    outs = tuple(
+        jax.ShapeDtypeStruct((len(group) * size, feats), jnp.float32)
+        for group, size in zip(groups, sizes)
+    )
+    count = sum(len(group) for group in groups)
+    return pl.pallas_call(
+        functools.partial(finish_kernel, entries, plan, len(squares)),
+        out_shape=outs,
+        in_specs=[vmem_spec()] * (len(squares) + len(arrays)),
         out_specs=(pl.BlockSpec(memory_space=pltpu.HBM),) * len(outs),
         scratch_shapes=scratch + [pltpu.SemaphoreType.DMA((count,))],
         compiler_params=params(12),
         name="finish",
-    )(*squares, *protos, *arrays)
+    )(*squares, *arrays)
 
 
 def swap(own, axis, mask):
@@ -538,13 +540,18 @@
     return bits
 
 
+def far_first(own, axis, step, count):
+    parts = {m: swap(own, axis, m * step) for m in reversed(range(1, count))}
+    return [parts[m] for m in range(1, count)]
+
+
 def proto_parts(own):
-    return [own] + [swap(own, "proto", m) for m in range(1, lax.axis_size("proto"))]
+    return [own] + far_first(own, "proto", 1, lax.axis_size("proto"))
 
 
 def batch_parts(own):
     pair = own + swap(own, "batch", 1)
-    return [pair] + [swap(pair, "batch", 2 * m) for m in range(1, lax.axis_size("batch") // 2)]
+    return [pair] + far_first(pair, "batch", 2, lax.axis_size("batch") // 2)
 
 
 def scatter_sums(groups):
@@ -572,6 +579,54 @@
     return [x for term in terms for x in term]
 
 
+def forward_kernel(near_ref, far_ref, x_ref, y_ref, pack_ref, slow_ref, fast_ref):
+    pack_ref[0] = near_ref[...]
+    pack_ref[1] = far_ref[...]
+    slow_ref[...] = y_ref[0]
+    fast_ref[...] = x_ref[1]
+
+
+def forwards(near, far, x, y):
+    view = jax.ShapeDtypeStruct(x.shape[1:], x.dtype)
+    return pl.pallas_call(
+        forward_kernel,
+        out_shape=(jax.ShapeDtypeStruct((2,) + near.shape, near.dtype), view, view),
+        in_specs=[vmem_spec()] * 4,
+        out_specs=(vmem_spec(),) * 3,
+        compiler_params=params(10),
+        name="forwards",
+    )(near, far, x, y)
+
+
+def copy_kernel(x_ref, *refs):
+    refs[-1][...] = x_ref[...]
+
+
+def copy_after(x, arrived):
+    return pl.pallas_call(
+        copy_kernel,
+        out_shape=jax.ShapeDtypeStruct(x.shape, x.dtype),
+        in_specs=[vmem_spec()] + [pl.BlockSpec(memory_space=pl.ANY)] * len(arrived),
+        out_specs=vmem_spec(),
+        compiler_params=params(8),
+        name="copy_after",
+    )(x, *arrived)
+
+
+def gather_pairs(proto, embed):
+    y, x = swap(embed, "proto", 2), swap(embed, "proto", 1)
+    far, near = swap(proto, "batch", 4), swap(proto, "batch", 2)
+    core = swap(proto, "batch", 1)
+    pack, slow, fast = forwards(near, far, x, y)
+    slow, fast = swap(slow, "proto", 1), swap(fast, "proto", 2)
+    corner = swap(far, "batch", 2)
+    core_pack = swap(pack, "batch", 1)
+    core_corner = swap(copy_after(corner, [slow, fast]), "batch", 1)
+    whole = [proto, core, near, (core_pack, 0), far, (core_pack, 1), corner, core_corner]
+    protos = [piece if isinstance(piece, tuple) else (piece, None) for piece in whole]
+    return protos, [[(embed, v), (x, v), (y, v), (last, None)] for v, last in enumerate((slow, fast))]
+
+
 def gather_batch(own):
     bits = list(reversed(range(lax.axis_size("batch").bit_length() - 1)))
     pieces = {0: own}
@@ -579,7 +634,7 @@
     for bit in bits:
         for m in list(pieces):
             pieces[m | 1 << bit] = first[bit] if m == 0 else swap(pieces[m], "batch", 1 << bit)
-    return [pieces[m] for m in range(len(pieces))]
+    return [(pieces[m], None) for m in range(len(pieces))]
 
 
 def gather_views(own, orders):
@@ -642,10 +697,15 @@
         groups.append(("proto", proto_orders[v], shares[2 * v], shares[2 * v + 1]))
     terms = scatter_sums(groups)
     grad_proto, grad_embed = project_shares(raws, terms)
-    proto_pieces = gather_batch(grad_proto)
-    view_pieces = gather_views(grad_embed, (proto_orders[1], proto_orders[0]))
-    squares = proto_parts(sum_squares(proto_pieces))
-    return finish((proto_entries, embed_entries), squares, proto_pieces, view_pieces)
+    if batch_bits == 3 and proto_bits == 2:
+        proto_pieces, view_pieces = gather_pairs(grad_proto, grad_embed)
+    else:
+        proto_pieces = gather_batch(grad_proto)
+        view_pieces = gather_views(grad_embed, (proto_orders[1], proto_orders[0]))
+    squares = proto_parts(sum_squares(proto_pieces, proto_rows))
+    sizes = (proto_rows, clip_rows, clip_rows)
+    groups = [proto_pieces] + view_pieces
+    return finish((proto_entries, embed_entries), squares, groups, sizes)
 
 
 def solution(mesh):

time: 142 us -> 144 us (1.014)
  waiting for transfers between devices: 59.1 us -> 62.8 us
    ppermute x44 -> x43, waiting for transfers between devices: 59.1 us -> 62.8 us  [swap(): lax.ppermute(own, axis, [(i, i ^ mask) for i in range(lax.axis_size(axis))])]
    ppermute x44 -> x43, starting transfers between devices: 44.6 us -> 43.8 us  [swap(): lax.ppermute(own, axis, [(i, i ^ mask) for i in range(lax.axis_size(axis))])]
  transfers between devices with their start and end apart: 44 -> 43, of which waited for: 29 -> 33; matrix products, arithmetic and copies ran while one was open for 1% -> 1% of each run, Pallas kernels for 3% -> 3%
where the time goes in v8:
time: 144 us
  waiting for transfers between devices  62.8 us (44%)
  starting transfers between devices  43.8 us (30%)
  Pallas kernels  34.5 us (24%)
  local copies, waits for them, and re-layouts  1.96 us (1%)
    ppermute x43, waiting for transfers between devices, swap(): lax.ppermute(own, axis, [(i, i ^ mask) for i in range(lax.axis_size(axis))])  62.8 us
    ppermute x43, starting transfers between devices, swap(): lax.ppermute(own, axis, [(i, i ^ mask) for i in range(lax.axis_size(axis))])  43.8 us
    pallas_call x1, Pallas kernels, scores(): pl.pallas_call(score_kernel, out_shape=(pltpu.VMEM((2, clips, count), jnp...  8.59 us
    pallas_call x1, Pallas kernels, send_gradients(): pl.pallas_call(functools.partial(send_kernel, orders, len(row_parts)), ou...  7.04 us
    pallas_call x3, Pallas kernels, row_pass(): pl.pallas_call(functools.partial(row_kernel, protos_all, extra), out_shap...  6.82 us
    pallas_call x2, Pallas kernels, col_pass(): pl.pallas_call(functools.partial(col_kernel, clips_all), out_shape=jax.Sh...  4.65 us
  transfers between devices with their start and end apart: 43, of which 33 were waited for; matrix products, arithmetic and copies ran while one was open for 1% of the time, Pallas kernels for 3%

profile of v8, /device:TPU:0, one launch (start us, length us, event | category | flops | bytes accessed | tf_op | source)
XLA Modules:
  0.0 143.9 jit_solution(7923993891055652935)
XLA Ops:
  0.6 8.6 %scores.1 = (f32[2,1024,2048]{2,1,0:T(8,128)S(1)}, f32[32,128]{1,0:T(8,128)S(1)}, f32[16,128]{1,0:T(8,128)S(1)}, bf16[256,2048]{1,0:T(8,128)(2,1)S(1)}, bf16[2048,256]{1,0:T(8,128)(2,1)S(1)}) custom-call(bf16[1024,256]{1,0:T(8,128)(2,1)} %slow.1, bf16[1024,256]{1,0:T(8,128)(2,1)} %fast.1, f32[2048,256]{1,0:T(8,128)} %protos.1), custom_call_target="tpu_custom_call" | custom-call | tf_op jit(solution)/shard_map/scores/pallas_call | solution.py:115
  10.6 2.9 %collective-permute-start.1 = (f32[32,128]{1,0:T(8,128)S(1)}, f32[32,128]{1,0:T(8,128)S(1)}, u32[]{:S(2)}, u32[]{:S(2)}) collective-permute-start(f32[32,128]{1,0:T(8,128)S(1)} %add.18.refs_0_), channel_id=1, source_target_pairs={{0,8},{4,12},{8,0},{12,4},{16,24},{20,28},{24,16},{28,20},{1,9},{5... | collective-permute-start | bytes 49160 | tf_op jit(solution)/shard_map/ppermute | solution.py:532
  13.5 2.6 %collective-permute-start.2 = (f32[32,128]{1,0:T(8,128)S(1)}, f32[32,128]{1,0:T(8,128)S(1)}, u32[]{:S(2)}, u32[]{:S(2)}) collective-permute-start(f32[32,128]{1,0:T(8,128)S(1)} %add.18.refs_0_), channel_id=1, source_target_pairs={{0,16},{4,20},{8,24},{12,28},{16,0},{20,4},{24,8},{28,12},{1,17},{... | collective-permute-start | bytes 49160 | tf_op jit(solution)/shard_map/ppermute | solution.py:532
  16.1 2.0 %collective-permute-done.2.refs_2_ = f32[32,128]{1,0:T(8,128)S(1)} collective-permute-done((f32[32,128]{1,0:T(8,128)S(1)}, f32[32,128]{1,0:T(8,128)S(1)}, u32[]{:S(2)}, u32[]{:S(2)}) %collective-permute-start.2) | collective-permute-done | bytes 16416 | tf_op jit(solution)/shard_map/ppermute | solution.py:532
  18.1 3.5 %collective-permute-done.3.refs_3_ = f32[32,128]{1,0:T(8,128)S(1)} collective-permute-done((f32[32,128]{1,0:T(8,128)S(1)}, f32[32,128]{1,0:T(8,128)S(1)}, u32[]{:S(2)}, u32[]{:S(2)}) %collective-permute-start.3) | collective-permute-done | bytes 16416 | tf_op jit(solution)/shard_map/ppermute | solution.py:532
  21.6 2.4 %row_pass.3 = (f32[32,128]{1,0:T(8,128)S(1)}, f32[32,128]{1,0:T(8,128)}) custom-call(f32[2,1024,2048]{2,1,0:T(8,128)S(1)} %get-tuple-element.35.t_ref, f32[16,128]{1,0:T(8,128)S(1)} %get-tuple-element.36.den_ref, f32[32,128]{1,0:T(8,128)S(1)} %add.18.refs_0_, f32[32,128]{1,0:T(8,128)S(1)} %collective-permute-done.1.refs_1_, ...), custom_call_target="tpu_custom_call" | custom-call | tf_op jit(solution)/shard_map/row_pass/pallas_call | solution.py:164
  29.2 2.4 %collective-permute-done.6.refs_3_.refs_7_ = f32[32,128]{1,0:T(8,128)S(1)} collective-permute-done((f32[32,128]{1,0:T(8,128)S(1)}, f32[32,128]{1,0:T(8,128)S(1)}, u32[]{:S(2)}, u32[]{:S(2)}) %collective-permute-start.6) | collective-permute-done | bytes 16416 | tf_op jit(solution)/shard_map/ppermute | solution.py:532
  31.6 2.3 %col_pass.2 = f32[32,128]{1,0:T(8,128)S(1)} custom-call(f32[2,1024,2048]{2,1,0:T(8,128)S(1)} %get-tuple-element.35.t_ref, f32[32,128]{1,0:T(8,128)S(1)} %get-tuple-element.38.refs_0_.refs_4_, f32[32,128]{1,0:T(8,128)S(1)} %collective-permute-done.4.refs_1_.refs_5_, f32[32,128]{1,0:T(8,128)S(1)} %collective-permute-done.5.refs_2_.refs_6_, ...), custom_call_target="tpu_custom_call" | custom-call | tf_op jit(solution)/shard_map/col_pass/pallas_call | solution.py:204
  35.4 4.2 %collective-permute-start.9 = (f32[32,128]{1,0:T(8,128)S(1)}, f32[32,128]{1,0:T(8,128)S(1)}, u32[]{:S(2)}, u32[]{:S(2)}) collective-permute-start(f32[32,128]{1,0:T(8,128)S(1)} %add.19.refs_0_), channel_id=1, source_target_pairs={{0,16},{4,20},{8,24},{12,28},{16,0},{20,4},{24,8},{28,12},{1,17},{... | collective-permute-start | bytes 49160 | tf_op jit(solution)/shard_map/ppermute | solution.py:532
  41.3 2.4 %row_pass.4 = (f32[16,128]{1,0:T(8,128)S(1)}, f32[32,128]{1,0:T(8,128)}) custom-call(f32[2,1024,2048]{2,1,0:T(8,128)S(1)} %get-tuple-element.35.t_ref, f32[16,128]{1,0:T(8,128)S(1)} %get-tuple-element.36.den_ref, f32[32,128]{1,0:T(8,128)S(1)} %add.19.refs_0_, f32[32,128]{1,0:T(8,128)S(1)} %collective-permute-done.8.refs_1_, ...), custom_call_target="tpu_custom_call" | custom-call | tf_op jit(solution)/shard_map/row_pass/pallas_call | solution.py:164
  44.7 2.4 %collective-permute-start.13 = (f32[16,128]{1,0:T(8,128)S(1)}, f32[16,128]{1,0:T(8,128)S(1)}, u32[]{:S(2)}, u32[]{:S(2)}) collective-permute-start(f32[16,128]{1,0:T(8,128)S(1)} %get-tuple-element.39.refs_0_), channel_id=1, source_target_pairs={{0,3},{1,2},{2,1},{3,0},{4,7},{5,6},{6,5},{7,4},{8,11},{9,10},{10,... | collective-permute-start | bytes 24584 | tf_op jit(solution)/shard_map/ppermute | solution.py:532
  49.3 2.3 %col_pass.3 = f32[32,128]{1,0:T(8,128)S(1)} custom-call(f32[2,1024,2048]{2,1,0:T(8,128)S(1)} %get-tuple-element.35.t_ref, f32[16,128]{1,0:T(8,128)S(1)} %get-tuple-element.39.refs_0_, f32[16,128]{1,0:T(8,128)S(1)} %collective-permute-done.11.refs_1_, f32[16,128]{1,0:T(8,128)S(1)} %collective-permute-done.12.refs_2_, ...), custom_call_target="tpu_custom_call" | custom-call | tf_op jit(solution)/shard_map/col_pass/pallas_call | solution.py:204
  53.6 2.3 %collective-permute-start.16 = (f32[32,128]{1,0:T(8,128)S(1)}, f32[32,128]{1,0:T(8,128)S(1)}, u32[]{:S(2)}, u32[]{:S(2)}) collective-permute-start(f32[32,128]{1,0:T(8,128)S(1)} %add.20.refs_0_), channel_id=1, source_target_pairs={{0,16},{4,20},{8,24},{12,28},{16,0},{20,4},{24,8},{28,12},{1,17},{... | collective-permute-start | bytes 49160 | tf_op jit(solution)/shard_map/ppermute | solution.py:532
  58.3 3.1 %collective-permute-done.17.refs_3_ = f32[32,128]{1,0:T(8,128)S(1)} collective-permute-done((f32[32,128]{1,0:T(8,128)S(1)}, f32[32,128]{1,0:T(8,128)S(1)}, u32[]{:S(2)}, u32[]{:S(2)}) %collective-permute-start.17) | collective-permute-done | bytes 16416 | tf_op jit(solution)/shard_map/ppermute | solution.py:532
  61.4 2.1 %row_pass.5 = (f32[16,128]{1,0:T(8,128)S(1)}, f32[32,128]{1,0:T(8,128)S(1)}) custom-call(f32[2,1024,2048]{2,1,0:T(8,128)S(1)} %get-tuple-element.35.t_ref, f32[16,128]{1,0:T(8,128)S(1)} %get-tuple-element.36.den_ref, f32[32,128]{1,0:T(8,128)S(1)} %add.20.refs_0_, f32[32,128]{1,0:T(8,128)S(1)} %collective-permute-done.15.refs_1_, ...), custom_call_target="tpu_custom_call" | custom-call | tf_op jit(solution)/shard_map/row_pass/pallas_call | solution.py:164
  63.5 1.6 %collective-permute-start.18 = (f32[16,128]{1,0:T(8,128)S(1)}, f32[16,128]{1,0:T(8,128)S(1)}, u32[]{:S(2)}, u32[]{:S(2)}) collective-permute-start(f32[16,128]{1,0:T(8,128)S(1)} %get-tuple-element.42.refs_0_), channel_id=1, source_target_pairs={{0,1},{1,0},{2,3},{3,2},{4,5},{5,4},{6,7},{7,6},{8,9},{9,8},{10,11... | collective-permute-start | bytes 24584 | tf_op jit(solution)/shard_map/ppermute | solution.py:532
  68.7 2.4 %collective-permute-done.20.refs_3_ = f32[16,128]{1,0:T(8,128)S(1)} collective-permute-done((f32[16,128]{1,0:T(8,128)S(1)}, f32[16,128]{1,0:T(8,128)S(1)}, u32[]{:S(2)}, u32[]{:S(2)}) %collective-permute-start.20) | collective-permute-done | bytes 8224 | tf_op jit(solution)/shard_map/ppermute | solution.py:532
  71.1 7.0 %send_gradients.1 = (f32[2,4,128,256]{3,2,1,0:T(8,128)S(1)}, bf16[2048,2048]{1,0:T(8,128)(2,1)S(1)}) custom-call(f32[2,1024,2048]{2,1,0:T(8,128)S(1)} %get-tuple-element.35.t_ref, f32[32,128]{1,0:T(8,128)S(1)} %get-tuple-element.40.r_ref, bf16[256,2048]{1,0:T(8,128)(2,1)S(1)} %get-tuple-element.41.ubt_ref, f32[16,128]{1,0:T(8,128)S(1)} %get-tuple-element.42.refs_0_, ...), custom_call_target="tpu_custom_call" | custom-call | flops 1073741824 | bytes 20971520 | tf_op jit(solution)/shard_map/send_gradients/pallas_call | solution.py:291
  78.3 2.3 %embed_gradients.1 = (f32[2,256,256]{2,1,0:T(8,128)S(1)}, f32[2,256,256]{2,1,0:T(8,128)S(1)}, f32[2,256,256]{2,1,0:T(8,128)S(1)}, f32[2,256,256]{2,1,0:T(8,128)S(1)}) custom-call(bf16[2048,2048]{1,0:T(8,128)(2,1)S(1)} %get-tuple-element.43.g_ref, bf16[2048,256]{1,0:T(8,128)(2,1)S(1)} %get-tuple-element.44.cb_ref), custom_call_target="tpu_custom_call" | custom-call | flops 2147483648 | bytes 11534336 | tf_op jit(solution)/shard_map/embed_gradients/pallas_call | solution.py:331
  81.7 1.9 %keep_gradients.1.refs_0_ = f32[2,4,128,256]{3,2,1,0:T(8,128)S(1)} custom-call(bf16[2048,2048]{1,0:T(8,128)(2,1)S(1)} %get-tuple-element.43.g_ref, bf16[256,2048]{1,0:T(8,128)(2,1)S(1)} %get-tuple-element.41.ubt_ref, f32[2,256,256]{2,1,0:T(8,128)S(1)} %get-tuple-element.45.after_ref), custom_call_target="tpu_custom_call" | custom-call | flops 1073741824 | bytes 6291456 | tf_op jit(solution)/shard_map/keep_gradients/pallas_call | solution.py:360
  84.0 1.8 %collective-permute-start.23 = (f32[2,128,256]{2,1,0:T(8,128)S(1)}, f32[2,128,256]{2,1,0:T(8,128)S(1)}, u32[]{:S(2)}, u32[]{:S(2)}) collective-permute-start(f32[2,128,256]{2,1,0:T(8,128)S(1)} %get-tuple-element.50), channel_id=1, source_target_pairs={{0,16},{4,20},{8,24},{12,28},{16,0},{20,4},{24,8},{28,12},{1,17},{... | collective-permute-start | bytes 786440 | tf_op jit(solution)/shard_map/ppermute | solution.py:532
  85.8 9.2 %collective-permute-done.24.refs_5_ = f32[2,256,256]{2,1,0:T(8,128)S(1)} collective-permute-done((f32[2,256,256]{2,1,0:T(8,128)S(1)}, f32[2,256,256]{2,1,0:T(8,128)S(1)}, u32[]{:S(2)}, u32[]{:S(2)}) %collective-permute-start.24) | collective-permute-done | bytes 524320 | tf_op jit(solution)/shard_map/ppermute | solution.py:532
  96.3 2.3 %collective-permute-done.23.refs_3_ = f32[2,128,256]{2,1,0:T(8,128)S(1)} collective-permute-done((f32[2,128,256]{2,1,0:T(8,128)S(1)}, f32[2,128,256]{2,1,0:T(8,128)S(1)}, u32[]{:S(2)}, u32[]{:S(2)}) %collective-permute-start.23) | collective-permute-done | bytes 262176 | tf_op jit(solution)/shard_map/ppermute | solution.py:532
  98.8 1.6 %collective-permute-start.28 = (f32[1,256,256]{2,1,0:T(8,128)S(1)}, f32[1,256,256]{2,1,0:T(8,128)S(1)}, u32[]{:S(2)}, u32[]{:S(2)}) collective-permute-start(f32[1,256,256]{2,1,0:T(8,128)S(1)} %get-tuple-element.59), channel_id=1, source_target_pairs={{0,2},{1,3},{2,0},{3,1},{4,6},{5,7},{6,4},{7,5},{8,10},{9,11},{10,... | collective-permute-start | bytes 786440 | tf_op jit(solution)/shard_map/ppermute | solution.py:532
  102.1 1.7 %collective-permute-start.27 = (f32[1,128,256]{2,1,0:T(8,128)S(1)}, f32[1,128,256]{2,1,0:T(8,128)S(1)}, u32[]{:S(2)}, u32[]{:S(2)}) collective-permute-start(f32[1,128,256]{2,1,0:T(8,128)S(1)} %get-tuple-element.57), channel_id=1, source_target_pairs={{0,8},{4,12},{8,0},{12,4},{16,24},{20,28},{24,16},{28,20},{1,9},{5... | collective-permute-start | bytes 393224 | tf_op jit(solution)/shard_map/ppermute | solution.py:532
  105.8 2.8 %collective-permute-done.26.refs_1_ = f32[1,128,256]{2,1,0:T(8,128)S(1)} collective-permute-done((f32[1,128,256]{2,1,0:T(8,128)S(1)}, f32[1,128,256]{2,1,0:T(8,128)S(1)}, u32[]{:S(2)}, u32[]{:S(2)}) %collective-permute-start.26) | collective-permute-done | bytes 131104 | tf_op jit(solution)/shard_map/ppermute | solution.py:532
  112.8 9.6 %collective-permute-done.32.far_ref.refs_4_.refs_8_ = f32[264,256]{1,0:T(8,128)S(1)} collective-permute-done((f32[264,256]{1,0:T(8,128)S(1)}, f32[264,256]{1,0:T(8,128)S(1)}, u32[]{:S(2)}, u32[]{:S(2)}) %collective-permute-start.32) | collective-permute-done | bytes 270368 | tf_op jit(solution)/shard_map/ppermute | solution.py:532
  125.0 1.6 %collective-permute-start.38 = (f32[256,256]{1,0:T(8,128)S(1)}, f32[256,256]{1,0:T(8,128)S(1)}, u32[]{:S(2)}, u32[]{:S(2)}) collective-permute-start(f32[256,256]{1,0:T(8,128)S(1)} %get-tuple-element.66), channel_id=1, source_target_pairs={{0,2},{1,3},{2,0},{3,1},{4,6},{5,7},{6,4},{7,5},{8,10},{9,11},{10,... | collective-permute-start | bytes 786440 | tf_op jit(solution)/shard_map/ppermute | solution.py:532
  126.6 3.1 %collective-permute-done.36.x_ref.refs_5_.refs_9_ = f32[264,256]{1,0:T(8,128)S(1)} collective-permute-done((f32[264,256]{1,0:T(8,128)S(1)}, f32[264,256]{1,0:T(8,128)S(1)}, u32[]{:S(2)}, u32[]{:S(2)}) %collective-permute-start.36) | collective-permute-done | bytes 270368 | tf_op jit(solution)/shard_map/ppermute | solution.py:532
  129.7 2.6 %collective-permute-done.37.refs_0_.refs_14_ = f32[256,256]{1,0:T(8,128)S(1)} collective-permute-done((f32[256,256]{1,0:T(8,128)S(1)}, f32[256,256]{1,0:T(8,128)S(1)}, u32[]{:S(2)}, u32[]{:S(2)}) %collective-permute-start.37) | collective-permute-done | bytes 262176 | tf_op jit(solution)/shard_map/ppermute | solution.py:532
  139.3 2.4 %collective-permute-done.42.refs_3_ = f32[2,8,128]{2,1,0:T(8,128)S(1)} collective-permute-done((f32[2,8,128]{2,1,0:T(8,128)S(1)}, f32[2,8,128]{2,1,0:T(8,128)S(1)}, u32[]{:S(2)}, u32[]{:S(2)}) %collective-permute-start.42) | collective-permute-done | bytes 8224 | tf_op jit(solution)/shard_map/ppermute | solution.py:532
  141.7 2.2 %finish.1 = (f32[2048,256]{1,0:T(8,128)}, f32[1024,256]{1,0:T(8,128)}, f32[1024,256]{1,0:T(8,128)}) custom-call(f32[2,8,128]{2,1,0:T(8,128)S(1)} %sum_squares.1.refs_0_, f32[2,8,128]{2,1,0:T(8,128)S(1)} %collective-permute-done.40.refs_1_, f32[2,8,128]{2,1,0:T(8,128)S(1)} %collective-permute-done.41.refs_2_, ...), custom_call_target="tpu_custom_call" | custom-call | tf_op jit(solution)/shard_map/finish/pallas_call | solution.py:520
  (75 shorter events, 41.6 us)
Async XLA Ops:
  10.6 5.5 %collective-permute-start.1 = (f32[32,128]{1,0:T(8,128)S(1)}, f32[32,128]{1,0:T(8,128)S(1)}, u32[]{:S(2)}, u32[]{:S(2)}) collective-permute-start(f32[32,128]{1,0:T(8,128)S(1)} %add.18.refs_0_), channel_id=1, source_target_pairs={{0,8},{4,12},{8,0},{12,4},{16,24},{20,28},{24,16},{28,20},{1,9},{5... | collective-permute-start | bytes 49160 | tf_op jit(solution)/shard_map/ppermute | solution.py:532
  13.5 4.6 %collective-permute-start.2 = (f32[32,128]{1,0:T(8,128)S(1)}, f32[32,128]{1,0:T(8,128)S(1)}, u32[]{:S(2)}, u32[]{:S(2)}) collective-permute-start(f32[32,128]{1,0:T(8,128)S(1)} %add.18.refs_0_), channel_id=1, source_target_pairs={{0,16},{4,20},{8,24},{12,28},{16,0},{20,4},{24,8},{28,12},{1,17},{... | collective-permute-start | bytes 49160 | tf_op jit(solution)/shard_map/ppermute | solution.py:532
  16.1 5.5 %collective-permute-start.3 = (f32[32,128]{1,0:T(8,128)S(1)}, f32[32,128]{1,0:T(8,128)S(1)}, u32[]{:S(2)}, u32[]{:S(2)}) collective-permute-start(f32[32,128]{1,0:T(8,128)S(1)} %add.18.refs_0_), channel_id=1, source_target_pairs={{0,24},{4,28},{8,16},{12,20},{16,8},{20,12},{24,0},{28,4},{1,25},{... | collective-permute-start | bytes 49160 | tf_op jit(solution)/shard_map/ppermute | solution.py:532
  24.0 3.8 %collective-permute-start.4 = (f32[32,128]{1,0:T(8,128)S(1)}, f32[32,128]{1,0:T(8,128)S(1)}, u32[]{:S(2)}, u32[]{:S(2)}) collective-permute-start(f32[32,128]{1,0:T(8,128)S(1)} %get-tuple-element.38.refs_0_.refs_4_), channel_id=1, source_target_pairs={{0,1},{1,0},{2,3},{3,2},{4,5},{5,4},{6,7},{7,6},{8,9},{9,8},{10,11... | collective-permute-start | bytes 49160 | tf_op jit(solution)/shard_map/ppermute | solution.py:532
  27.0 4.6 %collective-permute-start.6 = (f32[32,128]{1,0:T(8,128)S(1)}, f32[32,128]{1,0:T(8,128)S(1)}, u32[]{:S(2)}, u32[]{:S(2)}) collective-permute-start(f32[32,128]{1,0:T(8,128)S(1)} %get-tuple-element.38.refs_0_.refs_4_), channel_id=1, source_target_pairs={{0,3},{1,2},{2,1},{3,0},{4,7},{5,6},{6,5},{7,4},{8,11},{9,10},{10,... | collective-permute-start | bytes 49160 | tf_op jit(solution)/shard_map/ppermute | solution.py:532
  35.2 5.5 %collective-permute-start.10 = (f32[32,128]{1,0:T(8,128)S(1)}, f32[32,128]{1,0:T(8,128)S(1)}, u32[]{:S(2)}, u32[]{:S(2)}) collective-permute-start(f32[32,128]{1,0:T(8,128)S(1)} %add.19.refs_0_), channel_id=1, source_target_pairs={{0,24},{4,28},{8,16},{12,20},{16,8},{20,12},{24,0},{28,4},{1,25},{... | collective-permute-start | bytes 49160 | tf_op jit(solution)/shard_map/ppermute | solution.py:532
  35.4 5.3 %collective-permute-start.8 = (f32[32,128]{1,0:T(8,128)S(1)}, f32[32,128]{1,0:T(8,128)S(1)}, u32[]{:S(2)}, u32[]{:S(2)}) collective-permute-start(f32[32,128]{1,0:T(8,128)S(1)} %add.19.refs_0_), channel_id=1, source_target_pairs={{0,8},{4,12},{8,0},{12,4},{16,24},{20,28},{24,16},{28,20},{1,9},{5... | collective-permute-start | bytes 49160 | tf_op jit(solution)/shard_map/ppermute | solution.py:532
  35.4 5.9 %collective-permute-start.9 = (f32[32,128]{1,0:T(8,128)S(1)}, f32[32,128]{1,0:T(8,128)S(1)}, u32[]{:S(2)}, u32[]{:S(2)}) collective-permute-start(f32[32,128]{1,0:T(8,128)S(1)} %add.19.refs_0_), channel_id=1, source_target_pairs={{0,16},{4,20},{8,24},{12,28},{16,0},{20,4},{24,8},{28,12},{1,17},{... | collective-permute-start | bytes 49160 | tf_op jit(solution)/shard_map/ppermute | solution.py:532
  44.7 4.5 %collective-permute-start.13 = (f32[16,128]{1,0:T(8,128)S(1)}, f32[16,128]{1,0:T(8,128)S(1)}, u32[]{:S(2)}, u32[]{:S(2)}) collective-permute-start(f32[16,128]{1,0:T(8,128)S(1)} %get-tuple-element.39.refs_0_), channel_id=1, source_target_pairs={{0,3},{1,2},{2,1},{3,0},{4,7},{5,6},{6,5},{7,4},{8,11},{9,10},{10,... | collective-permute-start | bytes 24584 | tf_op jit(solution)/shard_map/ppermute | solution.py:532
  52.9 4.4 %collective-permute-start.15 = (f32[32,128]{1,0:T(8,128)S(1)}, f32[32,128]{1,0:T(8,128)S(1)}, u32[]{:S(2)}, u32[]{:S(2)}) collective-permute-start(f32[32,128]{1,0:T(8,128)S(1)} %add.20.refs_0_), channel_id=1, source_target_pairs={{0,8},{4,12},{8,0},{12,4},{16,24},{20,28},{24,16},{28,20},{1,9},{5... | collective-permute-start | bytes 49160 | tf_op jit(solution)/shard_map/ppermute | solution.py:532
  53.6 4.6 %collective-permute-start.16 = (f32[32,128]{1,0:T(8,128)S(1)}, f32[32,128]{1,0:T(8,128)S(1)}, u32[]{:S(2)}, u32[]{:S(2)}) collective-permute-start(f32[32,128]{1,0:T(8,128)S(1)} %add.20.refs_0_), channel_id=1, source_target_pairs={{0,16},{4,20},{8,24},{12,28},{16,0},{20,4},{24,8},{28,12},{1,17},{... | collective-permute-start | bytes 49160 | tf_op jit(solution)/shard_map/ppermute | solution.py:532
  55.9 5.5 %collective-permute-start.17 = (f32[32,128]{1,0:T(8,128)S(1)}, f32[32,128]{1,0:T(8,128)S(1)}, u32[]{:S(2)}, u32[]{:S(2)}) collective-permute-start(f32[32,128]{1,0:T(8,128)S(1)} %add.20.refs_0_), channel_id=1, source_target_pairs={{0,24},{4,28},{8,16},{12,20},{16,8},{20,12},{24,0},{28,4},{1,25},{... | collective-permute-start | bytes 49160 | tf_op jit(solution)/shard_map/ppermute | solution.py:532
  66.6 4.5 %collective-permute-start.20 = (f32[16,128]{1,0:T(8,128)S(1)}, f32[16,128]{1,0:T(8,128)S(1)}, u32[]{:S(2)}, u32[]{:S(2)}) collective-permute-start(f32[16,128]{1,0:T(8,128)S(1)} %get-tuple-element.42.refs_0_), channel_id=1, source_target_pairs={{0,3},{1,2},{2,1},{3,0},{4,7},{5,6},{6,5},{7,4},{8,11},{9,10},{10,... | collective-permute-start | bytes 24584 | tf_op jit(solution)/shard_map/ppermute | solution.py:532
  78.2 5.4 %collective-permute-start.21 = (f32[2,4,128,256]{3,2,1,0:T(8,128)S(1)}, f32[2,4,128,256]{3,2,1,0:T(8,128)S(1)}, u32[]{:S(2)}, u32[]{:S(2)}) collective-permute-start(f32[2,4,128,256]{3,2,1,0:T(8,128)S(1)} %get-tuple-element.46), channel_id=1, source_target_pairs={{0,4},{4,0},{8,12},{12,8},{16,20},{20,16},{24,28},{28,24},{1,5},{5... | collective-permute-start | bytes 3145736 | tf_op jit(solution)/shard_map/ppermute | solution.py:532
  80.6 14.4 %collective-permute-start.24 = (f32[2,256,256]{2,1,0:T(8,128)S(1)}, f32[2,256,256]{2,1,0:T(8,128)S(1)}, u32[]{:S(2)}, u32[]{:S(2)}) collective-permute-start(f32[2,256,256]{2,1,0:T(8,128)S(1)} %get-tuple-element.45.after_ref), channel_id=1, source_target_pairs={{0,1},{1,0},{2,3},{3,2},{4,5},{5,4},{6,7},{7,6},{8,9},{9,8},{10,11... | collective-permute-start | bytes 1572872 | tf_op jit(solution)/shard_map/ppermute | solution.py:532
  81.2 14.0 %collective-permute-start.25 = (f32[2,256,256]{2,1,0:T(8,128)S(1)}, f32[2,256,256]{2,1,0:T(8,128)S(1)}, u32[]{:S(2)}, u32[]{:S(2)}) collective-permute-start(f32[2,256,256]{2,1,0:T(8,128)S(1)} %get-tuple-element.53), channel_id=1, source_target_pairs={{0,2},{1,3},{2,0},{3,1},{4,6},{5,7},{6,4},{7,5},{8,10},{9,11},{10,... | collective-permute-start | bytes 1572872 | tf_op jit(solution)/shard_map/ppermute | solution.py:532
  83.7 12.6 %collective-permute-start.22 = (f32[2,128,256]{2,1,0:T(8,128)S(1)}, f32[2,128,256]{2,1,0:T(8,128)S(1)}, u32[]{:S(2)}, u32[]{:S(2)}) collective-permute-start(f32[2,128,256]{2,1,0:T(8,128)S(1)} %get-tuple-element.48), channel_id=1, source_target_pairs={{0,8},{4,12},{8,0},{12,4},{16,24},{20,28},{24,16},{28,20},{1,9},{5... | collective-permute-start | bytes 786440 | tf_op jit(solution)/shard_map/ppermute | solution.py:532
  84.0 14.6 %collective-permute-start.23 = (f32[2,128,256]{2,1,0:T(8,128)S(1)}, f32[2,128,256]{2,1,0:T(8,128)S(1)}, u32[]{:S(2)}, u32[]{:S(2)}) collective-permute-start(f32[2,128,256]{2,1,0:T(8,128)S(1)} %get-tuple-element.50), channel_id=1, source_target_pairs={{0,16},{4,20},{8,24},{12,28},{16,0},{20,4},{24,8},{28,12},{1,17},{... | collective-permute-start | bytes 786440 | tf_op jit(solution)/shard_map/ppermute | solution.py:532
  98.8 10.0 %collective-permute-start.28 = (f32[1,256,256]{2,1,0:T(8,128)S(1)}, f32[1,256,256]{2,1,0:T(8,128)S(1)}, u32[]{:S(2)}, u32[]{:S(2)}) collective-permute-start(f32[1,256,256]{2,1,0:T(8,128)S(1)} %get-tuple-element.59), channel_id=1, source_target_pairs={{0,2},{1,3},{2,0},{3,1},{4,6},{5,7},{6,4},{7,5},{8,10},{9,11},{10,... | collective-permute-start | bytes 786440 | tf_op jit(solution)/shard_map/ppermute | solution.py:532
  100.3 8.5 %collective-permute-start.29 = (f32[1,256,256]{2,1,0:T(8,128)S(1)}, f32[1,256,256]{2,1,0:T(8,128)S(1)}, u32[]{:S(2)}, u32[]{:S(2)}) collective-permute-start(f32[1,256,256]{2,1,0:T(8,128)S(1)} %get-tuple-element.61), channel_id=1, source_target_pairs={{0,1},{1,0},{2,3},{3,2},{4,5},{5,4},{6,7},{7,6},{8,9},{9,8},{10,11... | collective-permute-start | bytes 786440 | tf_op jit(solution)/shard_map/ppermute | solution.py:532
  101.8 6.7 %collective-permute-start.26 = (f32[1,128,256]{2,1,0:T(8,128)S(1)}, f32[1,128,256]{2,1,0:T(8,128)S(1)}, u32[]{:S(2)}, u32[]{:S(2)}) collective-permute-start(f32[1,128,256]{2,1,0:T(8,128)S(1)} %get-tuple-element.55), channel_id=1, source_target_pairs={{0,16},{4,20},{8,24},{12,28},{16,0},{20,4},{24,8},{28,12},{1,17},{... | collective-permute-start | bytes 393224 | tf_op jit(solution)/shard_map/ppermute | solution.py:532
  102.1 6.7 %collective-permute-start.27 = (f32[1,128,256]{2,1,0:T(8,128)S(1)}, f32[1,128,256]{2,1,0:T(8,128)S(1)}, u32[]{:S(2)}, u32[]{:S(2)}) collective-permute-start(f32[1,128,256]{2,1,0:T(8,128)S(1)} %get-tuple-element.57), channel_id=1, source_target_pairs={{0,8},{4,12},{8,0},{12,4},{16,24},{20,28},{24,16},{28,20},{1,9},{5... | collective-permute-start | bytes 393224 | tf_op jit(solution)/shard_map/ppermute | solution.py:532
  109.4 13.9 %collective-permute-start.33 = (f32[2,256,256]{2,1,0:T(8,128)S(1)}, f32[2,256,256]{2,1,0:T(8,128)S(1)}, u32[]{:S(2)}, u32[]{:S(2)}) collective-permute-start(f32[2,256,256]{2,1,0:T(8,128)S(1)} %get-tuple-element.63.refs_11_), channel_id=1, source_target_pairs={{0,1},{1,0},{2,3},{3,2},{4,5},{5,4},{6,7},{7,6},{8,9},{9,8},{10,11... | collective-permute-start | bytes 1572872 | tf_op jit(solution)/shard_map/ppermute | solution.py:532
  109.9 13.4 %collective-permute-start.34 = (f32[2,256,256]{2,1,0:T(8,128)S(1)}, f32[2,256,256]{2,1,0:T(8,128)S(1)}, u32[]{:S(2)}, u32[]{:S(2)}) collective-permute-start(f32[2,256,256]{2,1,0:T(8,128)S(1)} %get-tuple-element.63.refs_11_), channel_id=1, source_target_pairs={{0,2},{1,3},{2,0},{3,1},{4,6},{5,7},{6,4},{7,5},{8,10},{9,11},{10,... | collective-permute-start | bytes 1572872 | tf_op jit(solution)/shard_map/ppermute | solution.py:532
  110.5 12.0 %collective-permute-start.32 = (f32[264,256]{1,0:T(8,128)S(1)}, f32[264,256]{1,0:T(8,128)S(1)}, u32[]{:S(2)}, u32[]{:S(2)}) collective-permute-start(f32[264,256]{1,0:T(8,128)S(1)} %get-tuple-element.62.refs_0_.refs_4_), channel_id=1, source_target_pairs={{0,16},{4,20},{8,24},{12,28},{16,0},{20,4},{24,8},{28,12},{1,17},{... | collective-permute-start | bytes 811016 | tf_op jit(solution)/shard_map/ppermute | solution.py:532
  111.4 11.9 %collective-permute-start.31 = (f32[264,256]{1,0:T(8,128)S(1)}, f32[264,256]{1,0:T(8,128)S(1)}, u32[]{:S(2)}, u32[]{:S(2)}) collective-permute-start(f32[264,256]{1,0:T(8,128)S(1)} %get-tuple-element.62.refs_0_.refs_4_), channel_id=1, source_target_pairs={{0,8},{4,12},{8,0},{12,4},{16,24},{20,28},{24,16},{28,20},{1,9},{5... | collective-permute-start | bytes 811016 | tf_op jit(solution)/shard_map/ppermute | solution.py:532
  122.4 7.2 %collective-permute-start.36 = (f32[264,256]{1,0:T(8,128)S(1)}, f32[264,256]{1,0:T(8,128)S(1)}, u32[]{:S(2)}, u32[]{:S(2)}) collective-permute-start(f32[264,256]{1,0:T(8,128)S(1)} %collective-permute-done.32.far_ref.refs_4_.refs_8_), channel_id=1, source_target_pairs={{0,8},{4,12},{8,0},{12,4},{16,24},{20,28},{24,16},{28,20},{1,9},{5... | collective-permute-start | bytes 811016 | tf_op jit(solution)/shard_map/ppermute | solution.py:532
  123.4 11.6 %collective-permute-start.35 = (f32[2,264,256]{2,1,0:T(8,128)S(1)}, f32[2,264,256]{2,1,0:T(8,128)S(1)}, u32[]{:S(2)}, u32[]{:S(2)}) collective-permute-start(f32[2,264,256]{2,1,0:T(8,128)S(1)} %get-tuple-element.64), channel_id=1, source_target_pairs={{0,4},{4,0},{8,12},{12,8},{16,20},{20,16},{24,28},{28,24},{1,5},{5... | collective-permute-start | bytes 1622024 | tf_op jit(solution)/shard_map/ppermute | solution.py:532
  123.5 8.7 %collective-permute-start.37 = (f32[256,256]{1,0:T(8,128)S(1)}, f32[256,256]{1,0:T(8,128)S(1)}, u32[]{:S(2)}, u32[]{:S(2)}) collective-permute-start(f32[256,256]{1,0:T(8,128)S(1)} %get-tuple-element.65), channel_id=1, source_target_pairs={{0,1},{1,0},{2,3},{3,2},{4,5},{5,4},{6,7},{7,6},{8,9},{9,8},{10,11... | collective-permute-start | bytes 786440 | tf_op jit(solution)/shard_map/ppermute | solution.py:532
  125.0 8.4 %collective-permute-start.38 = (f32[256,256]{1,0:T(8,128)S(1)}, f32[256,256]{1,0:T(8,128)S(1)}, u32[]{:S(2)}, u32[]{:S(2)}) collective-permute-start(f32[256,256]{1,0:T(8,128)S(1)} %get-tuple-element.66), channel_id=1, source_target_pairs={{0,2},{1,3},{2,0},{3,1},{4,6},{5,7},{6,4},{7,5},{8,10},{9,11},{10,... | collective-permute-start | bytes 786440 | tf_op jit(solution)/shard_map/ppermute | solution.py:532
  126.6 6.9 %collective-permute-start.30 = (f32[264,256]{1,0:T(8,128)S(1)}, f32[264,256]{1,0:T(8,128)S(1)}, u32[]{:S(2)}, u32[]{:S(2)}) collective-permute-start(f32[264,256]{1,0:T(8,128)S(1)} %get-tuple-element.62.refs_0_.refs_4_), channel_id=1, source_target_pairs={{0,4},{4,0},{8,12},{12,8},{16,20},{20,16},{24,28},{28,24},{1,5},{5... | collective-permute-start | bytes 811016 | tf_op jit(solution)/shard_map/ppermute | solution.py:532
  137.2 4.5 %collective-permute-start.42 = (f32[2,8,128]{2,1,0:T(8,128)S(1)}, f32[2,8,128]{2,1,0:T(8,128)S(1)}, u32[]{:S(2)}, u32[]{:S(2)}) collective-permute-start(f32[2,8,128]{2,1,0:T(8,128)S(1)} %sum_squares.1.refs_0_), channel_id=1, source_target_pairs={{0,3},{1,2},{2,1},{3,0},{4,7},{5,6},{6,5},{7,4},{8,11},{9,10},{10,... | collective-permute-start | bytes 24584 | tf_op jit(solution)/shard_map/ppermute | solution.py:532
  (11 other events, 31.2 us)

commit v9 on v8

--- a/solution.py
+++ b/solution.py
@@ -541,17 +541,16 @@
 
 
 def far_first(own, axis, step, count):
-    parts = {m: swap(own, axis, m * step) for m in reversed(range(1, count))}
-    return [parts[m] for m in range(1, count)]
+    return [swap(own, axis, m * step) for m in reversed(range(1, count))]
 
 
 def proto_parts(own):
-    return [own] + far_first(own, "proto", 1, lax.axis_size("proto"))
+    return far_first(own, "proto", 1, lax.axis_size("proto")) + [own]
 
 
 def batch_parts(own):
     pair = own + swap(own, "batch", 1)
-    return [pair] + far_first(pair, "batch", 2, lax.axis_size("batch") // 2)
+    return far_first(pair, "batch", 2, lax.axis_size("batch") // 2) + [pair]
 
 
 def scatter_sums(groups):
@@ -702,7 +701,8 @@
     else:
         proto_pieces = gather_batch(grad_proto)
         view_pieces = gather_views(grad_embed, (proto_orders[1], proto_orders[0]))
-    squares = proto_parts(sum_squares(proto_pieces, proto_rows))
+    square = sum_squares(proto_pieces[::2], proto_rows)
+    squares = proto_parts(square + swap(square, "batch", 1))
     sizes = (proto_rows, clip_rows, clip_rows)
     groups = [proto_pieces] + view_pieces
     return finish((proto_entries, embed_entries), squares, groups, sizes)

time: 144 us -> 142 us (0.986)
  starting transfers between devices: 43.8 us -> 41.7 us
    ppermute x43 -> x44, starting transfers between devices: 43.8 us -> 41.7 us  [swap(): lax.ppermute(own, axis, [(i, i ^ mask) for i in range(lax.axis_size(axis))])]
    ppermute x43 -> x44, waiting for transfers between devices: 62.8 us -> 62.5 us  [swap(): lax.ppermute(own, axis, [(i, i ^ mask) for i in range(lax.axis_size(axis))])]
  transfers between devices with their start and end apart: 43 -> 44, of which waited for: 33 -> 34; matrix products, arithmetic and copies ran while one was open for 1% -> 1% of each run, Pallas kernels for 3% -> 3%
where the time goes in v9:
time: 142 us
  waiting for transfers between devices  62.5 us (44%)
  starting transfers between devices  41.7 us (29%)
  Pallas kernels  34.5 us (24%)
  local copies, waits for them, and re-layouts  1.96 us (1%)
    ppermute x44, waiting for transfers between devices, swap(): lax.ppermute(own, axis, [(i, i ^ mask) for i in range(lax.axis_size(axis))])  62.5 us
    ppermute x44, starting transfers between devices, swap(): lax.ppermute(own, axis, [(i, i ^ mask) for i in range(lax.axis_size(axis))])  41.7 us
    pallas_call x1, Pallas kernels, scores(): pl.pallas_call(score_kernel, out_shape=(pltpu.VMEM((2, clips, count), jnp...  8.59 us
    pallas_call x1, Pallas kernels, send_gradients(): pl.pallas_call(functools.partial(send_kernel, orders, len(row_parts)), ou...  7.04 us
    pallas_call x3, Pallas kernels, row_pass(): pl.pallas_call(functools.partial(row_kernel, protos_all, extra), out_shap...  6.82 us
    pallas_call x2, Pallas kernels, col_pass(): pl.pallas_call(functools.partial(col_kernel, clips_all), out_shape=jax.Sh...  4.65 us
  transfers between devices with their start and end apart: 44, of which 34 were waited for; matrix products, arithmetic and copies ran while one was open for 1% of the time, Pallas kernels for 3%

profile of v9, /device:TPU:0, one launch (start us, length us, event | category | flops | bytes accessed | tf_op | source)
XLA Modules:
  0.0 141.6 jit_solution(17731219843809460497)
XLA Ops:
  0.6 8.6 %scores.1 = (f32[2,1024,2048]{2,1,0:T(8,128)S(1)}, f32[32,128]{1,0:T(8,128)S(1)}, f32[16,128]{1,0:T(8,128)S(1)}, bf16[256,2048]{1,0:T(8,128)(2,1)S(1)}, bf16[2048,256]{1,0:T(8,128)(2,1)S(1)}) custom-call(bf16[1024,256]{1,0:T(8,128)(2,1)} %slow.1, bf16[1024,256]{1,0:T(8,128)(2,1)} %fast.1, f32[2048,256]{1,0:T(8,128)} %protos.1), custom_call_target="tpu_custom_call" | custom-call | tf_op jit(solution)/shard_map/scores/pallas_call | solution.py:115
  10.6 4.9 %collective-permute-start.1 = (f32[32,128]{1,0:T(8,128)S(1)}, f32[32,128]{1,0:T(8,128)S(1)}, u32[]{:S(2)}, u32[]{:S(2)}) collective-permute-start(f32[32,128]{1,0:T(8,128)S(1)} %add.21.refs_3_), channel_id=1, source_target_pairs={{0,24},{4,28},{8,16},{12,20},{16,8},{20,12},{24,0},{28,4},{1,25},{... | collective-permute-start | bytes 49160 | tf_op jit(solution)/shard_map/ppermute | solution.py:532
  17.2 2.9 %collective-permute-done.2.refs_1_ = f32[32,128]{1,0:T(8,128)S(1)} collective-permute-done((f32[32,128]{1,0:T(8,128)S(1)}, f32[32,128]{1,0:T(8,128)S(1)}, u32[]{:S(2)}, u32[]{:S(2)}) %collective-permute-start.2) | collective-permute-done | bytes 16416 | tf_op jit(solution)/shard_map/ppermute | solution.py:532
  20.2 2.4 %row_pass.3 = (f32[32,128]{1,0:T(8,128)S(1)}, f32[32,128]{1,0:T(8,128)}) custom-call(f32[2,1024,2048]{2,1,0:T(8,128)S(1)} %get-tuple-element.35.t_ref, f32[16,128]{1,0:T(8,128)S(1)} %get-tuple-element.36.den_ref, f32[32,128]{1,0:T(8,128)S(1)} %collective-permute-done.1.refs_0_, f32[32,128]{1,0:T(8,128)S(1)} %collective-permute-done.2.refs_1_, ...), custom_call_target="tpu_custom_call" | custom-call | tf_op jit(solution)/shard_map/row_pass/pallas_call | solution.py:164
  22.5 2.4 %collective-permute-start.4 = (f32[32,128]{1,0:T(8,128)S(1)}, f32[32,128]{1,0:T(8,128)S(1)}, u32[]{:S(2)}, u32[]{:S(2)}) collective-permute-start(f32[32,128]{1,0:T(8,128)S(1)} %get-tuple-element.38.refs_3_.refs_7_), channel_id=1, source_target_pairs={{0,3},{1,2},{2,1},{3,0},{4,7},{5,6},{6,5},{7,4},{8,11},{9,10},{10,... | collective-permute-start | bytes 49160 | tf_op jit(solution)/shard_map/ppermute | solution.py:532
  27.2 1.5 %collective-permute-done.5.refs_1_.refs_5_ = f32[32,128]{1,0:T(8,128)S(1)} collective-permute-done((f32[32,128]{1,0:T(8,128)S(1)}, f32[32,128]{1,0:T(8,128)S(1)}, u32[]{:S(2)}, u32[]{:S(2)}) %collective-permute-start.5) | collective-permute-done | bytes 16416 | tf_op jit(solution)/shard_map/ppermute | solution.py:532
  29.2 2.3 %col_pass.2 = f32[32,128]{1,0:T(8,128)S(1)} custom-call(f32[2,1024,2048]{2,1,0:T(8,128)S(1)} %get-tuple-element.35.t_ref, f32[32,128]{1,0:T(8,128)S(1)} %collective-permute-done.4.refs_0_.refs_4_, f32[32,128]{1,0:T(8,128)S(1)} %collective-permute-done.5.refs_1_.refs_5_, f32[32,128]{1,0:T(8,128)S(1)} %collective-permute-done.6.refs_2_.refs_6_, ...), custom_call_target="tpu_custom_call" | custom-call | tf_op jit(solution)/shard_map/col_pass/pallas_call | solution.py:204
  32.8 3.5 %collective-permute-start.8 = (f32[32,128]{1,0:T(8,128)S(1)}, f32[32,128]{1,0:T(8,128)S(1)}, u32[]{:S(2)}, u32[]{:S(2)}) collective-permute-start(f32[32,128]{1,0:T(8,128)S(1)} %add.22.refs_3_), channel_id=1, source_target_pairs={{0,24},{4,28},{8,16},{12,20},{16,8},{20,12},{24,0},{28,4},{1,25},{... | collective-permute-start | bytes 49160 | tf_op jit(solution)/shard_map/ppermute | solution.py:532
  36.5 2.0 %collective-permute-done.8.refs_0_ = f32[32,128]{1,0:T(8,128)S(1)} collective-permute-done((f32[32,128]{1,0:T(8,128)S(1)}, f32[32,128]{1,0:T(8,128)S(1)}, u32[]{:S(2)}, u32[]{:S(2)}) %collective-permute-start.8) | collective-permute-done | bytes 16416 | tf_op jit(solution)/shard_map/ppermute | solution.py:532
  38.6 2.3 %collective-permute-done.9.refs_1_ = f32[32,128]{1,0:T(8,128)S(1)} collective-permute-done((f32[32,128]{1,0:T(8,128)S(1)}, f32[32,128]{1,0:T(8,128)S(1)}, u32[]{:S(2)}, u32[]{:S(2)}) %collective-permute-start.9) | collective-permute-done | bytes 16416 | tf_op jit(solution)/shard_map/ppermute | solution.py:532
  40.9 2.4 %row_pass.4 = (f32[16,128]{1,0:T(8,128)S(1)}, f32[32,128]{1,0:T(8,128)}) custom-call(f32[2,1024,2048]{2,1,0:T(8,128)S(1)} %get-tuple-element.35.t_ref, f32[16,128]{1,0:T(8,128)S(1)} %get-tuple-element.36.den_ref, f32[32,128]{1,0:T(8,128)S(1)} %collective-permute-done.8.refs_0_, f32[32,128]{1,0:T(8,128)S(1)} %collective-permute-done.9.refs_1_, ...), custom_call_target="tpu_custom_call" | custom-call | tf_op jit(solution)/shard_map/row_pass/pallas_call | solution.py:164
  48.9 2.3 %col_pass.3 = f32[32,128]{1,0:T(8,128)S(1)} custom-call(f32[2,1024,2048]{2,1,0:T(8,128)S(1)} %get-tuple-element.35.t_ref, f32[16,128]{1,0:T(8,128)S(1)} %collective-permute-done.11.refs_0_, f32[16,128]{1,0:T(8,128)S(1)} %collective-permute-done.12.refs_1_, f32[16,128]{1,0:T(8,128)S(1)} %collective-permute-done.13.refs_2_, ...), custom_call_target="tpu_custom_call" | custom-call | tf_op jit(solution)/shard_map/col_pass/pallas_call | solution.py:204
  53.4 3.5 %collective-permute-start.17 = (f32[32,128]{1,0:T(8,128)S(1)}, f32[32,128]{1,0:T(8,128)S(1)}, u32[]{:S(2)}, u32[]{:S(2)}) collective-permute-start(f32[32,128]{1,0:T(8,128)S(1)} %add.23.refs_3_), channel_id=1, source_target_pairs={{0,8},{4,12},{8,0},{12,4},{16,24},{20,28},{24,16},{28,20},{1,9},{5... | collective-permute-start | bytes 49160 | tf_op jit(solution)/shard_map/ppermute | solution.py:532
  58.6 2.1 %row_pass.5 = (f32[16,128]{1,0:T(8,128)S(1)}, f32[32,128]{1,0:T(8,128)S(1)}) custom-call(f32[2,1024,2048]{2,1,0:T(8,128)S(1)} %get-tuple-element.35.t_ref, f32[16,128]{1,0:T(8,128)S(1)} %get-tuple-element.36.den_ref, f32[32,128]{1,0:T(8,128)S(1)} %collective-permute-done.15.refs_0_, f32[32,128]{1,0:T(8,128)S(1)} %collective-permute-done.16.refs_1_, ...), custom_call_target="tpu_custom_call" | custom-call | tf_op jit(solution)/shard_map/row_pass/pallas_call | solution.py:164
  60.7 2.5 %collective-permute-start.18 = (f32[16,128]{1,0:T(8,128)S(1)}, f32[16,128]{1,0:T(8,128)S(1)}, u32[]{:S(2)}, u32[]{:S(2)}) collective-permute-start(f32[16,128]{1,0:T(8,128)S(1)} %get-tuple-element.42.refs_3_), channel_id=1, source_target_pairs={{0,3},{1,2},{2,1},{3,0},{4,7},{5,6},{6,5},{7,4},{8,11},{9,10},{10,... | collective-permute-start | bytes 24584 | tf_op jit(solution)/shard_map/ppermute | solution.py:532
  65.4 1.5 %collective-permute-done.19.refs_1_ = f32[16,128]{1,0:T(8,128)S(1)} collective-permute-done((f32[16,128]{1,0:T(8,128)S(1)}, f32[16,128]{1,0:T(8,128)S(1)}, u32[]{:S(2)}, u32[]{:S(2)}) %collective-permute-start.19) | collective-permute-done | bytes 8224 | tf_op jit(solution)/shard_map/ppermute | solution.py:532
  67.4 7.0 %send_gradients.1 = (f32[2,4,128,256]{3,2,1,0:T(8,128)S(1)}, bf16[2048,2048]{1,0:T(8,128)(2,1)S(1)}) custom-call(f32[2,1024,2048]{2,1,0:T(8,128)S(1)} %get-tuple-element.35.t_ref, f32[32,128]{1,0:T(8,128)S(1)} %get-tuple-element.40.r_ref, bf16[256,2048]{1,0:T(8,128)(2,1)S(1)} %get-tuple-element.41.ubt_ref, f32[16,128]{1,0:T(8,128)S(1)} %collective-permute-done.18.refs_0_, ...), custom_call_target="tpu_custom_call" | custom-call | flops 1073741824 | bytes 20971520 | tf_op jit(solution)/shard_map/send_gradients/pallas_call | solution.py:291
  74.5 2.3 %embed_gradients.1 = (f32[2,256,256]{2,1,0:T(8,128)S(1)}, f32[2,256,256]{2,1,0:T(8,128)S(1)}, f32[2,256,256]{2,1,0:T(8,128)S(1)}, f32[2,256,256]{2,1,0:T(8,128)S(1)}) custom-call(bf16[2048,2048]{1,0:T(8,128)(2,1)S(1)} %get-tuple-element.43.g_ref, bf16[2048,256]{1,0:T(8,128)(2,1)S(1)} %get-tuple-element.44.cb_ref), custom_call_target="tpu_custom_call" | custom-call | flops 2147483648 | bytes 11534336 | tf_op jit(solution)/shard_map/embed_gradients/pallas_call | solution.py:331
  77.5 1.5 %collective-permute-start.25 = (f32[2,256,256]{2,1,0:T(8,128)S(1)}, f32[2,256,256]{2,1,0:T(8,128)S(1)}, u32[]{:S(2)}, u32[]{:S(2)}) collective-permute-start(f32[2,256,256]{2,1,0:T(8,128)S(1)} %get-tuple-element.53), channel_id=1, source_target_pairs={{0,2},{1,3},{2,0},{3,1},{4,6},{5,7},{6,4},{7,5},{8,10},{9,11},{10,... | collective-permute-start | bytes 1572872 | tf_op jit(solution)/shard_map/ppermute | solution.py:532
  79.0 1.9 %keep_gradients.1.refs_0_ = f32[2,4,128,256]{3,2,1,0:T(8,128)S(1)} custom-call(bf16[2048,2048]{1,0:T(8,128)(2,1)S(1)} %get-tuple-element.43.g_ref, bf16[256,2048]{1,0:T(8,128)(2,1)S(1)} %get-tuple-element.41.ubt_ref, f32[2,256,256]{2,1,0:T(8,128)S(1)} %get-tuple-element.45.after_ref), custom_call_target="tpu_custom_call" | custom-call | flops 1073741824 | bytes 6291456 | tf_op jit(solution)/shard_map/keep_gradients/pallas_call | solution.py:360
  81.0 2.1 %collective-permute-start.22 = (f32[2,128,256]{2,1,0:T(8,128)S(1)}, f32[2,128,256]{2,1,0:T(8,128)S(1)}, u32[]{:S(2)}, u32[]{:S(2)}) collective-permute-start(f32[2,128,256]{2,1,0:T(8,128)S(1)} %get-tuple-element.48), channel_id=1, source_target_pairs={{0,8},{4,12},{8,0},{12,4},{16,24},{20,28},{24,16},{28,20},{1,9},{5... | collective-permute-start | bytes 786440 | tf_op jit(solution)/shard_map/ppermute | solution.py:532
  84.0 7.2 %collective-permute-done.24.refs_5_ = f32[2,256,256]{2,1,0:T(8,128)S(1)} collective-permute-done((f32[2,256,256]{2,1,0:T(8,128)S(1)}, f32[2,256,256]{2,1,0:T(8,128)S(1)}, u32[]{:S(2)}, u32[]{:S(2)}) %collective-permute-start.24) | collective-permute-done | bytes 524320 | tf_op jit(solution)/shard_map/ppermute | solution.py:532
  91.5 1.9 %collective-permute-done.22.refs_1_ = f32[2,128,256]{2,1,0:T(8,128)S(1)} collective-permute-done((f32[2,128,256]{2,1,0:T(8,128)S(1)}, f32[2,128,256]{2,1,0:T(8,128)S(1)}, u32[]{:S(2)}, u32[]{:S(2)}) %collective-permute-start.22) | collective-permute-done | bytes 262176 | tf_op jit(solution)/shard_map/ppermute | solution.py:532
  93.4 4.1 %collective-permute-done.23.refs_3_ = f32[2,128,256]{2,1,0:T(8,128)S(1)} collective-permute-done((f32[2,128,256]{2,1,0:T(8,128)S(1)}, f32[2,128,256]{2,1,0:T(8,128)S(1)}, u32[]{:S(2)}, u32[]{:S(2)}) %collective-permute-start.23) | collective-permute-done | bytes 262176 | tf_op jit(solution)/shard_map/ppermute | solution.py:532
  102.0 4.2 %collective-permute-done.26.refs_1_ = f32[1,128,256]{2,1,0:T(8,128)S(1)} collective-permute-done((f32[1,128,256]{2,1,0:T(8,128)S(1)}, f32[1,128,256]{2,1,0:T(8,128)S(1)}, u32[]{:S(2)}, u32[]{:S(2)}) %collective-permute-start.26) | collective-permute-done | bytes 131104 | tf_op jit(solution)/shard_map/ppermute | solution.py:532
  107.6 1.5 %collective-permute-start.39 = (f32[2,256,256]{2,1,0:T(8,128)S(1)}, f32[2,256,256]{2,1,0:T(8,128)S(1)}, u32[]{:S(2)}, u32[]{:S(2)}) collective-permute-start(f32[2,256,256]{2,1,0:T(8,128)S(1)} %get-tuple-element.63.refs_11_), channel_id=1, source_target_pairs={{0,2},{1,3},{2,0},{3,1},{4,6},{5,7},{6,4},{7,5},{8,10},{9,11},{10,... | collective-permute-start | bytes 1572872 | tf_op jit(solution)/shard_map/ppermute | solution.py:532
  110.5 10.6 %collective-permute-done.31.refs_2_.far_ref.refs_8_ = f32[264,256]{1,0:T(8,128)S(1)} collective-permute-done((f32[264,256]{1,0:T(8,128)S(1)}, f32[264,256]{1,0:T(8,128)S(1)}, u32[]{:S(2)}, u32[]{:S(2)}) %collective-permute-start.31) | collective-permute-done | bytes 270368 | tf_op jit(solution)/shard_map/ppermute | solution.py:532
  122.1 1.6 %collective-permute-start.41 = (f32[256,256]{1,0:T(8,128)S(1)}, f32[256,256]{1,0:T(8,128)S(1)}, u32[]{:S(2)}, u32[]{:S(2)}) collective-permute-start(f32[256,256]{1,0:T(8,128)S(1)} %get-tuple-element.65), channel_id=1, source_target_pairs={{0,1},{1,0},{2,3},{3,2},{4,5},{5,4},{6,7},{7,6},{8,9},{9,8},{10,11... | collective-permute-start | bytes 786440 | tf_op jit(solution)/shard_map/ppermute | solution.py:532
  124.2 4.2 %collective-permute-done.32.refs_3_.x_ref.refs_9_ = f32[264,256]{1,0:T(8,128)S(1)} collective-permute-done((f32[264,256]{1,0:T(8,128)S(1)}, f32[264,256]{1,0:T(8,128)S(1)}, u32[]{:S(2)}, u32[]{:S(2)}) %collective-permute-start.32) | collective-permute-done | bytes 270368 | tf_op jit(solution)/shard_map/ppermute | solution.py:532
  128.4 2.5 %collective-permute-done.41.refs_0_.refs_14_ = f32[256,256]{1,0:T(8,128)S(1)} collective-permute-done((f32[256,256]{1,0:T(8,128)S(1)}, f32[256,256]{1,0:T(8,128)S(1)}, u32[]{:S(2)}, u32[]{:S(2)}) %collective-permute-start.41) | collective-permute-done | bytes 262176 | tf_op jit(solution)/shard_map/ppermute | solution.py:532
  135.7 1.5 %collective-permute-start.36 = (f32[2,8,128]{2,1,0:T(8,128)S(1)}, f32[2,8,128]{2,1,0:T(8,128)S(1)}, u32[]{:S(2)}, u32[]{:S(2)}) collective-permute-start(f32[2,8,128]{2,1,0:T(8,128)S(1)} %add.24.refs_3_), channel_id=1, source_target_pairs={{0,1},{1,0},{2,3},{3,2},{4,5},{5,4},{6,7},{7,6},{8,9},{9,8},{10,11... | collective-permute-start | bytes 24584 | tf_op jit(solution)/shard_map/ppermute | solution.py:532
  139.4 2.2 %finish.1 = (f32[2048,256]{1,0:T(8,128)}, f32[1024,256]{1,0:T(8,128)}, f32[1024,256]{1,0:T(8,128)}) custom-call(f32[2,8,128]{2,1,0:T(8,128)S(1)} %collective-permute-done.34.refs_0_, f32[2,8,128]{2,1,0:T(8,128)S(1)} %collective-permute-done.35.refs_1_, f32[2,8,128]{2,1,0:T(8,128)S(1)} %collective-permute-done.36.refs_2_, f32[2,8,128]{2,1,0:T(8,128)S(1)} %add.24.refs_3_, ...), custom_call_target="tpu_custom_call" | custom-call | tf_op jit(solution)/shard_map/finish/pallas_call | solution.py:520
  (78 shorter events, 37.0 us)
Async XLA Ops:
  10.6 6.7 %collective-permute-start.1 = (f32[32,128]{1,0:T(8,128)S(1)}, f32[32,128]{1,0:T(8,128)S(1)}, u32[]{:S(2)}, u32[]{:S(2)}) collective-permute-start(f32[32,128]{1,0:T(8,128)S(1)} %add.21.refs_3_), channel_id=1, source_target_pairs={{0,24},{4,28},{8,16},{12,20},{16,8},{20,12},{24,0},{28,4},{1,25},{... | collective-permute-start | bytes 49160 | tf_op jit(solution)/shard_map/ppermute | solution.py:532
  15.5 4.6 %collective-permute-start.2 = (f32[32,128]{1,0:T(8,128)S(1)}, f32[32,128]{1,0:T(8,128)S(1)}, u32[]{:S(2)}, u32[]{:S(2)}) collective-permute-start(f32[32,128]{1,0:T(8,128)S(1)} %add.21.refs_3_), channel_id=1, source_target_pairs={{0,16},{4,20},{8,24},{12,28},{16,0},{20,4},{24,8},{28,12},{1,17},{... | collective-permute-start | bytes 49160 | tf_op jit(solution)/shard_map/ppermute | solution.py:532
  15.5 4.6 %collective-permute-start.3 = (f32[32,128]{1,0:T(8,128)S(1)}, f32[32,128]{1,0:T(8,128)S(1)}, u32[]{:S(2)}, u32[]{:S(2)}) collective-permute-start(f32[32,128]{1,0:T(8,128)S(1)} %add.21.refs_3_), channel_id=1, source_target_pairs={{0,8},{4,12},{8,0},{12,4},{16,24},{20,28},{24,16},{28,20},{1,9},{5... | collective-permute-start | bytes 49160 | tf_op jit(solution)/shard_map/ppermute | solution.py:532
  22.5 4.6 %collective-permute-start.4 = (f32[32,128]{1,0:T(8,128)S(1)}, f32[32,128]{1,0:T(8,128)S(1)}, u32[]{:S(2)}, u32[]{:S(2)}) collective-permute-start(f32[32,128]{1,0:T(8,128)S(1)} %get-tuple-element.38.refs_3_.refs_7_), channel_id=1, source_target_pairs={{0,3},{1,2},{2,1},{3,0},{4,7},{5,6},{6,5},{7,4},{8,11},{9,10},{10,... | collective-permute-start | bytes 49160 | tf_op jit(solution)/shard_map/ppermute | solution.py:532
  32.8 5.8 %collective-permute-start.8 = (f32[32,128]{1,0:T(8,128)S(1)}, f32[32,128]{1,0:T(8,128)S(1)}, u32[]{:S(2)}, u32[]{:S(2)}) collective-permute-start(f32[32,128]{1,0:T(8,128)S(1)} %add.22.refs_3_), channel_id=1, source_target_pairs={{0,24},{4,28},{8,16},{12,20},{16,8},{20,12},{24,0},{28,4},{1,25},{... | collective-permute-start | bytes 49160 | tf_op jit(solution)/shard_map/ppermute | solution.py:532
  36.3 4.6 %collective-permute-start.9 = (f32[32,128]{1,0:T(8,128)S(1)}, f32[32,128]{1,0:T(8,128)S(1)}, u32[]{:S(2)}, u32[]{:S(2)}) collective-permute-start(f32[32,128]{1,0:T(8,128)S(1)} %add.22.refs_3_), channel_id=1, source_target_pairs={{0,16},{4,20},{8,24},{12,28},{16,0},{20,4},{24,8},{28,12},{1,17},{... | collective-permute-start | bytes 49160 | tf_op jit(solution)/shard_map/ppermute | solution.py:532
  43.3 4.5 %collective-permute-start.11 = (f32[16,128]{1,0:T(8,128)S(1)}, f32[16,128]{1,0:T(8,128)S(1)}, u32[]{:S(2)}, u32[]{:S(2)}) collective-permute-start(f32[16,128]{1,0:T(8,128)S(1)} %get-tuple-element.39.refs_3_), channel_id=1, source_target_pairs={{0,3},{1,2},{2,1},{3,0},{4,7},{5,6},{6,5},{7,4},{8,11},{9,10},{10,... | collective-permute-start | bytes 24584 | tf_op jit(solution)/shard_map/ppermute | solution.py:532
  52.5 5.6 %collective-permute-start.15 = (f32[32,128]{1,0:T(8,128)S(1)}, f32[32,128]{1,0:T(8,128)S(1)}, u32[]{:S(2)}, u32[]{:S(2)}) collective-permute-start(f32[32,128]{1,0:T(8,128)S(1)} %add.23.refs_3_), channel_id=1, source_target_pairs={{0,24},{4,28},{8,16},{12,20},{16,8},{20,12},{24,0},{28,4},{1,25},{... | collective-permute-start | bytes 49160 | tf_op jit(solution)/shard_map/ppermute | solution.py:532
  53.4 4.9 %collective-permute-start.16 = (f32[32,128]{1,0:T(8,128)S(1)}, f32[32,128]{1,0:T(8,128)S(1)}, u32[]{:S(2)}, u32[]{:S(2)}) collective-permute-start(f32[32,128]{1,0:T(8,128)S(1)} %add.23.refs_3_), channel_id=1, source_target_pairs={{0,16},{4,20},{8,24},{12,28},{16,0},{20,4},{24,8},{28,12},{1,17},{... | collective-permute-start | bytes 49160 | tf_op jit(solution)/shard_map/ppermute | solution.py:532
  53.4 5.2 %collective-permute-start.17 = (f32[32,128]{1,0:T(8,128)S(1)}, f32[32,128]{1,0:T(8,128)S(1)}, u32[]{:S(2)}, u32[]{:S(2)}) collective-permute-start(f32[32,128]{1,0:T(8,128)S(1)} %add.23.refs_3_), channel_id=1, source_target_pairs={{0,8},{4,12},{8,0},{12,4},{16,24},{20,28},{24,16},{28,20},{1,9},{5... | collective-permute-start | bytes 49160 | tf_op jit(solution)/shard_map/ppermute | solution.py:532
  60.7 4.6 %collective-permute-start.18 = (f32[16,128]{1,0:T(8,128)S(1)}, f32[16,128]{1,0:T(8,128)S(1)}, u32[]{:S(2)}, u32[]{:S(2)}) collective-permute-start(f32[16,128]{1,0:T(8,128)S(1)} %get-tuple-element.42.refs_3_), channel_id=1, source_target_pairs={{0,3},{1,2},{2,1},{3,0},{4,7},{5,6},{6,5},{7,4},{8,11},{9,10},{10,... | collective-permute-start | bytes 24584 | tf_op jit(solution)/shard_map/ppermute | solution.py:532
  74.5 6.4 %collective-permute-start.21 = (f32[2,4,128,256]{3,2,1,0:T(8,128)S(1)}, f32[2,4,128,256]{3,2,1,0:T(8,128)S(1)}, u32[]{:S(2)}, u32[]{:S(2)}) collective-permute-start(f32[2,4,128,256]{3,2,1,0:T(8,128)S(1)} %get-tuple-element.46), channel_id=1, source_target_pairs={{0,4},{4,0},{8,12},{12,8},{16,20},{20,16},{24,28},{28,24},{1,5},{5... | collective-permute-start | bytes 3145736 | tf_op jit(solution)/shard_map/ppermute | solution.py:532
  76.9 14.4 %collective-permute-start.24 = (f32[2,256,256]{2,1,0:T(8,128)S(1)}, f32[2,256,256]{2,1,0:T(8,128)S(1)}, u32[]{:S(2)}, u32[]{:S(2)}) collective-permute-start(f32[2,256,256]{2,1,0:T(8,128)S(1)} %get-tuple-element.45.after_ref), channel_id=1, source_target_pairs={{0,1},{1,0},{2,3},{3,2},{4,5},{5,4},{6,7},{7,6},{8,9},{9,8},{10,11... | collective-permute-start | bytes 1572872 | tf_op jit(solution)/shard_map/ppermute | solution.py:532
  77.5 14.0 %collective-permute-start.25 = (f32[2,256,256]{2,1,0:T(8,128)S(1)}, f32[2,256,256]{2,1,0:T(8,128)S(1)}, u32[]{:S(2)}, u32[]{:S(2)}) collective-permute-start(f32[2,256,256]{2,1,0:T(8,128)S(1)} %get-tuple-element.53), channel_id=1, source_target_pairs={{0,2},{1,3},{2,0},{3,1},{4,6},{5,7},{6,4},{7,5},{8,10},{9,11},{10,... | collective-permute-start | bytes 1572872 | tf_op jit(solution)/shard_map/ppermute | solution.py:532
  81.0 12.4 %collective-permute-start.22 = (f32[2,128,256]{2,1,0:T(8,128)S(1)}, f32[2,128,256]{2,1,0:T(8,128)S(1)}, u32[]{:S(2)}, u32[]{:S(2)}) collective-permute-start(f32[2,128,256]{2,1,0:T(8,128)S(1)} %get-tuple-element.48), channel_id=1, source_target_pairs={{0,8},{4,12},{8,0},{12,4},{16,24},{20,28},{24,16},{28,20},{1,9},{5... | collective-permute-start | bytes 786440 | tf_op jit(solution)/shard_map/ppermute | solution.py:532
  83.1 14.4 %collective-permute-start.23 = (f32[2,128,256]{2,1,0:T(8,128)S(1)}, f32[2,128,256]{2,1,0:T(8,128)S(1)}, u32[]{:S(2)}, u32[]{:S(2)}) collective-permute-start(f32[2,128,256]{2,1,0:T(8,128)S(1)} %get-tuple-element.50), channel_id=1, source_target_pairs={{0,16},{4,20},{8,24},{12,28},{16,0},{20,4},{24,8},{28,12},{1,17},{... | collective-permute-start | bytes 786440 | tf_op jit(solution)/shard_map/ppermute | solution.py:532
  97.7 8.8 %collective-permute-start.28 = (f32[1,256,256]{2,1,0:T(8,128)S(1)}, f32[1,256,256]{2,1,0:T(8,128)S(1)}, u32[]{:S(2)}, u32[]{:S(2)}) collective-permute-start(f32[1,256,256]{2,1,0:T(8,128)S(1)} %get-tuple-element.59), channel_id=1, source_target_pairs={{0,2},{1,3},{2,0},{3,1},{4,6},{5,7},{6,4},{7,5},{8,10},{9,11},{10,... | collective-permute-start | bytes 786440 | tf_op jit(solution)/shard_map/ppermute | solution.py:532
  98.3 8.2 %collective-permute-start.29 = (f32[1,256,256]{2,1,0:T(8,128)S(1)}, f32[1,256,256]{2,1,0:T(8,128)S(1)}, u32[]{:S(2)}, u32[]{:S(2)}) collective-permute-start(f32[1,256,256]{2,1,0:T(8,128)S(1)} %get-tuple-element.61), channel_id=1, source_target_pairs={{0,1},{1,0},{2,3},{3,2},{4,5},{5,4},{6,7},{7,6},{8,9},{9,8},{10,11... | collective-permute-start | bytes 786440 | tf_op jit(solution)/shard_map/ppermute | solution.py:532
  99.8 6.4 %collective-permute-start.26 = (f32[1,128,256]{2,1,0:T(8,128)S(1)}, f32[1,128,256]{2,1,0:T(8,128)S(1)}, u32[]{:S(2)}, u32[]{:S(2)}) collective-permute-start(f32[1,128,256]{2,1,0:T(8,128)S(1)} %get-tuple-element.55), channel_id=1, source_target_pairs={{0,16},{4,20},{8,24},{12,28},{16,0},{20,4},{24,8},{28,12},{1,17},{... | collective-permute-start | bytes 393224 | tf_op jit(solution)/shard_map/ppermute | solution.py:532
  100.0 6.4 %collective-permute-start.27 = (f32[1,128,256]{2,1,0:T(8,128)S(1)}, f32[1,128,256]{2,1,0:T(8,128)S(1)}, u32[]{:S(2)}, u32[]{:S(2)}) collective-permute-start(f32[1,128,256]{2,1,0:T(8,128)S(1)} %get-tuple-element.57), channel_id=1, source_target_pairs={{0,8},{4,12},{8,0},{12,4},{16,24},{20,28},{24,16},{28,20},{1,9},{5... | collective-permute-start | bytes 393224 | tf_op jit(solution)/shard_map/ppermute | solution.py:532
  107.1 14.9 %collective-permute-start.38 = (f32[2,256,256]{2,1,0:T(8,128)S(1)}, f32[2,256,256]{2,1,0:T(8,128)S(1)}, u32[]{:S(2)}, u32[]{:S(2)}) collective-permute-start(f32[2,256,256]{2,1,0:T(8,128)S(1)} %get-tuple-element.63.refs_11_), channel_id=1, source_target_pairs={{0,1},{1,0},{2,3},{3,2},{4,5},{5,4},{6,7},{7,6},{8,9},{9,8},{10,11... | collective-permute-start | bytes 1572872 | tf_op jit(solution)/shard_map/ppermute | solution.py:532
  107.6 14.3 %collective-permute-start.39 = (f32[2,256,256]{2,1,0:T(8,128)S(1)}, f32[2,256,256]{2,1,0:T(8,128)S(1)}, u32[]{:S(2)}, u32[]{:S(2)}) collective-permute-start(f32[2,256,256]{2,1,0:T(8,128)S(1)} %get-tuple-element.63.refs_11_), channel_id=1, source_target_pairs={{0,2},{1,3},{2,0},{3,1},{4,6},{5,7},{6,4},{7,5},{8,10},{9,11},{10,... | collective-permute-start | bytes 1572872 | tf_op jit(solution)/shard_map/ppermute | solution.py:532
  109.2 12.0 %collective-permute-start.31 = (f32[264,256]{1,0:T(8,128)S(1)}, f32[264,256]{1,0:T(8,128)S(1)}, u32[]{:S(2)}, u32[]{:S(2)}) collective-permute-start(f32[264,256]{1,0:T(8,128)S(1)} %get-tuple-element.62.refs_0_.refs_4_), channel_id=1, source_target_pairs={{0,16},{4,20},{8,24},{12,28},{16,0},{20,4},{24,8},{28,12},{1,17},{... | collective-permute-start | bytes 811016 | tf_op jit(solution)/shard_map/ppermute | solution.py:532
  110.4 11.6 %collective-permute-start.30 = (f32[264,256]{1,0:T(8,128)S(1)}, f32[264,256]{1,0:T(8,128)S(1)}, u32[]{:S(2)}, u32[]{:S(2)}) collective-permute-start(f32[264,256]{1,0:T(8,128)S(1)} %get-tuple-element.62.refs_0_.refs_4_), channel_id=1, source_target_pairs={{0,8},{4,12},{8,0},{12,4},{16,24},{20,28},{24,16},{28,20},{1,9},{5... | collective-permute-start | bytes 811016 | tf_op jit(solution)/shard_map/ppermute | solution.py:532
  121.2 7.2 %collective-permute-start.32 = (f32[264,256]{1,0:T(8,128)S(1)}, f32[264,256]{1,0:T(8,128)S(1)}, u32[]{:S(2)}, u32[]{:S(2)}) collective-permute-start(f32[264,256]{1,0:T(8,128)S(1)} %collective-permute-done.31.refs_2_.far_ref.refs_8_), channel_id=1, source_target_pairs={{0,8},{4,12},{8,0},{12,4},{16,24},{20,28},{24,16},{28,20},{1,9},{5... | collective-permute-start | bytes 811016 | tf_op jit(solution)/shard_map/ppermute | solution.py:532
  122.1 17.3 %collective-permute-start.40 = (f32[2,264,256]{2,1,0:T(8,128)S(1)}, f32[2,264,256]{2,1,0:T(8,128)S(1)}, u32[]{:S(2)}, u32[]{:S(2)}) collective-permute-start(f32[2,264,256]{2,1,0:T(8,128)S(1)} %get-tuple-element.64), channel_id=1, source_target_pairs={{0,4},{4,0},{8,12},{12,8},{16,20},{20,16},{24,28},{28,24},{1,5},{5... | collective-permute-start | bytes 1622024 | tf_op jit(solution)/shard_map/ppermute | solution.py:532
  122.1 8.7 %collective-permute-start.41 = (f32[256,256]{1,0:T(8,128)S(1)}, f32[256,256]{1,0:T(8,128)S(1)}, u32[]{:S(2)}, u32[]{:S(2)}) collective-permute-start(f32[256,256]{1,0:T(8,128)S(1)} %get-tuple-element.65), channel_id=1, source_target_pairs={{0,1},{1,0},{2,3},{3,2},{4,5},{5,4},{6,7},{7,6},{8,9},{9,8},{10,11... | collective-permute-start | bytes 786440 | tf_op jit(solution)/shard_map/ppermute | solution.py:532
  123.7 8.4 %collective-permute-start.42 = (f32[256,256]{1,0:T(8,128)S(1)}, f32[256,256]{1,0:T(8,128)S(1)}, u32[]{:S(2)}, u32[]{:S(2)}) collective-permute-start(f32[256,256]{1,0:T(8,128)S(1)} %get-tuple-element.66), channel_id=1, source_target_pairs={{0,2},{1,3},{2,0},{3,1},{4,6},{5,7},{6,4},{7,5},{8,10},{9,11},{10,... | collective-permute-start | bytes 786440 | tf_op jit(solution)/shard_map/ppermute | solution.py:532
  124.2 11.5 %collective-permute-start.37 = (f32[264,256]{1,0:T(8,128)S(1)}, f32[264,256]{1,0:T(8,128)S(1)}, u32[]{:S(2)}, u32[]{:S(2)}) collective-permute-start(f32[264,256]{1,0:T(8,128)S(1)} %get-tuple-element.62.refs_0_.refs_4_), channel_id=1, source_target_pairs={{0,4},{4,0},{8,12},{12,8},{16,20},{20,16},{24,28},{28,24},{1,5},{5... | collective-permute-start | bytes 811016 | tf_op jit(solution)/shard_map/ppermute | solution.py:532
  132.1 7.3 %collective-permute-start.43 = (f32[264,256]{1,0:T(8,128)S(1)}, f32[264,256]{1,0:T(8,128)S(1)}, u32[]{:S(2)}, u32[]{:S(2)}) collective-permute-start(f32[264,256]{1,0:T(8,128)S(1)} %copy_after.1), channel_id=1, source_target_pairs={{0,4},{4,0},{8,12},{12,8},{16,20},{20,16},{24,28},{28,24},{1,5},{5... | collective-permute-start | bytes 811016 | tf_op jit(solution)/shard_map/ppermute | solution.py:532
  133.7 4.5 %collective-permute-start.34 = (f32[2,8,128]{2,1,0:T(8,128)S(1)}, f32[2,8,128]{2,1,0:T(8,128)S(1)}, u32[]{:S(2)}, u32[]{:S(2)}) collective-permute-start(f32[2,8,128]{2,1,0:T(8,128)S(1)} %add.24.refs_3_), channel_id=1, source_target_pairs={{0,3},{1,2},{2,1},{3,0},{4,7},{5,6},{6,5},{7,4},{8,11},{9,10},{10,... | collective-permute-start | bytes 24584 | tf_op jit(solution)/shard_map/ppermute | solution.py:532
  134.2 4.1 %collective-permute-start.35 = (f32[2,8,128]{2,1,0:T(8,128)S(1)}, f32[2,8,128]{2,1,0:T(8,128)S(1)}, u32[]{:S(2)}, u32[]{:S(2)}) collective-permute-start(f32[2,8,128]{2,1,0:T(8,128)S(1)} %add.24.refs_3_), channel_id=1, source_target_pairs={{0,2},{1,3},{2,0},{3,1},{4,6},{5,7},{6,4},{7,5},{8,10},{9,11},{10,... | collective-permute-start | bytes 24584 | tf_op jit(solution)/shard_map/ppermute | solution.py:532
  (12 other events, 34.9 us)

commit v10 on v9

--- a/solution.py
+++ b/solution.py
@@ -55,7 +55,7 @@
 LOG2E = 1.4426950408889634
 
 
-def score_kernel(slow, fast, protos, t_ref, col_ref, den_ref, ubt_ref, cb_ref, raw_s, w_s, ub_s, den_s, sems):
+def score_kernel(slow, fast, protos, t_ref, col_ref, den_ref, ub_ref, cb_ref, raw_s, w_s, den_s, sems):
     clips, feats = slow.shape
     count = protos.shape[0]
     loads = []
@@ -70,9 +70,7 @@
             rows = pl.ds(first, 256)
             x = raw_s[v, rows, :].astype(jnp.float32)
             length = jnp.sqrt(jnp.sum(x * x, axis=-1, keepdims=True) + 1e-12)
-            u = x / length
-            ub_s[v, rows, :] = u.astype(jnp.bfloat16)
-            ubt_ref[:, v * clips + first : v * clips + first + 256] = u.T.astype(jnp.bfloat16)
+            ub_ref[v, rows, :] = (x / length).astype(jnp.bfloat16)
     den_s[...] = jnp.zeros_like(den_s)
     loads[2].wait()
 
@@ -87,7 +85,7 @@
             cols = jnp.zeros((8, 256), jnp.float32)
             for r in range(0, clips, 512):
                 s = jnp.dot(
-                    ub_s[v, r : r + 512, :], weights, preferred_element_type=jnp.float32
+                    ub_ref[v, r : r + 512, :], weights, preferred_element_type=jnp.float32
                 )
                 for q in range(0, 512, 64):
                     rows = pl.ds(r + q, 64)
@@ -118,7 +116,7 @@
             pltpu.VMEM((2, clips, count), jnp.float32),
             jax.ShapeDtypeStruct((2 * count // LANES, LANES), jnp.float32),
             jax.ShapeDtypeStruct((2 * clips // LANES, LANES), jnp.float32),
-            jax.ShapeDtypeStruct((feats, 2 * clips), jnp.bfloat16),
+            jax.ShapeDtypeStruct((2, clips, feats), jnp.bfloat16),
             jax.ShapeDtypeStruct((count, feats), jnp.bfloat16),
         ),
         in_specs=[pl.BlockSpec(memory_space=pltpu.HBM)] * 3,
@@ -126,13 +124,35 @@
         scratch_shapes=[
             pltpu.VMEM((2, clips, feats), jnp.bfloat16),
             pltpu.VMEM((count, feats), jnp.float32),
-            pltpu.VMEM((2, clips, feats), jnp.bfloat16),
             pltpu.VMEM((2, clips, LANES), jnp.float32),
             pltpu.SemaphoreType.DMA((3,)),
         ],
         compiler_params=params(24),
         name="scores",
     )(*[pltpu.with_memory_space_constraint(x, pltpu.HBM) for x in (slow, fast, protos)])
+
+
+def turn_kernel(ub_ref, ubt_ref):
+    clips = ub_ref.shape[1]
+    for v in range(2):
+        for first in range(0, clips, 256):
+            u = ub_ref[v, first : first + 256, :].astype(jnp.float32)
+            ubt_ref[:, v * clips + first : v * clips + first + 256] = u.T.astype(jnp.bfloat16)
+
+
+def turned(ub):
+    clips, feats = ub.shape[1:]
+    return pl.pallas_call(
+        turn_kernel,
+        out_shape=jax.ShapeDtypeStruct((feats, 2 * clips), ub.dtype),
+        in_specs=[vmem_spec()],
+        out_specs=vmem_spec(),
+        compiler_params=params(8),
+        cost_estimate=pl.CostEstimate(
+            flops=2 * clips * feats, bytes_accessed=4 * MIB, transcendentals=0
+        ),
+        name="turned",
+    )(ub)
 
 
 def row_kernel(protos_all, extra, t_ref, den_ref, *refs):
@@ -578,54 +598,6 @@
     return [x for term in terms for x in term]
 
 
-def forward_kernel(near_ref, far_ref, x_ref, y_ref, pack_ref, slow_ref, fast_ref):
-    pack_ref[0] = near_ref[...]
-    pack_ref[1] = far_ref[...]
-    slow_ref[...] = y_ref[0]
-    fast_ref[...] = x_ref[1]
-
-
-def forwards(near, far, x, y):
-    view = jax.ShapeDtypeStruct(x.shape[1:], x.dtype)
-    return pl.pallas_call(
-        forward_kernel,
-        out_shape=(jax.ShapeDtypeStruct((2,) + near.shape, near.dtype), view, view),
-        in_specs=[vmem_spec()] * 4,
-        out_specs=(vmem_spec(),) * 3,
-        compiler_params=params(10),
-        name="forwards",
-    )(near, far, x, y)
-
-
-def copy_kernel(x_ref, *refs):
-    refs[-1][...] = x_ref[...]
-
-
-def copy_after(x, arrived):
-    return pl.pallas_call(
-        copy_kernel,
-        out_shape=jax.ShapeDtypeStruct(x.shape, x.dtype),
-        in_specs=[vmem_spec()] + [pl.BlockSpec(memory_space=pl.ANY)] * len(arrived),
-        out_specs=vmem_spec(),
-        compiler_params=params(8),
-        name="copy_after",
-    )(x, *arrived)
-
-
-def gather_pairs(proto, embed):
-    y, x = swap(embed, "proto", 2), swap(embed, "proto", 1)
-    far, near = swap(proto, "batch", 4), swap(proto, "batch", 2)
-    core = swap(proto, "batch", 1)
-    pack, slow, fast = forwards(near, far, x, y)
-    slow, fast = swap(slow, "proto", 1), swap(fast, "proto", 2)
-    corner = swap(far, "batch", 2)
-    core_pack = swap(pack, "batch", 1)
-    core_corner = swap(copy_after(corner, [slow, fast]), "batch", 1)
-    whole = [proto, core, near, (core_pack, 0), far, (core_pack, 1), corner, core_corner]
-    protos = [piece if isinstance(piece, tuple) else (piece, None) for piece in whole]
-    return protos, [[(embed, v), (x, v), (y, v), (last, None)] for v, last in enumerate((slow, fast))]
-
-
 def gather_batch(own):
     bits = list(reversed(range(lax.axis_size("batch").bit_length() - 1)))
     pieces = {0: own}
@@ -665,7 +637,8 @@
     batch_bits, proto_bits = bits_of("batch"), bits_of("proto")
     me_batch, me_proto = lax.axis_index("batch"), lax.axis_index("proto")
 
-    t, col, den, unit_bt, proto_b = scores(slow_embed, fast_embed, prototypes)
+    t, col, den, unit_b, proto_b = scores(slow_embed, fast_embed, prototypes)
+    unit_bt = turned(unit_b)
     for iteration in range(ITERS):
         rows, r = row_pass(t, den, batch_parts(col), protos_all, iteration == 0)
         row_parts = proto_parts(rows)
@@ -696,13 +669,9 @@
         groups.append(("proto", proto_orders[v], shares[2 * v], shares[2 * v + 1]))
     terms = scatter_sums(groups)
     grad_proto, grad_embed = project_shares(raws, terms)
-    if batch_bits == 3 and proto_bits == 2:
-        proto_pieces, view_pieces = gather_pairs(grad_proto, grad_embed)
-    else:
-        proto_pieces = gather_batch(grad_proto)
-        view_pieces = gather_views(grad_embed, (proto_orders[1], proto_orders[0]))
-    square = sum_squares(proto_pieces[::2], proto_rows)
-    squares = proto_parts(square + swap(square, "batch", 1))
+    proto_pieces = gather_batch(grad_proto)
+    view_pieces = gather_views(grad_embed, (proto_orders[1], proto_orders[0]))
+    squares = proto_parts(sum_squares(proto_pieces, proto_rows))
     sizes = (proto_rows, clip_rows, clip_rows)
     groups = [proto_pieces] + view_pieces
     return finish((proto_entries, embed_entries), squares, groups, sizes)

time: 142 us -> 140 us (0.986)
  waiting for transfers between devices: 62.5 us -> 60.1 us
    ppermute x44, waiting for transfers between devices: 62.5 us -> 60.1 us  [swap(): lax.ppermute(own, axis, [(i, i ^ mask) for i in range(lax.axis_size(axis))])]
  transfers between devices with their start and end apart: 44 -> 44, of which waited for: 34 -> 32; matrix products, arithmetic and copies ran while one was open for 1% -> 1% of each run, Pallas kernels for 3% -> 3%
where the time goes in v10:
time: 140 us
  waiting for transfers between devices  60.1 us (43%)
  starting transfers between devices  42 us (30%)
  Pallas kernels  34.8 us (25%)
  local copies, waits for them, and re-layouts  1.99 us (1%)
    ppermute x44, waiting for transfers between devices, swap(): lax.ppermute(own, axis, [(i, i ^ mask) for i in range(lax.axis_size(axis))])  60.1 us
    ppermute x44, starting transfers between devices, swap(): lax.ppermute(own, axis, [(i, i ^ mask) for i in range(lax.axis_size(axis))])  42 us
    pallas_call x1, Pallas kernels, scores(): pl.pallas_call(score_kernel, out_shape=(pltpu.VMEM((2, clips, count), jnp...  8.38 us
    pallas_call x1, Pallas kernels, send_gradients(): pl.pallas_call(functools.partial(send_kernel, orders, len(row_parts)), ou...  7.04 us
    pallas_call x3, Pallas kernels, row_pass(): pl.pallas_call(functools.partial(row_kernel, protos_all, extra), out_shap...  6.82 us
    pallas_call x2, Pallas kernels, col_pass(): pl.pallas_call(functools.partial(col_kernel, clips_all), out_shape=jax.Sh...  4.65 us
  transfers between devices with their start and end apart: 44, of which 32 were waited for; matrix products, arithmetic and copies ran while one was open for 1% of the time, Pallas kernels for 3%

profile of v10, /device:TPU:0, one launch (start us, length us, event | category | flops | bytes accessed | tf_op | source)
XLA Modules:
  0.0 139.9 jit_solution(11804356640943028039)
XLA Ops:
  0.6 8.4 %scores.1 = (f32[2,1024,2048]{2,1,0:T(8,128)S(1)}, f32[32,128]{1,0:T(8,128)S(1)}, f32[16,128]{1,0:T(8,128)S(1)}, bf16[2,1024,256]{2,1,0:T(8,128)(2,1)S(1)}, bf16[2048,256]{1,0:T(8,128)(2,1)S(1)}) custom-call(bf16[1024,256]{1,0:T(8,128)(2,1)} %slow.1, bf16[1024,256]{1,0:T(8,128)(2,1)} %fast.1, f32[2048,256]{1,0:T(8,128)} %protos.1), custom_call_target="tpu_custom_call" | custom-call | tf_op jit(solution)/shard_map/scores/pallas_call | solution.py:113
  10.4 4.9 %collective-permute-start.1 = (f32[32,128]{1,0:T(8,128)S(1)}, f32[32,128]{1,0:T(8,128)S(1)}, u32[]{:S(2)}, u32[]{:S(2)}) collective-permute-start(f32[32,128]{1,0:T(8,128)S(1)} %add.18.refs_3_), channel_id=1, source_target_pairs={{0,24},{4,28},{8,16},{12,20},{16,8},{20,12},{24,0},{28,4},{1,25},{... | collective-permute-start | bytes 49160 | tf_op jit(solution)/shard_map/ppermute | solution.py:552
  17.0 2.9 %collective-permute-done.2.refs_1_ = f32[32,128]{1,0:T(8,128)S(1)} collective-permute-done((f32[32,128]{1,0:T(8,128)S(1)}, f32[32,128]{1,0:T(8,128)S(1)}, u32[]{:S(2)}, u32[]{:S(2)}) %collective-permute-start.2) | collective-permute-done | bytes 16416 | tf_op jit(solution)/shard_map/ppermute | solution.py:552
  20.0 2.4 %row_pass.3 = (f32[32,128]{1,0:T(8,128)S(1)}, f32[32,128]{1,0:T(8,128)}) custom-call(f32[2,1024,2048]{2,1,0:T(8,128)S(1)} %get-tuple-element.32.t_ref, f32[16,128]{1,0:T(8,128)S(1)} %get-tuple-element.33.den_ref, f32[32,128]{1,0:T(8,128)S(1)} %collective-permute-done.1.refs_0_, f32[32,128]{1,0:T(8,128)S(1)} %collective-permute-done.2.refs_1_, ...), custom_call_target="tpu_custom_call" | custom-call | tf_op jit(solution)/shard_map/row_pass/pallas_call | solution.py:184
  22.3 2.4 %collective-permute-start.4 = (f32[32,128]{1,0:T(8,128)S(1)}, f32[32,128]{1,0:T(8,128)S(1)}, u32[]{:S(2)}, u32[]{:S(2)}) collective-permute-start(f32[32,128]{1,0:T(8,128)S(1)} %get-tuple-element.35.refs_3_.refs_7_), channel_id=1, source_target_pairs={{0,3},{1,2},{2,1},{3,0},{4,7},{5,6},{6,5},{7,4},{8,11},{9,10},{10,... | collective-permute-start | bytes 49160 | tf_op jit(solution)/shard_map/ppermute | solution.py:552
  27.0 1.5 %collective-permute-done.5.refs_1_.refs_5_ = f32[32,128]{1,0:T(8,128)S(1)} collective-permute-done((f32[32,128]{1,0:T(8,128)S(1)}, f32[32,128]{1,0:T(8,128)S(1)}, u32[]{:S(2)}, u32[]{:S(2)}) %collective-permute-start.5) | collective-permute-done | bytes 16416 | tf_op jit(solution)/shard_map/ppermute | solution.py:552
  29.0 2.3 %col_pass.2 = f32[32,128]{1,0:T(8,128)S(1)} custom-call(f32[2,1024,2048]{2,1,0:T(8,128)S(1)} %get-tuple-element.32.t_ref, f32[32,128]{1,0:T(8,128)S(1)} %collective-permute-done.4.refs_0_.refs_4_, f32[32,128]{1,0:T(8,128)S(1)} %collective-permute-done.5.refs_1_.refs_5_, f32[32,128]{1,0:T(8,128)S(1)} %collective-permute-done.6.refs_2_.refs_6_, ...), custom_call_target="tpu_custom_call" | custom-call | tf_op jit(solution)/shard_map/col_pass/pallas_call | solution.py:224
  32.6 3.5 %collective-permute-start.8 = (f32[32,128]{1,0:T(8,128)S(1)}, f32[32,128]{1,0:T(8,128)S(1)}, u32[]{:S(2)}, u32[]{:S(2)}) collective-permute-start(f32[32,128]{1,0:T(8,128)S(1)} %add.19.refs_3_), channel_id=1, source_target_pairs={{0,24},{4,28},{8,16},{12,20},{16,8},{20,12},{24,0},{28,4},{1,25},{... | collective-permute-start | bytes 49160 | tf_op jit(solution)/shard_map/ppermute | solution.py:552
  36.3 2.0 %collective-permute-done.8.refs_0_ = f32[32,128]{1,0:T(8,128)S(1)} collective-permute-done((f32[32,128]{1,0:T(8,128)S(1)}, f32[32,128]{1,0:T(8,128)S(1)}, u32[]{:S(2)}, u32[]{:S(2)}) %collective-permute-start.8) | collective-permute-done | bytes 16416 | tf_op jit(solution)/shard_map/ppermute | solution.py:552
  38.4 2.3 %collective-permute-done.9.refs_1_ = f32[32,128]{1,0:T(8,128)S(1)} collective-permute-done((f32[32,128]{1,0:T(8,128)S(1)}, f32[32,128]{1,0:T(8,128)S(1)}, u32[]{:S(2)}, u32[]{:S(2)}) %collective-permute-start.9) | collective-permute-done | bytes 16416 | tf_op jit(solution)/shard_map/ppermute | solution.py:552
  40.7 2.4 %row_pass.4 = (f32[16,128]{1,0:T(8,128)S(1)}, f32[32,128]{1,0:T(8,128)}) custom-call(f32[2,1024,2048]{2,1,0:T(8,128)S(1)} %get-tuple-element.32.t_ref, f32[16,128]{1,0:T(8,128)S(1)} %get-tuple-element.33.den_ref, f32[32,128]{1,0:T(8,128)S(1)} %collective-permute-done.8.refs_0_, f32[32,128]{1,0:T(8,128)S(1)} %collective-permute-done.9.refs_1_, ...), custom_call_target="tpu_custom_call" | custom-call | tf_op jit(solution)/shard_map/row_pass/pallas_call | solution.py:184
  43.1 1.5 %collective-permute-start.11 = (f32[16,128]{1,0:T(8,128)S(1)}, f32[16,128]{1,0:T(8,128)S(1)}, u32[]{:S(2)}, u32[]{:S(2)}) collective-permute-start(f32[16,128]{1,0:T(8,128)S(1)} %get-tuple-element.36.refs_3_), channel_id=1, source_target_pairs={{0,3},{1,2},{2,1},{3,0},{4,7},{5,6},{6,5},{7,4},{8,11},{9,10},{10,... | collective-permute-start | bytes 24584 | tf_op jit(solution)/shard_map/ppermute | solution.py:552
  48.7 2.3 %col_pass.3 = f32[32,128]{1,0:T(8,128)S(1)} custom-call(f32[2,1024,2048]{2,1,0:T(8,128)S(1)} %get-tuple-element.32.t_ref, f32[16,128]{1,0:T(8,128)S(1)} %collective-permute-done.11.refs_0_, f32[16,128]{1,0:T(8,128)S(1)} %collective-permute-done.12.refs_1_, f32[16,128]{1,0:T(8,128)S(1)} %collective-permute-done.13.refs_2_, ...), custom_call_target="tpu_custom_call" | custom-call | tf_op jit(solution)/shard_map/col_pass/pallas_call | solution.py:224
  53.2 3.5 %collective-permute-start.17 = (f32[32,128]{1,0:T(8,128)S(1)}, f32[32,128]{1,0:T(8,128)S(1)}, u32[]{:S(2)}, u32[]{:S(2)}) collective-permute-start(f32[32,128]{1,0:T(8,128)S(1)} %add.20.refs_3_), channel_id=1, source_target_pairs={{0,8},{4,12},{8,0},{12,4},{16,24},{20,28},{24,16},{28,20},{1,9},{5... | collective-permute-start | bytes 49160 | tf_op jit(solution)/shard_map/ppermute | solution.py:552
  58.4 2.1 %row_pass.5 = (f32[16,128]{1,0:T(8,128)S(1)}, f32[32,128]{1,0:T(8,128)S(1)}) custom-call(f32[2,1024,2048]{2,1,0:T(8,128)S(1)} %get-tuple-element.32.t_ref, f32[16,128]{1,0:T(8,128)S(1)} %get-tuple-element.33.den_ref, f32[32,128]{1,0:T(8,128)S(1)} %collective-permute-done.15.refs_0_, f32[32,128]{1,0:T(8,128)S(1)} %collective-permute-done.16.refs_1_, ...), custom_call_target="tpu_custom_call" | custom-call | tf_op jit(solution)/shard_map/row_pass/pallas_call | solution.py:184
  60.5 2.5 %collective-permute-start.18 = (f32[16,128]{1,0:T(8,128)S(1)}, f32[16,128]{1,0:T(8,128)S(1)}, u32[]{:S(2)}, u32[]{:S(2)}) collective-permute-start(f32[16,128]{1,0:T(8,128)S(1)} %get-tuple-element.39.refs_3_), channel_id=1, source_target_pairs={{0,3},{1,2},{2,1},{3,0},{4,7},{5,6},{6,5},{7,4},{8,11},{9,10},{10,... | collective-permute-start | bytes 24584 | tf_op jit(solution)/shard_map/ppermute | solution.py:552
  65.2 1.5 %collective-permute-done.19.refs_1_ = f32[16,128]{1,0:T(8,128)S(1)} collective-permute-done((f32[16,128]{1,0:T(8,128)S(1)}, f32[16,128]{1,0:T(8,128)S(1)}, u32[]{:S(2)}, u32[]{:S(2)}) %collective-permute-start.19) | collective-permute-done | bytes 8224 | tf_op jit(solution)/shard_map/ppermute | solution.py:552
  67.2 7.0 %send_gradients.1 = (f32[2,4,128,256]{3,2,1,0:T(8,128)S(1)}, bf16[2048,2048]{1,0:T(8,128)(2,1)S(1)}) custom-call(f32[2,1024,2048]{2,1,0:T(8,128)S(1)} %get-tuple-element.32.t_ref, f32[32,128]{1,0:T(8,128)S(1)} %get-tuple-element.37.r_ref, bf16[256,2048]{1,0:T(8,128)(2,1)S(1)} %turned.1.ubt_ref, f32[16,128]{1,0:T(8,128)S(1)} %collective-permute-done.18.refs_0_, ...), custom_call_target="tpu_custom_call" | custom-call | flops 1073741824 | bytes 20971520 | tf_op jit(solution)/shard_map/send_gradients/pallas_call | solution.py:311
  74.3 2.3 %embed_gradients.1 = (f32[2,256,256]{2,1,0:T(8,128)S(1)}, f32[2,256,256]{2,1,0:T(8,128)S(1)}, f32[2,256,256]{2,1,0:T(8,128)S(1)}, f32[2,256,256]{2,1,0:T(8,128)S(1)}) custom-call(bf16[2048,2048]{1,0:T(8,128)(2,1)S(1)} %get-tuple-element.40.g_ref, bf16[2048,256]{1,0:T(8,128)(2,1)S(1)} %get-tuple-element.41.cb_ref), custom_call_target="tpu_custom_call" | custom-call | flops 2147483648 | bytes 11534336 | tf_op jit(solution)/shard_map/embed_gradients/pallas_call | solution.py:351
  77.3 1.5 %collective-permute-start.25 = (f32[2,256,256]{2,1,0:T(8,128)S(1)}, f32[2,256,256]{2,1,0:T(8,128)S(1)}, u32[]{:S(2)}, u32[]{:S(2)}) collective-permute-start(f32[2,256,256]{2,1,0:T(8,128)S(1)} %get-tuple-element.50), channel_id=1, source_target_pairs={{0,2},{1,3},{2,0},{3,1},{4,6},{5,7},{6,4},{7,5},{8,10},{9,11},{10,... | collective-permute-start | bytes 1572872 | tf_op jit(solution)/shard_map/ppermute | solution.py:552
  78.8 2.1 %keep_gradients.1.refs_0_ = f32[2,4,128,256]{3,2,1,0:T(8,128)S(1)} custom-call(bf16[2048,2048]{1,0:T(8,128)(2,1)S(1)} %get-tuple-element.40.g_ref, bf16[256,2048]{1,0:T(8,128)(2,1)S(1)} %turned.1.ubt_ref, f32[2,256,256]{2,1,0:T(8,128)S(1)} %get-tuple-element.42.after_ref), custom_call_target="tpu_custom_call" | custom-call | flops 1073741824 | bytes 6291456 | tf_op jit(solution)/shard_map/keep_gradients/pallas_call | solution.py:380
  81.0 2.1 %collective-permute-start.22 = (f32[2,128,256]{2,1,0:T(8,128)S(1)}, f32[2,128,256]{2,1,0:T(8,128)S(1)}, u32[]{:S(2)}, u32[]{:S(2)}) collective-permute-start(f32[2,128,256]{2,1,0:T(8,128)S(1)} %get-tuple-element.45), channel_id=1, source_target_pairs={{0,8},{4,12},{8,0},{12,4},{16,24},{20,28},{24,16},{28,20},{1,9},{5... | collective-permute-start | bytes 786440 | tf_op jit(solution)/shard_map/ppermute | solution.py:552
  84.0 7.1 %collective-permute-done.24.refs_5_ = f32[2,256,256]{2,1,0:T(8,128)S(1)} collective-permute-done((f32[2,256,256]{2,1,0:T(8,128)S(1)}, f32[2,256,256]{2,1,0:T(8,128)S(1)}, u32[]{:S(2)}, u32[]{:S(2)}) %collective-permute-start.24) | collective-permute-done | bytes 524320 | tf_op jit(solution)/shard_map/ppermute | solution.py:552
  91.3 2.1 %collective-permute-done.22.refs_1_ = f32[2,128,256]{2,1,0:T(8,128)S(1)} collective-permute-done((f32[2,128,256]{2,1,0:T(8,128)S(1)}, f32[2,128,256]{2,1,0:T(8,128)S(1)}, u32[]{:S(2)}, u32[]{:S(2)}) %collective-permute-start.22) | collective-permute-done | bytes 262176 | tf_op jit(solution)/shard_map/ppermute | solution.py:552
  93.4 4.1 %collective-permute-done.23.refs_3_ = f32[2,128,256]{2,1,0:T(8,128)S(1)} collective-permute-done((f32[2,128,256]{2,1,0:T(8,128)S(1)}, f32[2,128,256]{2,1,0:T(8,128)S(1)}, u32[]{:S(2)}, u32[]{:S(2)}) %collective-permute-start.23) | collective-permute-done | bytes 262176 | tf_op jit(solution)/shard_map/ppermute | solution.py:552
  102.0 4.3 %collective-permute-done.26.refs_1_ = f32[1,128,256]{2,1,0:T(8,128)S(1)} collective-permute-done((f32[1,128,256]{2,1,0:T(8,128)S(1)}, f32[1,128,256]{2,1,0:T(8,128)S(1)}, u32[]{:S(2)}, u32[]{:S(2)}) %collective-permute-start.26) | collective-permute-done | bytes 131104 | tf_op jit(solution)/shard_map/ppermute | solution.py:552
  107.1 1.6 %collective-permute-start.41 = (f32[2,256,256]{2,1,0:T(8,128)S(1)}, f32[2,256,256]{2,1,0:T(8,128)S(1)}, u32[]{:S(2)}, u32[]{:S(2)}) collective-permute-start(f32[2,256,256]{2,1,0:T(8,128)S(1)} %get-tuple-element.60.refs_12_), channel_id=1, source_target_pairs={{0,2},{1,3},{2,0},{3,1},{4,6},{5,7},{6,4},{7,5},{8,10},{9,11},{10,... | collective-permute-start | bytes 1572872 | tf_op jit(solution)/shard_map/ppermute | solution.py:552
  110.6 10.3 %collective-permute-done.33.refs_4_.refs_8_ = f32[264,256]{1,0:T(8,128)S(1)} collective-permute-done((f32[264,256]{1,0:T(8,128)S(1)}, f32[264,256]{1,0:T(8,128)S(1)}, u32[]{:S(2)}, u32[]{:S(2)}) %collective-permute-start.33) | collective-permute-done | bytes 270368 | tf_op jit(solution)/shard_map/ppermute | solution.py:552
  122.5 1.9 %collective-permute-start.42 = (f32[256,256]{1,0:T(8,128)S(1)}, f32[256,256]{1,0:T(8,128)S(1)}, u32[]{:S(2)}, u32[]{:S(2)}) collective-permute-start(f32[256,256]{1,0:T(8,128)S(1)} %slice_bitcast_fusion.1), channel_id=1, source_target_pairs={{0,1},{1,0},{2,3},{3,2},{4,5},{5,4},{6,7},{7,6},{8,9},{9,8},{10,11... | collective-permute-start | bytes 786440 | tf_op jit(solution)/shard_map/ppermute | solution.py:552
  124.4 3.9 %collective-permute-done.35.refs_6_.refs_10_ = f32[264,256]{1,0:T(8,128)S(1)} collective-permute-done((f32[264,256]{1,0:T(8,128)S(1)}, f32[264,256]{1,0:T(8,128)S(1)}, u32[]{:S(2)}, u32[]{:S(2)}) %collective-permute-start.35) | collective-permute-done | bytes 270368 | tf_op jit(solution)/shard_map/ppermute | solution.py:552
  133.4 4.0 %collective-permute-done.43.refs_16_ = f32[256,256]{1,0:T(8,128)S(1)} collective-permute-done((f32[256,256]{1,0:T(8,128)S(1)}, f32[256,256]{1,0:T(8,128)S(1)}, u32[]{:S(2)}, u32[]{:S(2)}) %collective-permute-start.43) | collective-permute-done | bytes 262176 | tf_op jit(solution)/shard_map/ppermute | solution.py:552
  137.5 2.2 %finish.1 = (f32[2048,256]{1,0:T(8,128)}, f32[1024,256]{1,0:T(8,128)}, f32[1024,256]{1,0:T(8,128)}) custom-call(f32[2,8,128]{2,1,0:T(8,128)S(1)} %collective-permute-done.37.refs_0_, f32[2,8,128]{2,1,0:T(8,128)S(1)} %collective-permute-done.38.refs_1_, f32[2,8,128]{2,1,0:T(8,128)S(1)} %collective-permute-done.39.refs_2_, ...), custom_call_target="tpu_custom_call" | custom-call | tf_op jit(solution)/shard_map/finish/pallas_call | solution.py:540
  (78 shorter events, 33.8 us)
Async XLA Ops:
  10.4 6.7 %collective-permute-start.1 = (f32[32,128]{1,0:T(8,128)S(1)}, f32[32,128]{1,0:T(8,128)S(1)}, u32[]{:S(2)}, u32[]{:S(2)}) collective-permute-start(f32[32,128]{1,0:T(8,128)S(1)} %add.18.refs_3_), channel_id=1, source_target_pairs={{0,24},{4,28},{8,16},{12,20},{16,8},{20,12},{24,0},{28,4},{1,25},{... | collective-permute-start | bytes 49160 | tf_op jit(solution)/shard_map/ppermute | solution.py:552
  15.3 4.6 %collective-permute-start.2 = (f32[32,128]{1,0:T(8,128)S(1)}, f32[32,128]{1,0:T(8,128)S(1)}, u32[]{:S(2)}, u32[]{:S(2)}) collective-permute-start(f32[32,128]{1,0:T(8,128)S(1)} %add.18.refs_3_), channel_id=1, source_target_pairs={{0,16},{4,20},{8,24},{12,28},{16,0},{20,4},{24,8},{28,12},{1,17},{... | collective-permute-start | bytes 49160 | tf_op jit(solution)/shard_map/ppermute | solution.py:552
  15.3 4.6 %collective-permute-start.3 = (f32[32,128]{1,0:T(8,128)S(1)}, f32[32,128]{1,0:T(8,128)S(1)}, u32[]{:S(2)}, u32[]{:S(2)}) collective-permute-start(f32[32,128]{1,0:T(8,128)S(1)} %add.18.refs_3_), channel_id=1, source_target_pairs={{0,8},{4,12},{8,0},{12,4},{16,24},{20,28},{24,16},{28,20},{1,9},{5... | collective-permute-start | bytes 49160 | tf_op jit(solution)/shard_map/ppermute | solution.py:552
  22.3 4.6 %collective-permute-start.4 = (f32[32,128]{1,0:T(8,128)S(1)}, f32[32,128]{1,0:T(8,128)S(1)}, u32[]{:S(2)}, u32[]{:S(2)}) collective-permute-start(f32[32,128]{1,0:T(8,128)S(1)} %get-tuple-element.35.refs_3_.refs_7_), channel_id=1, source_target_pairs={{0,3},{1,2},{2,1},{3,0},{4,7},{5,6},{6,5},{7,4},{8,11},{9,10},{10,... | collective-permute-start | bytes 49160 | tf_op jit(solution)/shard_map/ppermute | solution.py:552
  32.6 5.8 %collective-permute-start.8 = (f32[32,128]{1,0:T(8,128)S(1)}, f32[32,128]{1,0:T(8,128)S(1)}, u32[]{:S(2)}, u32[]{:S(2)}) collective-permute-start(f32[32,128]{1,0:T(8,128)S(1)} %add.19.refs_3_), channel_id=1, source_target_pairs={{0,24},{4,28},{8,16},{12,20},{16,8},{20,12},{24,0},{28,4},{1,25},{... | collective-permute-start | bytes 49160 | tf_op jit(solution)/shard_map/ppermute | solution.py:552
  36.1 4.6 %collective-permute-start.9 = (f32[32,128]{1,0:T(8,128)S(1)}, f32[32,128]{1,0:T(8,128)S(1)}, u32[]{:S(2)}, u32[]{:S(2)}) collective-permute-start(f32[32,128]{1,0:T(8,128)S(1)} %add.19.refs_3_), channel_id=1, source_target_pairs={{0,16},{4,20},{8,24},{12,28},{16,0},{20,4},{24,8},{28,12},{1,17},{... | collective-permute-start | bytes 49160 | tf_op jit(solution)/shard_map/ppermute | solution.py:552
  52.3 5.6 %collective-permute-start.15 = (f32[32,128]{1,0:T(8,128)S(1)}, f32[32,128]{1,0:T(8,128)S(1)}, u32[]{:S(2)}, u32[]{:S(2)}) collective-permute-start(f32[32,128]{1,0:T(8,128)S(1)} %add.20.refs_3_), channel_id=1, source_target_pairs={{0,24},{4,28},{8,16},{12,20},{16,8},{20,12},{24,0},{28,4},{1,25},{... | collective-permute-start | bytes 49160 | tf_op jit(solution)/shard_map/ppermute | solution.py:552
  53.2 4.9 %collective-permute-start.16 = (f32[32,128]{1,0:T(8,128)S(1)}, f32[32,128]{1,0:T(8,128)S(1)}, u32[]{:S(2)}, u32[]{:S(2)}) collective-permute-start(f32[32,128]{1,0:T(8,128)S(1)} %add.20.refs_3_), channel_id=1, source_target_pairs={{0,16},{4,20},{8,24},{12,28},{16,0},{20,4},{24,8},{28,12},{1,17},{... | collective-permute-start | bytes 49160 | tf_op jit(solution)/shard_map/ppermute | solution.py:552
  53.2 5.2 %collective-permute-start.17 = (f32[32,128]{1,0:T(8,128)S(1)}, f32[32,128]{1,0:T(8,128)S(1)}, u32[]{:S(2)}, u32[]{:S(2)}) collective-permute-start(f32[32,128]{1,0:T(8,128)S(1)} %add.20.refs_3_), channel_id=1, source_target_pairs={{0,8},{4,12},{8,0},{12,4},{16,24},{20,28},{24,16},{28,20},{1,9},{5... | collective-permute-start | bytes 49160 | tf_op jit(solution)/shard_map/ppermute | solution.py:552
  60.5 4.6 %collective-permute-start.18 = (f32[16,128]{1,0:T(8,128)S(1)}, f32[16,128]{1,0:T(8,128)S(1)}, u32[]{:S(2)}, u32[]{:S(2)}) collective-permute-start(f32[16,128]{1,0:T(8,128)S(1)} %get-tuple-element.39.refs_3_), channel_id=1, source_target_pairs={{0,3},{1,2},{2,1},{3,0},{4,7},{5,6},{6,5},{7,4},{8,11},{9,10},{10,... | collective-permute-start | bytes 24584 | tf_op jit(solution)/shard_map/ppermute | solution.py:552
  74.3 6.6 %collective-permute-start.21 = (f32[2,4,128,256]{3,2,1,0:T(8,128)S(1)}, f32[2,4,128,256]{3,2,1,0:T(8,128)S(1)}, u32[]{:S(2)}, u32[]{:S(2)}) collective-permute-start(f32[2,4,128,256]{3,2,1,0:T(8,128)S(1)} %get-tuple-element.43), channel_id=1, source_target_pairs={{0,4},{4,0},{8,12},{12,8},{16,20},{20,16},{24,28},{28,24},{1,5},{5... | collective-permute-start | bytes 3145736 | tf_op jit(solution)/shard_map/ppermute | solution.py:552
  76.7 14.4 %collective-permute-start.24 = (f32[2,256,256]{2,1,0:T(8,128)S(1)}, f32[2,256,256]{2,1,0:T(8,128)S(1)}, u32[]{:S(2)}, u32[]{:S(2)}) collective-permute-start(f32[2,256,256]{2,1,0:T(8,128)S(1)} %get-tuple-element.42.after_ref), channel_id=1, source_target_pairs={{0,1},{1,0},{2,3},{3,2},{4,5},{5,4},{6,7},{7,6},{8,9},{9,8},{10,11... | collective-permute-start | bytes 1572872 | tf_op jit(solution)/shard_map/ppermute | solution.py:552
  77.3 14.0 %collective-permute-start.25 = (f32[2,256,256]{2,1,0:T(8,128)S(1)}, f32[2,256,256]{2,1,0:T(8,128)S(1)}, u32[]{:S(2)}, u32[]{:S(2)}) collective-permute-start(f32[2,256,256]{2,1,0:T(8,128)S(1)} %get-tuple-element.50), channel_id=1, source_target_pairs={{0,2},{1,3},{2,0},{3,1},{4,6},{5,7},{6,4},{7,5},{8,10},{9,11},{10,... | collective-permute-start | bytes 1572872 | tf_op jit(solution)/shard_map/ppermute | solution.py:552
  81.0 12.4 %collective-permute-start.22 = (f32[2,128,256]{2,1,0:T(8,128)S(1)}, f32[2,128,256]{2,1,0:T(8,128)S(1)}, u32[]{:S(2)}, u32[]{:S(2)}) collective-permute-start(f32[2,128,256]{2,1,0:T(8,128)S(1)} %get-tuple-element.45), channel_id=1, source_target_pairs={{0,8},{4,12},{8,0},{12,4},{16,24},{20,28},{24,16},{28,20},{1,9},{5... | collective-permute-start | bytes 786440 | tf_op jit(solution)/shard_map/ppermute | solution.py:552
  83.1 14.4 %collective-permute-start.23 = (f32[2,128,256]{2,1,0:T(8,128)S(1)}, f32[2,128,256]{2,1,0:T(8,128)S(1)}, u32[]{:S(2)}, u32[]{:S(2)}) collective-permute-start(f32[2,128,256]{2,1,0:T(8,128)S(1)} %get-tuple-element.47), channel_id=1, source_target_pairs={{0,16},{4,20},{8,24},{12,28},{16,0},{20,4},{24,8},{28,12},{1,17},{... | collective-permute-start | bytes 786440 | tf_op jit(solution)/shard_map/ppermute | solution.py:552
  97.7 8.7 %collective-permute-start.28 = (f32[1,256,256]{2,1,0:T(8,128)S(1)}, f32[1,256,256]{2,1,0:T(8,128)S(1)}, u32[]{:S(2)}, u32[]{:S(2)}) collective-permute-start(f32[1,256,256]{2,1,0:T(8,128)S(1)} %get-tuple-element.56), channel_id=1, source_target_pairs={{0,2},{1,3},{2,0},{3,1},{4,6},{5,7},{6,4},{7,5},{8,10},{9,11},{10,... | collective-permute-start | bytes 786440 | tf_op jit(solution)/shard_map/ppermute | solution.py:552
  98.3 8.2 %collective-permute-start.29 = (f32[1,256,256]{2,1,0:T(8,128)S(1)}, f32[1,256,256]{2,1,0:T(8,128)S(1)}, u32[]{:S(2)}, u32[]{:S(2)}) collective-permute-start(f32[1,256,256]{2,1,0:T(8,128)S(1)} %get-tuple-element.58), channel_id=1, source_target_pairs={{0,1},{1,0},{2,3},{3,2},{4,5},{5,4},{6,7},{7,6},{8,9},{9,8},{10,11... | collective-permute-start | bytes 786440 | tf_op jit(solution)/shard_map/ppermute | solution.py:552
  99.8 6.5 %collective-permute-start.26 = (f32[1,128,256]{2,1,0:T(8,128)S(1)}, f32[1,128,256]{2,1,0:T(8,128)S(1)}, u32[]{:S(2)}, u32[]{:S(2)}) collective-permute-start(f32[1,128,256]{2,1,0:T(8,128)S(1)} %get-tuple-element.52), channel_id=1, source_target_pairs={{0,16},{4,20},{8,24},{12,28},{16,0},{20,4},{24,8},{28,12},{1,17},{... | collective-permute-start | bytes 393224 | tf_op jit(solution)/shard_map/ppermute | solution.py:552
  100.0 6.4 %collective-permute-start.27 = (f32[1,128,256]{2,1,0:T(8,128)S(1)}, f32[1,128,256]{2,1,0:T(8,128)S(1)}, u32[]{:S(2)}, u32[]{:S(2)}) collective-permute-start(f32[1,128,256]{2,1,0:T(8,128)S(1)} %get-tuple-element.54), channel_id=1, source_target_pairs={{0,8},{4,12},{8,0},{12,4},{16,24},{20,28},{24,16},{28,20},{1,9},{5... | collective-permute-start | bytes 393224 | tf_op jit(solution)/shard_map/ppermute | solution.py:552
  107.1 14.9 %collective-permute-start.41 = (f32[2,256,256]{2,1,0:T(8,128)S(1)}, f32[2,256,256]{2,1,0:T(8,128)S(1)}, u32[]{:S(2)}, u32[]{:S(2)}) collective-permute-start(f32[2,256,256]{2,1,0:T(8,128)S(1)} %get-tuple-element.60.refs_12_), channel_id=1, source_target_pairs={{0,2},{1,3},{2,0},{3,1},{4,6},{5,7},{6,4},{7,5},{8,10},{9,11},{10,... | collective-permute-start | bytes 1572872 | tf_op jit(solution)/shard_map/ppermute | solution.py:552
  108.6 12.2 %collective-permute-start.33 = (f32[264,256]{1,0:T(8,128)S(1)}, f32[264,256]{1,0:T(8,128)S(1)}, u32[]{:S(2)}, u32[]{:S(2)}) collective-permute-start(f32[264,256]{1,0:T(8,128)S(1)} %get-tuple-element.59.refs_0_.refs_4_), channel_id=1, source_target_pairs={{0,16},{4,20},{8,24},{12,28},{16,0},{20,4},{24,8},{28,12},{1,17},{... | collective-permute-start | bytes 811016 | tf_op jit(solution)/shard_map/ppermute | solution.py:552
  109.8 12.7 %collective-permute-start.40 = (f32[2,256,256]{2,1,0:T(8,128)S(1)}, f32[2,256,256]{2,1,0:T(8,128)S(1)}, u32[]{:S(2)}, u32[]{:S(2)}) collective-permute-start(f32[2,256,256]{2,1,0:T(8,128)S(1)} %get-tuple-element.60.refs_12_), channel_id=1, source_target_pairs={{0,1},{1,0},{2,3},{3,2},{4,5},{5,4},{6,7},{7,6},{8,9},{9,8},{10,11... | collective-permute-start | bytes 1572872 | tf_op jit(solution)/shard_map/ppermute | solution.py:552
  110.4 11.6 %collective-permute-start.31 = (f32[264,256]{1,0:T(8,128)S(1)}, f32[264,256]{1,0:T(8,128)S(1)}, u32[]{:S(2)}, u32[]{:S(2)}) collective-permute-start(f32[264,256]{1,0:T(8,128)S(1)} %get-tuple-element.59.refs_0_.refs_4_), channel_id=1, source_target_pairs={{0,8},{4,12},{8,0},{12,4},{16,24},{20,28},{24,16},{28,20},{1,9},{5... | collective-permute-start | bytes 811016 | tf_op jit(solution)/shard_map/ppermute | solution.py:552
  120.9 7.5 %collective-permute-start.35 = (f32[264,256]{1,0:T(8,128)S(1)}, f32[264,256]{1,0:T(8,128)S(1)}, u32[]{:S(2)}, u32[]{:S(2)}) collective-permute-start(f32[264,256]{1,0:T(8,128)S(1)} %collective-permute-done.33.refs_4_.refs_8_), channel_id=1, source_target_pairs={{0,8},{4,12},{8,0},{12,4},{16,24},{20,28},{24,16},{28,20},{1,9},{5... | collective-permute-start | bytes 811016 | tf_op jit(solution)/shard_map/ppermute | solution.py:552
  120.9 7.5 %collective-permute-start.30 = (f32[264,256]{1,0:T(8,128)S(1)}, f32[264,256]{1,0:T(8,128)S(1)}, u32[]{:S(2)}, u32[]{:S(2)}) collective-permute-start(f32[264,256]{1,0:T(8,128)S(1)} %get-tuple-element.59.refs_0_.refs_4_), channel_id=1, source_target_pairs={{0,4},{4,0},{8,12},{12,8},{16,20},{20,16},{24,28},{28,24},{1,5},{5... | collective-permute-start | bytes 811016 | tf_op jit(solution)/shard_map/ppermute | solution.py:552
  122.0 6.9 %collective-permute-start.34 = (f32[264,256]{1,0:T(8,128)S(1)}, f32[264,256]{1,0:T(8,128)S(1)}, u32[]{:S(2)}, u32[]{:S(2)}) collective-permute-start(f32[264,256]{1,0:T(8,128)S(1)} %collective-permute-done.33.refs_4_.refs_8_), channel_id=1, source_target_pairs={{0,4},{4,0},{8,12},{12,8},{16,20},{20,16},{24,28},{28,24},{1,5},{5... | collective-permute-start | bytes 811016 | tf_op jit(solution)/shard_map/ppermute | solution.py:552
  122.0 6.9 %collective-permute-start.32 = (f32[264,256]{1,0:T(8,128)S(1)}, f32[264,256]{1,0:T(8,128)S(1)}, u32[]{:S(2)}, u32[]{:S(2)}) collective-permute-start(f32[264,256]{1,0:T(8,128)S(1)} %collective-permute-done.31.refs_2_.refs_6_), channel_id=1, source_target_pairs={{0,4},{4,0},{8,12},{12,8},{16,20},{20,16},{24,28},{28,24},{1,5},{5... | collective-permute-start | bytes 811016 | tf_op jit(solution)/shard_map/ppermute | solution.py:552
  122.5 10.9 %collective-permute-start.42 = (f32[256,256]{1,0:T(8,128)S(1)}, f32[256,256]{1,0:T(8,128)S(1)}, u32[]{:S(2)}, u32[]{:S(2)}) collective-permute-start(f32[256,256]{1,0:T(8,128)S(1)} %slice_bitcast_fusion.1), channel_id=1, source_target_pairs={{0,1},{1,0},{2,3},{3,2},{4,5},{5,4},{6,7},{7,6},{8,9},{9,8},{10,11... | collective-permute-start | bytes 786440 | tf_op jit(solution)/shard_map/ppermute | solution.py:552
  128.4 9.0 %collective-permute-start.43 = (f32[256,256]{1,0:T(8,128)S(1)}, f32[256,256]{1,0:T(8,128)S(1)}, u32[]{:S(2)}, u32[]{:S(2)}) collective-permute-start(f32[256,256]{1,0:T(8,128)S(1)} %slice_bitcast_fusion), channel_id=1, source_target_pairs={{0,2},{1,3},{2,0},{3,1},{4,6},{5,7},{6,4},{7,5},{8,10},{9,11},{10,... | collective-permute-start | bytes 786440 | tf_op jit(solution)/shard_map/ppermute | solution.py:552
  129.9 7.5 %collective-permute-start.37 = (f32[2,8,128]{2,1,0:T(8,128)S(1)}, f32[2,8,128]{2,1,0:T(8,128)S(1)}, u32[]{:S(2)}, u32[]{:S(2)}) collective-permute-start(f32[2,8,128]{2,1,0:T(8,128)S(1)} %sum_squares.1.refs_3_), channel_id=1, source_target_pairs={{0,3},{1,2},{2,1},{3,0},{4,7},{5,6},{6,5},{7,4},{8,11},{9,10},{10,... | collective-permute-start | bytes 24584 | tf_op jit(solution)/shard_map/ppermute | solution.py:552
  130.9 6.6 %collective-permute-start.38 = (f32[2,8,128]{2,1,0:T(8,128)S(1)}, f32[2,8,128]{2,1,0:T(8,128)S(1)}, u32[]{:S(2)}, u32[]{:S(2)}) collective-permute-start(f32[2,8,128]{2,1,0:T(8,128)S(1)} %sum_squares.1.refs_3_), channel_id=1, source_target_pairs={{0,2},{1,3},{2,0},{3,1},{4,6},{5,7},{6,4},{7,5},{8,10},{9,11},{10,... | collective-permute-start | bytes 24584 | tf_op jit(solution)/shard_map/ppermute | solution.py:552
  132.3 5.2 %collective-permute-start.39 = (f32[2,8,128]{2,1,0:T(8,128)S(1)}, f32[2,8,128]{2,1,0:T(8,128)S(1)}, u32[]{:S(2)}, u32[]{:S(2)}) collective-permute-start(f32[2,8,128]{2,1,0:T(8,128)S(1)} %sum_squares.1.refs_3_), channel_id=1, source_target_pairs={{0,1},{1,0},{2,3},{3,2},{4,5},{5,4},{6,7},{7,6},{8,9},{9,8},{10,11... | collective-permute-start | bytes 24584 | tf_op jit(solution)/shard_map/ppermute | solution.py:552
  (12 other events, 35.8 us)

commit v11 on v10

--- a/solution.py
+++ b/solution.py
@@ -568,9 +568,10 @@
     return far_first(own, "proto", 1, lax.axis_size("proto")) + [own]
 
 
-def batch_parts(own):
+def batch_parts(own, turn):
     pair = own + swap(own, "batch", 1)
-    return far_first(pair, "batch", 2, lax.axis_size("batch") // 2) + [pair]
+    parts = far_first(pair, "batch", 2, lax.axis_size("batch") // 2)
+    return parts[turn:] + parts[:turn] + [pair]
 
 
 def scatter_sums(groups):
@@ -640,7 +641,7 @@
     t, col, den, unit_b, proto_b = scores(slow_embed, fast_embed, prototypes)
     unit_bt = turned(unit_b)
     for iteration in range(ITERS):
-        rows, r = row_pass(t, den, batch_parts(col), protos_all, iteration == 0)
+        rows, r = row_pass(t, den, batch_parts(col, iteration % 2), protos_all, iteration == 0)
         row_parts = proto_parts(rows)
         if iteration == 0:
             den_parts = row_parts
@@ -661,13 +662,14 @@
         raws.append(lax.dynamic_slice_in_dim(x, me_proto * clip_rows, clip_rows, 0))
     recv = swap(send, "batch", 1)
     halves = split_add([keep, recv], [(0, 1, h) for h in range(2)])
-    groups = []
-    for h in range(2):
+    z_groups, proto_groups = [], []
+    for h in reversed(range(2)):
         order = tuple(bit + 1 for bit in batch_orders[h])
-        groups.append(("batch", order) + tuple(halves[h]))
-    for v in range(2):
-        groups.append(("proto", proto_orders[v], shares[2 * v], shares[2 * v + 1]))
-    terms = scatter_sums(groups)
+        z_groups.append(("batch", order) + tuple(halves[h]))
+    for v in range(2):
+        proto_groups.append(("proto", proto_orders[v], shares[2 * v], shares[2 * v + 1]))
+    far_terms = scatter_sums(z_groups)
+    terms = far_terms[2:] + far_terms[:2] + scatter_sums(proto_groups)
     grad_proto, grad_embed = project_shares(raws, terms)
     proto_pieces = gather_batch(grad_proto)
     view_pieces = gather_views(grad_embed, (proto_orders[1], proto_orders[0]))

time: 140 us -> 138 us (0.986)
  waiting for transfers between devices: 60.1 us -> 55 us
  starting transfers between devices: 42 us -> 44.7 us
    ppermute x44, waiting for transfers between devices: 60.1 us -> 55 us  [swap(): lax.ppermute(own, axis, [(i, i ^ mask) for i in range(lax.axis_size(axis))])]
    ppermute x44, starting transfers between devices: 42 us -> 44.7 us  [swap(): lax.ppermute(own, axis, [(i, i ^ mask) for i in range(lax.axis_size(axis))])]
  transfers between devices with their start and end apart: 44 -> 44, of which waited for: 32 -> 31; matrix products, arithmetic and copies ran while one was open for 1% -> 1% of each run, Pallas kernels for 3% -> 4%
where the time goes in v11:
time: 138 us
  waiting for transfers between devices  55 us (40%)
  starting transfers between devices  44.7 us (32%)
  Pallas kernels  34.8 us (25%)
  local copies, waits for them, and re-layouts  1.99 us (1%)
    ppermute x44, waiting for transfers between devices, swap(): lax.ppermute(own, axis, [(i, i ^ mask) for i in range(lax.axis_size(axis))])  55 us
    ppermute x44, starting transfers between devices, swap(): lax.ppermute(own, axis, [(i, i ^ mask) for i in range(lax.axis_size(axis))])  44.7 us
    pallas_call x1, Pallas kernels, scores(): pl.pallas_call(score_kernel, out_shape=(pltpu.VMEM((2, clips, count), jnp...  8.38 us
    pallas_call x1, Pallas kernels, send_gradients(): pl.pallas_call(functools.partial(send_kernel, orders, len(row_parts)), ou...  7.04 us
    pallas_call x3, Pallas kernels, row_pass(): pl.pallas_call(functools.partial(row_kernel, protos_all, extra), out_shap...  6.82 us
    pallas_call x2, Pallas kernels, col_pass(): pl.pallas_call(functools.partial(col_kernel, clips_all), out_shape=jax.Sh...  4.65 us
  transfers between devices with their start and end apart: 44, of which 31 were waited for; matrix products, arithmetic and copies ran while one was open for 1% of the time, Pallas kernels for 4%

profile of v11, /device:TPU:0, one launch (start us, length us, event | category | flops | bytes accessed | tf_op | source)
XLA Modules:
  0.0 137.5 jit_solution(4533030269482742241)
XLA Ops:
  0.6 8.4 %scores.1 = (f32[2,1024,2048]{2,1,0:T(8,128)S(1)}, f32[32,128]{1,0:T(8,128)S(1)}, f32[16,128]{1,0:T(8,128)S(1)}, bf16[2,1024,256]{2,1,0:T(8,128)(2,1)S(1)}, bf16[2048,256]{1,0:T(8,128)(2,1)S(1)}) custom-call(bf16[1024,256]{1,0:T(8,128)(2,1)} %slow.1, bf16[1024,256]{1,0:T(8,128)(2,1)} %fast.1, f32[2048,256]{1,0:T(8,128)} %protos.1), custom_call_target="tpu_custom_call" | custom-call | tf_op jit(solution)/shard_map/scores/pallas_call | solution.py:113
  10.4 4.9 %collective-permute-start.1 = (f32[32,128]{1,0:T(8,128)S(1)}, f32[32,128]{1,0:T(8,128)S(1)}, u32[]{:S(2)}, u32[]{:S(2)}) collective-permute-start(f32[32,128]{1,0:T(8,128)S(1)} %add.18.refs_3_), channel_id=1, source_target_pairs={{0,24},{4,28},{8,16},{12,20},{16,8},{20,12},{24,0},{28,4},{1,25},{... | collective-permute-start | bytes 49160 | tf_op jit(solution)/shard_map/ppermute | solution.py:552
  17.0 2.9 %collective-permute-done.2.refs_1_ = f32[32,128]{1,0:T(8,128)S(1)} collective-permute-done((f32[32,128]{1,0:T(8,128)S(1)}, f32[32,128]{1,0:T(8,128)S(1)}, u32[]{:S(2)}, u32[]{:S(2)}) %collective-permute-start.2) | collective-permute-done | bytes 16416 | tf_op jit(solution)/shard_map/ppermute | solution.py:552
  20.0 2.4 %row_pass.3 = (f32[32,128]{1,0:T(8,128)S(1)}, f32[32,128]{1,0:T(8,128)}) custom-call(f32[2,1024,2048]{2,1,0:T(8,128)S(1)} %get-tuple-element.32.t_ref, f32[16,128]{1,0:T(8,128)S(1)} %get-tuple-element.33.den_ref, f32[32,128]{1,0:T(8,128)S(1)} %collective-permute-done.1.refs_0_, f32[32,128]{1,0:T(8,128)S(1)} %collective-permute-done.2.refs_1_, ...), custom_call_target="tpu_custom_call" | custom-call | tf_op jit(solution)/shard_map/row_pass/pallas_call | solution.py:184
  22.3 2.4 %collective-permute-start.4 = (f32[32,128]{1,0:T(8,128)S(1)}, f32[32,128]{1,0:T(8,128)S(1)}, u32[]{:S(2)}, u32[]{:S(2)}) collective-permute-start(f32[32,128]{1,0:T(8,128)S(1)} %get-tuple-element.35.refs_3_.refs_7_), channel_id=1, source_target_pairs={{0,3},{1,2},{2,1},{3,0},{4,7},{5,6},{6,5},{7,4},{8,11},{9,10},{10,... | collective-permute-start | bytes 49160 | tf_op jit(solution)/shard_map/ppermute | solution.py:552
  27.0 1.5 %collective-permute-done.5.refs_1_.refs_5_ = f32[32,128]{1,0:T(8,128)S(1)} collective-permute-done((f32[32,128]{1,0:T(8,128)S(1)}, f32[32,128]{1,0:T(8,128)S(1)}, u32[]{:S(2)}, u32[]{:S(2)}) %collective-permute-start.5) | collective-permute-done | bytes 16416 | tf_op jit(solution)/shard_map/ppermute | solution.py:552
  29.0 2.3 %col_pass.2 = f32[32,128]{1,0:T(8,128)S(1)} custom-call(f32[2,1024,2048]{2,1,0:T(8,128)S(1)} %get-tuple-element.32.t_ref, f32[32,128]{1,0:T(8,128)S(1)} %collective-permute-done.4.refs_0_.refs_4_, f32[32,128]{1,0:T(8,128)S(1)} %collective-permute-done.5.refs_1_.refs_5_, f32[32,128]{1,0:T(8,128)S(1)} %collective-permute-done.6.refs_2_.refs_6_, ...), custom_call_target="tpu_custom_call" | custom-call | tf_op jit(solution)/shard_map/col_pass/pallas_call | solution.py:224
  34.7 2.3 %collective-permute-start.9 = (f32[32,128]{1,0:T(8,128)S(1)}, f32[32,128]{1,0:T(8,128)S(1)}, u32[]{:S(2)}, u32[]{:S(2)}) collective-permute-start(f32[32,128]{1,0:T(8,128)S(1)} %add.19.refs_3_), channel_id=1, source_target_pairs={{0,8},{4,12},{8,0},{12,4},{16,24},{20,28},{24,16},{28,20},{1,9},{5... | collective-permute-start | bytes 49160 | tf_op jit(solution)/shard_map/ppermute | solution.py:552
  38.9 2.4 %row_pass.4 = (f32[16,128]{1,0:T(8,128)S(1)}, f32[32,128]{1,0:T(8,128)}) custom-call(f32[2,1024,2048]{2,1,0:T(8,128)S(1)} %get-tuple-element.32.t_ref, f32[16,128]{1,0:T(8,128)S(1)} %get-tuple-element.33.den_ref, f32[32,128]{1,0:T(8,128)S(1)} %collective-permute-done.8.refs_0_, f32[32,128]{1,0:T(8,128)S(1)} %collective-permute-done.9.refs_1_, ...), custom_call_target="tpu_custom_call" | custom-call | tf_op jit(solution)/shard_map/row_pass/pallas_call | solution.py:184
  41.2 1.5 %collective-permute-start.11 = (f32[16,128]{1,0:T(8,128)S(1)}, f32[16,128]{1,0:T(8,128)S(1)}, u32[]{:S(2)}, u32[]{:S(2)}) collective-permute-start(f32[16,128]{1,0:T(8,128)S(1)} %get-tuple-element.36.refs_3_), channel_id=1, source_target_pairs={{0,3},{1,2},{2,1},{3,0},{4,7},{5,6},{6,5},{7,4},{8,11},{9,10},{10,... | collective-permute-start | bytes 24584 | tf_op jit(solution)/shard_map/ppermute | solution.py:552
  43.2 1.5 %collective-permute-start.13 = (f32[16,128]{1,0:T(8,128)S(1)}, f32[16,128]{1,0:T(8,128)S(1)}, u32[]{:S(2)}, u32[]{:S(2)}) collective-permute-start(f32[16,128]{1,0:T(8,128)S(1)} %get-tuple-element.36.refs_3_), channel_id=1, source_target_pairs={{0,1},{1,0},{2,3},{3,2},{4,5},{5,4},{6,7},{7,6},{8,9},{9,8},{10,11... | collective-permute-start | bytes 24584 | tf_op jit(solution)/shard_map/ppermute | solution.py:552
  46.9 2.3 %col_pass.3 = f32[32,128]{1,0:T(8,128)S(1)} custom-call(f32[2,1024,2048]{2,1,0:T(8,128)S(1)} %get-tuple-element.32.t_ref, f32[16,128]{1,0:T(8,128)S(1)} %collective-permute-done.11.refs_0_, f32[16,128]{1,0:T(8,128)S(1)} %collective-permute-done.12.refs_1_, f32[16,128]{1,0:T(8,128)S(1)} %collective-permute-done.13.refs_2_, ...), custom_call_target="tpu_custom_call" | custom-call | tf_op jit(solution)/shard_map/col_pass/pallas_call | solution.py:224
  50.5 2.4 %collective-permute-start.15 = (f32[32,128]{1,0:T(8,128)S(1)}, f32[32,128]{1,0:T(8,128)S(1)}, u32[]{:S(2)}, u32[]{:S(2)}) collective-permute-start(f32[32,128]{1,0:T(8,128)S(1)} %add.20.refs_3_), channel_id=1, source_target_pairs={{0,24},{4,28},{8,16},{12,20},{16,8},{20,12},{24,0},{28,4},{1,25},{... | collective-permute-start | bytes 49160 | tf_op jit(solution)/shard_map/ppermute | solution.py:552
  57.7 2.1 %row_pass.5 = (f32[16,128]{1,0:T(8,128)S(1)}, f32[32,128]{1,0:T(8,128)S(1)}) custom-call(f32[2,1024,2048]{2,1,0:T(8,128)S(1)} %get-tuple-element.32.t_ref, f32[16,128]{1,0:T(8,128)S(1)} %get-tuple-element.33.den_ref, f32[32,128]{1,0:T(8,128)S(1)} %collective-permute-done.15.refs_0_, f32[32,128]{1,0:T(8,128)S(1)} %collective-permute-done.16.refs_1_, ...), custom_call_target="tpu_custom_call" | custom-call | tf_op jit(solution)/shard_map/row_pass/pallas_call | solution.py:184
  59.8 2.5 %collective-permute-start.18 = (f32[16,128]{1,0:T(8,128)S(1)}, f32[16,128]{1,0:T(8,128)S(1)}, u32[]{:S(2)}, u32[]{:S(2)}) collective-permute-start(f32[16,128]{1,0:T(8,128)S(1)} %get-tuple-element.39.refs_3_), channel_id=1, source_target_pairs={{0,3},{1,2},{2,1},{3,0},{4,7},{5,6},{6,5},{7,4},{8,11},{9,10},{10,... | collective-permute-start | bytes 24584 | tf_op jit(solution)/shard_map/ppermute | solution.py:552
  64.5 1.5 %collective-permute-done.19.refs_1_ = f32[16,128]{1,0:T(8,128)S(1)} collective-permute-done((f32[16,128]{1,0:T(8,128)S(1)}, f32[16,128]{1,0:T(8,128)S(1)}, u32[]{:S(2)}, u32[]{:S(2)}) %collective-permute-start.19) | collective-permute-done | bytes 8224 | tf_op jit(solution)/shard_map/ppermute | solution.py:552
  66.5 7.0 %send_gradients.1 = (f32[2,4,128,256]{3,2,1,0:T(8,128)S(1)}, bf16[2048,2048]{1,0:T(8,128)(2,1)S(1)}) custom-call(f32[2,1024,2048]{2,1,0:T(8,128)S(1)} %get-tuple-element.32.t_ref, f32[32,128]{1,0:T(8,128)S(1)} %get-tuple-element.37.r_ref, bf16[256,2048]{1,0:T(8,128)(2,1)S(1)} %turned.1.ubt_ref, f32[16,128]{1,0:T(8,128)S(1)} %collective-permute-done.18.refs_0_, ...), custom_call_target="tpu_custom_call" | custom-call | flops 1073741824 | bytes 20971520 | tf_op jit(solution)/shard_map/send_gradients/pallas_call | solution.py:311
  73.6 2.3 %embed_gradients.1 = (f32[2,256,256]{2,1,0:T(8,128)S(1)}, f32[2,256,256]{2,1,0:T(8,128)S(1)}, f32[2,256,256]{2,1,0:T(8,128)S(1)}, f32[2,256,256]{2,1,0:T(8,128)S(1)}) custom-call(bf16[2048,2048]{1,0:T(8,128)(2,1)S(1)} %get-tuple-element.40.g_ref, bf16[2048,256]{1,0:T(8,128)(2,1)S(1)} %get-tuple-element.41.cb_ref), custom_call_target="tpu_custom_call" | custom-call | flops 2147483648 | bytes 11534336 | tf_op jit(solution)/shard_map/embed_gradients/pallas_call | solution.py:351
  76.5 1.5 %collective-permute-start.27 = (f32[2,256,256]{2,1,0:T(8,128)S(1)}, f32[2,256,256]{2,1,0:T(8,128)S(1)}, u32[]{:S(2)}, u32[]{:S(2)}) collective-permute-start(f32[2,256,256]{2,1,0:T(8,128)S(1)} %get-tuple-element.54), channel_id=1, source_target_pairs={{0,2},{1,3},{2,0},{3,1},{4,6},{5,7},{6,4},{7,5},{8,10},{9,11},{10,... | collective-permute-start | bytes 1572872 | tf_op jit(solution)/shard_map/ppermute | solution.py:552
  78.1 2.1 %keep_gradients.1.refs_0_ = f32[2,4,128,256]{3,2,1,0:T(8,128)S(1)} custom-call(bf16[2048,2048]{1,0:T(8,128)(2,1)S(1)} %get-tuple-element.40.g_ref, bf16[256,2048]{1,0:T(8,128)(2,1)S(1)} %turned.1.ubt_ref, f32[2,256,256]{2,1,0:T(8,128)S(1)} %get-tuple-element.42.after_ref), custom_call_target="tpu_custom_call" | custom-call | flops 1073741824 | bytes 6291456 | tf_op jit(solution)/shard_map/keep_gradients/pallas_call | solution.py:380
  80.3 1.9 %collective-permute-start.22 = (f32[2,128,256]{2,1,0:T(8,128)S(1)}, f32[2,128,256]{2,1,0:T(8,128)S(1)}, u32[]{:S(2)}, u32[]{:S(2)}) collective-permute-start(f32[2,128,256]{2,1,0:T(8,128)S(1)} %get-tuple-element.45), channel_id=1, source_target_pairs={{0,16},{4,20},{8,24},{12,28},{16,0},{20,4},{24,8},{28,12},{1,17},{... | collective-permute-start | bytes 786440 | tf_op jit(solution)/shard_map/ppermute | solution.py:552
  82.3 8.0 %collective-permute-done.26.refs_1_ = f32[2,256,256]{2,1,0:T(8,128)S(1)} collective-permute-done((f32[2,256,256]{2,1,0:T(8,128)S(1)}, f32[2,256,256]{2,1,0:T(8,128)S(1)}, u32[]{:S(2)}, u32[]{:S(2)}) %collective-permute-start.26) | collective-permute-done | bytes 524320 | tf_op jit(solution)/shard_map/ppermute | solution.py:552
  90.7 1.6 %collective-permute-start.28 = (f32[1,256,256]{2,1,0:T(8,128)S(1)}, f32[1,256,256]{2,1,0:T(8,128)S(1)}, u32[]{:S(2)}, u32[]{:S(2)}) collective-permute-start(f32[1,256,256]{2,1,0:T(8,128)S(1)} %get-tuple-element.56), channel_id=1, source_target_pairs={{0,2},{1,3},{2,0},{3,1},{4,6},{5,7},{6,4},{7,5},{8,10},{9,11},{10,... | collective-permute-start | bytes 786440 | tf_op jit(solution)/shard_map/ppermute | solution.py:552
  99.7 4.1 %collective-permute-done.24.refs_1_ = f32[1,128,256]{2,1,0:T(8,128)S(1)} collective-permute-done((f32[1,128,256]{2,1,0:T(8,128)S(1)}, f32[1,128,256]{2,1,0:T(8,128)S(1)}, u32[]{:S(2)}, u32[]{:S(2)}) %collective-permute-start.24) | collective-permute-done | bytes 131104 | tf_op jit(solution)/shard_map/ppermute | solution.py:552
  105.5 1.5 %collective-permute-start.40 = (f32[2,256,256]{2,1,0:T(8,128)S(1)}, f32[2,256,256]{2,1,0:T(8,128)S(1)}, u32[]{:S(2)}, u32[]{:S(2)}) collective-permute-start(f32[2,256,256]{2,1,0:T(8,128)S(1)} %get-tuple-element.60.refs_12_), channel_id=1, source_target_pairs={{0,1},{1,0},{2,3},{3,2},{4,5},{5,4},{6,7},{7,6},{8,9},{9,8},{10,11... | collective-permute-start | bytes 1572872 | tf_op jit(solution)/shard_map/ppermute | solution.py:552
  108.2 9.5 %collective-permute-done.33.refs_4_.refs_8_ = f32[264,256]{1,0:T(8,128)S(1)} collective-permute-done((f32[264,256]{1,0:T(8,128)S(1)}, f32[264,256]{1,0:T(8,128)S(1)}, u32[]{:S(2)}, u32[]{:S(2)}) %collective-permute-start.33) | collective-permute-done | bytes 270368 | tf_op jit(solution)/shard_map/ppermute | solution.py:552
  117.6 2.3 %collective-permute-done.31.refs_2_.refs_6_ = f32[264,256]{1,0:T(8,128)S(1)} collective-permute-done((f32[264,256]{1,0:T(8,128)S(1)}, f32[264,256]{1,0:T(8,128)S(1)}, u32[]{:S(2)}, u32[]{:S(2)}) %collective-permute-start.31) | collective-permute-done | bytes 270368 | tf_op jit(solution)/shard_map/ppermute | solution.py:552
  121.0 4.9 %collective-permute-done.35.refs_6_.refs_10_ = f32[264,256]{1,0:T(8,128)S(1)} collective-permute-done((f32[264,256]{1,0:T(8,128)S(1)}, f32[264,256]{1,0:T(8,128)S(1)}, u32[]{:S(2)}, u32[]{:S(2)}) %collective-permute-start.35) | collective-permute-done | bytes 270368 | tf_op jit(solution)/shard_map/ppermute | solution.py:552
  126.0 1.7 %collective-permute-start.43 = (f32[256,256]{1,0:T(8,128)S(1)}, f32[256,256]{1,0:T(8,128)S(1)}, u32[]{:S(2)}, u32[]{:S(2)}) collective-permute-start(f32[256,256]{1,0:T(8,128)S(1)} %slice_bitcast_fusion), channel_id=1, source_target_pairs={{0,2},{1,3},{2,0},{3,1},{4,6},{5,7},{6,4},{7,5},{8,10},{9,11},{10,... | collective-permute-start | bytes 786440 | tf_op jit(solution)/shard_map/ppermute | solution.py:552
  127.7 2.3 %collective-permute-start.37 = (f32[2,8,128]{2,1,0:T(8,128)S(1)}, f32[2,8,128]{2,1,0:T(8,128)S(1)}, u32[]{:S(2)}, u32[]{:S(2)}) collective-permute-start(f32[2,8,128]{2,1,0:T(8,128)S(1)} %sum_squares.1.refs_3_), channel_id=1, source_target_pairs={{0,3},{1,2},{2,1},{3,0},{4,7},{5,6},{6,5},{7,4},{8,11},{9,10},{10,... | collective-permute-start | bytes 24584 | tf_op jit(solution)/shard_map/ppermute | solution.py:552
  131.3 3.8 %collective-permute-done.43.refs_16_ = f32[256,256]{1,0:T(8,128)S(1)} collective-permute-done((f32[256,256]{1,0:T(8,128)S(1)}, f32[256,256]{1,0:T(8,128)S(1)}, u32[]{:S(2)}, u32[]{:S(2)}) %collective-permute-start.43) | collective-permute-done | bytes 262176 | tf_op jit(solution)/shard_map/ppermute | solution.py:552
  135.1 2.2 %finish.1 = (f32[2048,256]{1,0:T(8,128)}, f32[1024,256]{1,0:T(8,128)}, f32[1024,256]{1,0:T(8,128)}) custom-call(f32[2,8,128]{2,1,0:T(8,128)S(1)} %collective-permute-done.37.refs_0_, f32[2,8,128]{2,1,0:T(8,128)S(1)} %collective-permute-done.38.refs_1_, f32[2,8,128]{2,1,0:T(8,128)S(1)} %collective-permute-done.39.refs_2_, ...), custom_call_target="tpu_custom_call" | custom-call | tf_op jit(solution)/shard_map/finish/pallas_call | solution.py:540
  (79 shorter events, 36.4 us)
Async XLA Ops:
  10.4 6.7 %collective-permute-start.1 = (f32[32,128]{1,0:T(8,128)S(1)}, f32[32,128]{1,0:T(8,128)S(1)}, u32[]{:S(2)}, u32[]{:S(2)}) collective-permute-start(f32[32,128]{1,0:T(8,128)S(1)} %add.18.refs_3_), channel_id=1, source_target_pairs={{0,24},{4,28},{8,16},{12,20},{16,8},{20,12},{24,0},{28,4},{1,25},{... | collective-permute-start | bytes 49160 | tf_op jit(solution)/shard_map/ppermute | solution.py:552
  15.3 4.6 %collective-permute-start.2 = (f32[32,128]{1,0:T(8,128)S(1)}, f32[32,128]{1,0:T(8,128)S(1)}, u32[]{:S(2)}, u32[]{:S(2)}) collective-permute-start(f32[32,128]{1,0:T(8,128)S(1)} %add.18.refs_3_), channel_id=1, source_target_pairs={{0,16},{4,20},{8,24},{12,28},{16,0},{20,4},{24,8},{28,12},{1,17},{... | collective-permute-start | bytes 49160 | tf_op jit(solution)/shard_map/ppermute | solution.py:552
  15.3 4.6 %collective-permute-start.3 = (f32[32,128]{1,0:T(8,128)S(1)}, f32[32,128]{1,0:T(8,128)S(1)}, u32[]{:S(2)}, u32[]{:S(2)}) collective-permute-start(f32[32,128]{1,0:T(8,128)S(1)} %add.18.refs_3_), channel_id=1, source_target_pairs={{0,8},{4,12},{8,0},{12,4},{16,24},{20,28},{24,16},{28,20},{1,9},{5... | collective-permute-start | bytes 49160 | tf_op jit(solution)/shard_map/ppermute | solution.py:552
  22.3 4.6 %collective-permute-start.4 = (f32[32,128]{1,0:T(8,128)S(1)}, f32[32,128]{1,0:T(8,128)S(1)}, u32[]{:S(2)}, u32[]{:S(2)}) collective-permute-start(f32[32,128]{1,0:T(8,128)S(1)} %get-tuple-element.35.refs_3_.refs_7_), channel_id=1, source_target_pairs={{0,3},{1,2},{2,1},{3,0},{4,7},{5,6},{6,5},{7,4},{8,11},{9,10},{10,... | collective-permute-start | bytes 49160 | tf_op jit(solution)/shard_map/ppermute | solution.py:552
  32.6 5.7 %collective-permute-start.10 = (f32[32,128]{1,0:T(8,128)S(1)}, f32[32,128]{1,0:T(8,128)S(1)}, u32[]{:S(2)}, u32[]{:S(2)}) collective-permute-start(f32[32,128]{1,0:T(8,128)S(1)} %add.19.refs_3_), channel_id=1, source_target_pairs={{0,24},{4,28},{8,16},{12,20},{16,8},{20,12},{24,0},{28,4},{1,25},{... | collective-permute-start | bytes 49160 | tf_op jit(solution)/shard_map/ppermute | solution.py:552
  34.1 4.7 %collective-permute-start.8 = (f32[32,128]{1,0:T(8,128)S(1)}, f32[32,128]{1,0:T(8,128)S(1)}, u32[]{:S(2)}, u32[]{:S(2)}) collective-permute-start(f32[32,128]{1,0:T(8,128)S(1)} %add.19.refs_3_), channel_id=1, source_target_pairs={{0,16},{4,20},{8,24},{12,28},{16,0},{20,4},{24,8},{28,12},{1,17},{... | collective-permute-start | bytes 49160 | tf_op jit(solution)/shard_map/ppermute | solution.py:552
  41.2 4.5 %collective-permute-start.11 = (f32[16,128]{1,0:T(8,128)S(1)}, f32[16,128]{1,0:T(8,128)S(1)}, u32[]{:S(2)}, u32[]{:S(2)}) collective-permute-start(f32[16,128]{1,0:T(8,128)S(1)} %get-tuple-element.36.refs_3_), channel_id=1, source_target_pairs={{0,3},{1,2},{2,1},{3,0},{4,7},{5,6},{6,5},{7,4},{8,11},{9,10},{10,... | collective-permute-start | bytes 24584 | tf_op jit(solution)/shard_map/ppermute | solution.py:552
  50.5 5.6 %collective-permute-start.15 = (f32[32,128]{1,0:T(8,128)S(1)}, f32[32,128]{1,0:T(8,128)S(1)}, u32[]{:S(2)}, u32[]{:S(2)}) collective-permute-start(f32[32,128]{1,0:T(8,128)S(1)} %add.20.refs_3_), channel_id=1, source_target_pairs={{0,24},{4,28},{8,16},{12,20},{16,8},{20,12},{24,0},{28,4},{1,25},{... | collective-permute-start | bytes 49160 | tf_op jit(solution)/shard_map/ppermute | solution.py:552
  52.9 4.7 %collective-permute-start.16 = (f32[32,128]{1,0:T(8,128)S(1)}, f32[32,128]{1,0:T(8,128)S(1)}, u32[]{:S(2)}, u32[]{:S(2)}) collective-permute-start(f32[32,128]{1,0:T(8,128)S(1)} %add.20.refs_3_), channel_id=1, source_target_pairs={{0,16},{4,20},{8,24},{12,28},{16,0},{20,4},{24,8},{28,12},{1,17},{... | collective-permute-start | bytes 49160 | tf_op jit(solution)/shard_map/ppermute | solution.py:552
  59.8 4.7 %collective-permute-start.18 = (f32[16,128]{1,0:T(8,128)S(1)}, f32[16,128]{1,0:T(8,128)S(1)}, u32[]{:S(2)}, u32[]{:S(2)}) collective-permute-start(f32[16,128]{1,0:T(8,128)S(1)} %get-tuple-element.39.refs_3_), channel_id=1, source_target_pairs={{0,3},{1,2},{2,1},{3,0},{4,7},{5,6},{6,5},{7,4},{8,11},{9,10},{10,... | collective-permute-start | bytes 24584 | tf_op jit(solution)/shard_map/ppermute | solution.py:552
  73.5 6.6 %collective-permute-start.21 = (f32[2,4,128,256]{3,2,1,0:T(8,128)S(1)}, f32[2,4,128,256]{3,2,1,0:T(8,128)S(1)}, u32[]{:S(2)}, u32[]{:S(2)}) collective-permute-start(f32[2,4,128,256]{3,2,1,0:T(8,128)S(1)} %get-tuple-element.43), channel_id=1, source_target_pairs={{0,4},{4,0},{8,12},{12,8},{16,20},{20,16},{24,28},{28,24},{1,5},{5... | collective-permute-start | bytes 3145736 | tf_op jit(solution)/shard_map/ppermute | solution.py:552
  75.9 14.4 %collective-permute-start.26 = (f32[2,256,256]{2,1,0:T(8,128)S(1)}, f32[2,256,256]{2,1,0:T(8,128)S(1)}, u32[]{:S(2)}, u32[]{:S(2)}) collective-permute-start(f32[2,256,256]{2,1,0:T(8,128)S(1)} %get-tuple-element.42.after_ref), channel_id=1, source_target_pairs={{0,1},{1,0},{2,3},{3,2},{4,5},{5,4},{6,7},{7,6},{8,9},{9,8},{10,11... | collective-permute-start | bytes 1572872 | tf_op jit(solution)/shard_map/ppermute | solution.py:552
  76.5 14.0 %collective-permute-start.27 = (f32[2,256,256]{2,1,0:T(8,128)S(1)}, f32[2,256,256]{2,1,0:T(8,128)S(1)}, u32[]{:S(2)}, u32[]{:S(2)}) collective-permute-start(f32[2,256,256]{2,1,0:T(8,128)S(1)} %get-tuple-element.54), channel_id=1, source_target_pairs={{0,2},{1,3},{2,0},{3,1},{4,6},{5,7},{6,4},{7,5},{8,10},{9,11},{10,... | collective-permute-start | bytes 1572872 | tf_op jit(solution)/shard_map/ppermute | solution.py:552
  80.3 14.8 %collective-permute-start.22 = (f32[2,128,256]{2,1,0:T(8,128)S(1)}, f32[2,128,256]{2,1,0:T(8,128)S(1)}, u32[]{:S(2)}, u32[]{:S(2)}) collective-permute-start(f32[2,128,256]{2,1,0:T(8,128)S(1)} %get-tuple-element.45), channel_id=1, source_target_pairs={{0,16},{4,20},{8,24},{12,28},{16,0},{20,4},{24,8},{28,12},{1,17},{... | collective-permute-start | bytes 786440 | tf_op jit(solution)/shard_map/ppermute | solution.py:552
  82.2 13.1 %collective-permute-start.23 = (f32[2,128,256]{2,1,0:T(8,128)S(1)}, f32[2,128,256]{2,1,0:T(8,128)S(1)}, u32[]{:S(2)}, u32[]{:S(2)}) collective-permute-start(f32[2,128,256]{2,1,0:T(8,128)S(1)} %get-tuple-element.47), channel_id=1, source_target_pairs={{0,8},{4,12},{8,0},{12,4},{16,24},{20,28},{24,16},{28,20},{1,9},{5... | collective-permute-start | bytes 786440 | tf_op jit(solution)/shard_map/ppermute | solution.py:552
  90.7 8.4 %collective-permute-start.28 = (f32[1,256,256]{2,1,0:T(8,128)S(1)}, f32[1,256,256]{2,1,0:T(8,128)S(1)}, u32[]{:S(2)}, u32[]{:S(2)}) collective-permute-start(f32[1,256,256]{2,1,0:T(8,128)S(1)} %get-tuple-element.56), channel_id=1, source_target_pairs={{0,2},{1,3},{2,0},{3,1},{4,6},{5,7},{6,4},{7,5},{8,10},{9,11},{10,... | collective-permute-start | bytes 786440 | tf_op jit(solution)/shard_map/ppermute | solution.py:552
  92.3 7.4 %collective-permute-start.29 = (f32[1,256,256]{2,1,0:T(8,128)S(1)}, f32[1,256,256]{2,1,0:T(8,128)S(1)}, u32[]{:S(2)}, u32[]{:S(2)}) collective-permute-start(f32[1,256,256]{2,1,0:T(8,128)S(1)} %get-tuple-element.58), channel_id=1, source_target_pairs={{0,1},{1,0},{2,3},{3,2},{4,5},{5,4},{6,7},{7,6},{8,9},{9,8},{10,11... | collective-permute-start | bytes 786440 | tf_op jit(solution)/shard_map/ppermute | solution.py:552
  95.3 8.5 %collective-permute-start.24 = (f32[1,128,256]{2,1,0:T(8,128)S(1)}, f32[1,128,256]{2,1,0:T(8,128)S(1)}, u32[]{:S(2)}, u32[]{:S(2)}) collective-permute-start(f32[1,128,256]{2,1,0:T(8,128)S(1)} %get-tuple-element.49), channel_id=1, source_target_pairs={{0,16},{4,20},{8,24},{12,28},{16,0},{20,4},{24,8},{28,12},{1,17},{... | collective-permute-start | bytes 393224 | tf_op jit(solution)/shard_map/ppermute | solution.py:552
  96.1 7.7 %collective-permute-start.25 = (f32[1,128,256]{2,1,0:T(8,128)S(1)}, f32[1,128,256]{2,1,0:T(8,128)S(1)}, u32[]{:S(2)}, u32[]{:S(2)}) collective-permute-start(f32[1,128,256]{2,1,0:T(8,128)S(1)} %get-tuple-element.51), channel_id=1, source_target_pairs={{0,8},{4,12},{8,0},{12,4},{16,24},{20,28},{24,16},{28,20},{1,9},{5... | collective-permute-start | bytes 393224 | tf_op jit(solution)/shard_map/ppermute | solution.py:552
  104.5 15.4 %collective-permute-start.41 = (f32[2,256,256]{2,1,0:T(8,128)S(1)}, f32[2,256,256]{2,1,0:T(8,128)S(1)}, u32[]{:S(2)}, u32[]{:S(2)}) collective-permute-start(f32[2,256,256]{2,1,0:T(8,128)S(1)} %get-tuple-element.60.refs_12_), channel_id=1, source_target_pairs={{0,2},{1,3},{2,0},{3,1},{4,6},{5,7},{6,4},{7,5},{8,10},{9,11},{10,... | collective-permute-start | bytes 1572872 | tf_op jit(solution)/shard_map/ppermute | solution.py:552
  104.9 12.7 %collective-permute-start.33 = (f32[264,256]{1,0:T(8,128)S(1)}, f32[264,256]{1,0:T(8,128)S(1)}, u32[]{:S(2)}, u32[]{:S(2)}) collective-permute-start(f32[264,256]{1,0:T(8,128)S(1)} %get-tuple-element.59.refs_0_.refs_4_), channel_id=1, source_target_pairs={{0,16},{4,20},{8,24},{12,28},{16,0},{20,4},{24,8},{28,12},{1,17},{... | collective-permute-start | bytes 811016 | tf_op jit(solution)/shard_map/ppermute | solution.py:552
  105.5 14.9 %collective-permute-start.40 = (f32[2,256,256]{2,1,0:T(8,128)S(1)}, f32[2,256,256]{2,1,0:T(8,128)S(1)}, u32[]{:S(2)}, u32[]{:S(2)}) collective-permute-start(f32[2,256,256]{2,1,0:T(8,128)S(1)} %get-tuple-element.60.refs_12_), channel_id=1, source_target_pairs={{0,1},{1,0},{2,3},{3,2},{4,5},{5,4},{6,7},{7,6},{8,9},{9,8},{10,11... | collective-permute-start | bytes 1572872 | tf_op jit(solution)/shard_map/ppermute | solution.py:552
  107.0 12.9 %collective-permute-start.31 = (f32[264,256]{1,0:T(8,128)S(1)}, f32[264,256]{1,0:T(8,128)S(1)}, u32[]{:S(2)}, u32[]{:S(2)}) collective-permute-start(f32[264,256]{1,0:T(8,128)S(1)} %get-tuple-element.59.refs_0_.refs_4_), channel_id=1, source_target_pairs={{0,8},{4,12},{8,0},{12,4},{16,24},{20,28},{24,16},{28,20},{1,9},{5... | collective-permute-start | bytes 811016 | tf_op jit(solution)/shard_map/ppermute | solution.py:552
  117.6 8.3 %collective-permute-start.35 = (f32[264,256]{1,0:T(8,128)S(1)}, f32[264,256]{1,0:T(8,128)S(1)}, u32[]{:S(2)}, u32[]{:S(2)}) collective-permute-start(f32[264,256]{1,0:T(8,128)S(1)} %collective-permute-done.33.refs_4_.refs_8_), channel_id=1, source_target_pairs={{0,8},{4,12},{8,0},{12,4},{16,24},{20,28},{24,16},{28,20},{1,9},{5... | collective-permute-start | bytes 811016 | tf_op jit(solution)/shard_map/ppermute | solution.py:552
  117.6 8.4 %collective-permute-start.30 = (f32[264,256]{1,0:T(8,128)S(1)}, f32[264,256]{1,0:T(8,128)S(1)}, u32[]{:S(2)}, u32[]{:S(2)}) collective-permute-start(f32[264,256]{1,0:T(8,128)S(1)} %get-tuple-element.59.refs_0_.refs_4_), channel_id=1, source_target_pairs={{0,4},{4,0},{8,12},{12,8},{16,20},{20,16},{24,28},{28,24},{1,5},{5... | collective-permute-start | bytes 811016 | tf_op jit(solution)/shard_map/ppermute | solution.py:552
  119.9 7.8 %collective-permute-start.34 = (f32[264,256]{1,0:T(8,128)S(1)}, f32[264,256]{1,0:T(8,128)S(1)}, u32[]{:S(2)}, u32[]{:S(2)}) collective-permute-start(f32[264,256]{1,0:T(8,128)S(1)} %collective-permute-done.33.refs_4_.refs_8_), channel_id=1, source_target_pairs={{0,4},{4,0},{8,12},{12,8},{16,20},{20,16},{24,28},{28,24},{1,5},{5... | collective-permute-start | bytes 811016 | tf_op jit(solution)/shard_map/ppermute | solution.py:552
  119.9 7.8 %collective-permute-start.32 = (f32[264,256]{1,0:T(8,128)S(1)}, f32[264,256]{1,0:T(8,128)S(1)}, u32[]{:S(2)}, u32[]{:S(2)}) collective-permute-start(f32[264,256]{1,0:T(8,128)S(1)} %collective-permute-done.31.refs_2_.refs_6_), channel_id=1, source_target_pairs={{0,4},{4,0},{8,12},{12,8},{16,20},{20,16},{24,28},{28,24},{1,5},{5... | collective-permute-start | bytes 811016 | tf_op jit(solution)/shard_map/ppermute | solution.py:552
  120.4 10.8 %collective-permute-start.42 = (f32[256,256]{1,0:T(8,128)S(1)}, f32[256,256]{1,0:T(8,128)S(1)}, u32[]{:S(2)}, u32[]{:S(2)}) collective-permute-start(f32[256,256]{1,0:T(8,128)S(1)} %slice_bitcast_fusion.1), channel_id=1, source_target_pairs={{0,1},{1,0},{2,3},{3,2},{4,5},{5,4},{6,7},{7,6},{8,9},{9,8},{10,11... | collective-permute-start | bytes 786440 | tf_op jit(solution)/shard_map/ppermute | solution.py:552
  126.0 9.0 %collective-permute-start.43 = (f32[256,256]{1,0:T(8,128)S(1)}, f32[256,256]{1,0:T(8,128)S(1)}, u32[]{:S(2)}, u32[]{:S(2)}) collective-permute-start(f32[256,256]{1,0:T(8,128)S(1)} %slice_bitcast_fusion), channel_id=1, source_target_pairs={{0,2},{1,3},{2,0},{3,1},{4,6},{5,7},{6,4},{7,5},{8,10},{9,11},{10,... | collective-permute-start | bytes 786440 | tf_op jit(solution)/shard_map/ppermute | solution.py:552
  127.7 7.4 %collective-permute-start.37 = (f32[2,8,128]{2,1,0:T(8,128)S(1)}, f32[2,8,128]{2,1,0:T(8,128)S(1)}, u32[]{:S(2)}, u32[]{:S(2)}) collective-permute-start(f32[2,8,128]{2,1,0:T(8,128)S(1)} %sum_squares.1.refs_3_), channel_id=1, source_target_pairs={{0,3},{1,2},{2,1},{3,0},{4,7},{5,6},{6,5},{7,4},{8,11},{9,10},{10,... | collective-permute-start | bytes 24584 | tf_op jit(solution)/shard_map/ppermute | solution.py:552
  130.0 5.2 %collective-permute-start.38 = (f32[2,8,128]{2,1,0:T(8,128)S(1)}, f32[2,8,128]{2,1,0:T(8,128)S(1)}, u32[]{:S(2)}, u32[]{:S(2)}) collective-permute-start(f32[2,8,128]{2,1,0:T(8,128)S(1)} %sum_squares.1.refs_3_), channel_id=1, source_target_pairs={{0,2},{1,3},{2,0},{3,1},{4,6},{5,7},{6,4},{7,5},{8,10},{9,11},{10,... | collective-permute-start | bytes 24584 | tf_op jit(solution)/shard_map/ppermute | solution.py:552
  130.6 4.6 %collective-permute-start.39 = (f32[2,8,128]{2,1,0:T(8,128)S(1)}, f32[2,8,128]{2,1,0:T(8,128)S(1)}, u32[]{:S(2)}, u32[]{:S(2)}) collective-permute-start(f32[2,8,128]{2,1,0:T(8,128)S(1)} %sum_squares.1.refs_3_), channel_id=1, source_target_pairs={{0,1},{1,0},{2,3},{3,2},{4,5},{5,4},{6,7},{7,6},{8,9},{9,8},{10,11... | collective-permute-start | bytes 24584 | tf_op jit(solution)/shard_map/ppermute | solution.py:552
  (12 other events, 35.7 us)

commit v12 on v11

--- a/solution.py
+++ b/solution.py
@@ -55,7 +55,7 @@
 LOG2E = 1.4426950408889634
 
 
-def score_kernel(slow, fast, protos, t_ref, col_ref, den_ref, ub_ref, cb_ref, raw_s, w_s, den_s, sems):
+def score_kernel(slow, fast, protos, t_ref, col_ref, den_ref, ub_ref, cb_ref, raw_s, w_s, ct_s, den_s, sems):
     clips, feats = slow.shape
     count = protos.shape[0]
     loads = []
@@ -73,14 +73,16 @@
             ub_ref[v, rows, :] = (x / length).astype(jnp.bfloat16)
     den_s[...] = jnp.zeros_like(den_s)
     loads[2].wait()
+    for first in range(0, count, 256):
+        w = w_s[first : first + 256, :]
+        length = jnp.sqrt(jnp.sum(w * w, axis=-1, keepdims=True) + 1e-12)
+        c = w / length
+        cb_ref[first : first + 256, :] = c.astype(jnp.bfloat16)
+        ct_s[:, first : first + 256] = c.T.astype(jnp.bfloat16)
 
     def chunk(j, _):
         first = pl.multiple_of(j * 256, 256)
-        w = w_s[pl.ds(first, 256), :]
-        length = jnp.sqrt(jnp.sum(w * w, axis=-1, keepdims=True) + 1e-12)
-        c = w / length
-        cb_ref[pl.ds(first, 256), :] = c.astype(jnp.bfloat16)
-        weights = c.T.astype(jnp.bfloat16)
+        weights = ct_s[:, pl.ds(first, 256)]
         for v in range(2):
             cols = jnp.zeros((8, 256), jnp.float32)
             for r in range(0, clips, 512):
@@ -124,6 +126,7 @@
         scratch_shapes=[
             pltpu.VMEM((2, clips, feats), jnp.bfloat16),
             pltpu.VMEM((count, feats), jnp.float32),
+            pltpu.VMEM((feats, count), jnp.bfloat16),
             pltpu.VMEM((2, clips, LANES), jnp.float32),
             pltpu.SemaphoreType.DMA((3,)),
         ],
@@ -199,13 +202,15 @@
     row_parts, (col_ref, acc_s, s_s) = refs[:-3], refs[-3:]
     clips, count = t_ref.shape[1:]
     groups, lines = clips // LANES, count // LANES
-    s_s[...] = 1.0 / (float(clips_all) * sum_of(row_parts, 0, 2 * groups))
+    scale = 1.0 / (float(clips_all) * sum_of(row_parts, 0, 2 * groups))
+    for line in range(2 * groups):
+        s_s[line * LANES : (line + 1) * LANES, :] = to_columns(scale[line : line + 1, :])
     acc_s[...] = jnp.zeros_like(acc_s)
     for v in range(2):
 
         def step(i, _, v=v):
             rows = pl.ds(pl.multiple_of(i * LANES, LANES), LANES)
-            scale = to_columns(s_s[pl.ds(v * groups + i, 1), :])
+            scale = s_s[pl.ds(pl.multiple_of((v * groups + i) * LANES, LANES), LANES), :]
             for j in range(lines):
                 span = slice(j * LANES, (j + 1) * LANES)
                 t = t_ref[v, rows, span]
@@ -228,7 +233,7 @@
         out_specs=vmem_spec(),
         scratch_shapes=[
             pltpu.VMEM((2, 8, count), jnp.float32),
-            pltpu.VMEM((2 * clips // LANES, LANES), jnp.float32),
+            pltpu.VMEM((2 * clips, LANES), jnp.float32),
         ],
         compiler_params=params(8),
         name="col_pass",
@@ -257,28 +262,46 @@
         out_ref[h, place_of(i, orders[h])] = dct[h * half : (h + 1) * half]
 
 
-def send_kernel(orders, parts, t_ref, r_ref, ubt_ref, *refs):
-    row_parts, den_parts = refs[:parts], refs[parts : 2 * parts]
-    send_ref, g_ref, chunk_s, code_s, prob_s = refs[2 * parts :]
+def prob_kernel(*refs):
+    den_parts, prob_ref = refs[:-1], refs[-1]
+    lines = den_parts[0].shape[0] // 2
+    prob = (1.0 / TEMPER) / sum_of(den_parts, lines, lines)
+    for line in range(lines):
+        prob_ref[line * LANES : (line + 1) * LANES, :] = to_columns(prob[line : line + 1, :])
+
+
+def prob_columns(den_parts):
+    lines = den_parts[0].shape[0] // 2
+    return pl.pallas_call(
+        prob_kernel,
+        out_shape=jax.ShapeDtypeStruct((lines * LANES, LANES), jnp.float32),
+        in_specs=[vmem_spec()] * len(den_parts),
+        out_specs=vmem_spec(),
+        compiler_params=params(8),
+        cost_estimate=pl.CostEstimate(
+            flops=lines * LANES * LANES, bytes_accessed=2 * MIB, transcendentals=0
+        ),
+        name="prob_columns",
+    )(*den_parts)
+
+
+def send_kernel(orders, parts, t_ref, r_ref, ubt_ref, prob_s, *refs):
+    row_parts = refs[:parts]
+    send_ref, g_ref, chunk_s, code_s = refs[parts:]
     clips, count = t_ref.shape[1:]
     groups, lines = clips // LANES, count // LANES
     pieces = 1 << len(orders[0])
     width = count // (2 * pieces)
     code = (1.0 / TEMPER) / sum_of(row_parts, 0, 2 * groups)
-    prob = (1.0 / TEMPER) / sum_of(den_parts, 2 * groups, 2 * groups)
-    for v in range(2):
-        for i in range(groups):
-            line = v * groups + i
-            rows = slice(i * LANES, (i + 1) * LANES)
-            code_s[v, rows, :] = to_columns(code[line : line + 1, :])
-            prob_s[v, rows, :] = to_columns(prob[line : line + 1, :])
+    for line in range(2 * groups):
+        code_s[line * LANES : (line + 1) * LANES, :] = to_columns(code[line : line + 1, :])
 
     def score_grads(m, keep_chunk):
         which, first = chunk_span(m, width)
         for i in range(0, clips, 32):
             rows = slice(i, i + 32)
-            codes = [code_s[v, rows, :] for v in range(2)]
-            probs = [prob_s[v, rows, :] for v in range(2)]
+            codes = [code_s[v * clips + i : v * clips + i + 32, :] for v in range(2)]
+            probs = [prob_s[v * clips + i : v * clips + i + 32, :] for v in range(2)]
             for h in range(width // LANES):
                 span = pl.ds(first + h * LANES, LANES)
                 line = which * (width // LANES) + h
@@ -303,7 +326,7 @@
     lax.fori_loop(0, pieces, pair, 0)
 
 
-def send_gradients(t, r, ubt, row_parts, den_parts, orders):
+def send_gradients(t, r, ubt, prob, row_parts, orders):
     clips, count = t.shape[1:]
     feats = ubt.shape[0]
     pieces = 1 << len(orders[0])
@@ -314,19 +337,18 @@
             jax.ShapeDtypeStruct((2, pieces, feats // 2, width), jnp.float32),
             pltpu.VMEM((2 * clips, count), jnp.bfloat16),
         ),
-        in_specs=[vmem_spec()] * (3 + 2 * len(row_parts)),
+        in_specs=[vmem_spec()] * (4 + len(row_parts)),
         out_specs=(vmem_spec(),) * 2,
         scratch_shapes=[
             pltpu.VMEM((2 * clips, width), jnp.bfloat16),
-            pltpu.VMEM((2, clips, LANES), jnp.float32),
-            pltpu.VMEM((2, clips, LANES), jnp.float32),
+            pltpu.VMEM((2 * clips, LANES), jnp.float32),
         ],
         compiler_params=params(14),
         cost_estimate=pl.CostEstimate(
             flops=2 * clips * count * feats, bytes_accessed=20 * MIB, transcendentals=0
         ),
         name="send_gradients",
-    )(pltpu.with_memory_space_constraint(t, pltpu.VMEM), r, ubt, *row_parts, *den_parts)
+    )(pltpu.with_memory_space_constraint(t, pltpu.VMEM), r, ubt, prob, *row_parts)
 
 
 def embed_grad_kernel(orders, g_ref, cb_ref, *outs):
@@ -644,14 +666,14 @@
         rows, r = row_pass(t, den, batch_parts(col, iteration % 2), protos_all, iteration == 0)
         row_parts = proto_parts(rows)
         if iteration == 0:
-            den_parts = row_parts
+            prob = prob_columns(row_parts)
         if iteration + 1 < ITERS:
             col = col_pass(t, row_parts, clips_all)
 
     near = tuple(range(batch_bits - 1))
     batch_orders = (near, tuple(reversed(near)))
     proto_orders = (tuple(range(proto_bits)), tuple(reversed(range(proto_bits))))
-    send, g = send_gradients(t, r, unit_bt, row_parts, den_parts, batch_orders)
+    send, g = send_gradients(t, r, unit_bt, prob, row_parts, batch_orders)
     shares = embed_gradients(g, proto_b, proto_orders)
     keep = keep_gradients(g, unit_bt, shares[0], batch_orders)
 

time: 138 us -> 136 us (0.986)
  no operation moved by 1% of the time
where the time goes in v12:
time: 136 us
  waiting for transfers between devices  54.6 us (40%)
  starting transfers between devices  44.8 us (33%)
  Pallas kernels  33.6 us (25%)
  local copies, waits for them, and re-layouts  1.99 us (1%)
    ppermute x44, waiting for transfers between devices, swap(): lax.ppermute(own, axis, [(i, i ^ mask) for i in range(lax.axis_size(axis))])  54.6 us
    ppermute x44, starting transfers between devices, swap(): lax.ppermute(own, axis, [(i, i ^ mask) for i in range(lax.axis_size(axis))])  44.8 us
    pallas_call x1, Pallas kernels, scores(): pl.pallas_call(score_kernel, out_shape=(pltpu.VMEM((2, clips, count), jnp...  7.71 us
    pallas_call x3, Pallas kernels, row_pass(): pl.pallas_call(functools.partial(row_kernel, protos_all, extra), out_shap...  6.82 us
    pallas_call x1, Pallas kernels, send_gradients(): pl.pallas_call(functools.partial(send_kernel, orders, len(row_parts)), ou...  6.52 us
    pallas_call x2, Pallas kernels, col_pass(): pl.pallas_call(functools.partial(col_kernel, clips_all), out_shape=jax.Sh...  4.37 us
  transfers between devices with their start and end apart: 44, of which 31 were waited for; matrix products, arithmetic and copies ran while one was open for 1% of the time, Pallas kernels for 4%

profile of v12, /device:TPU:0, one launch (start us, length us, event | category | flops | bytes accessed | tf_op | source)
XLA Modules:
  0.0 136.0 jit_solution(5179927477518158064)
XLA Ops:
  0.6 7.7 %scores.1 = (f32[2,1024,2048]{2,1,0:T(8,128)S(1)}, f32[32,128]{1,0:T(8,128)S(1)}, f32[16,128]{1,0:T(8,128)S(1)}, bf16[2,1024,256]{2,1,0:T(8,128)(2,1)S(1)}, bf16[2048,256]{1,0:T(8,128)(2,1)S(1)}) custom-call(bf16[1024,256]{1,0:T(8,128)(2,1)} %slow.1, bf16[1024,256]{1,0:T(8,128)(2,1)} %fast.1, f32[2048,256]{1,0:T(8,128)} %protos.1), custom_call_target="tpu_custom_call" | custom-call | tf_op jit(solution)/shard_map/scores/pallas_call | solution.py:115
  9.7 4.9 %collective-permute-start.1 = (f32[32,128]{1,0:T(8,128)S(1)}, f32[32,128]{1,0:T(8,128)S(1)}, u32[]{:S(2)}, u32[]{:S(2)}) collective-permute-start(f32[32,128]{1,0:T(8,128)S(1)} %add.18.refs_3_), channel_id=1, source_target_pairs={{0,24},{4,28},{8,16},{12,20},{16,8},{20,12},{24,0},{28,4},{1,25},{... | collective-permute-start | bytes 49160 | tf_op jit(solution)/shard_map/ppermute | solution.py:574
  16.4 2.9 %collective-permute-done.2.refs_1_ = f32[32,128]{1,0:T(8,128)S(1)} collective-permute-done((f32[32,128]{1,0:T(8,128)S(1)}, f32[32,128]{1,0:T(8,128)S(1)}, u32[]{:S(2)}, u32[]{:S(2)}) %collective-permute-start.2) | collective-permute-done | bytes 16416 | tf_op jit(solution)/shard_map/ppermute | solution.py:574
  19.3 2.4 %row_pass.3 = (f32[32,128]{1,0:T(8,128)S(1)}, f32[32,128]{1,0:T(8,128)}) custom-call(f32[2,1024,2048]{2,1,0:T(8,128)S(1)} %get-tuple-element.32.t_ref, f32[16,128]{1,0:T(8,128)S(1)} %get-tuple-element.33.den_ref, f32[32,128]{1,0:T(8,128)S(1)} %collective-permute-done.1.refs_0_, f32[32,128]{1,0:T(8,128)S(1)} %collective-permute-done.2.refs_1_, ...), custom_call_target="tpu_custom_call" | custom-call | tf_op jit(solution)/shard_map/row_pass/pallas_call | solution.py:187
  21.7 2.4 %collective-permute-start.4 = (f32[32,128]{1,0:T(8,128)S(1)}, f32[32,128]{1,0:T(8,128)S(1)}, u32[]{:S(2)}, u32[]{:S(2)}) collective-permute-start(f32[32,128]{1,0:T(8,128)S(1)} %get-tuple-element.35.refs_3_), channel_id=1, source_target_pairs={{0,3},{1,2},{2,1},{3,0},{4,7},{5,6},{6,5},{7,4},{8,11},{9,10},{10,... | collective-permute-start | bytes 49160 | tf_op jit(solution)/shard_map/ppermute | solution.py:574
  26.3 1.5 %collective-permute-done.5.refs_1_ = f32[32,128]{1,0:T(8,128)S(1)} collective-permute-done((f32[32,128]{1,0:T(8,128)S(1)}, f32[32,128]{1,0:T(8,128)S(1)}, u32[]{:S(2)}, u32[]{:S(2)}) %collective-permute-start.5) | collective-permute-done | bytes 16416 | tf_op jit(solution)/shard_map/ppermute | solution.py:574
  28.3 2.2 %col_pass.2 = f32[32,128]{1,0:T(8,128)S(1)} custom-call(f32[2,1024,2048]{2,1,0:T(8,128)S(1)} %get-tuple-element.32.t_ref, f32[32,128]{1,0:T(8,128)S(1)} %collective-permute-done.4.refs_0_, f32[32,128]{1,0:T(8,128)S(1)} %collective-permute-done.5.refs_1_, f32[32,128]{1,0:T(8,128)S(1)} %collective-permute-done.6.refs_2_, f32[32,128]{1,0:T(8,128)S(1)} %get-tuple-element.35.refs_3_), custom_call_target="tpu_custom_call" | custom-call | tf_op jit(solution)/shard_map/col_pass/pallas_call | solution.py:229
  33.9 2.3 %collective-permute-start.9 = (f32[32,128]{1,0:T(8,128)S(1)}, f32[32,128]{1,0:T(8,128)S(1)}, u32[]{:S(2)}, u32[]{:S(2)}) collective-permute-start(f32[32,128]{1,0:T(8,128)S(1)} %add.19.refs_3_), channel_id=1, source_target_pairs={{0,8},{4,12},{8,0},{12,4},{16,24},{20,28},{24,16},{28,20},{1,9},{5... | collective-permute-start | bytes 49160 | tf_op jit(solution)/shard_map/ppermute | solution.py:574
  38.1 2.4 %row_pass.4 = (f32[16,128]{1,0:T(8,128)S(1)}, f32[32,128]{1,0:T(8,128)}) custom-call(f32[2,1024,2048]{2,1,0:T(8,128)S(1)} %get-tuple-element.32.t_ref, f32[16,128]{1,0:T(8,128)S(1)} %get-tuple-element.33.den_ref, f32[32,128]{1,0:T(8,128)S(1)} %collective-permute-done.8.refs_0_, f32[32,128]{1,0:T(8,128)S(1)} %collective-permute-done.9.refs_1_, ...), custom_call_target="tpu_custom_call" | custom-call | tf_op jit(solution)/shard_map/row_pass/pallas_call | solution.py:187
  40.4 1.5 %collective-permute-start.11 = (f32[16,128]{1,0:T(8,128)S(1)}, f32[16,128]{1,0:T(8,128)S(1)}, u32[]{:S(2)}, u32[]{:S(2)}) collective-permute-start(f32[16,128]{1,0:T(8,128)S(1)} %get-tuple-element.36.refs_3_), channel_id=1, source_target_pairs={{0,3},{1,2},{2,1},{3,0},{4,7},{5,6},{6,5},{7,4},{8,11},{9,10},{10,... | collective-permute-start | bytes 24584 | tf_op jit(solution)/shard_map/ppermute | solution.py:574
  42.4 1.5 %collective-permute-start.13 = (f32[16,128]{1,0:T(8,128)S(1)}, f32[16,128]{1,0:T(8,128)S(1)}, u32[]{:S(2)}, u32[]{:S(2)}) collective-permute-start(f32[16,128]{1,0:T(8,128)S(1)} %get-tuple-element.36.refs_3_), channel_id=1, source_target_pairs={{0,1},{1,0},{2,3},{3,2},{4,5},{5,4},{6,7},{7,6},{8,9},{9,8},{10,11... | collective-permute-start | bytes 24584 | tf_op jit(solution)/shard_map/ppermute | solution.py:574
  46.1 2.2 %col_pass.3 = f32[32,128]{1,0:T(8,128)S(1)} custom-call(f32[2,1024,2048]{2,1,0:T(8,128)S(1)} %get-tuple-element.32.t_ref, f32[16,128]{1,0:T(8,128)S(1)} %collective-permute-done.11.refs_0_, f32[16,128]{1,0:T(8,128)S(1)} %collective-permute-done.12.refs_1_, f32[16,128]{1,0:T(8,128)S(1)} %collective-permute-done.13.refs_2_, ...), custom_call_target="tpu_custom_call" | custom-call | tf_op jit(solution)/shard_map/col_pass/pallas_call | solution.py:229
  49.5 2.4 %collective-permute-start.15 = (f32[32,128]{1,0:T(8,128)S(1)}, f32[32,128]{1,0:T(8,128)S(1)}, u32[]{:S(2)}, u32[]{:S(2)}) collective-permute-start(f32[32,128]{1,0:T(8,128)S(1)} %add.20.refs_3_), channel_id=1, source_target_pairs={{0,24},{4,28},{8,16},{12,20},{16,8},{20,12},{24,0},{28,4},{1,25},{... | collective-permute-start | bytes 49160 | tf_op jit(solution)/shard_map/ppermute | solution.py:574
  56.7 2.1 %row_pass.5 = (f32[16,128]{1,0:T(8,128)S(1)}, f32[32,128]{1,0:T(8,128)S(1)}) custom-call(f32[2,1024,2048]{2,1,0:T(8,128)S(1)} %get-tuple-element.32.t_ref, f32[16,128]{1,0:T(8,128)S(1)} %get-tuple-element.33.den_ref, f32[32,128]{1,0:T(8,128)S(1)} %collective-permute-done.15.refs_0_, f32[32,128]{1,0:T(8,128)S(1)} %collective-permute-done.16.refs_1_, ...), custom_call_target="tpu_custom_call" | custom-call | tf_op jit(solution)/shard_map/row_pass/pallas_call | solution.py:187
  58.9 2.5 %collective-permute-start.18 = (f32[16,128]{1,0:T(8,128)S(1)}, f32[16,128]{1,0:T(8,128)S(1)}, u32[]{:S(2)}, u32[]{:S(2)}) collective-permute-start(f32[16,128]{1,0:T(8,128)S(1)} %get-tuple-element.39.refs_3_), channel_id=1, source_target_pairs={{0,3},{1,2},{2,1},{3,0},{4,7},{5,6},{6,5},{7,4},{8,11},{9,10},{10,... | collective-permute-start | bytes 24584 | tf_op jit(solution)/shard_map/ppermute | solution.py:574
  63.5 1.5 %collective-permute-done.19.refs_1_ = f32[16,128]{1,0:T(8,128)S(1)} collective-permute-done((f32[16,128]{1,0:T(8,128)S(1)}, f32[16,128]{1,0:T(8,128)S(1)}, u32[]{:S(2)}, u32[]{:S(2)}) %collective-permute-start.19) | collective-permute-done | bytes 8224 | tf_op jit(solution)/shard_map/ppermute | solution.py:574
  65.5 6.5 %send_gradients.1 = (f32[2,4,128,256]{3,2,1,0:T(8,128)S(1)}, bf16[2048,2048]{1,0:T(8,128)(2,1)S(1)}) custom-call(f32[2,1024,2048]{2,1,0:T(8,128)S(1)} %get-tuple-element.32.t_ref, f32[32,128]{1,0:T(8,128)S(1)} %get-tuple-element.37.r_ref, bf16[256,2048]{1,0:T(8,128)(2,1)S(1)} %turned.1.ubt_ref, f32[2048,128]{1,0:T(8,128)S(1)} %prob_columns.1.prob_s, ...), custom_call_target="tpu_custom_call" | custom-call | flops 1073741824 | bytes 20971520 | tf_op jit(solution)/shard_map/send_gradients/pallas_call | solution.py:334
  72.1 2.3 %embed_gradients.1 = (f32[2,256,256]{2,1,0:T(8,128)S(1)}, f32[2,256,256]{2,1,0:T(8,128)S(1)}, f32[2,256,256]{2,1,0:T(8,128)S(1)}, f32[2,256,256]{2,1,0:T(8,128)S(1)}) custom-call(bf16[2048,2048]{1,0:T(8,128)(2,1)S(1)} %get-tuple-element.40.g_ref, bf16[2048,256]{1,0:T(8,128)(2,1)S(1)} %get-tuple-element.41.cb_ref), custom_call_target="tpu_custom_call" | custom-call | flops 2147483648 | bytes 11534336 | tf_op jit(solution)/shard_map/embed_gradients/pallas_call | solution.py:373
  75.1 1.5 %collective-permute-start.27 = (f32[2,256,256]{2,1,0:T(8,128)S(1)}, f32[2,256,256]{2,1,0:T(8,128)S(1)}, u32[]{:S(2)}, u32[]{:S(2)}) collective-permute-start(f32[2,256,256]{2,1,0:T(8,128)S(1)} %get-tuple-element.54), channel_id=1, source_target_pairs={{0,2},{1,3},{2,0},{3,1},{4,6},{5,7},{6,4},{7,5},{8,10},{9,11},{10,... | collective-permute-start | bytes 1572872 | tf_op jit(solution)/shard_map/ppermute | solution.py:574
  76.6 2.1 %keep_gradients.1.refs_0_ = f32[2,4,128,256]{3,2,1,0:T(8,128)S(1)} custom-call(bf16[2048,2048]{1,0:T(8,128)(2,1)S(1)} %get-tuple-element.40.g_ref, bf16[256,2048]{1,0:T(8,128)(2,1)S(1)} %turned.1.ubt_ref, f32[2,256,256]{2,1,0:T(8,128)S(1)} %get-tuple-element.42.after_ref), custom_call_target="tpu_custom_call" | custom-call | flops 1073741824 | bytes 6291456 | tf_op jit(solution)/shard_map/keep_gradients/pallas_call | solution.py:402
  78.8 1.9 %collective-permute-start.22 = (f32[2,128,256]{2,1,0:T(8,128)S(1)}, f32[2,128,256]{2,1,0:T(8,128)S(1)}, u32[]{:S(2)}, u32[]{:S(2)}) collective-permute-start(f32[2,128,256]{2,1,0:T(8,128)S(1)} %get-tuple-element.45), channel_id=1, source_target_pairs={{0,16},{4,20},{8,24},{12,28},{16,0},{20,4},{24,8},{28,12},{1,17},{... | collective-permute-start | bytes 786440 | tf_op jit(solution)/shard_map/ppermute | solution.py:574
  80.8 8.0 %collective-permute-done.26.refs_1_ = f32[2,256,256]{2,1,0:T(8,128)S(1)} collective-permute-done((f32[2,256,256]{2,1,0:T(8,128)S(1)}, f32[2,256,256]{2,1,0:T(8,128)S(1)}, u32[]{:S(2)}, u32[]{:S(2)}) %collective-permute-start.26) | collective-permute-done | bytes 524320 | tf_op jit(solution)/shard_map/ppermute | solution.py:574
  89.2 1.6 %collective-permute-start.28 = (f32[1,256,256]{2,1,0:T(8,128)S(1)}, f32[1,256,256]{2,1,0:T(8,128)S(1)}, u32[]{:S(2)}, u32[]{:S(2)}) collective-permute-start(f32[1,256,256]{2,1,0:T(8,128)S(1)} %get-tuple-element.56), channel_id=1, source_target_pairs={{0,2},{1,3},{2,0},{3,1},{4,6},{5,7},{6,4},{7,5},{8,10},{9,11},{10,... | collective-permute-start | bytes 786440 | tf_op jit(solution)/shard_map/ppermute | solution.py:574
  98.2 4.1 %collective-permute-done.24.refs_1_ = f32[1,128,256]{2,1,0:T(8,128)S(1)} collective-permute-done((f32[1,128,256]{2,1,0:T(8,128)S(1)}, f32[1,128,256]{2,1,0:T(8,128)S(1)}, u32[]{:S(2)}, u32[]{:S(2)}) %collective-permute-start.24) | collective-permute-done | bytes 131104 | tf_op jit(solution)/shard_map/ppermute | solution.py:574
  104.1 1.5 %collective-permute-start.40 = (f32[2,256,256]{2,1,0:T(8,128)S(1)}, f32[2,256,256]{2,1,0:T(8,128)S(1)}, u32[]{:S(2)}, u32[]{:S(2)}) collective-permute-start(f32[2,256,256]{2,1,0:T(8,128)S(1)} %get-tuple-element.60.refs_12_), channel_id=1, source_target_pairs={{0,1},{1,0},{2,3},{3,2},{4,5},{5,4},{6,7},{7,6},{8,9},{9,8},{10,11... | collective-permute-start | bytes 1572872 | tf_op jit(solution)/shard_map/ppermute | solution.py:574
  106.7 9.4 %collective-permute-done.33.refs_4_.refs_8_ = f32[264,256]{1,0:T(8,128)S(1)} collective-permute-done((f32[264,256]{1,0:T(8,128)S(1)}, f32[264,256]{1,0:T(8,128)S(1)}, u32[]{:S(2)}, u32[]{:S(2)}) %collective-permute-start.33) | collective-permute-done | bytes 270368 | tf_op jit(solution)/shard_map/ppermute | solution.py:574
  116.1 2.4 %collective-permute-done.31.refs_2_.refs_6_ = f32[264,256]{1,0:T(8,128)S(1)} collective-permute-done((f32[264,256]{1,0:T(8,128)S(1)}, f32[264,256]{1,0:T(8,128)S(1)}, u32[]{:S(2)}, u32[]{:S(2)}) %collective-permute-start.31) | collective-permute-done | bytes 270368 | tf_op jit(solution)/shard_map/ppermute | solution.py:574
  119.7 4.8 %collective-permute-done.35.refs_6_.refs_10_ = f32[264,256]{1,0:T(8,128)S(1)} collective-permute-done((f32[264,256]{1,0:T(8,128)S(1)}, f32[264,256]{1,0:T(8,128)S(1)}, u32[]{:S(2)}, u32[]{:S(2)}) %collective-permute-start.35) | collective-permute-done | bytes 270368 | tf_op jit(solution)/shard_map/ppermute | solution.py:574
  124.5 1.7 %collective-permute-start.43 = (f32[256,256]{1,0:T(8,128)S(1)}, f32[256,256]{1,0:T(8,128)S(1)}, u32[]{:S(2)}, u32[]{:S(2)}) collective-permute-start(f32[256,256]{1,0:T(8,128)S(1)} %slice_bitcast_fusion), channel_id=1, source_target_pairs={{0,2},{1,3},{2,0},{3,1},{4,6},{5,7},{6,4},{7,5},{8,10},{9,11},{10,... | collective-permute-start | bytes 786440 | tf_op jit(solution)/shard_map/ppermute | solution.py:574
  126.2 2.4 %collective-permute-start.37 = (f32[2,8,128]{2,1,0:T(8,128)S(1)}, f32[2,8,128]{2,1,0:T(8,128)S(1)}, u32[]{:S(2)}, u32[]{:S(2)}) collective-permute-start(f32[2,8,128]{2,1,0:T(8,128)S(1)} %sum_squares.1.refs_3_), channel_id=1, source_target_pairs={{0,3},{1,2},{2,1},{3,0},{4,7},{5,6},{6,5},{7,4},{8,11},{9,10},{10,... | collective-permute-start | bytes 24584 | tf_op jit(solution)/shard_map/ppermute | solution.py:574
  129.7 3.8 %collective-permute-done.43.refs_16_ = f32[256,256]{1,0:T(8,128)S(1)} collective-permute-done((f32[256,256]{1,0:T(8,128)S(1)}, f32[256,256]{1,0:T(8,128)S(1)}, u32[]{:S(2)}, u32[]{:S(2)}) %collective-permute-start.43) | collective-permute-done | bytes 262176 | tf_op jit(solution)/shard_map/ppermute | solution.py:574
  133.6 2.2 %finish.1 = (f32[2048,256]{1,0:T(8,128)}, f32[1024,256]{1,0:T(8,128)}, f32[1024,256]{1,0:T(8,128)}) custom-call(f32[2,8,128]{2,1,0:T(8,128)S(1)} %collective-permute-done.37.refs_0_, f32[2,8,128]{2,1,0:T(8,128)S(1)} %collective-permute-done.38.refs_1_, f32[2,8,128]{2,1,0:T(8,128)S(1)} %collective-permute-done.39.refs_2_, ...), custom_call_target="tpu_custom_call" | custom-call | tf_op jit(solution)/shard_map/finish/pallas_call | solution.py:562
  (80 shorter events, 36.3 us)
Async XLA Ops:
  9.7 6.7 %collective-permute-start.1 = (f32[32,128]{1,0:T(8,128)S(1)}, f32[32,128]{1,0:T(8,128)S(1)}, u32[]{:S(2)}, u32[]{:S(2)}) collective-permute-start(f32[32,128]{1,0:T(8,128)S(1)} %add.18.refs_3_), channel_id=1, source_target_pairs={{0,24},{4,28},{8,16},{12,20},{16,8},{20,12},{24,0},{28,4},{1,25},{... | collective-permute-start | bytes 49160 | tf_op jit(solution)/shard_map/ppermute | solution.py:574
  14.7 4.6 %collective-permute-start.2 = (f32[32,128]{1,0:T(8,128)S(1)}, f32[32,128]{1,0:T(8,128)S(1)}, u32[]{:S(2)}, u32[]{:S(2)}) collective-permute-start(f32[32,128]{1,0:T(8,128)S(1)} %add.18.refs_3_), channel_id=1, source_target_pairs={{0,16},{4,20},{8,24},{12,28},{16,0},{20,4},{24,8},{28,12},{1,17},{... | collective-permute-start | bytes 49160 | tf_op jit(solution)/shard_map/ppermute | solution.py:574
  14.7 4.6 %collective-permute-start.3 = (f32[32,128]{1,0:T(8,128)S(1)}, f32[32,128]{1,0:T(8,128)S(1)}, u32[]{:S(2)}, u32[]{:S(2)}) collective-permute-start(f32[32,128]{1,0:T(8,128)S(1)} %add.18.refs_3_), channel_id=1, source_target_pairs={{0,8},{4,12},{8,0},{12,4},{16,24},{20,28},{24,16},{28,20},{1,9},{5... | collective-permute-start | bytes 49160 | tf_op jit(solution)/shard_map/ppermute | solution.py:574
  21.7 4.6 %collective-permute-start.4 = (f32[32,128]{1,0:T(8,128)S(1)}, f32[32,128]{1,0:T(8,128)S(1)}, u32[]{:S(2)}, u32[]{:S(2)}) collective-permute-start(f32[32,128]{1,0:T(8,128)S(1)} %get-tuple-element.35.refs_3_), channel_id=1, source_target_pairs={{0,3},{1,2},{2,1},{3,0},{4,7},{5,6},{6,5},{7,4},{8,11},{9,10},{10,... | collective-permute-start | bytes 49160 | tf_op jit(solution)/shard_map/ppermute | solution.py:574
  31.8 5.7 %collective-permute-start.10 = (f32[32,128]{1,0:T(8,128)S(1)}, f32[32,128]{1,0:T(8,128)S(1)}, u32[]{:S(2)}, u32[]{:S(2)}) collective-permute-start(f32[32,128]{1,0:T(8,128)S(1)} %add.19.refs_3_), channel_id=1, source_target_pairs={{0,24},{4,28},{8,16},{12,20},{16,8},{20,12},{24,0},{28,4},{1,25},{... | collective-permute-start | bytes 49160 | tf_op jit(solution)/shard_map/ppermute | solution.py:574
  33.3 4.7 %collective-permute-start.8 = (f32[32,128]{1,0:T(8,128)S(1)}, f32[32,128]{1,0:T(8,128)S(1)}, u32[]{:S(2)}, u32[]{:S(2)}) collective-permute-start(f32[32,128]{1,0:T(8,128)S(1)} %add.19.refs_3_), channel_id=1, source_target_pairs={{0,16},{4,20},{8,24},{12,28},{16,0},{20,4},{24,8},{28,12},{1,17},{... | collective-permute-start | bytes 49160 | tf_op jit(solution)/shard_map/ppermute | solution.py:574
  40.4 4.5 %collective-permute-start.11 = (f32[16,128]{1,0:T(8,128)S(1)}, f32[16,128]{1,0:T(8,128)S(1)}, u32[]{:S(2)}, u32[]{:S(2)}) collective-permute-start(f32[16,128]{1,0:T(8,128)S(1)} %get-tuple-element.36.refs_3_), channel_id=1, source_target_pairs={{0,3},{1,2},{2,1},{3,0},{4,7},{5,6},{6,5},{7,4},{8,11},{9,10},{10,... | collective-permute-start | bytes 24584 | tf_op jit(solution)/shard_map/ppermute | solution.py:574
  49.5 5.6 %collective-permute-start.15 = (f32[32,128]{1,0:T(8,128)S(1)}, f32[32,128]{1,0:T(8,128)S(1)}, u32[]{:S(2)}, u32[]{:S(2)}) collective-permute-start(f32[32,128]{1,0:T(8,128)S(1)} %add.20.refs_3_), channel_id=1, source_target_pairs={{0,24},{4,28},{8,16},{12,20},{16,8},{20,12},{24,0},{28,4},{1,25},{... | collective-permute-start | bytes 49160 | tf_op jit(solution)/shard_map/ppermute | solution.py:574
  51.9 4.7 %collective-permute-start.16 = (f32[32,128]{1,0:T(8,128)S(1)}, f32[32,128]{1,0:T(8,128)S(1)}, u32[]{:S(2)}, u32[]{:S(2)}) collective-permute-start(f32[32,128]{1,0:T(8,128)S(1)} %add.20.refs_3_), channel_id=1, source_target_pairs={{0,16},{4,20},{8,24},{12,28},{16,0},{20,4},{24,8},{28,12},{1,17},{... | collective-permute-start | bytes 49160 | tf_op jit(solution)/shard_map/ppermute | solution.py:574
  58.9 4.7 %collective-permute-start.18 = (f32[16,128]{1,0:T(8,128)S(1)}, f32[16,128]{1,0:T(8,128)S(1)}, u32[]{:S(2)}, u32[]{:S(2)}) collective-permute-start(f32[16,128]{1,0:T(8,128)S(1)} %get-tuple-element.39.refs_3_), channel_id=1, source_target_pairs={{0,3},{1,2},{2,1},{3,0},{4,7},{5,6},{6,5},{7,4},{8,11},{9,10},{10,... | collective-permute-start | bytes 24584 | tf_op jit(solution)/shard_map/ppermute | solution.py:574
  72.1 6.6 %collective-permute-start.21 = (f32[2,4,128,256]{3,2,1,0:T(8,128)S(1)}, f32[2,4,128,256]{3,2,1,0:T(8,128)S(1)}, u32[]{:S(2)}, u32[]{:S(2)}) collective-permute-start(f32[2,4,128,256]{3,2,1,0:T(8,128)S(1)} %get-tuple-element.43), channel_id=1, source_target_pairs={{0,4},{4,0},{8,12},{12,8},{16,20},{20,16},{24,28},{28,24},{1,5},{5... | collective-permute-start | bytes 3145736 | tf_op jit(solution)/shard_map/ppermute | solution.py:574
  74.5 14.4 %collective-permute-start.26 = (f32[2,256,256]{2,1,0:T(8,128)S(1)}, f32[2,256,256]{2,1,0:T(8,128)S(1)}, u32[]{:S(2)}, u32[]{:S(2)}) collective-permute-start(f32[2,256,256]{2,1,0:T(8,128)S(1)} %get-tuple-element.42.after_ref), channel_id=1, source_target_pairs={{0,1},{1,0},{2,3},{3,2},{4,5},{5,4},{6,7},{7,6},{8,9},{9,8},{10,11... | collective-permute-start | bytes 1572872 | tf_op jit(solution)/shard_map/ppermute | solution.py:574
  75.1 14.0 %collective-permute-start.27 = (f32[2,256,256]{2,1,0:T(8,128)S(1)}, f32[2,256,256]{2,1,0:T(8,128)S(1)}, u32[]{:S(2)}, u32[]{:S(2)}) collective-permute-start(f32[2,256,256]{2,1,0:T(8,128)S(1)} %get-tuple-element.54), channel_id=1, source_target_pairs={{0,2},{1,3},{2,0},{3,1},{4,6},{5,7},{6,4},{7,5},{8,10},{9,11},{10,... | collective-permute-start | bytes 1572872 | tf_op jit(solution)/shard_map/ppermute | solution.py:574
  78.8 14.8 %collective-permute-start.22 = (f32[2,128,256]{2,1,0:T(8,128)S(1)}, f32[2,128,256]{2,1,0:T(8,128)S(1)}, u32[]{:S(2)}, u32[]{:S(2)}) collective-permute-start(f32[2,128,256]{2,1,0:T(8,128)S(1)} %get-tuple-element.45), channel_id=1, source_target_pairs={{0,16},{4,20},{8,24},{12,28},{16,0},{20,4},{24,8},{28,12},{1,17},{... | collective-permute-start | bytes 786440 | tf_op jit(solution)/shard_map/ppermute | solution.py:574
  80.7 13.0 %collective-permute-start.23 = (f32[2,128,256]{2,1,0:T(8,128)S(1)}, f32[2,128,256]{2,1,0:T(8,128)S(1)}, u32[]{:S(2)}, u32[]{:S(2)}) collective-permute-start(f32[2,128,256]{2,1,0:T(8,128)S(1)} %get-tuple-element.47), channel_id=1, source_target_pairs={{0,8},{4,12},{8,0},{12,4},{16,24},{20,28},{24,16},{28,20},{1,9},{5... | collective-permute-start | bytes 786440 | tf_op jit(solution)/shard_map/ppermute | solution.py:574
  89.2 8.4 %collective-permute-start.28 = (f32[1,256,256]{2,1,0:T(8,128)S(1)}, f32[1,256,256]{2,1,0:T(8,128)S(1)}, u32[]{:S(2)}, u32[]{:S(2)}) collective-permute-start(f32[1,256,256]{2,1,0:T(8,128)S(1)} %get-tuple-element.56), channel_id=1, source_target_pairs={{0,2},{1,3},{2,0},{3,1},{4,6},{5,7},{6,4},{7,5},{8,10},{9,11},{10,... | collective-permute-start | bytes 786440 | tf_op jit(solution)/shard_map/ppermute | solution.py:574
  90.8 7.4 %collective-permute-start.29 = (f32[1,256,256]{2,1,0:T(8,128)S(1)}, f32[1,256,256]{2,1,0:T(8,128)S(1)}, u32[]{:S(2)}, u32[]{:S(2)}) collective-permute-start(f32[1,256,256]{2,1,0:T(8,128)S(1)} %get-tuple-element.58), channel_id=1, source_target_pairs={{0,1},{1,0},{2,3},{3,2},{4,5},{5,4},{6,7},{7,6},{8,9},{9,8},{10,11... | collective-permute-start | bytes 786440 | tf_op jit(solution)/shard_map/ppermute | solution.py:574
  93.8 8.5 %collective-permute-start.24 = (f32[1,128,256]{2,1,0:T(8,128)S(1)}, f32[1,128,256]{2,1,0:T(8,128)S(1)}, u32[]{:S(2)}, u32[]{:S(2)}) collective-permute-start(f32[1,128,256]{2,1,0:T(8,128)S(1)} %get-tuple-element.49), channel_id=1, source_target_pairs={{0,16},{4,20},{8,24},{12,28},{16,0},{20,4},{24,8},{28,12},{1,17},{... | collective-permute-start | bytes 393224 | tf_op jit(solution)/shard_map/ppermute | solution.py:574
  94.6 7.7 %collective-permute-start.25 = (f32[1,128,256]{2,1,0:T(8,128)S(1)}, f32[1,128,256]{2,1,0:T(8,128)S(1)}, u32[]{:S(2)}, u32[]{:S(2)}) collective-permute-start(f32[1,128,256]{2,1,0:T(8,128)S(1)} %get-tuple-element.51), channel_id=1, source_target_pairs={{0,8},{4,12},{8,0},{12,4},{16,24},{20,28},{24,16},{28,20},{1,9},{5... | collective-permute-start | bytes 393224 | tf_op jit(solution)/shard_map/ppermute | solution.py:574
  103.0 15.5 %collective-permute-start.41 = (f32[2,256,256]{2,1,0:T(8,128)S(1)}, f32[2,256,256]{2,1,0:T(8,128)S(1)}, u32[]{:S(2)}, u32[]{:S(2)}) collective-permute-start(f32[2,256,256]{2,1,0:T(8,128)S(1)} %get-tuple-element.60.refs_12_), channel_id=1, source_target_pairs={{0,2},{1,3},{2,0},{3,1},{4,6},{5,7},{6,4},{7,5},{8,10},{9,11},{10,... | collective-permute-start | bytes 1572872 | tf_op jit(solution)/shard_map/ppermute | solution.py:574
  103.5 12.6 %collective-permute-start.33 = (f32[264,256]{1,0:T(8,128)S(1)}, f32[264,256]{1,0:T(8,128)S(1)}, u32[]{:S(2)}, u32[]{:S(2)}) collective-permute-start(f32[264,256]{1,0:T(8,128)S(1)} %get-tuple-element.59.refs_0_.refs_4_), channel_id=1, source_target_pairs={{0,16},{4,20},{8,24},{12,28},{16,0},{20,4},{24,8},{28,12},{1,17},{... | collective-permute-start | bytes 811016 | tf_op jit(solution)/shard_map/ppermute | solution.py:574
  104.1 15.0 %collective-permute-start.40 = (f32[2,256,256]{2,1,0:T(8,128)S(1)}, f32[2,256,256]{2,1,0:T(8,128)S(1)}, u32[]{:S(2)}, u32[]{:S(2)}) collective-permute-start(f32[2,256,256]{2,1,0:T(8,128)S(1)} %get-tuple-element.60.refs_12_), channel_id=1, source_target_pairs={{0,1},{1,0},{2,3},{3,2},{4,5},{5,4},{6,7},{7,6},{8,9},{9,8},{10,11... | collective-permute-start | bytes 1572872 | tf_op jit(solution)/shard_map/ppermute | solution.py:574
  105.6 12.9 %collective-permute-start.31 = (f32[264,256]{1,0:T(8,128)S(1)}, f32[264,256]{1,0:T(8,128)S(1)}, u32[]{:S(2)}, u32[]{:S(2)}) collective-permute-start(f32[264,256]{1,0:T(8,128)S(1)} %get-tuple-element.59.refs_0_.refs_4_), channel_id=1, source_target_pairs={{0,8},{4,12},{8,0},{12,4},{16,24},{20,28},{24,16},{28,20},{1,9},{5... | collective-permute-start | bytes 811016 | tf_op jit(solution)/shard_map/ppermute | solution.py:574
  116.1 8.3 %collective-permute-start.35 = (f32[264,256]{1,0:T(8,128)S(1)}, f32[264,256]{1,0:T(8,128)S(1)}, u32[]{:S(2)}, u32[]{:S(2)}) collective-permute-start(f32[264,256]{1,0:T(8,128)S(1)} %collective-permute-done.33.refs_4_.refs_8_), channel_id=1, source_target_pairs={{0,8},{4,12},{8,0},{12,4},{16,24},{20,28},{24,16},{28,20},{1,9},{5... | collective-permute-start | bytes 811016 | tf_op jit(solution)/shard_map/ppermute | solution.py:574
  116.1 8.4 %collective-permute-start.30 = (f32[264,256]{1,0:T(8,128)S(1)}, f32[264,256]{1,0:T(8,128)S(1)}, u32[]{:S(2)}, u32[]{:S(2)}) collective-permute-start(f32[264,256]{1,0:T(8,128)S(1)} %get-tuple-element.59.refs_0_.refs_4_), channel_id=1, source_target_pairs={{0,4},{4,0},{8,12},{12,8},{16,20},{20,16},{24,28},{28,24},{1,5},{5... | collective-permute-start | bytes 811016 | tf_op jit(solution)/shard_map/ppermute | solution.py:574
  118.5 7.7 %collective-permute-start.34 = (f32[264,256]{1,0:T(8,128)S(1)}, f32[264,256]{1,0:T(8,128)S(1)}, u32[]{:S(2)}, u32[]{:S(2)}) collective-permute-start(f32[264,256]{1,0:T(8,128)S(1)} %collective-permute-done.33.refs_4_.refs_8_), channel_id=1, source_target_pairs={{0,4},{4,0},{8,12},{12,8},{16,20},{20,16},{24,28},{28,24},{1,5},{5... | collective-permute-start | bytes 811016 | tf_op jit(solution)/shard_map/ppermute | solution.py:574
  118.5 7.6 %collective-permute-start.32 = (f32[264,256]{1,0:T(8,128)S(1)}, f32[264,256]{1,0:T(8,128)S(1)}, u32[]{:S(2)}, u32[]{:S(2)}) collective-permute-start(f32[264,256]{1,0:T(8,128)S(1)} %collective-permute-done.31.refs_2_.refs_6_), channel_id=1, source_target_pairs={{0,4},{4,0},{8,12},{12,8},{16,20},{20,16},{24,28},{28,24},{1,5},{5... | collective-permute-start | bytes 811016 | tf_op jit(solution)/shard_map/ppermute | solution.py:574
  119.0 10.7 %collective-permute-start.42 = (f32[256,256]{1,0:T(8,128)S(1)}, f32[256,256]{1,0:T(8,128)S(1)}, u32[]{:S(2)}, u32[]{:S(2)}) collective-permute-start(f32[256,256]{1,0:T(8,128)S(1)} %slice_bitcast_fusion.1), channel_id=1, source_target_pairs={{0,1},{1,0},{2,3},{3,2},{4,5},{5,4},{6,7},{7,6},{8,9},{9,8},{10,11... | collective-permute-start | bytes 786440 | tf_op jit(solution)/shard_map/ppermute | solution.py:574
  124.5 9.0 %collective-permute-start.43 = (f32[256,256]{1,0:T(8,128)S(1)}, f32[256,256]{1,0:T(8,128)S(1)}, u32[]{:S(2)}, u32[]{:S(2)}) collective-permute-start(f32[256,256]{1,0:T(8,128)S(1)} %slice_bitcast_fusion), channel_id=1, source_target_pairs={{0,2},{1,3},{2,0},{3,1},{4,6},{5,7},{6,4},{7,5},{8,10},{9,11},{10,... | collective-permute-start | bytes 786440 | tf_op jit(solution)/shard_map/ppermute | solution.py:574
  126.2 7.4 %collective-permute-start.37 = (f32[2,8,128]{2,1,0:T(8,128)S(1)}, f32[2,8,128]{2,1,0:T(8,128)S(1)}, u32[]{:S(2)}, u32[]{:S(2)}) collective-permute-start(f32[2,8,128]{2,1,0:T(8,128)S(1)} %sum_squares.1.refs_3_), channel_id=1, source_target_pairs={{0,3},{1,2},{2,1},{3,0},{4,7},{5,6},{6,5},{7,4},{8,11},{9,10},{10,... | collective-permute-start | bytes 24584 | tf_op jit(solution)/shard_map/ppermute | solution.py:574
  128.6 5.0 %collective-permute-start.38 = (f32[2,8,128]{2,1,0:T(8,128)S(1)}, f32[2,8,128]{2,1,0:T(8,128)S(1)}, u32[]{:S(2)}, u32[]{:S(2)}) collective-permute-start(f32[2,8,128]{2,1,0:T(8,128)S(1)} %sum_squares.1.refs_3_), channel_id=1, source_target_pairs={{0,2},{1,3},{2,0},{3,1},{4,6},{5,7},{6,4},{7,5},{8,10},{9,11},{10,... | collective-permute-start | bytes 24584 | tf_op jit(solution)/shard_map/ppermute | solution.py:574
  129.2 4.4 %collective-permute-start.39 = (f32[2,8,128]{2,1,0:T(8,128)S(1)}, f32[2,8,128]{2,1,0:T(8,128)S(1)}, u32[]{:S(2)}, u32[]{:S(2)}) collective-permute-start(f32[2,8,128]{2,1,0:T(8,128)S(1)} %sum_squares.1.refs_3_), channel_id=1, source_target_pairs={{0,1},{1,0},{2,3},{3,2},{4,5},{5,4},{6,7},{7,6},{8,9},{9,8},{10,11... | collective-permute-start | bytes 24584 | tf_op jit(solution)/shard_map/ppermute | solution.py:574
  (12 other events, 35.7 us)

commit v13 on v12

--- a/solution.py
+++ b/solution.py
@@ -55,7 +55,7 @@
 LOG2E = 1.4426950408889634
 
 
-def score_kernel(slow, fast, protos, t_ref, col_ref, den_ref, ub_ref, cb_ref, raw_s, w_s, ct_s, den_s, sems):
+def score_kernel(slow, fast, protos, t_ref, col_ref, ub_ref, cb_ref, raw_s, w_s, ct_s, sems):
     clips, feats = slow.shape
     count = protos.shape[0]
     loads = []
@@ -71,7 +71,6 @@
             x = raw_s[v, rows, :].astype(jnp.float32)
             length = jnp.sqrt(jnp.sum(x * x, axis=-1, keepdims=True) + 1e-12)
             ub_ref[v, rows, :] = (x / length).astype(jnp.bfloat16)
-    den_s[...] = jnp.zeros_like(den_s)
     loads[2].wait()
     for first in range(0, count, 256):
         w = w_s[first : first + 256, :]
@@ -94,7 +93,6 @@
                     t = jnp.exp2(s[q : q + 64] * (LOG2E / TEMPER))
                     t_ref[v, rows, pl.ds(first, 256)] = t
                     cols = cols + row_fold(t * t)
-                    den_s[v, rows, :] += lane_sum(t)
             line = jnp.sum(cols, axis=0, keepdims=True)
             for h in range(2):
                 col_ref[pl.ds(v * (count // LANES) + j * 2 + h, 1), :] = line[
@@ -103,10 +101,6 @@
         return 0
 
     lax.fori_loop(0, count // 256, chunk, 0)
-    groups = clips // LANES
-    for v in range(2):
-        for i in range(groups):
-            den_ref[pl.ds(v * groups + i, 1), :] = to_line(den_s[v, i * LANES : (i + 1) * LANES, :])
 
 
 def scores(slow, fast, protos):
@@ -117,17 +111,15 @@
         out_shape=(
             pltpu.VMEM((2, clips, count), jnp.float32),
             jax.ShapeDtypeStruct((2 * count // LANES, LANES), jnp.float32),
-            jax.ShapeDtypeStruct((2 * clips // LANES, LANES), jnp.float32),
             jax.ShapeDtypeStruct((2, clips, feats), jnp.bfloat16),
             jax.ShapeDtypeStruct((count, feats), jnp.bfloat16),
         ),
         in_specs=[pl.BlockSpec(memory_space=pltpu.HBM)] * 3,
-        out_specs=(vmem_spec(),) * 5,
+        out_specs=(vmem_spec(),) * 4,
         scratch_shapes=[
             pltpu.VMEM((2, clips, feats), jnp.bfloat16),
             pltpu.VMEM((count, feats), jnp.float32),
             pltpu.VMEM((feats, count), jnp.bfloat16),
-            pltpu.VMEM((2, clips, LANES), jnp.float32),
             pltpu.SemaphoreType.DMA((3,)),
         ],
         compiler_params=params(24),
@@ -158,30 +150,34 @@
     )(ub)
 
 
-def row_kernel(protos_all, extra, t_ref, den_ref, *refs):
+def row_kernel(protos_all, extra, t_ref, *refs):
     col_parts, (row_ref, r_ref, acc_s) = refs[:-3], refs[-3:]
     clips, count = t_ref.shape[1:]
     groups, lines = clips // LANES, count // LANES
     r_ref[...] = 1.0 / (float(protos_all) * sum_of(col_parts))
-    if extra:
-        row_ref[2 * groups :, :] = den_ref[...]
     for v in range(2):
 
         def step(i, _, v=v):
             rows = pl.ds(pl.multiple_of(i * LANES, LANES), LANES)
             acc = jnp.zeros((LANES, LANES), jnp.float32)
+            den = jnp.zeros((LANES, LANES), jnp.float32)
             for j in range(lines):
                 t = t_ref[v, rows, j * LANES : (j + 1) * LANES]
                 acc = acc + t * t * r_ref[v * lines + j : v * lines + j + 1, :]
-            acc_s[pl.ds(pl.multiple_of((v * groups + i) * LANES, LANES), LANES), :] = acc
+                if extra:
+                    den = den + t
+            first = pl.multiple_of((v * groups + i) * LANES, LANES)
+            acc_s[pl.ds(first, LANES), :] = acc
+            if extra:
+                acc_s[pl.ds(2 * clips + first, LANES), :] = den
             return 0
 
         lax.fori_loop(0, groups, step, 0)
-    for line in range(2 * groups):
+    for line in range(row_ref.shape[0]):
         row_ref[line : line + 1, :] = to_line(acc_s[line * LANES : (line + 1) * LANES, :])
 
 
-def row_pass(t, den, col_parts, protos_all, extra):
+def row_pass(t, col_parts, protos_all, extra):
     clips, count = t.shape[1:]
     lines = 2 * clips // LANES * (2 if extra else 1)
     return pl.pallas_call(
@@ -190,12 +186,12 @@
             jax.ShapeDtypeStruct((lines, LANES), jnp.float32),
             jax.ShapeDtypeStruct((2 * count // LANES, LANES), jnp.float32),
         ),
-        in_specs=[vmem_spec()] * (2 + len(col_parts)),
+        in_specs=[vmem_spec()] * (1 + len(col_parts)),
         out_specs=(vmem_spec(),) * 2,
-        scratch_shapes=[pltpu.VMEM((2 * clips, LANES), jnp.float32)],
+        scratch_shapes=[pltpu.VMEM((lines * LANES, LANES), jnp.float32)],
         compiler_params=params(8),
         name="row_pass",
-    )(pltpu.with_memory_space_constraint(t, pltpu.VMEM), den, *col_parts)
+    )(pltpu.with_memory_space_constraint(t, pltpu.VMEM), *col_parts)
 
 
 def col_kernel(clips_all, t_ref, *refs):
@@ -287,7 +283,7 @@
 
 def send_kernel(orders, parts, t_ref, r_ref, ubt_ref, prob_s, *refs):
     row_parts = refs[:parts]
-    send_ref, g_ref, chunk_s, code_s = refs[parts:]
+    send_ref, g_ref, first_s, second_s, code_s = refs[parts:]
     clips, count = t_ref.shape[1:]
     groups, lines = clips // LANES, count // LANES
     pieces = 1 << len(orders[0])
@@ -296,34 +292,35 @@
     for line in range(2 * groups):
         code_s[line * LANES : (line + 1) * LANES, :] = to_columns(code[line : line + 1, :])
 
-    def score_grads(m, keep_chunk):
-        which, first = chunk_span(m, width)
-        for i in range(0, clips, 32):
-            rows = slice(i, i + 32)
-            codes = [code_s[v * clips + i : v * clips + i + 32, :] for v in range(2)]
-            probs = [prob_s[v * clips + i : v * clips + i + 32, :] for v in range(2)]
-            for h in range(width // LANES):
-                span = pl.ds(first + h * LANES, LANES)
-                line = which * (width // LANES) + h
-                t = [t_ref[v, rows, span] for v in range(2)]
-                q = [
-                    t[v] * t[v] * r_ref[pl.ds(v * lines + line, 1), :] * codes[v]
-                    for v in range(2)
-                ]
-                for v in range(2):
-                    g = (t[v] * probs[v] - q[1 - v]).astype(jnp.bfloat16)
-                    own = slice(v * clips + i, v * clips + i + 32)
-                    g_ref[own, span] = g
-                    if keep_chunk:
-                        chunk_s[own, h * LANES : (h + 1) * LANES] = g
-
-    def pair(i, _):
-        score_grads(2 * i + 1, True)
-        score_grads(2 * i, False)
-        proto_grads(ubt_ref[...], chunk_s[...], orders, i, send_ref)
+    def score_grads(i, chunk_s):
+        places = [chunk_span(2 * i + core, width) for core in range(2)]
+        for row in range(0, clips, 32):
+            codes = [code_s[v * clips + row : v * clips + row + 32, :] for v in range(2)]
+            probs = [prob_s[v * clips + row : v * clips + row + 32, :] for v in range(2)]
+            for core, (which, first) in enumerate(places):
+                for h in range(width // LANES):
+                    span = pl.ds(first + h * LANES, LANES)
+                    line = which * (width // LANES) + h
+                    t = [t_ref[v, row : row + 32, span] for v in range(2)]
+                    q = [
+                        t[v] * t[v] * r_ref[pl.ds(v * lines + line, 1), :] * codes[v]
+                        for v in range(2)
+                    ]
+                    for v in range(2):
+                        g = (t[v] * probs[v] - q[1 - v]).astype(jnp.bfloat16)
+                        own = slice(v * clips + row, v * clips + row + 32)
+                        g_ref[own, span] = g
+                        if core == 1:
+                            chunk_s[own, h * LANES : (h + 1) * LANES] = g
+
+    def two_pairs(k, _):
+        score_grads(2 * k, first_s)
+        score_grads(2 * k + 1, second_s)
+        proto_grads(ubt_ref[...], first_s[...], orders, 2 * k, send_ref)
+        proto_grads(ubt_ref[...], second_s[...], orders, 2 * k + 1, send_ref)
         return 0
 
-    lax.fori_loop(0, pieces, pair, 0)
+    lax.fori_loop(0, pieces // 2, two_pairs, 0)
 
 
 def send_gradients(t, r, ubt, prob, row_parts, orders):
@@ -340,6 +337,7 @@
         in_specs=[vmem_spec()] * (4 + len(row_parts)),
         out_specs=(vmem_spec(),) * 2,
         scratch_shapes=[
+            pltpu.VMEM((2 * clips, width), jnp.bfloat16),
             pltpu.VMEM((2 * clips, width), jnp.bfloat16),
             pltpu.VMEM((2 * clips, LANES), jnp.float32),
         ],
@@ -660,10 +658,12 @@
     batch_bits, proto_bits = bits_of("batch"), bits_of("proto")
     me_batch, me_proto = lax.axis_index("batch"), lax.axis_index("proto")
 
-    t, col, den, unit_b, proto_b = scores(slow_embed, fast_embed, prototypes)
+    t, col, unit_b, proto_b = scores(slow_embed, fast_embed, prototypes)
     unit_bt = turned(unit_b)
     for iteration in range(ITERS):
-        rows, r = row_pass(t, den, batch_parts(col, iteration % 2), protos_all, iteration == 0)
+        rows, r = row_pass(
+            t, batch_parts(col, iteration % 2), protos_all, iteration == 0
+        )
         row_parts = proto_parts(rows)
         if iteration == 0:
             prob = prob_columns(row_parts)

time: 136 us -> 136 us (level)
  no operation moved by 1% of the time
where the time goes in v13:
time: 136 us
  waiting for transfers between devices  54.7 us (40%)
  starting transfers between devices  44.8 us (33%)
  Pallas kernels  33.4 us (25%)
  local copies, waits for them, and re-layouts  1.99 us (1%)
    ppermute x44, waiting for transfers between devices, swap(): lax.ppermute(own, axis, [(i, i ^ mask) for i in range(lax.axis_size(axis))])  54.7 us
    ppermute x44, starting transfers between devices, swap(): lax.ppermute(own, axis, [(i, i ^ mask) for i in range(lax.axis_size(axis))])  44.8 us
    pallas_call x3, Pallas kernels, row_pass(): pl.pallas_call(functools.partial(row_kernel, protos_all, extra), out_shap...  7.49 us
    pallas_call x1, Pallas kernels, scores(): pl.pallas_call(score_kernel, out_shape=(pltpu.VMEM((2, clips, count), jnp...  6.73 us
    pallas_call x1, Pallas kernels, send_gradients(): pl.pallas_call(functools.partial(send_kernel, orders, len(row_parts)), ou...  6.61 us
    pallas_call x2, Pallas kernels, col_pass(): pl.pallas_call(functools.partial(col_kernel, clips_all), out_shape=jax.Sh...  4.37 us
  transfers between devices with their start and end apart: 44, of which 31 were waited for; matrix products, arithmetic and copies ran while one was open for 1% of the time, Pallas kernels for 4%

profile of v13, /device:TPU:0, one launch (start us, length us, event | category | flops | bytes accessed | tf_op | source)
XLA Modules:
  0.0 135.8 jit_solution(1193778003083998412)
XLA Ops:
  0.6 6.7 %scores.1 = (f32[2,1024,2048]{2,1,0:T(8,128)S(1)}, f32[32,128]{1,0:T(8,128)S(1)}, bf16[2,1024,256]{2,1,0:T(8,128)(2,1)S(1)}, bf16[2048,256]{1,0:T(8,128)(2,1)S(1)}) custom-call(bf16[1024,256]{1,0:T(8,128)(2,1)} %slow.1, bf16[1024,256]{1,0:T(8,128)(2,1)} %fast.1, f32[2048,256]{1,0:T(8,128)} %protos.1), custom_call_target="tpu_custom_call" | custom-call | tf_op jit(solution)/shard_map/scores/pallas_call | solution.py:109
  8.7 4.9 %collective-permute-start.1 = (f32[32,128]{1,0:T(8,128)S(1)}, f32[32,128]{1,0:T(8,128)S(1)}, u32[]{:S(2)}, u32[]{:S(2)}) collective-permute-start(f32[32,128]{1,0:T(8,128)S(1)} %add.18.refs_3_), channel_id=1, source_target_pairs={{0,24},{4,28},{8,16},{12,20},{16,8},{20,12},{24,0},{28,4},{1,25},{... | collective-permute-start | bytes 49160 | tf_op jit(solution)/shard_map/ppermute | solution.py:572
  15.4 2.9 %collective-permute-done.2.refs_1_ = f32[32,128]{1,0:T(8,128)S(1)} collective-permute-done((f32[32,128]{1,0:T(8,128)S(1)}, f32[32,128]{1,0:T(8,128)S(1)}, u32[]{:S(2)}, u32[]{:S(2)}) %collective-permute-start.2) | collective-permute-done | bytes 16416 | tf_op jit(solution)/shard_map/ppermute | solution.py:572
  18.3 3.0 %row_pass.3 = (f32[32,128]{1,0:T(8,128)S(1)}, f32[32,128]{1,0:T(8,128)}) custom-call(f32[2,1024,2048]{2,1,0:T(8,128)S(1)} %get-tuple-element.31.t_ref, f32[32,128]{1,0:T(8,128)S(1)} %collective-permute-done.1.refs_0_, f32[32,128]{1,0:T(8,128)S(1)} %collective-permute-done.2.refs_1_, f32[32,128]{1,0:T(8,128)S(1)} %collective-permute-done.3.refs_2_, ...), custom_call_target="tpu_custom_call" | custom-call | tf_op jit(solution)/shard_map/row_pass/pallas_call | solution.py:183
  21.4 2.5 %collective-permute-start.4 = (f32[32,128]{1,0:T(8,128)S(1)}, f32[32,128]{1,0:T(8,128)S(1)}, u32[]{:S(2)}, u32[]{:S(2)}) collective-permute-start(f32[32,128]{1,0:T(8,128)S(1)} %get-tuple-element.33.refs_3_), channel_id=1, source_target_pairs={{0,3},{1,2},{2,1},{3,0},{4,7},{5,6},{6,5},{7,4},{8,11},{9,10},{10,... | collective-permute-start | bytes 49160 | tf_op jit(solution)/shard_map/ppermute | solution.py:572
  26.1 1.5 %collective-permute-done.5.refs_1_ = f32[32,128]{1,0:T(8,128)S(1)} collective-permute-done((f32[32,128]{1,0:T(8,128)S(1)}, f32[32,128]{1,0:T(8,128)S(1)}, u32[]{:S(2)}, u32[]{:S(2)}) %collective-permute-start.5) | collective-permute-done | bytes 16416 | tf_op jit(solution)/shard_map/ppermute | solution.py:572
  28.1 2.2 %col_pass.2 = f32[32,128]{1,0:T(8,128)S(1)} custom-call(f32[2,1024,2048]{2,1,0:T(8,128)S(1)} %get-tuple-element.31.t_ref, f32[32,128]{1,0:T(8,128)S(1)} %collective-permute-done.4.refs_0_, f32[32,128]{1,0:T(8,128)S(1)} %collective-permute-done.5.refs_1_, f32[32,128]{1,0:T(8,128)S(1)} %collective-permute-done.6.refs_2_, f32[32,128]{1,0:T(8,128)S(1)} %get-tuple-element.33.refs_3_), custom_call_target="tpu_custom_call" | custom-call | tf_op jit(solution)/shard_map/col_pass/pallas_call | solution.py:225
  33.6 2.3 %collective-permute-start.9 = (f32[32,128]{1,0:T(8,128)S(1)}, f32[32,128]{1,0:T(8,128)S(1)}, u32[]{:S(2)}, u32[]{:S(2)}) collective-permute-start(f32[32,128]{1,0:T(8,128)S(1)} %add.19.refs_3_), channel_id=1, source_target_pairs={{0,8},{4,12},{8,0},{12,4},{16,24},{20,28},{24,16},{28,20},{1,9},{5... | collective-permute-start | bytes 49160 | tf_op jit(solution)/shard_map/ppermute | solution.py:572
  37.8 2.4 %row_pass.4 = (f32[16,128]{1,0:T(8,128)S(1)}, f32[32,128]{1,0:T(8,128)}) custom-call(f32[2,1024,2048]{2,1,0:T(8,128)S(1)} %get-tuple-element.31.t_ref, f32[32,128]{1,0:T(8,128)S(1)} %collective-permute-done.8.refs_0_, f32[32,128]{1,0:T(8,128)S(1)} %collective-permute-done.9.refs_1_, f32[32,128]{1,0:T(8,128)S(1)} %collective-permute-done.10.refs_2_, ...), custom_call_target="tpu_custom_call" | custom-call | tf_op jit(solution)/shard_map/row_pass/pallas_call | solution.py:183
  40.2 1.5 %collective-permute-start.11 = (f32[16,128]{1,0:T(8,128)S(1)}, f32[16,128]{1,0:T(8,128)S(1)}, u32[]{:S(2)}, u32[]{:S(2)}) collective-permute-start(f32[16,128]{1,0:T(8,128)S(1)} %get-tuple-element.34.refs_3_), channel_id=1, source_target_pairs={{0,3},{1,2},{2,1},{3,0},{4,7},{5,6},{6,5},{7,4},{8,11},{9,10},{10,... | collective-permute-start | bytes 24584 | tf_op jit(solution)/shard_map/ppermute | solution.py:572
  42.2 1.5 %collective-permute-start.13 = (f32[16,128]{1,0:T(8,128)S(1)}, f32[16,128]{1,0:T(8,128)S(1)}, u32[]{:S(2)}, u32[]{:S(2)}) collective-permute-start(f32[16,128]{1,0:T(8,128)S(1)} %get-tuple-element.34.refs_3_), channel_id=1, source_target_pairs={{0,1},{1,0},{2,3},{3,2},{4,5},{5,4},{6,7},{7,6},{8,9},{9,8},{10,11... | collective-permute-start | bytes 24584 | tf_op jit(solution)/shard_map/ppermute | solution.py:572
  45.8 2.2 %col_pass.3 = f32[32,128]{1,0:T(8,128)S(1)} custom-call(f32[2,1024,2048]{2,1,0:T(8,128)S(1)} %get-tuple-element.31.t_ref, f32[16,128]{1,0:T(8,128)S(1)} %collective-permute-done.11.refs_0_, f32[16,128]{1,0:T(8,128)S(1)} %collective-permute-done.12.refs_1_, f32[16,128]{1,0:T(8,128)S(1)} %collective-permute-done.13.refs_2_, ...), custom_call_target="tpu_custom_call" | custom-call | tf_op jit(solution)/shard_map/col_pass/pallas_call | solution.py:225
  49.3 2.4 %collective-permute-start.15 = (f32[32,128]{1,0:T(8,128)S(1)}, f32[32,128]{1,0:T(8,128)S(1)}, u32[]{:S(2)}, u32[]{:S(2)}) collective-permute-start(f32[32,128]{1,0:T(8,128)S(1)} %add.20.refs_3_), channel_id=1, source_target_pairs={{0,24},{4,28},{8,16},{12,20},{16,8},{20,12},{24,0},{28,4},{1,25},{... | collective-permute-start | bytes 49160 | tf_op jit(solution)/shard_map/ppermute | solution.py:572
  56.5 2.1 %row_pass.5 = (f32[16,128]{1,0:T(8,128)S(1)}, f32[32,128]{1,0:T(8,128)S(1)}) custom-call(f32[2,1024,2048]{2,1,0:T(8,128)S(1)} %get-tuple-element.31.t_ref, f32[32,128]{1,0:T(8,128)S(1)} %collective-permute-done.15.refs_0_, f32[32,128]{1,0:T(8,128)S(1)} %collective-permute-done.16.refs_1_, f32[32,128]{1,0:T(8,128)S(1)} %collective-permute-done.17.refs_2_, ...), custom_call_target="tpu_custom_call" | custom-call | tf_op jit(solution)/shard_map/row_pass/pallas_call | solution.py:183
  58.6 2.5 %collective-permute-start.18 = (f32[16,128]{1,0:T(8,128)S(1)}, f32[16,128]{1,0:T(8,128)S(1)}, u32[]{:S(2)}, u32[]{:S(2)}) collective-permute-start(f32[16,128]{1,0:T(8,128)S(1)} %get-tuple-element.37.refs_3_), channel_id=1, source_target_pairs={{0,3},{1,2},{2,1},{3,0},{4,7},{5,6},{6,5},{7,4},{8,11},{9,10},{10,... | collective-permute-start | bytes 24584 | tf_op jit(solution)/shard_map/ppermute | solution.py:572
  63.3 1.5 %collective-permute-done.19.refs_1_ = f32[16,128]{1,0:T(8,128)S(1)} collective-permute-done((f32[16,128]{1,0:T(8,128)S(1)}, f32[16,128]{1,0:T(8,128)S(1)}, u32[]{:S(2)}, u32[]{:S(2)}) %collective-permute-start.19) | collective-permute-done | bytes 8224 | tf_op jit(solution)/shard_map/ppermute | solution.py:572
  65.3 6.6 %send_gradients.1 = (f32[2,4,128,256]{3,2,1,0:T(8,128)S(1)}, bf16[2048,2048]{1,0:T(8,128)(2,1)S(1)}) custom-call(f32[2,1024,2048]{2,1,0:T(8,128)S(1)} %get-tuple-element.31.t_ref, f32[32,128]{1,0:T(8,128)S(1)} %get-tuple-element.35.r_ref, bf16[256,2048]{1,0:T(8,128)(2,1)S(1)} %turned.1.ubt_ref, f32[2048,128]{1,0:T(8,128)S(1)} %prob_columns.1.prob_s, ...), custom_call_target="tpu_custom_call" | custom-call | flops 1073741824 | bytes 20971520 | tf_op jit(solution)/shard_map/send_gradients/pallas_call | solution.py:331
  72.0 2.3 %embed_gradients.1 = (f32[2,256,256]{2,1,0:T(8,128)S(1)}, f32[2,256,256]{2,1,0:T(8,128)S(1)}, f32[2,256,256]{2,1,0:T(8,128)S(1)}, f32[2,256,256]{2,1,0:T(8,128)S(1)}) custom-call(bf16[2048,2048]{1,0:T(8,128)(2,1)S(1)} %get-tuple-element.38.g_ref, bf16[2048,256]{1,0:T(8,128)(2,1)S(1)} %get-tuple-element.39.cb_ref), custom_call_target="tpu_custom_call" | custom-call | flops 2147483648 | bytes 11534336 | tf_op jit(solution)/shard_map/embed_gradients/pallas_call | solution.py:371
  74.9 1.5 %collective-permute-start.27 = (f32[2,256,256]{2,1,0:T(8,128)S(1)}, f32[2,256,256]{2,1,0:T(8,128)S(1)}, u32[]{:S(2)}, u32[]{:S(2)}) collective-permute-start(f32[2,256,256]{2,1,0:T(8,128)S(1)} %get-tuple-element.52), channel_id=1, source_target_pairs={{0,2},{1,3},{2,0},{3,1},{4,6},{5,7},{6,4},{7,5},{8,10},{9,11},{10,... | collective-permute-start | bytes 1572872 | tf_op jit(solution)/shard_map/ppermute | solution.py:572
  76.4 2.1 %keep_gradients.1.refs_0_ = f32[2,4,128,256]{3,2,1,0:T(8,128)S(1)} custom-call(bf16[2048,2048]{1,0:T(8,128)(2,1)S(1)} %get-tuple-element.38.g_ref, bf16[256,2048]{1,0:T(8,128)(2,1)S(1)} %turned.1.ubt_ref, f32[2,256,256]{2,1,0:T(8,128)S(1)} %get-tuple-element.40.after_ref), custom_call_target="tpu_custom_call" | custom-call | flops 1073741824 | bytes 6291456 | tf_op jit(solution)/shard_map/keep_gradients/pallas_call | solution.py:400
  78.7 1.9 %collective-permute-start.22 = (f32[2,128,256]{2,1,0:T(8,128)S(1)}, f32[2,128,256]{2,1,0:T(8,128)S(1)}, u32[]{:S(2)}, u32[]{:S(2)}) collective-permute-start(f32[2,128,256]{2,1,0:T(8,128)S(1)} %get-tuple-element.43), channel_id=1, source_target_pairs={{0,16},{4,20},{8,24},{12,28},{16,0},{20,4},{24,8},{28,12},{1,17},{... | collective-permute-start | bytes 786440 | tf_op jit(solution)/shard_map/ppermute | solution.py:572
  80.7 8.0 %collective-permute-done.26.refs_1_ = f32[2,256,256]{2,1,0:T(8,128)S(1)} collective-permute-done((f32[2,256,256]{2,1,0:T(8,128)S(1)}, f32[2,256,256]{2,1,0:T(8,128)S(1)}, u32[]{:S(2)}, u32[]{:S(2)}) %collective-permute-start.26) | collective-permute-done | bytes 524320 | tf_op jit(solution)/shard_map/ppermute | solution.py:572
  89.1 1.6 %collective-permute-start.28 = (f32[1,256,256]{2,1,0:T(8,128)S(1)}, f32[1,256,256]{2,1,0:T(8,128)S(1)}, u32[]{:S(2)}, u32[]{:S(2)}) collective-permute-start(f32[1,256,256]{2,1,0:T(8,128)S(1)} %get-tuple-element.54), channel_id=1, source_target_pairs={{0,2},{1,3},{2,0},{3,1},{4,6},{5,7},{6,4},{7,5},{8,10},{9,11},{10,... | collective-permute-start | bytes 786440 | tf_op jit(solution)/shard_map/ppermute | solution.py:572
  90.7 1.5 %collective-permute-start.29 = (f32[1,256,256]{2,1,0:T(8,128)S(1)}, f32[1,256,256]{2,1,0:T(8,128)S(1)}, u32[]{:S(2)}, u32[]{:S(2)}) collective-permute-start(f32[1,256,256]{2,1,0:T(8,128)S(1)} %get-tuple-element.56), channel_id=1, source_target_pairs={{0,1},{1,0},{2,3},{3,2},{4,5},{5,4},{6,7},{7,6},{8,9},{9,8},{10,11... | collective-permute-start | bytes 786440 | tf_op jit(solution)/shard_map/ppermute | solution.py:572
  98.0 4.1 %collective-permute-done.24.refs_1_ = f32[1,128,256]{2,1,0:T(8,128)S(1)} collective-permute-done((f32[1,128,256]{2,1,0:T(8,128)S(1)}, f32[1,128,256]{2,1,0:T(8,128)S(1)}, u32[]{:S(2)}, u32[]{:S(2)}) %collective-permute-start.24) | collective-permute-done | bytes 131104 | tf_op jit(solution)/shard_map/ppermute | solution.py:572
  106.6 9.4 %collective-permute-done.33.refs_4_.refs_8_ = f32[264,256]{1,0:T(8,128)S(1)} collective-permute-done((f32[264,256]{1,0:T(8,128)S(1)}, f32[264,256]{1,0:T(8,128)S(1)}, u32[]{:S(2)}, u32[]{:S(2)}) %collective-permute-start.33) | collective-permute-done | bytes 270368 | tf_op jit(solution)/shard_map/ppermute | solution.py:572
  116.0 2.3 %collective-permute-done.31.refs_2_.refs_6_ = f32[264,256]{1,0:T(8,128)S(1)} collective-permute-done((f32[264,256]{1,0:T(8,128)S(1)}, f32[264,256]{1,0:T(8,128)S(1)}, u32[]{:S(2)}, u32[]{:S(2)}) %collective-permute-start.31) | collective-permute-done | bytes 270368 | tf_op jit(solution)/shard_map/ppermute | solution.py:572
  119.4 4.9 %collective-permute-done.35.refs_6_.refs_10_ = f32[264,256]{1,0:T(8,128)S(1)} collective-permute-done((f32[264,256]{1,0:T(8,128)S(1)}, f32[264,256]{1,0:T(8,128)S(1)}, u32[]{:S(2)}, u32[]{:S(2)}) %collective-permute-start.35) | collective-permute-done | bytes 270368 | tf_op jit(solution)/shard_map/ppermute | solution.py:572
  124.3 1.7 %collective-permute-start.43 = (f32[256,256]{1,0:T(8,128)S(1)}, f32[256,256]{1,0:T(8,128)S(1)}, u32[]{:S(2)}, u32[]{:S(2)}) collective-permute-start(f32[256,256]{1,0:T(8,128)S(1)} %slice_bitcast_fusion), channel_id=1, source_target_pairs={{0,2},{1,3},{2,0},{3,1},{4,6},{5,7},{6,4},{7,5},{8,10},{9,11},{10,... | collective-permute-start | bytes 786440 | tf_op jit(solution)/shard_map/ppermute | solution.py:572
  126.0 2.3 %collective-permute-start.37 = (f32[2,8,128]{2,1,0:T(8,128)S(1)}, f32[2,8,128]{2,1,0:T(8,128)S(1)}, u32[]{:S(2)}, u32[]{:S(2)}) collective-permute-start(f32[2,8,128]{2,1,0:T(8,128)S(1)} %sum_squares.1.refs_3_), channel_id=1, source_target_pairs={{0,3},{1,2},{2,1},{3,0},{4,7},{5,6},{6,5},{7,4},{8,11},{9,10},{10,... | collective-permute-start | bytes 24584 | tf_op jit(solution)/shard_map/ppermute | solution.py:572
  129.6 3.8 %collective-permute-done.43.refs_16_ = f32[256,256]{1,0:T(8,128)S(1)} collective-permute-done((f32[256,256]{1,0:T(8,128)S(1)}, f32[256,256]{1,0:T(8,128)S(1)}, u32[]{:S(2)}, u32[]{:S(2)}) %collective-permute-start.43) | collective-permute-done | bytes 262176 | tf_op jit(solution)/shard_map/ppermute | solution.py:572
  133.5 2.2 %finish.1 = (f32[2048,256]{1,0:T(8,128)}, f32[1024,256]{1,0:T(8,128)}, f32[1024,256]{1,0:T(8,128)}) custom-call(f32[2,8,128]{2,1,0:T(8,128)S(1)} %collective-permute-done.37.refs_0_, f32[2,8,128]{2,1,0:T(8,128)S(1)} %collective-permute-done.38.refs_1_, f32[2,8,128]{2,1,0:T(8,128)S(1)} %collective-permute-done.39.refs_2_, ...), custom_call_target="tpu_custom_call" | custom-call | tf_op jit(solution)/shard_map/finish/pallas_call | solution.py:560
  (80 shorter events, 36.4 us)
Async XLA Ops:
  8.7 6.7 %collective-permute-start.1 = (f32[32,128]{1,0:T(8,128)S(1)}, f32[32,128]{1,0:T(8,128)S(1)}, u32[]{:S(2)}, u32[]{:S(2)}) collective-permute-start(f32[32,128]{1,0:T(8,128)S(1)} %add.18.refs_3_), channel_id=1, source_target_pairs={{0,24},{4,28},{8,16},{12,20},{16,8},{20,12},{24,0},{28,4},{1,25},{... | collective-permute-start | bytes 49160 | tf_op jit(solution)/shard_map/ppermute | solution.py:572
  13.7 4.6 %collective-permute-start.2 = (f32[32,128]{1,0:T(8,128)S(1)}, f32[32,128]{1,0:T(8,128)S(1)}, u32[]{:S(2)}, u32[]{:S(2)}) collective-permute-start(f32[32,128]{1,0:T(8,128)S(1)} %add.18.refs_3_), channel_id=1, source_target_pairs={{0,16},{4,20},{8,24},{12,28},{16,0},{20,4},{24,8},{28,12},{1,17},{... | collective-permute-start | bytes 49160 | tf_op jit(solution)/shard_map/ppermute | solution.py:572
  13.7 4.6 %collective-permute-start.3 = (f32[32,128]{1,0:T(8,128)S(1)}, f32[32,128]{1,0:T(8,128)S(1)}, u32[]{:S(2)}, u32[]{:S(2)}) collective-permute-start(f32[32,128]{1,0:T(8,128)S(1)} %add.18.refs_3_), channel_id=1, source_target_pairs={{0,8},{4,12},{8,0},{12,4},{16,24},{20,28},{24,16},{28,20},{1,9},{5... | collective-permute-start | bytes 49160 | tf_op jit(solution)/shard_map/ppermute | solution.py:572
  21.4 4.7 %collective-permute-start.4 = (f32[32,128]{1,0:T(8,128)S(1)}, f32[32,128]{1,0:T(8,128)S(1)}, u32[]{:S(2)}, u32[]{:S(2)}) collective-permute-start(f32[32,128]{1,0:T(8,128)S(1)} %get-tuple-element.33.refs_3_), channel_id=1, source_target_pairs={{0,3},{1,2},{2,1},{3,0},{4,7},{5,6},{6,5},{7,4},{8,11},{9,10},{10,... | collective-permute-start | bytes 49160 | tf_op jit(solution)/shard_map/ppermute | solution.py:572
  31.6 5.7 %collective-permute-start.10 = (f32[32,128]{1,0:T(8,128)S(1)}, f32[32,128]{1,0:T(8,128)S(1)}, u32[]{:S(2)}, u32[]{:S(2)}) collective-permute-start(f32[32,128]{1,0:T(8,128)S(1)} %add.19.refs_3_), channel_id=1, source_target_pairs={{0,24},{4,28},{8,16},{12,20},{16,8},{20,12},{24,0},{28,4},{1,25},{... | collective-permute-start | bytes 49160 | tf_op jit(solution)/shard_map/ppermute | solution.py:572
  33.0 4.7 %collective-permute-start.8 = (f32[32,128]{1,0:T(8,128)S(1)}, f32[32,128]{1,0:T(8,128)S(1)}, u32[]{:S(2)}, u32[]{:S(2)}) collective-permute-start(f32[32,128]{1,0:T(8,128)S(1)} %add.19.refs_3_), channel_id=1, source_target_pairs={{0,16},{4,20},{8,24},{12,28},{16,0},{20,4},{24,8},{28,12},{1,17},{... | collective-permute-start | bytes 49160 | tf_op jit(solution)/shard_map/ppermute | solution.py:572
  40.2 4.5 %collective-permute-start.11 = (f32[16,128]{1,0:T(8,128)S(1)}, f32[16,128]{1,0:T(8,128)S(1)}, u32[]{:S(2)}, u32[]{:S(2)}) collective-permute-start(f32[16,128]{1,0:T(8,128)S(1)} %get-tuple-element.34.refs_3_), channel_id=1, source_target_pairs={{0,3},{1,2},{2,1},{3,0},{4,7},{5,6},{6,5},{7,4},{8,11},{9,10},{10,... | collective-permute-start | bytes 24584 | tf_op jit(solution)/shard_map/ppermute | solution.py:572
  49.3 5.6 %collective-permute-start.15 = (f32[32,128]{1,0:T(8,128)S(1)}, f32[32,128]{1,0:T(8,128)S(1)}, u32[]{:S(2)}, u32[]{:S(2)}) collective-permute-start(f32[32,128]{1,0:T(8,128)S(1)} %add.20.refs_3_), channel_id=1, source_target_pairs={{0,24},{4,28},{8,16},{12,20},{16,8},{20,12},{24,0},{28,4},{1,25},{... | collective-permute-start | bytes 49160 | tf_op jit(solution)/shard_map/ppermute | solution.py:572
  51.7 4.7 %collective-permute-start.16 = (f32[32,128]{1,0:T(8,128)S(1)}, f32[32,128]{1,0:T(8,128)S(1)}, u32[]{:S(2)}, u32[]{:S(2)}) collective-permute-start(f32[32,128]{1,0:T(8,128)S(1)} %add.20.refs_3_), channel_id=1, source_target_pairs={{0,16},{4,20},{8,24},{12,28},{16,0},{20,4},{24,8},{28,12},{1,17},{... | collective-permute-start | bytes 49160 | tf_op jit(solution)/shard_map/ppermute | solution.py:572
  58.6 4.7 %collective-permute-start.18 = (f32[16,128]{1,0:T(8,128)S(1)}, f32[16,128]{1,0:T(8,128)S(1)}, u32[]{:S(2)}, u32[]{:S(2)}) collective-permute-start(f32[16,128]{1,0:T(8,128)S(1)} %get-tuple-element.37.refs_3_), channel_id=1, source_target_pairs={{0,3},{1,2},{2,1},{3,0},{4,7},{5,6},{6,5},{7,4},{8,11},{9,10},{10,... | collective-permute-start | bytes 24584 | tf_op jit(solution)/shard_map/ppermute | solution.py:572
  71.9 6.6 %collective-permute-start.21 = (f32[2,4,128,256]{3,2,1,0:T(8,128)S(1)}, f32[2,4,128,256]{3,2,1,0:T(8,128)S(1)}, u32[]{:S(2)}, u32[]{:S(2)}) collective-permute-start(f32[2,4,128,256]{3,2,1,0:T(8,128)S(1)} %get-tuple-element.41), channel_id=1, source_target_pairs={{0,4},{4,0},{8,12},{12,8},{16,20},{20,16},{24,28},{28,24},{1,5},{5... | collective-permute-start | bytes 3145736 | tf_op jit(solution)/shard_map/ppermute | solution.py:572
  74.3 14.4 %collective-permute-start.26 = (f32[2,256,256]{2,1,0:T(8,128)S(1)}, f32[2,256,256]{2,1,0:T(8,128)S(1)}, u32[]{:S(2)}, u32[]{:S(2)}) collective-permute-start(f32[2,256,256]{2,1,0:T(8,128)S(1)} %get-tuple-element.40.after_ref), channel_id=1, source_target_pairs={{0,1},{1,0},{2,3},{3,2},{4,5},{5,4},{6,7},{7,6},{8,9},{9,8},{10,11... | collective-permute-start | bytes 1572872 | tf_op jit(solution)/shard_map/ppermute | solution.py:572
  74.9 14.0 %collective-permute-start.27 = (f32[2,256,256]{2,1,0:T(8,128)S(1)}, f32[2,256,256]{2,1,0:T(8,128)S(1)}, u32[]{:S(2)}, u32[]{:S(2)}) collective-permute-start(f32[2,256,256]{2,1,0:T(8,128)S(1)} %get-tuple-element.52), channel_id=1, source_target_pairs={{0,2},{1,3},{2,0},{3,1},{4,6},{5,7},{6,4},{7,5},{8,10},{9,11},{10,... | collective-permute-start | bytes 1572872 | tf_op jit(solution)/shard_map/ppermute | solution.py:572
  78.7 14.8 %collective-permute-start.22 = (f32[2,128,256]{2,1,0:T(8,128)S(1)}, f32[2,128,256]{2,1,0:T(8,128)S(1)}, u32[]{:S(2)}, u32[]{:S(2)}) collective-permute-start(f32[2,128,256]{2,1,0:T(8,128)S(1)} %get-tuple-element.43), channel_id=1, source_target_pairs={{0,16},{4,20},{8,24},{12,28},{16,0},{20,4},{24,8},{28,12},{1,17},{... | collective-permute-start | bytes 786440 | tf_op jit(solution)/shard_map/ppermute | solution.py:572
  80.6 13.1 %collective-permute-start.23 = (f32[2,128,256]{2,1,0:T(8,128)S(1)}, f32[2,128,256]{2,1,0:T(8,128)S(1)}, u32[]{:S(2)}, u32[]{:S(2)}) collective-permute-start(f32[2,128,256]{2,1,0:T(8,128)S(1)} %get-tuple-element.45), channel_id=1, source_target_pairs={{0,8},{4,12},{8,0},{12,4},{16,24},{20,28},{24,16},{28,20},{1,9},{5... | collective-permute-start | bytes 786440 | tf_op jit(solution)/shard_map/ppermute | solution.py:572
  89.1 8.4 %collective-permute-start.28 = (f32[1,256,256]{2,1,0:T(8,128)S(1)}, f32[1,256,256]{2,1,0:T(8,128)S(1)}, u32[]{:S(2)}, u32[]{:S(2)}) collective-permute-start(f32[1,256,256]{2,1,0:T(8,128)S(1)} %get-tuple-element.54), channel_id=1, source_target_pairs={{0,2},{1,3},{2,0},{3,1},{4,6},{5,7},{6,4},{7,5},{8,10},{9,11},{10,... | collective-permute-start | bytes 786440 | tf_op jit(solution)/shard_map/ppermute | solution.py:572
  90.7 7.4 %collective-permute-start.29 = (f32[1,256,256]{2,1,0:T(8,128)S(1)}, f32[1,256,256]{2,1,0:T(8,128)S(1)}, u32[]{:S(2)}, u32[]{:S(2)}) collective-permute-start(f32[1,256,256]{2,1,0:T(8,128)S(1)} %get-tuple-element.56), channel_id=1, source_target_pairs={{0,1},{1,0},{2,3},{3,2},{4,5},{5,4},{6,7},{7,6},{8,9},{9,8},{10,11... | collective-permute-start | bytes 786440 | tf_op jit(solution)/shard_map/ppermute | solution.py:572
  93.7 8.5 %collective-permute-start.24 = (f32[1,128,256]{2,1,0:T(8,128)S(1)}, f32[1,128,256]{2,1,0:T(8,128)S(1)}, u32[]{:S(2)}, u32[]{:S(2)}) collective-permute-start(f32[1,128,256]{2,1,0:T(8,128)S(1)} %get-tuple-element.47), channel_id=1, source_target_pairs={{0,16},{4,20},{8,24},{12,28},{16,0},{20,4},{24,8},{28,12},{1,17},{... | collective-permute-start | bytes 393224 | tf_op jit(solution)/shard_map/ppermute | solution.py:572
  94.4 7.8 %collective-permute-start.25 = (f32[1,128,256]{2,1,0:T(8,128)S(1)}, f32[1,128,256]{2,1,0:T(8,128)S(1)}, u32[]{:S(2)}, u32[]{:S(2)}) collective-permute-start(f32[1,128,256]{2,1,0:T(8,128)S(1)} %get-tuple-element.49), channel_id=1, source_target_pairs={{0,8},{4,12},{8,0},{12,4},{16,24},{20,28},{24,16},{28,20},{1,9},{5... | collective-permute-start | bytes 393224 | tf_op jit(solution)/shard_map/ppermute | solution.py:572
  102.8 15.5 %collective-permute-start.41 = (f32[2,256,256]{2,1,0:T(8,128)S(1)}, f32[2,256,256]{2,1,0:T(8,128)S(1)}, u32[]{:S(2)}, u32[]{:S(2)}) collective-permute-start(f32[2,256,256]{2,1,0:T(8,128)S(1)} %get-tuple-element.58.refs_12_), channel_id=1, source_target_pairs={{0,2},{1,3},{2,0},{3,1},{4,6},{5,7},{6,4},{7,5},{8,10},{9,11},{10,... | collective-permute-start | bytes 1572872 | tf_op jit(solution)/shard_map/ppermute | solution.py:572
  103.3 12.6 %collective-permute-start.33 = (f32[264,256]{1,0:T(8,128)S(1)}, f32[264,256]{1,0:T(8,128)S(1)}, u32[]{:S(2)}, u32[]{:S(2)}) collective-permute-start(f32[264,256]{1,0:T(8,128)S(1)} %get-tuple-element.57.refs_0_.refs_4_), channel_id=1, source_target_pairs={{0,16},{4,20},{8,24},{12,28},{16,0},{20,4},{24,8},{28,12},{1,17},{... | collective-permute-start | bytes 811016 | tf_op jit(solution)/shard_map/ppermute | solution.py:572
  103.9 14.9 %collective-permute-start.40 = (f32[2,256,256]{2,1,0:T(8,128)S(1)}, f32[2,256,256]{2,1,0:T(8,128)S(1)}, u32[]{:S(2)}, u32[]{:S(2)}) collective-permute-start(f32[2,256,256]{2,1,0:T(8,128)S(1)} %get-tuple-element.58.refs_12_), channel_id=1, source_target_pairs={{0,1},{1,0},{2,3},{3,2},{4,5},{5,4},{6,7},{7,6},{8,9},{9,8},{10,11... | collective-permute-start | bytes 1572872 | tf_op jit(solution)/shard_map/ppermute | solution.py:572
  105.4 12.9 %collective-permute-start.31 = (f32[264,256]{1,0:T(8,128)S(1)}, f32[264,256]{1,0:T(8,128)S(1)}, u32[]{:S(2)}, u32[]{:S(2)}) collective-permute-start(f32[264,256]{1,0:T(8,128)S(1)} %get-tuple-element.57.refs_0_.refs_4_), channel_id=1, source_target_pairs={{0,8},{4,12},{8,0},{12,4},{16,24},{20,28},{24,16},{28,20},{1,9},{5... | collective-permute-start | bytes 811016 | tf_op jit(solution)/shard_map/ppermute | solution.py:572
  116.0 8.3 %collective-permute-start.35 = (f32[264,256]{1,0:T(8,128)S(1)}, f32[264,256]{1,0:T(8,128)S(1)}, u32[]{:S(2)}, u32[]{:S(2)}) collective-permute-start(f32[264,256]{1,0:T(8,128)S(1)} %collective-permute-done.33.refs_4_.refs_8_), channel_id=1, source_target_pairs={{0,8},{4,12},{8,0},{12,4},{16,24},{20,28},{24,16},{28,20},{1,9},{5... | collective-permute-start | bytes 811016 | tf_op jit(solution)/shard_map/ppermute | solution.py:572
  116.0 8.4 %collective-permute-start.30 = (f32[264,256]{1,0:T(8,128)S(1)}, f32[264,256]{1,0:T(8,128)S(1)}, u32[]{:S(2)}, u32[]{:S(2)}) collective-permute-start(f32[264,256]{1,0:T(8,128)S(1)} %get-tuple-element.57.refs_0_.refs_4_), channel_id=1, source_target_pairs={{0,4},{4,0},{8,12},{12,8},{16,20},{20,16},{24,28},{28,24},{1,5},{5... | collective-permute-start | bytes 811016 | tf_op jit(solution)/shard_map/ppermute | solution.py:572
  118.3 7.7 %collective-permute-start.34 = (f32[264,256]{1,0:T(8,128)S(1)}, f32[264,256]{1,0:T(8,128)S(1)}, u32[]{:S(2)}, u32[]{:S(2)}) collective-permute-start(f32[264,256]{1,0:T(8,128)S(1)} %collective-permute-done.33.refs_4_.refs_8_), channel_id=1, source_target_pairs={{0,4},{4,0},{8,12},{12,8},{16,20},{20,16},{24,28},{28,24},{1,5},{5... | collective-permute-start | bytes 811016 | tf_op jit(solution)/shard_map/ppermute | solution.py:572
  118.3 7.7 %collective-permute-start.32 = (f32[264,256]{1,0:T(8,128)S(1)}, f32[264,256]{1,0:T(8,128)S(1)}, u32[]{:S(2)}, u32[]{:S(2)}) collective-permute-start(f32[264,256]{1,0:T(8,128)S(1)} %collective-permute-done.31.refs_2_.refs_6_), channel_id=1, source_target_pairs={{0,4},{4,0},{8,12},{12,8},{16,20},{20,16},{24,28},{28,24},{1,5},{5... | collective-permute-start | bytes 811016 | tf_op jit(solution)/shard_map/ppermute | solution.py:572
  118.8 10.8 %collective-permute-start.42 = (f32[256,256]{1,0:T(8,128)S(1)}, f32[256,256]{1,0:T(8,128)S(1)}, u32[]{:S(2)}, u32[]{:S(2)}) collective-permute-start(f32[256,256]{1,0:T(8,128)S(1)} %slice_bitcast_fusion.1), channel_id=1, source_target_pairs={{0,1},{1,0},{2,3},{3,2},{4,5},{5,4},{6,7},{7,6},{8,9},{9,8},{10,11... | collective-permute-start | bytes 786440 | tf_op jit(solution)/shard_map/ppermute | solution.py:572
  124.3 9.0 %collective-permute-start.43 = (f32[256,256]{1,0:T(8,128)S(1)}, f32[256,256]{1,0:T(8,128)S(1)}, u32[]{:S(2)}, u32[]{:S(2)}) collective-permute-start(f32[256,256]{1,0:T(8,128)S(1)} %slice_bitcast_fusion), channel_id=1, source_target_pairs={{0,2},{1,3},{2,0},{3,1},{4,6},{5,7},{6,4},{7,5},{8,10},{9,11},{10,... | collective-permute-start | bytes 786440 | tf_op jit(solution)/shard_map/ppermute | solution.py:572
  126.0 7.4 %collective-permute-start.37 = (f32[2,8,128]{2,1,0:T(8,128)S(1)}, f32[2,8,128]{2,1,0:T(8,128)S(1)}, u32[]{:S(2)}, u32[]{:S(2)}) collective-permute-start(f32[2,8,128]{2,1,0:T(8,128)S(1)} %sum_squares.1.refs_3_), channel_id=1, source_target_pairs={{0,3},{1,2},{2,1},{3,0},{4,7},{5,6},{6,5},{7,4},{8,11},{9,10},{10,... | collective-permute-start | bytes 24584 | tf_op jit(solution)/shard_map/ppermute | solution.py:572
  128.4 5.1 %collective-permute-start.38 = (f32[2,8,128]{2,1,0:T(8,128)S(1)}, f32[2,8,128]{2,1,0:T(8,128)S(1)}, u32[]{:S(2)}, u32[]{:S(2)}) collective-permute-start(f32[2,8,128]{2,1,0:T(8,128)S(1)} %sum_squares.1.refs_3_), channel_id=1, source_target_pairs={{0,2},{1,3},{2,0},{3,1},{4,6},{5,7},{6,4},{7,5},{8,10},{9,11},{10,... | collective-permute-start | bytes 24584 | tf_op jit(solution)/shard_map/ppermute | solution.py:572
  129.0 4.5 %collective-permute-start.39 = (f32[2,8,128]{2,1,0:T(8,128)S(1)}, f32[2,8,128]{2,1,0:T(8,128)S(1)}, u32[]{:S(2)}, u32[]{:S(2)}) collective-permute-start(f32[2,8,128]{2,1,0:T(8,128)S(1)} %sum_squares.1.refs_3_), channel_id=1, source_target_pairs={{0,1},{1,0},{2,3},{3,2},{4,5},{5,4},{6,7},{7,6},{8,9},{9,8},{10,11... | collective-permute-start | bytes 24584 | tf_op jit(solution)/shard_map/ppermute | solution.py:572
  (12 other events, 35.7 us)

commit v14 on v12

--- a/solution.py
+++ b/solution.py
@@ -55,7 +55,7 @@
 LOG2E = 1.4426950408889634
 
 
-def score_kernel(slow, fast, protos, t_ref, col_ref, den_ref, ub_ref, cb_ref, raw_s, w_s, ct_s, den_s, sems):
+def score_kernel(slow, fast, protos, e_ref, col_ref, den_ref, ub_ref, cb_ref, raw_s, w_s, ct_s, den_s, sems):
     clips, feats = slow.shape
     count = protos.shape[0]
     loads = []
@@ -92,8 +92,9 @@
                 for q in range(0, 512, 64):
                     rows = pl.ds(r + q, 64)
                     t = jnp.exp2(s[q : q + 64] * (LOG2E / TEMPER))
-                    t_ref[v, rows, pl.ds(first, 256)] = t
-                    cols = cols + row_fold(t * t)
+                    e = t * t
+                    e_ref[v, rows, pl.ds(first, 256)] = e
+                    cols = cols + row_fold(e)
                     den_s[v, rows, :] += lane_sum(t)
             line = jnp.sum(cols, axis=0, keepdims=True)
             for h in range(2):
@@ -158,9 +159,9 @@
     )(ub)
 
 
-def row_kernel(protos_all, extra, t_ref, den_ref, *refs):
+def row_kernel(protos_all, extra, e_ref, den_ref, *refs):
     col_parts, (row_ref, r_ref, acc_s) = refs[:-3], refs[-3:]
-    clips, count = t_ref.shape[1:]
+    clips, count = e_ref.shape[1:]
     groups, lines = clips // LANES, count // LANES
     r_ref[...] = 1.0 / (float(protos_all) * sum_of(col_parts))
     if extra:
@@ -171,8 +172,8 @@
             rows = pl.ds(pl.multiple_of(i * LANES, LANES), LANES)
             acc = jnp.zeros((LANES, LANES), jnp.float32)
             for j in range(lines):
-                t = t_ref[v, rows, j * LANES : (j + 1) * LANES]
-                acc = acc + t * t * r_ref[v * lines + j : v * lines + j + 1, :]
+                e = e_ref[v, rows, j * LANES : (j + 1) * LANES]
+                acc = acc + e * r_ref[v * lines + j : v * lines + j + 1, :]
             acc_s[pl.ds(pl.multiple_of((v * groups + i) * LANES, LANES), LANES), :] = acc
             return 0
 
@@ -181,8 +182,8 @@
         row_ref[line : line + 1, :] = to_line(acc_s[line * LANES : (line + 1) * LANES, :])
 
 
-def row_pass(t, den, col_parts, protos_all, extra):
-    clips, count = t.shape[1:]
+def row_pass(e, den, col_parts, protos_all, extra):
+    clips, count = e.shape[1:]
     lines = 2 * clips // LANES * (2 if extra else 1)
     return pl.pallas_call(
         functools.partial(row_kernel, protos_all, extra),
@@ -195,12 +196,12 @@
         scratch_shapes=[pltpu.VMEM((2 * clips, LANES), jnp.float32)],
         compiler_params=params(8),
         name="row_pass",
-    )(pltpu.with_memory_space_constraint(t, pltpu.VMEM), den, *col_parts)
-
-
-def col_kernel(clips_all, t_ref, *refs):
+    )(pltpu.with_memory_space_constraint(e, pltpu.VMEM), den, *col_parts)
+
+
+def col_kernel(clips_all, e_ref, *refs):
     row_parts, (col_ref, acc_s, s_s) = refs[:-3], refs[-3:]
-    clips, count = t_ref.shape[1:]
+    clips, count = e_ref.shape[1:]
     groups, lines = clips // LANES, count // LANES
     scale = 1.0 / (float(clips_all) * sum_of(row_parts, 0, 2 * groups))
     for line in range(2 * groups):
@@ -213,8 +214,7 @@
             scale = s_s[pl.ds(pl.multiple_of((v * groups + i) * LANES, LANES), LANES), :]
             for j in range(lines):
                 span = slice(j * LANES, (j + 1) * LANES)
-                t = t_ref[v, rows, span]
-                acc_s[v, :, span] += row_fold(t * t * scale)
+                acc_s[v, :, span] += row_fold(e_ref[v, rows, span] * scale)
             return 0
 
         lax.fori_loop(0, groups, step, 0)
@@ -224,8 +224,8 @@
             )
 
 
-def col_pass(t, row_parts, clips_all):
-    clips, count = t.shape[1:]
+def col_pass(e, row_parts, clips_all):
+    clips, count = e.shape[1:]
     return pl.pallas_call(
         functools.partial(col_kernel, clips_all),
         out_shape=jax.ShapeDtypeStruct((2 * count // LANES, LANES), jnp.float32),
@@ -237,7 +237,7 @@
         ],
         compiler_params=params(8),
         name="col_pass",
-    )(pltpu.with_memory_space_constraint(t, pltpu.VMEM), *row_parts)
+    )(pltpu.with_memory_space_constraint(e, pltpu.VMEM), *row_parts)
 
 
 def piece_of(position, order):
@@ -255,11 +255,11 @@
     return which, pl.multiple_of(which * width, width)
 
 
-def proto_grads(ubt, chunk, orders, i, out_ref):
+def proto_grads(ubt, chunk, orders, i, oue_ref):
     dct = jnp.dot(ubt, chunk, preferred_element_type=jnp.float32)
     half = dct.shape[0] // 2
     for h in range(2):
-        out_ref[h, place_of(i, orders[h])] = dct[h * half : (h + 1) * half]
+        oue_ref[h, place_of(i, orders[h])] = dct[h * half : (h + 1) * half]
 
 
 def prob_kernel(*refs):
@@ -285,10 +285,10 @@
     )(*den_parts)
 
 
-def send_kernel(orders, parts, t_ref, r_ref, ubt_ref, prob_s, *refs):
+def send_kernel(orders, parts, e_ref, r_ref, ubt_ref, prob_s, *refs):
     row_parts = refs[:parts]
     send_ref, g_ref, chunk_s, code_s = refs[parts:]
-    clips, count = t_ref.shape[1:]
+    clips, count = e_ref.shape[1:]
     groups, lines = clips // LANES, count // LANES
     pieces = 1 << len(orders[0])
     width = count // (2 * pieces)
@@ -305,9 +305,10 @@
             for h in range(width // LANES):
                 span = pl.ds(first + h * LANES, LANES)
                 line = which * (width // LANES) + h
-                t = [t_ref[v, rows, span] for v in range(2)]
+                e = [e_ref[v, rows, span] for v in range(2)]
+                t = [e[v] * lax.rsqrt(e[v]) for v in range(2)]
                 q = [
-                    t[v] * t[v] * r_ref[pl.ds(v * lines + line, 1), :] * codes[v]
+                    e[v] * r_ref[pl.ds(v * lines + line, 1), :] * codes[v]
                     for v in range(2)
                 ]
                 for v in range(2):
@@ -326,8 +327,8 @@
     lax.fori_loop(0, pieces, pair, 0)
 
 
-def send_gradients(t, r, ubt, prob, row_parts, orders):
-    clips, count = t.shape[1:]
+def send_gradients(e, r, ubt, prob, row_parts, orders):
+    clips, count = e.shape[1:]
     feats = ubt.shape[0]
     pieces = 1 << len(orders[0])
     width = count // (2 * pieces)
@@ -348,7 +349,7 @@
             flops=2 * clips * count * feats, bytes_accessed=20 * MIB, transcendentals=0
         ),
         name="send_gradients",
-    )(pltpu.with_memory_space_constraint(t, pltpu.VMEM), r, ubt, prob, *row_parts)
+    )(pltpu.with_memory_space_constraint(e, pltpu.VMEM), r, ubt, prob, *row_parts)
 
 
 def embed_grad_kernel(orders, g_ref, cb_ref, *outs):
@@ -660,20 +661,20 @@
     batch_bits, proto_bits = bits_of("batch"), bits_of("proto")
     me_batch, me_proto = lax.axis_index("batch"), lax.axis_index("proto")
 
-    t, col, den, unit_b, proto_b = scores(slow_embed, fast_embed, prototypes)
+    e, col, den, unit_b, proto_b = scores(slow_embed, fast_embed, prototypes)
     unit_bt = turned(unit_b)
     for iteration in range(ITERS):
-        rows, r = row_pass(t, den, batch_parts(col, iteration % 2), protos_all, iteration == 0)
+        rows, r = row_pass(e, den, batch_parts(col, iteration % 2), protos_all, iteration == 0)
         row_parts = proto_parts(rows)
         if iteration == 0:
             prob = prob_columns(row_parts)
         if iteration + 1 < ITERS:
-            col = col_pass(t, row_parts, clips_all)
+            col = col_pass(e, row_parts, clips_all)
 
     near = tuple(range(batch_bits - 1))
     batch_orders = (near, tuple(reversed(near)))
     proto_orders = (tuple(range(proto_bits)), tuple(reversed(range(proto_bits))))
-    send, g = send_gradients(t, r, unit_bt, prob, row_parts, batch_orders)
+    send, g = send_gradients(e, r, unit_bt, prob, row_parts, batch_orders)
     shares = embed_gradients(g, proto_b, proto_orders)
     keep = keep_gradients(g, unit_bt, shares[0], batch_orders)
 

time: 136 us -> 134 us (0.985)
  Pallas kernels: 33.6 us -> 31.1 us
    pallas_call x3, Pallas kernels: 6.82 us -> 5.33 us  [row_pass(): pl.pallas_call(functools.partial(row_kernel, protos_all, extra), out_shap...]
where the time goes in v14:
time: 134 us; the launch traced here: 133 us
  waiting for transfers between devices  54.8 us (41%)
  starting transfers between devices  44.7 us (33%)
  Pallas kernels  31.1 us (23%)
  local copies, waits for them, and re-layouts  1.99 us (1%)
    ppermute x44, waiting for transfers between devices, swap(): lax.ppermute(own, axis, [(i, i ^ mask) for i in range(lax.axis_size(axis))])  54.8 us
    ppermute x44, starting transfers between devices, swap(): lax.ppermute(own, axis, [(i, i ^ mask) for i in range(lax.axis_size(axis))])  44.7 us
    pallas_call x1, Pallas kernels, scores(): pl.pallas_call(score_kernel, out_shape=(pltpu.VMEM((2, clips, count), jnp...  7.7 us
    pallas_call x1, Pallas kernels, send_gradients(): pl.pallas_call(functools.partial(send_kernel, orders, len(row_parts)), ou...  6.67 us
    pallas_call x3, Pallas kernels, row_pass(): pl.pallas_call(functools.partial(row_kernel, protos_all, extra), out_shap...  5.33 us
    pallas_call x2, Pallas kernels, col_pass(): pl.pallas_call(functools.partial(col_kernel, clips_all), out_shape=jax.Sh...  3.33 us
  transfers between devices with their start and end apart: 44, of which 31 were waited for; matrix products, arithmetic and copies ran while one was open for 1% of the time, Pallas kernels for 4%

profile of v14, /device:TPU:0, one launch (start us, length us, event | category | flops | bytes accessed | tf_op | source)
XLA Modules:
  0.0 133.3 jit_solution(7209927111885005571)
XLA Ops:
  0.6 7.7 %scores.1 = (f32[2,1024,2048]{2,1,0:T(8,128)S(1)}, f32[32,128]{1,0:T(8,128)S(1)}, f32[16,128]{1,0:T(8,128)S(1)}, bf16[2,1024,256]{2,1,0:T(8,128)(2,1)S(1)}, bf16[2048,256]{1,0:T(8,128)(2,1)S(1)}) custom-call(bf16[1024,256]{1,0:T(8,128)(2,1)} %slow.1, bf16[1024,256]{1,0:T(8,128)(2,1)} %fast.1, f32[2048,256]{1,0:T(8,128)} %protos.1), custom_call_target="tpu_custom_call" | custom-call | tf_op jit(solution)/shard_map/scores/pallas_call | solution.py:116
  9.7 4.9 %collective-permute-start.1 = (f32[32,128]{1,0:T(8,128)S(1)}, f32[32,128]{1,0:T(8,128)S(1)}, u32[]{:S(2)}, u32[]{:S(2)}) collective-permute-start(f32[32,128]{1,0:T(8,128)S(1)} %add.18.refs_3_), channel_id=1, source_target_pairs={{0,24},{4,28},{8,16},{12,20},{16,8},{20,12},{24,0},{28,4},{1,25},{... | collective-permute-start | bytes 49160 | tf_op jit(solution)/shard_map/ppermute | solution.py:575
  16.4 2.9 %collective-permute-done.2.refs_1_ = f32[32,128]{1,0:T(8,128)S(1)} collective-permute-done((f32[32,128]{1,0:T(8,128)S(1)}, f32[32,128]{1,0:T(8,128)S(1)}, u32[]{:S(2)}, u32[]{:S(2)}) %collective-permute-start.2) | collective-permute-done | bytes 16416 | tf_op jit(solution)/shard_map/ppermute | solution.py:575
  19.3 1.9 %row_pass.3 = (f32[32,128]{1,0:T(8,128)S(1)}, f32[32,128]{1,0:T(8,128)}) custom-call(f32[2,1024,2048]{2,1,0:T(8,128)S(1)} %get-tuple-element.32.e_ref, f32[16,128]{1,0:T(8,128)S(1)} %get-tuple-element.33.den_ref, f32[32,128]{1,0:T(8,128)S(1)} %collective-permute-done.1.refs_0_, f32[32,128]{1,0:T(8,128)S(1)} %collective-permute-done.2.refs_1_, ...), custom_call_target="tpu_custom_call" | custom-call | tf_op jit(solution)/shard_map/row_pass/pallas_call | solution.py:188
  21.1 2.4 %collective-permute-start.4 = (f32[32,128]{1,0:T(8,128)S(1)}, f32[32,128]{1,0:T(8,128)S(1)}, u32[]{:S(2)}, u32[]{:S(2)}) collective-permute-start(f32[32,128]{1,0:T(8,128)S(1)} %get-tuple-element.35.refs_3_), channel_id=1, source_target_pairs={{0,3},{1,2},{2,1},{3,0},{4,7},{5,6},{6,5},{7,4},{8,11},{9,10},{10,... | collective-permute-start | bytes 49160 | tf_op jit(solution)/shard_map/ppermute | solution.py:575
  25.8 1.5 %collective-permute-done.5.refs_1_ = f32[32,128]{1,0:T(8,128)S(1)} collective-permute-done((f32[32,128]{1,0:T(8,128)S(1)}, f32[32,128]{1,0:T(8,128)S(1)}, u32[]{:S(2)}, u32[]{:S(2)}) %collective-permute-start.5) | collective-permute-done | bytes 16416 | tf_op jit(solution)/shard_map/ppermute | solution.py:575
  27.8 1.7 %col_pass.2 = f32[32,128]{1,0:T(8,128)S(1)} custom-call(f32[2,1024,2048]{2,1,0:T(8,128)S(1)} %get-tuple-element.32.e_ref, f32[32,128]{1,0:T(8,128)S(1)} %collective-permute-done.4.refs_0_, f32[32,128]{1,0:T(8,128)S(1)} %collective-permute-done.5.refs_1_, f32[32,128]{1,0:T(8,128)S(1)} %collective-permute-done.6.refs_2_, f32[32,128]{1,0:T(8,128)S(1)} %get-tuple-element.35.refs_3_), custom_call_target="tpu_custom_call" | custom-call | tf_op jit(solution)/shard_map/col_pass/pallas_call | solution.py:229
  32.9 2.3 %collective-permute-start.9 = (f32[32,128]{1,0:T(8,128)S(1)}, f32[32,128]{1,0:T(8,128)S(1)}, u32[]{:S(2)}, u32[]{:S(2)}) collective-permute-start(f32[32,128]{1,0:T(8,128)S(1)} %add.19.refs_3_), channel_id=1, source_target_pairs={{0,8},{4,12},{8,0},{12,4},{16,24},{20,28},{24,16},{28,20},{1,9},{5... | collective-permute-start | bytes 49160 | tf_op jit(solution)/shard_map/ppermute | solution.py:575
  37.0 1.9 %row_pass.4 = (f32[16,128]{1,0:T(8,128)S(1)}, f32[32,128]{1,0:T(8,128)}) custom-call(f32[2,1024,2048]{2,1,0:T(8,128)S(1)} %get-tuple-element.32.e_ref, f32[16,128]{1,0:T(8,128)S(1)} %get-tuple-element.33.den_ref, f32[32,128]{1,0:T(8,128)S(1)} %collective-permute-done.8.refs_0_, f32[32,128]{1,0:T(8,128)S(1)} %collective-permute-done.9.refs_1_, ...), custom_call_target="tpu_custom_call" | custom-call | tf_op jit(solution)/shard_map/row_pass/pallas_call | solution.py:188
  38.9 1.5 %collective-permute-start.11 = (f32[16,128]{1,0:T(8,128)S(1)}, f32[16,128]{1,0:T(8,128)S(1)}, u32[]{:S(2)}, u32[]{:S(2)}) collective-permute-start(f32[16,128]{1,0:T(8,128)S(1)} %get-tuple-element.36.refs_3_), channel_id=1, source_target_pairs={{0,3},{1,2},{2,1},{3,0},{4,7},{5,6},{6,5},{7,4},{8,11},{9,10},{10,... | collective-permute-start | bytes 24584 | tf_op jit(solution)/shard_map/ppermute | solution.py:575
  44.5 1.7 %col_pass.3 = f32[32,128]{1,0:T(8,128)S(1)} custom-call(f32[2,1024,2048]{2,1,0:T(8,128)S(1)} %get-tuple-element.32.e_ref, f32[16,128]{1,0:T(8,128)S(1)} %collective-permute-done.11.refs_0_, f32[16,128]{1,0:T(8,128)S(1)} %collective-permute-done.12.refs_1_, f32[16,128]{1,0:T(8,128)S(1)} %collective-permute-done.13.refs_2_, ...), custom_call_target="tpu_custom_call" | custom-call | tf_op jit(solution)/shard_map/col_pass/pallas_call | solution.py:229
  47.5 2.4 %collective-permute-start.15 = (f32[32,128]{1,0:T(8,128)S(1)}, f32[32,128]{1,0:T(8,128)S(1)}, u32[]{:S(2)}, u32[]{:S(2)}) collective-permute-start(f32[32,128]{1,0:T(8,128)S(1)} %add.20.refs_3_), channel_id=1, source_target_pairs={{0,24},{4,28},{8,16},{12,20},{16,8},{20,12},{24,0},{28,4},{1,25},{... | collective-permute-start | bytes 49160 | tf_op jit(solution)/shard_map/ppermute | solution.py:575
  54.7 1.6 %row_pass.5 = (f32[16,128]{1,0:T(8,128)S(1)}, f32[32,128]{1,0:T(8,128)S(1)}) custom-call(f32[2,1024,2048]{2,1,0:T(8,128)S(1)} %get-tuple-element.32.e_ref, f32[16,128]{1,0:T(8,128)S(1)} %get-tuple-element.33.den_ref, f32[32,128]{1,0:T(8,128)S(1)} %collective-permute-done.15.refs_0_, f32[32,128]{1,0:T(8,128)S(1)} %collective-permute-done.16.refs_1_, ...), custom_call_target="tpu_custom_call" | custom-call | tf_op jit(solution)/shard_map/row_pass/pallas_call | solution.py:188
  56.3 2.5 %collective-permute-start.18 = (f32[16,128]{1,0:T(8,128)S(1)}, f32[16,128]{1,0:T(8,128)S(1)}, u32[]{:S(2)}, u32[]{:S(2)}) collective-permute-start(f32[16,128]{1,0:T(8,128)S(1)} %get-tuple-element.39.refs_3_), channel_id=1, source_target_pairs={{0,3},{1,2},{2,1},{3,0},{4,7},{5,6},{6,5},{7,4},{8,11},{9,10},{10,... | collective-permute-start | bytes 24584 | tf_op jit(solution)/shard_map/ppermute | solution.py:575
  61.0 1.5 %collective-permute-done.19.refs_1_ = f32[16,128]{1,0:T(8,128)S(1)} collective-permute-done((f32[16,128]{1,0:T(8,128)S(1)}, f32[16,128]{1,0:T(8,128)S(1)}, u32[]{:S(2)}, u32[]{:S(2)}) %collective-permute-start.19) | collective-permute-done | bytes 8224 | tf_op jit(solution)/shard_map/ppermute | solution.py:575
  63.0 6.7 %send_gradients.1 = (f32[2,4,128,256]{3,2,1,0:T(8,128)S(1)}, bf16[2048,2048]{1,0:T(8,128)(2,1)S(1)}) custom-call(f32[2,1024,2048]{2,1,0:T(8,128)S(1)} %get-tuple-element.32.e_ref, f32[32,128]{1,0:T(8,128)S(1)} %get-tuple-element.37.r_ref, bf16[256,2048]{1,0:T(8,128)(2,1)S(1)} %turned.1.ubt_ref, f32[2048,128]{1,0:T(8,128)S(1)} %prob_columns.1.prob_s, ...), custom_call_target="tpu_custom_call" | custom-call | flops 1073741824 | bytes 20971520 | tf_op jit(solution)/shard_map/send_gradients/pallas_call | solution.py:335
  69.7 2.3 %embed_gradients.1 = (f32[2,256,256]{2,1,0:T(8,128)S(1)}, f32[2,256,256]{2,1,0:T(8,128)S(1)}, f32[2,256,256]{2,1,0:T(8,128)S(1)}, f32[2,256,256]{2,1,0:T(8,128)S(1)}) custom-call(bf16[2048,2048]{1,0:T(8,128)(2,1)S(1)} %get-tuple-element.40.g_ref, bf16[2048,256]{1,0:T(8,128)(2,1)S(1)} %get-tuple-element.41.cb_ref), custom_call_target="tpu_custom_call" | custom-call | flops 2147483648 | bytes 11534336 | tf_op jit(solution)/shard_map/embed_gradients/pallas_call | solution.py:374
  72.7 1.5 %collective-permute-start.27 = (f32[2,256,256]{2,1,0:T(8,128)S(1)}, f32[2,256,256]{2,1,0:T(8,128)S(1)}, u32[]{:S(2)}, u32[]{:S(2)}) collective-permute-start(f32[2,256,256]{2,1,0:T(8,128)S(1)} %get-tuple-element.54), channel_id=1, source_target_pairs={{0,2},{1,3},{2,0},{3,1},{4,6},{5,7},{6,4},{7,5},{8,10},{9,11},{10,... | collective-permute-start | bytes 1572872 | tf_op jit(solution)/shard_map/ppermute | solution.py:575
  74.2 1.9 %keep_gradients.1.refs_0_ = f32[2,4,128,256]{3,2,1,0:T(8,128)S(1)} custom-call(bf16[2048,2048]{1,0:T(8,128)(2,1)S(1)} %get-tuple-element.40.g_ref, bf16[256,2048]{1,0:T(8,128)(2,1)S(1)} %turned.1.ubt_ref, f32[2,256,256]{2,1,0:T(8,128)S(1)} %get-tuple-element.42.after_ref), custom_call_target="tpu_custom_call" | custom-call | flops 1073741824 | bytes 6291456 | tf_op jit(solution)/shard_map/keep_gradients/pallas_call | solution.py:403
  76.2 1.9 %collective-permute-start.22 = (f32[2,128,256]{2,1,0:T(8,128)S(1)}, f32[2,128,256]{2,1,0:T(8,128)S(1)}, u32[]{:S(2)}, u32[]{:S(2)}) collective-permute-start(f32[2,128,256]{2,1,0:T(8,128)S(1)} %get-tuple-element.45), channel_id=1, source_target_pairs={{0,16},{4,20},{8,24},{12,28},{16,0},{20,4},{24,8},{28,12},{1,17},{... | collective-permute-start | bytes 786440 | tf_op jit(solution)/shard_map/ppermute | solution.py:575
  78.3 8.2 %collective-permute-done.26.refs_1_ = f32[2,256,256]{2,1,0:T(8,128)S(1)} collective-permute-done((f32[2,256,256]{2,1,0:T(8,128)S(1)}, f32[2,256,256]{2,1,0:T(8,128)S(1)}, u32[]{:S(2)}, u32[]{:S(2)}) %collective-permute-start.26) | collective-permute-done | bytes 524320 | tf_op jit(solution)/shard_map/ppermute | solution.py:575
  86.8 1.6 %collective-permute-start.28 = (f32[1,256,256]{2,1,0:T(8,128)S(1)}, f32[1,256,256]{2,1,0:T(8,128)S(1)}, u32[]{:S(2)}, u32[]{:S(2)}) collective-permute-start(f32[1,256,256]{2,1,0:T(8,128)S(1)} %get-tuple-element.56), channel_id=1, source_target_pairs={{0,2},{1,3},{2,0},{3,1},{4,6},{5,7},{6,4},{7,5},{8,10},{9,11},{10,... | collective-permute-start | bytes 786440 | tf_op jit(solution)/shard_map/ppermute | solution.py:575
  88.4 1.5 %collective-permute-start.29 = (f32[1,256,256]{2,1,0:T(8,128)S(1)}, f32[1,256,256]{2,1,0:T(8,128)S(1)}, u32[]{:S(2)}, u32[]{:S(2)}) collective-permute-start(f32[1,256,256]{2,1,0:T(8,128)S(1)} %get-tuple-element.58), channel_id=1, source_target_pairs={{0,1},{1,0},{2,3},{3,2},{4,5},{5,4},{6,7},{7,6},{8,9},{9,8},{10,11... | collective-permute-start | bytes 786440 | tf_op jit(solution)/shard_map/ppermute | solution.py:575
  95.8 3.9 %collective-permute-done.24.refs_1_ = f32[1,128,256]{2,1,0:T(8,128)S(1)} collective-permute-done((f32[1,128,256]{2,1,0:T(8,128)S(1)}, f32[1,128,256]{2,1,0:T(8,128)S(1)}, u32[]{:S(2)}, u32[]{:S(2)}) %collective-permute-start.24) | collective-permute-done | bytes 131104 | tf_op jit(solution)/shard_map/ppermute | solution.py:575
  101.5 1.5 %collective-permute-start.40 = (f32[2,256,256]{2,1,0:T(8,128)S(1)}, f32[2,256,256]{2,1,0:T(8,128)S(1)}, u32[]{:S(2)}, u32[]{:S(2)}) collective-permute-start(f32[2,256,256]{2,1,0:T(8,128)S(1)} %get-tuple-element.60.refs_12_), channel_id=1, source_target_pairs={{0,1},{1,0},{2,3},{3,2},{4,5},{5,4},{6,7},{7,6},{8,9},{9,8},{10,11... | collective-permute-start | bytes 1572872 | tf_op jit(solution)/shard_map/ppermute | solution.py:575
  104.1 9.5 %collective-permute-done.33.refs_4_.refs_8_ = f32[264,256]{1,0:T(8,128)S(1)} collective-permute-done((f32[264,256]{1,0:T(8,128)S(1)}, f32[264,256]{1,0:T(8,128)S(1)}, u32[]{:S(2)}, u32[]{:S(2)}) %collective-permute-start.33) | collective-permute-done | bytes 270368 | tf_op jit(solution)/shard_map/ppermute | solution.py:575
  113.6 2.3 %collective-permute-done.31.refs_2_.refs_6_ = f32[264,256]{1,0:T(8,128)S(1)} collective-permute-done((f32[264,256]{1,0:T(8,128)S(1)}, f32[264,256]{1,0:T(8,128)S(1)}, u32[]{:S(2)}, u32[]{:S(2)}) %collective-permute-start.31) | collective-permute-done | bytes 270368 | tf_op jit(solution)/shard_map/ppermute | solution.py:575
  117.1 4.9 %collective-permute-done.35.refs_6_.refs_10_ = f32[264,256]{1,0:T(8,128)S(1)} collective-permute-done((f32[264,256]{1,0:T(8,128)S(1)}, f32[264,256]{1,0:T(8,128)S(1)}, u32[]{:S(2)}, u32[]{:S(2)}) %collective-permute-start.35) | collective-permute-done | bytes 270368 | tf_op jit(solution)/shard_map/ppermute | solution.py:575
  122.0 1.5 %collective-permute-start.43 = (f32[256,256]{1,0:T(8,128)S(1)}, f32[256,256]{1,0:T(8,128)S(1)}, u32[]{:S(2)}, u32[]{:S(2)}) collective-permute-start(f32[256,256]{1,0:T(8,128)S(1)} %slice_bitcast_fusion), channel_id=1, source_target_pairs={{0,2},{1,3},{2,0},{3,1},{4,6},{5,7},{6,4},{7,5},{8,10},{9,11},{10,... | collective-permute-start | bytes 786440 | tf_op jit(solution)/shard_map/ppermute | solution.py:575
  123.5 2.4 %collective-permute-start.37 = (f32[2,8,128]{2,1,0:T(8,128)S(1)}, f32[2,8,128]{2,1,0:T(8,128)S(1)}, u32[]{:S(2)}, u32[]{:S(2)}) collective-permute-start(f32[2,8,128]{2,1,0:T(8,128)S(1)} %sum_squares.1.refs_3_), channel_id=1, source_target_pairs={{0,3},{1,2},{2,1},{3,0},{4,7},{5,6},{6,5},{7,4},{8,11},{9,10},{10,... | collective-permute-start | bytes 24584 | tf_op jit(solution)/shard_map/ppermute | solution.py:575
  127.1 3.9 %collective-permute-done.43.refs_16_ = f32[256,256]{1,0:T(8,128)S(1)} collective-permute-done((f32[256,256]{1,0:T(8,128)S(1)}, f32[256,256]{1,0:T(8,128)S(1)}, u32[]{:S(2)}, u32[]{:S(2)}) %collective-permute-start.43) | collective-permute-done | bytes 262176 | tf_op jit(solution)/shard_map/ppermute | solution.py:575
  131.1 2.2 %finish.1 = (f32[2048,256]{1,0:T(8,128)}, f32[1024,256]{1,0:T(8,128)}, f32[1024,256]{1,0:T(8,128)}) custom-call(f32[2,8,128]{2,1,0:T(8,128)S(1)} %collective-permute-done.37.refs_0_, f32[2,8,128]{2,1,0:T(8,128)S(1)} %collective-permute-done.38.refs_1_, f32[2,8,128]{2,1,0:T(8,128)S(1)} %collective-permute-done.39.refs_2_, ...), custom_call_target="tpu_custom_call" | custom-call | tf_op jit(solution)/shard_map/finish/pallas_call | solution.py:563
  (80 shorter events, 36.3 us)
Async XLA Ops:
  9.7 6.7 %collective-permute-start.1 = (f32[32,128]{1,0:T(8,128)S(1)}, f32[32,128]{1,0:T(8,128)S(1)}, u32[]{:S(2)}, u32[]{:S(2)}) collective-permute-start(f32[32,128]{1,0:T(8,128)S(1)} %add.18.refs_3_), channel_id=1, source_target_pairs={{0,24},{4,28},{8,16},{12,20},{16,8},{20,12},{24,0},{28,4},{1,25},{... | collective-permute-start | bytes 49160 | tf_op jit(solution)/shard_map/ppermute | solution.py:575
  14.6 4.6 %collective-permute-start.2 = (f32[32,128]{1,0:T(8,128)S(1)}, f32[32,128]{1,0:T(8,128)S(1)}, u32[]{:S(2)}, u32[]{:S(2)}) collective-permute-start(f32[32,128]{1,0:T(8,128)S(1)} %add.18.refs_3_), channel_id=1, source_target_pairs={{0,16},{4,20},{8,24},{12,28},{16,0},{20,4},{24,8},{28,12},{1,17},{... | collective-permute-start | bytes 49160 | tf_op jit(solution)/shard_map/ppermute | solution.py:575
  14.6 4.6 %collective-permute-start.3 = (f32[32,128]{1,0:T(8,128)S(1)}, f32[32,128]{1,0:T(8,128)S(1)}, u32[]{:S(2)}, u32[]{:S(2)}) collective-permute-start(f32[32,128]{1,0:T(8,128)S(1)} %add.18.refs_3_), channel_id=1, source_target_pairs={{0,8},{4,12},{8,0},{12,4},{16,24},{20,28},{24,16},{28,20},{1,9},{5... | collective-permute-start | bytes 49160 | tf_op jit(solution)/shard_map/ppermute | solution.py:575
  21.1 4.6 %collective-permute-start.4 = (f32[32,128]{1,0:T(8,128)S(1)}, f32[32,128]{1,0:T(8,128)S(1)}, u32[]{:S(2)}, u32[]{:S(2)}) collective-permute-start(f32[32,128]{1,0:T(8,128)S(1)} %get-tuple-element.35.refs_3_), channel_id=1, source_target_pairs={{0,3},{1,2},{2,1},{3,0},{4,7},{5,6},{6,5},{7,4},{8,11},{9,10},{10,... | collective-permute-start | bytes 49160 | tf_op jit(solution)/shard_map/ppermute | solution.py:575
  30.8 5.7 %collective-permute-start.10 = (f32[32,128]{1,0:T(8,128)S(1)}, f32[32,128]{1,0:T(8,128)S(1)}, u32[]{:S(2)}, u32[]{:S(2)}) collective-permute-start(f32[32,128]{1,0:T(8,128)S(1)} %add.19.refs_3_), channel_id=1, source_target_pairs={{0,24},{4,28},{8,16},{12,20},{16,8},{20,12},{24,0},{28,4},{1,25},{... | collective-permute-start | bytes 49160 | tf_op jit(solution)/shard_map/ppermute | solution.py:575
  32.2 4.7 %collective-permute-start.8 = (f32[32,128]{1,0:T(8,128)S(1)}, f32[32,128]{1,0:T(8,128)S(1)}, u32[]{:S(2)}, u32[]{:S(2)}) collective-permute-start(f32[32,128]{1,0:T(8,128)S(1)} %add.19.refs_3_), channel_id=1, source_target_pairs={{0,16},{4,20},{8,24},{12,28},{16,0},{20,4},{24,8},{28,12},{1,17},{... | collective-permute-start | bytes 49160 | tf_op jit(solution)/shard_map/ppermute | solution.py:575
  38.9 4.5 %collective-permute-start.11 = (f32[16,128]{1,0:T(8,128)S(1)}, f32[16,128]{1,0:T(8,128)S(1)}, u32[]{:S(2)}, u32[]{:S(2)}) collective-permute-start(f32[16,128]{1,0:T(8,128)S(1)} %get-tuple-element.36.refs_3_), channel_id=1, source_target_pairs={{0,3},{1,2},{2,1},{3,0},{4,7},{5,6},{6,5},{7,4},{8,11},{9,10},{10,... | collective-permute-start | bytes 24584 | tf_op jit(solution)/shard_map/ppermute | solution.py:575
  47.5 5.6 %collective-permute-start.15 = (f32[32,128]{1,0:T(8,128)S(1)}, f32[32,128]{1,0:T(8,128)S(1)}, u32[]{:S(2)}, u32[]{:S(2)}) collective-permute-start(f32[32,128]{1,0:T(8,128)S(1)} %add.20.refs_3_), channel_id=1, source_target_pairs={{0,24},{4,28},{8,16},{12,20},{16,8},{20,12},{24,0},{28,4},{1,25},{... | collective-permute-start | bytes 49160 | tf_op jit(solution)/shard_map/ppermute | solution.py:575
  49.9 4.7 %collective-permute-start.16 = (f32[32,128]{1,0:T(8,128)S(1)}, f32[32,128]{1,0:T(8,128)S(1)}, u32[]{:S(2)}, u32[]{:S(2)}) collective-permute-start(f32[32,128]{1,0:T(8,128)S(1)} %add.20.refs_3_), channel_id=1, source_target_pairs={{0,16},{4,20},{8,24},{12,28},{16,0},{20,4},{24,8},{28,12},{1,17},{... | collective-permute-start | bytes 49160 | tf_op jit(solution)/shard_map/ppermute | solution.py:575
  56.3 4.7 %collective-permute-start.18 = (f32[16,128]{1,0:T(8,128)S(1)}, f32[16,128]{1,0:T(8,128)S(1)}, u32[]{:S(2)}, u32[]{:S(2)}) collective-permute-start(f32[16,128]{1,0:T(8,128)S(1)} %get-tuple-element.39.refs_3_), channel_id=1, source_target_pairs={{0,3},{1,2},{2,1},{3,0},{4,7},{5,6},{6,5},{7,4},{8,11},{9,10},{10,... | collective-permute-start | bytes 24584 | tf_op jit(solution)/shard_map/ppermute | solution.py:575
  69.7 6.4 %collective-permute-start.21 = (f32[2,4,128,256]{3,2,1,0:T(8,128)S(1)}, f32[2,4,128,256]{3,2,1,0:T(8,128)S(1)}, u32[]{:S(2)}, u32[]{:S(2)}) collective-permute-start(f32[2,4,128,256]{3,2,1,0:T(8,128)S(1)} %get-tuple-element.43), channel_id=1, source_target_pairs={{0,4},{4,0},{8,12},{12,8},{16,20},{20,16},{24,28},{28,24},{1,5},{5... | collective-permute-start | bytes 3145736 | tf_op jit(solution)/shard_map/ppermute | solution.py:575
  72.1 14.4 %collective-permute-start.26 = (f32[2,256,256]{2,1,0:T(8,128)S(1)}, f32[2,256,256]{2,1,0:T(8,128)S(1)}, u32[]{:S(2)}, u32[]{:S(2)}) collective-permute-start(f32[2,256,256]{2,1,0:T(8,128)S(1)} %get-tuple-element.42.after_ref), channel_id=1, source_target_pairs={{0,1},{1,0},{2,3},{3,2},{4,5},{5,4},{6,7},{7,6},{8,9},{9,8},{10,11... | collective-permute-start | bytes 1572872 | tf_op jit(solution)/shard_map/ppermute | solution.py:575
  72.7 14.0 %collective-permute-start.27 = (f32[2,256,256]{2,1,0:T(8,128)S(1)}, f32[2,256,256]{2,1,0:T(8,128)S(1)}, u32[]{:S(2)}, u32[]{:S(2)}) collective-permute-start(f32[2,256,256]{2,1,0:T(8,128)S(1)} %get-tuple-element.54), channel_id=1, source_target_pairs={{0,2},{1,3},{2,0},{3,1},{4,6},{5,7},{6,4},{7,5},{8,10},{9,11},{10,... | collective-permute-start | bytes 1572872 | tf_op jit(solution)/shard_map/ppermute | solution.py:575
  76.2 14.8 %collective-permute-start.22 = (f32[2,128,256]{2,1,0:T(8,128)S(1)}, f32[2,128,256]{2,1,0:T(8,128)S(1)}, u32[]{:S(2)}, u32[]{:S(2)}) collective-permute-start(f32[2,128,256]{2,1,0:T(8,128)S(1)} %get-tuple-element.45), channel_id=1, source_target_pairs={{0,16},{4,20},{8,24},{12,28},{16,0},{20,4},{24,8},{28,12},{1,17},{... | collective-permute-start | bytes 786440 | tf_op jit(solution)/shard_map/ppermute | solution.py:575
  78.1 13.0 %collective-permute-start.23 = (f32[2,128,256]{2,1,0:T(8,128)S(1)}, f32[2,128,256]{2,1,0:T(8,128)S(1)}, u32[]{:S(2)}, u32[]{:S(2)}) collective-permute-start(f32[2,128,256]{2,1,0:T(8,128)S(1)} %get-tuple-element.47), channel_id=1, source_target_pairs={{0,8},{4,12},{8,0},{12,4},{16,24},{20,28},{24,16},{28,20},{1,9},{5... | collective-permute-start | bytes 786440 | tf_op jit(solution)/shard_map/ppermute | solution.py:575
  86.8 8.2 %collective-permute-start.28 = (f32[1,256,256]{2,1,0:T(8,128)S(1)}, f32[1,256,256]{2,1,0:T(8,128)S(1)}, u32[]{:S(2)}, u32[]{:S(2)}) collective-permute-start(f32[1,256,256]{2,1,0:T(8,128)S(1)} %get-tuple-element.56), channel_id=1, source_target_pairs={{0,2},{1,3},{2,0},{3,1},{4,6},{5,7},{6,4},{7,5},{8,10},{9,11},{10,... | collective-permute-start | bytes 786440 | tf_op jit(solution)/shard_map/ppermute | solution.py:575
  88.4 7.4 %collective-permute-start.29 = (f32[1,256,256]{2,1,0:T(8,128)S(1)}, f32[1,256,256]{2,1,0:T(8,128)S(1)}, u32[]{:S(2)}, u32[]{:S(2)}) collective-permute-start(f32[1,256,256]{2,1,0:T(8,128)S(1)} %get-tuple-element.58), channel_id=1, source_target_pairs={{0,1},{1,0},{2,3},{3,2},{4,5},{5,4},{6,7},{7,6},{8,9},{9,8},{10,11... | collective-permute-start | bytes 786440 | tf_op jit(solution)/shard_map/ppermute | solution.py:575
  91.2 8.5 %collective-permute-start.24 = (f32[1,128,256]{2,1,0:T(8,128)S(1)}, f32[1,128,256]{2,1,0:T(8,128)S(1)}, u32[]{:S(2)}, u32[]{:S(2)}) collective-permute-start(f32[1,128,256]{2,1,0:T(8,128)S(1)} %get-tuple-element.49), channel_id=1, source_target_pairs={{0,16},{4,20},{8,24},{12,28},{16,0},{20,4},{24,8},{28,12},{1,17},{... | collective-permute-start | bytes 393224 | tf_op jit(solution)/shard_map/ppermute | solution.py:575
  92.0 7.7 %collective-permute-start.25 = (f32[1,128,256]{2,1,0:T(8,128)S(1)}, f32[1,128,256]{2,1,0:T(8,128)S(1)}, u32[]{:S(2)}, u32[]{:S(2)}) collective-permute-start(f32[1,128,256]{2,1,0:T(8,128)S(1)} %get-tuple-element.51), channel_id=1, source_target_pairs={{0,8},{4,12},{8,0},{12,4},{16,24},{20,28},{24,16},{28,20},{1,9},{5... | collective-permute-start | bytes 393224 | tf_op jit(solution)/shard_map/ppermute | solution.py:575
  100.4 15.5 %collective-permute-start.41 = (f32[2,256,256]{2,1,0:T(8,128)S(1)}, f32[2,256,256]{2,1,0:T(8,128)S(1)}, u32[]{:S(2)}, u32[]{:S(2)}) collective-permute-start(f32[2,256,256]{2,1,0:T(8,128)S(1)} %get-tuple-element.60.refs_12_), channel_id=1, source_target_pairs={{0,2},{1,3},{2,0},{3,1},{4,6},{5,7},{6,4},{7,5},{8,10},{9,11},{10,... | collective-permute-start | bytes 1572872 | tf_op jit(solution)/shard_map/ppermute | solution.py:575
  100.9 12.7 %collective-permute-start.33 = (f32[264,256]{1,0:T(8,128)S(1)}, f32[264,256]{1,0:T(8,128)S(1)}, u32[]{:S(2)}, u32[]{:S(2)}) collective-permute-start(f32[264,256]{1,0:T(8,128)S(1)} %get-tuple-element.59.refs_0_.refs_4_), channel_id=1, source_target_pairs={{0,16},{4,20},{8,24},{12,28},{16,0},{20,4},{24,8},{28,12},{1,17},{... | collective-permute-start | bytes 811016 | tf_op jit(solution)/shard_map/ppermute | solution.py:575
  101.5 15.0 %collective-permute-start.40 = (f32[2,256,256]{2,1,0:T(8,128)S(1)}, f32[2,256,256]{2,1,0:T(8,128)S(1)}, u32[]{:S(2)}, u32[]{:S(2)}) collective-permute-start(f32[2,256,256]{2,1,0:T(8,128)S(1)} %get-tuple-element.60.refs_12_), channel_id=1, source_target_pairs={{0,1},{1,0},{2,3},{3,2},{4,5},{5,4},{6,7},{7,6},{8,9},{9,8},{10,11... | collective-permute-start | bytes 1572872 | tf_op jit(solution)/shard_map/ppermute | solution.py:575
  103.0 12.9 %collective-permute-start.31 = (f32[264,256]{1,0:T(8,128)S(1)}, f32[264,256]{1,0:T(8,128)S(1)}, u32[]{:S(2)}, u32[]{:S(2)}) collective-permute-start(f32[264,256]{1,0:T(8,128)S(1)} %get-tuple-element.59.refs_0_.refs_4_), channel_id=1, source_target_pairs={{0,8},{4,12},{8,0},{12,4},{16,24},{20,28},{24,16},{28,20},{1,9},{5... | collective-permute-start | bytes 811016 | tf_op jit(solution)/shard_map/ppermute | solution.py:575
  113.6 8.3 %collective-permute-start.35 = (f32[264,256]{1,0:T(8,128)S(1)}, f32[264,256]{1,0:T(8,128)S(1)}, u32[]{:S(2)}, u32[]{:S(2)}) collective-permute-start(f32[264,256]{1,0:T(8,128)S(1)} %collective-permute-done.33.refs_4_.refs_8_), channel_id=1, source_target_pairs={{0,8},{4,12},{8,0},{12,4},{16,24},{20,28},{24,16},{28,20},{1,9},{5... | collective-permute-start | bytes 811016 | tf_op jit(solution)/shard_map/ppermute | solution.py:575
  113.6 8.4 %collective-permute-start.30 = (f32[264,256]{1,0:T(8,128)S(1)}, f32[264,256]{1,0:T(8,128)S(1)}, u32[]{:S(2)}, u32[]{:S(2)}) collective-permute-start(f32[264,256]{1,0:T(8,128)S(1)} %get-tuple-element.59.refs_0_.refs_4_), channel_id=1, source_target_pairs={{0,4},{4,0},{8,12},{12,8},{16,20},{20,16},{24,28},{28,24},{1,5},{5... | collective-permute-start | bytes 811016 | tf_op jit(solution)/shard_map/ppermute | solution.py:575
  115.9 7.6 %collective-permute-start.34 = (f32[264,256]{1,0:T(8,128)S(1)}, f32[264,256]{1,0:T(8,128)S(1)}, u32[]{:S(2)}, u32[]{:S(2)}) collective-permute-start(f32[264,256]{1,0:T(8,128)S(1)} %collective-permute-done.33.refs_4_.refs_8_), channel_id=1, source_target_pairs={{0,4},{4,0},{8,12},{12,8},{16,20},{20,16},{24,28},{28,24},{1,5},{5... | collective-permute-start | bytes 811016 | tf_op jit(solution)/shard_map/ppermute | solution.py:575
  115.9 7.6 %collective-permute-start.32 = (f32[264,256]{1,0:T(8,128)S(1)}, f32[264,256]{1,0:T(8,128)S(1)}, u32[]{:S(2)}, u32[]{:S(2)}) collective-permute-start(f32[264,256]{1,0:T(8,128)S(1)} %collective-permute-done.31.refs_2_.refs_6_), channel_id=1, source_target_pairs={{0,4},{4,0},{8,12},{12,8},{16,20},{20,16},{24,28},{28,24},{1,5},{5... | collective-permute-start | bytes 811016 | tf_op jit(solution)/shard_map/ppermute | solution.py:575
  116.4 10.6 %collective-permute-start.42 = (f32[256,256]{1,0:T(8,128)S(1)}, f32[256,256]{1,0:T(8,128)S(1)}, u32[]{:S(2)}, u32[]{:S(2)}) collective-permute-start(f32[256,256]{1,0:T(8,128)S(1)} %slice_bitcast_fusion.1), channel_id=1, source_target_pairs={{0,1},{1,0},{2,3},{3,2},{4,5},{5,4},{6,7},{7,6},{8,9},{9,8},{10,11... | collective-permute-start | bytes 786440 | tf_op jit(solution)/shard_map/ppermute | solution.py:575
  122.0 9.0 %collective-permute-start.43 = (f32[256,256]{1,0:T(8,128)S(1)}, f32[256,256]{1,0:T(8,128)S(1)}, u32[]{:S(2)}, u32[]{:S(2)}) collective-permute-start(f32[256,256]{1,0:T(8,128)S(1)} %slice_bitcast_fusion), channel_id=1, source_target_pairs={{0,2},{1,3},{2,0},{3,1},{4,6},{5,7},{6,4},{7,5},{8,10},{9,11},{10,... | collective-permute-start | bytes 786440 | tf_op jit(solution)/shard_map/ppermute | solution.py:575
  123.5 7.5 %collective-permute-start.37 = (f32[2,8,128]{2,1,0:T(8,128)S(1)}, f32[2,8,128]{2,1,0:T(8,128)S(1)}, u32[]{:S(2)}, u32[]{:S(2)}) collective-permute-start(f32[2,8,128]{2,1,0:T(8,128)S(1)} %sum_squares.1.refs_3_), channel_id=1, source_target_pairs={{0,3},{1,2},{2,1},{3,0},{4,7},{5,6},{6,5},{7,4},{8,11},{9,10},{10,... | collective-permute-start | bytes 24584 | tf_op jit(solution)/shard_map/ppermute | solution.py:575
  126.0 5.2 %collective-permute-start.38 = (f32[2,8,128]{2,1,0:T(8,128)S(1)}, f32[2,8,128]{2,1,0:T(8,128)S(1)}, u32[]{:S(2)}, u32[]{:S(2)}) collective-permute-start(f32[2,8,128]{2,1,0:T(8,128)S(1)} %sum_squares.1.refs_3_), channel_id=1, source_target_pairs={{0,2},{1,3},{2,0},{3,1},{4,6},{5,7},{6,4},{7,5},{8,10},{9,11},{10,... | collective-permute-start | bytes 24584 | tf_op jit(solution)/shard_map/ppermute | solution.py:575
  126.6 4.6 %collective-permute-start.39 = (f32[2,8,128]{2,1,0:T(8,128)S(1)}, f32[2,8,128]{2,1,0:T(8,128)S(1)}, u32[]{:S(2)}, u32[]{:S(2)}) collective-permute-start(f32[2,8,128]{2,1,0:T(8,128)S(1)} %sum_squares.1.refs_3_), channel_id=1, source_target_pairs={{0,1},{1,0},{2,3},{3,2},{4,5},{5,4},{6,7},{7,6},{8,9},{9,8},{10,11... | collective-permute-start | bytes 24584 | tf_op jit(solution)/shard_map/ppermute | solution.py:575
  (12 other events, 35.6 us)
